TPU v7x, 128 devices: a whole 4x4x4 slice. The times are simulated.
128 devices in a mesh: group: 8 (over x_lo, z), tp: 16 (over x_hi, y, core).
Axes of the slice: x: 4 (x_hi: 2, x_lo: 2; x = x_hi * 2 + x_lo), y: 4, z: 4, core: 2. Of those that a mesh axis runs over, the one named last changes fastest.
Arguments:
- layer_input: bfloat16 [8, 256, 8192], P('group', None, 'tp'), may hold values from -6 to 6
- query_weight: bfloat16 [8192, 4096], P(None, 'tp'), may hold values from -0.1875 to 0.1875
- kv_weight: bfloat16 [8192, 2048], P(None, 'tp'), may hold values from -0.1875 to 0.1875
- out_weight: bfloat16 [4096, 8192], P('tp'), may hold values from -0.125 to 0.125
- cache_keys: bfloat16 [8, 64, 4096, 128], P('group', None, 'tp'), may hold values from -480 to 480
- cache_values: bfloat16 [8, 64, 4096, 128], P('group', None, 'tp'), may hold values from -6 to 6
- lengths: int32 [8, 64], P('group'), may hold values from 1 to 512, as said below
- placement: int32 [16, 2], replicated, may hold values from 0 to 7, as said below
Outputs:
- projected: bfloat16 [8, 256, 8192], P('group', None, 'tp')
- incoming: bfloat16 [8, 4, 128, 256], P('group', None, 'tp')
Inputs may be any that keep to these rules, and one draw needn't show every extreme that they name: `lengths`: each group has a row of length 512. `placement`: column 0 is a decode group from 1 to 7 and column 1 a slot below 4; no two blocks share a group and slot; some group receives 4 blocks, and the group whose index is half of 8, rounded down, receives at least one.
All inputs are finite; a program needn't handle non-finite values.
Results may differ from a plain program's by a relative error of at most 0.03.
Values may be sent and summed in bfloat16 or wider, within the bound.
No kernel may reach another device: no remote copies, remote signals or barrier semaphores. Data moves between devices by JAX's collectives and lax.ppermute only.
A program may use at most 128 MiB of HBM per device.

v0:
```python
import jax
import jax.numpy as jnp
from jax import lax
from jax.sharding import PartitionSpec as P

HD = 128
KVH = 8
STEPS = 4
NPR = 2
BS = 16
R = 64
GQ = 4
TOK = 256
CH = 128
RP = 32


NEG_FILL = -1e30


def as_sent(shard):
    return jax.tree.map(lambda a: a.astype(jnp.bfloat16) if a.dtype == jnp.float32 else a, shard)


def swapped(shard, axis, distance):
    return lax.ppermute(shard, axis, [(i, i ^ 1 << distance) for i in range(lax.axis_size(axis))])


def rotate(values, positions):
    midpoint = values.shape[-1] // 2
    frequency = jnp.exp(
        -jnp.log(500000.0) * jnp.arange(midpoint, dtype=jnp.float32) * 2.0 / values.shape[-1]
    )
    angles = positions.astype(jnp.float32)[:, None] * frequency[None, :]
    cosine = jnp.cos(angles)[:, None, :]
    sine_term = jnp.sin(angles)[:, None, :]
    first = values[..., :midpoint]
    second = values[..., midpoint:]
    return jnp.concatenate(
        [first * cosine - second * sine_term, second * cosine + first * sine_term], axis=-1
    )


def partial_block(
    query_vectors, key_row_block, value_rows, present, fresh_keys, new_values, new_allowed
):
    score_scale = key_row_block.shape[-1] ** (-0.5)
    cached = (
        jnp.einsum("jwt,jrt->jwr", query_vectors, key_row_block, preferred_element_type=jnp.float32)
        * score_scale
    )
    recent = (
        jnp.einsum("jwt,jrt->jwr", query_vectors, fresh_keys, preferred_element_type=jnp.float32)
        * score_scale
    )
    cached_mask = jnp.broadcast_to(present[:, None, :], cached.shape)
    recent_mask = jnp.broadcast_to(new_allowed[None], recent.shape)
    cached = jnp.where(cached_mask, cached, NEG_FILL)
    recent = jnp.where(recent_mask, recent, NEG_FILL)
    largest = jnp.maximum(jnp.max(cached, axis=2), jnp.max(recent, axis=2))
    cached_weights = jnp.where(cached_mask, jnp.exp(cached - largest[..., None]), 0.0)
    recent_weights = jnp.where(recent_mask, jnp.exp(recent - largest[..., None]), 0.0)
    summed = jnp.sum(cached_weights, axis=2) + jnp.sum(recent_weights, axis=2)
    mixed = jnp.einsum(
        "ciz,czm->cim",
        cached_weights.astype(jnp.bfloat16),
        value_rows,
        preferred_element_type=jnp.float32,
    )
    mixed = mixed + jnp.einsum(
        "ciz,czm->cim",
        recent_weights.astype(jnp.bfloat16),
        new_values,
        preferred_element_type=jnp.float32,
    )
    return (largest, summed, mixed)


def combine(first, second):
    largest = jnp.maximum(first[0], second[0])
    first_scale = jnp.exp(first[0] - largest)
    second_scale = jnp.exp(second[0] - largest)
    summed = first[1] * first_scale + second[1] * second_scale
    mixed = first[2] * first_scale[..., None] + second[2] * second_scale[..., None]
    return (largest, summed, mixed)


def on_device(
    layer_input, query_weight, kv_weight, out_weight, cache_keys, cache_values, lengths, placement
):
    tp_count = lax.axis_size("tp")
    group_count = lax.axis_size("group")
    splits = tp_count // KVH
    tp_rank = lax.axis_index("tp")
    group_rank = lax.axis_index("group")
    kv_head = tp_rank // splits
    block_index = tp_rank % splits
    last_block = block_index == splits - 1
    is_prefill = group_rank == 0
    tokens = layer_input[0]
    row_lengths = lengths[0]
    query_count = query_weight.shape[1] // HD
    pair_count = kv_weight.shape[1] // HD
    kv_width = KVH * HD
    prefix = jnp.sum(row_lengths.reshape(NPR, RP), axis=1)
    prompt_positions = (prefix[:, None] + jnp.arange(CH, dtype=jnp.int32)[None, :]).reshape(TOK)
    decode_step_positions = (
        row_lengths[None, :] + jnp.arange(STEPS, dtype=jnp.int32)[:, None]
    ).reshape(TOK)
    positions = jnp.where(is_prefill, prompt_positions, decode_step_positions)
    piece = lax.all_gather(tokens, "tp", axis=1, tiled=True)
    query_rows = query_weight
    query_part = jnp.dot(piece, query_rows, preferred_element_type=jnp.float32)
    pair_part = jnp.dot(piece, kv_weight, preferred_element_type=jnp.float32)
    query_local = (
        rotate(query_part.reshape(TOK, query_count, HD), positions)
        .astype(jnp.bfloat16)
        .reshape(TOK, query_count * HD)
    )
    pair_split = pair_part.reshape(TOK, pair_count, HD)
    head_numbers = tp_rank * pair_count + jnp.arange(pair_count, dtype=jnp.int32)
    pair_rotated = jnp.where(
        (head_numbers < KVH)[None, :, None], rotate(pair_split, positions), pair_split
    ).astype(jnp.bfloat16)
    group_width = GQ * HD
    pair_local = pair_rotated.reshape(TOK, pair_count * HD)
    query_all, pair_all = (
        lax.all_gather(query_local, "tp", axis=1, tiled=True),
        lax.all_gather(pair_local, "tp", axis=1, tiled=True),
    )
    my_queries = lax.dynamic_slice_in_dim(query_all, kv_head * group_width, group_width, 1).reshape(
        TOK, GQ, HD
    )
    my_keys = lax.dynamic_slice_in_dim(pair_all, kv_head * HD, HD, 1)
    my_values = lax.dynamic_slice_in_dim(pair_all, kv_width + kv_head * HD, HD, 1)
    local_keys = cache_keys[0]
    local_values = cache_values[0]
    span = local_keys.shape[1]
    present = (block_index * span + jnp.arange(span, dtype=jnp.int32))[None, :] < row_lengths[
        :, None
    ]

    def prefill_part():
        prompt_queries = my_queries.reshape(NPR, CH * GQ, HD)
        prompt_keys = local_keys.reshape(NPR, RP * span, HD)
        prompt_values = local_values.reshape(NPR, RP * span, HD)
        prompt_present = present.reshape(NPR, RP * span)
        stretch_keys = my_keys.reshape(NPR, CH, HD)
        stretch_values = my_values.reshape(NPR, CH, HD)
        query_rows = jnp.arange(CH * GQ, dtype=jnp.int32) // GQ
        new_allowed = (jnp.arange(CH, dtype=jnp.int32)[None, :] <= query_rows[:, None]) & last_block

        def one_prompt(operands):
            return partial_block(
                operands[0][None],
                operands[1][None],
                operands[2][None],
                operands[3][None],
                operands[4][None],
                operands[5][None],
                new_allowed,
            )

        largest, summed, mixed = lax.map(
            one_prompt,
            (
                prompt_queries,
                prompt_keys,
                prompt_values,
                prompt_present,
                stretch_keys,
                stretch_values,
            ),
        )
        return (largest.reshape(TOK, GQ), summed.reshape(TOK, GQ), mixed.reshape(TOK, GQ, HD))

    def decode_part():
        row_queries = (
            my_queries.reshape(STEPS, R, GQ, HD).transpose(1, 0, 2, 3).reshape(R, STEPS * GQ, HD)
        )
        step_keys = my_keys.reshape(STEPS, R, HD).transpose(1, 0, 2)
        step_values = my_values.reshape(STEPS, R, HD).transpose(1, 0, 2)
        query_rows = jnp.arange(STEPS * GQ, dtype=jnp.int32) // GQ
        new_allowed = (
            jnp.arange(STEPS, dtype=jnp.int32)[None, :] <= query_rows[:, None]
        ) & last_block
        largest, summed, mixed = partial_block(
            row_queries, local_keys, local_values, present, step_keys, step_values, new_allowed
        )
        largest = largest.reshape(R, STEPS, GQ).transpose(1, 0, 2).reshape(TOK, GQ)
        summed = summed.reshape(R, STEPS, GQ).transpose(1, 0, 2).reshape(TOK, GQ)
        mixed = mixed.reshape(R, STEPS, GQ, HD).transpose(1, 0, 2, 3).reshape(TOK, GQ, HD)
        return (largest, summed, mixed)

    state = lax.cond(is_prefill, prefill_part, decode_part)
    partner = jax.tree.map(
        lambda part, own: part.astype(own.dtype), swapped(as_sent(state), "tp", 0), state
    )
    state = combine(state, partner)
    normalized = state[2] / state[1][..., None]
    own_heads = lax.dynamic_slice_in_dim(normalized, block_index * query_count, query_count, 1)
    own_heads = own_heads.astype(jnp.bfloat16).reshape(TOK, query_count * HD)
    summed_out = lax.psum_scatter(
        jnp.dot(own_heads, out_weight, preferred_element_type=jnp.float32).astype(jnp.bfloat16),
        "tp",
        scatter_dimension=1,
        tiled=True,
    )
    projected = summed_out[None]
    block_count = TOK // BS
    slot_count = 2 * block_count // (group_count - 1)
    sliver = BS // splits
    paired = jnp.concatenate([my_keys, my_values], axis=1)
    mine = lax.dynamic_index_in_dim(
        paired.reshape(block_count, splits, sliver, 2 * HD), block_index, axis=1, keepdims=False
    )
    cells = placement[:, 0] * slot_count + placement[:, 1]
    routing = (
        cells[None, :] == jnp.arange(group_count * slot_count, dtype=jnp.int32)[:, None]
    ) & is_prefill
    outgoing_blocks = jnp.dot(
        routing.astype(jnp.bfloat16),
        mine.reshape(block_count, sliver * 2 * HD),
        preferred_element_type=jnp.float32,
    )
    outgoing_blocks = outgoing_blocks.astype(jnp.bfloat16).reshape(
        group_count, slot_count, sliver, 2 * HD
    )
    arrived_blocks = lax.all_to_all(
        outgoing_blocks, "group", split_axis=0, concat_axis=0, tiled=True
    )
    incoming = arrived_blocks[0:1]
    return (projected, incoming)


def solution(mesh):
    in_specs = (
        P("group", None, "tp"),
        P(None, "tp"),
        P(None, "tp"),
        P("tp", None),
        P("group", None, "tp", None),
        P("group", None, "tp", None),
        P("group", None),
        P(),
    )
    out_specs = (P("group", None, "tp"), P("group", None, "tp", None))
    return jax.shard_map(
        on_device, mesh=mesh, in_specs=in_specs, out_specs=out_specs, check_vma=False
    )
```

profile of v0, /device:TPU:0, one launch (start us, length us, event | category | flops | bytes accessed | tf_op | source)
XLA Modules:
  0.0 289.4 jit_solution(10126609375067961670)
XLA Ops:
  9.2 1.3 reduce.15
  10.8 58.5 %all-gather.9.cloned.1.call-done = bf16[1,256,8192]{2,1,0:T(8,128)(2,1)} async-done(((bf16[1,256,512]{2,1,0:T(8,128)(2,1)}), bf16[1,256,8192]{2,1,0:T(8,128)(2,1)}) %all-gather.9.cloned.1.call-update) | async-done | bytes 4194320 | tf_op jit(solution)/shard_map/all_gather | solution.py:111
  69.4 3.7 %fusion.77 = f32[256,128]{0,1:T(8,128)S(1)} fusion(bf16[8192,128]{1,0:T(8,128)(2,1)S(1)} %copy-done, bf16[1,256,8192]{2,1,0:T(8,128)(2,1)} %all-gather.9.cloned.1.call-done), kind=kOutput, calls=%fused_computation.88 | convolution fusion | flops 536870912 | bytes 6422528 | tf_op jit(solution)/shard_map/dot_general | solution.py:114
  74.4 5.2 %fusion.79 = f32[256,256]{0,1:T(8,128)S(1)} fusion(bf16[8192,256]{1,0:T(8,128)(2,1)} %param.13, bf16[1,256,8192]{2,1,0:T(8,128)(2,1)} %all-gather.9.cloned.1.call-done), kind=kOutput, calls=%fused_computation.90 | convolution fusion | flops 1073741824 | bytes 8650752 | tf_op jit(solution)/shard_map/dot_general | solution.py:113
  79.7 0.8 copy.70
  80.7 36.0 %all-gather.7.cloned.1.call-done = bf16[256,2048]{0,1:T(8,128)(2,1)} async-done(((bf16[256,128]{0,1:T(8,128)(2,1)}), bf16[256,2048]{0,1:T(8,128)(2,1)}) %all-gather.7.cloned.1.call-update) | async-done | bytes 1048592 | tf_op jit(solution)/shard_map/all_gather | solution.py:129
  116.7 0.9 constant_dynamic-slice_fusion.4
  117.6 47.6 %all-gather.5.cloned.1.call-done = bf16[256,4096]{1,0:T(8,128)(2,1)} async-done(((bf16[256,256]{1,0:T(8,128)(2,1)}), bf16[256,4096]{1,0:T(8,128)(2,1)}) %all-gather.5.cloned.1.call-update) | async-done | bytes 2097168 | tf_op jit(solution)/shard_map/all_gather | solution.py:128
  165.2 1.0 constant_dynamic-slice_fusion.6
  166.2 29.8 %conditional.1 = (f32[256,4]{0,1:T(4,128)S(1)}, f32[256,4]{0,1:T(4,128)S(1)}, f32[256,4,128]{2,1,0:T(4,128)}) conditional(s32[]{:T(128)} %convert_element_type.62, (pred[64,256]{1,0:T(8,128)(4,1)S(1)}, bf16[256,512]{1,0:T(8,128)(2,1)S(1)}, bf16[1,64,256,128]{3,2,1,0:T(8,128)(2,1)}, pred[]{:T(512)}, bf16[256,128]{0,1:T(8,128)(2,1)S(1)}, ...), branch_computations={%region_1.6_spmd, %region_6.13_spmd} | conditional | flops 2236615680 | bytes 74161976 | solution.py:195
  166.9 28.6 %while.14 = (s32[]{:T(128)}, f32[2,1,512]{2,1,0:T(1,128)S(1)}, f32[2,1,512]{2,1,0:T(1,128)S(1)}, f32[2,1,512,128]{3,2,1,0:T(8,128)}, pred[2,8192]{1,0:T(4,128)(4...) while((s32[]{:T(128)}, f32[2,1,512]{2,1,0:T(1,128)S(1)}, ...), condition=%wide.region_12.12_spmd.clone, body=%wide.region_7.11_spmd.clone.sunk | while | flops 2236611584 | bytes 73291440 | solution.py:164
  167.0 4.2 %fusion.127 = (f32[512]{0:T(512)S(1)}, f32[512,8192]{1,0:T(8,128)S(1)}) fusion(pred[8192]{0:T(1024)(128)(4,1)S(1)} %dynamic-slice_reduce_fusion.2, bf16[2,8192,128]{2,1,0:T(8,128)(2,1)} %get-tuple-element.365, s32[]{:T(128)S(6)} %copy.95, bf16[2,512,128]{2,1,0:T(8,128)(2,1)S(1)} %get-tuple-element.364), kind=kOutput, calls=%fused_computation.37.clone.1 | convolution fusion | flops 1086324224 | bytes 19016704 | tf_op jit(solution)/shard_map/cond/branch_1_fun/while/body/eval_jaxpr/jwt,jrt->jwr/dot_general | solution.py:49
  171.5 5.2 %fusion.129 = f32[512]{0:T(512)S(1)} fusion(f32[512,8192]{1,0:T(8,128)S(1)} %get-tuple-element.327, f32[512]{0:T(512)S(1)} %max.45, pred[8192]{0:T(1024)(128)(4,1)S(1)} %dynamic-slice_reduce_fusion.2), kind=kLoop, calls=%fused_computation.39.clone.1 | loop fusion | flops 20971008 | bytes 16789504 | tf_op jit(solution)/shard_map/cond/branch_1_fun/while/body/eval_jaxpr/reduce_sum | solution.py:63
  176.8 3.4 %fusion.131 = f32[512,128]{1,0:T(8,128)S(1)} fusion(f32[512,8192]{1,0:T(8,128)S(1)} %get-tuple-element.327, f32[512]{0:T(512)S(1)} %max.45, pred[8192]{0:T(1024)(128)(4,1)S(1)} %dynamic-slice_reduce_fusion.2, bf16[2,8192,128]{2,1,0:T(8,128)(2,1)S(1)} %copy-done.1, s32[]{:T(128)S(6)} %copy.95), kind=kOutput, calls=%fused_computation.40.clone.1 | convolution fusion | flops 1094713344 | bytes 19146756 | tf_op jit(solution)/shard_map/cond/branch_1_fun/while/body/eval_jaxpr/ciz,czm->cim/dot_general | solution.py:64
  180.3 0.9 fusion.132
  181.3 4.2 %fusion.127 = (f32[512]{0:T(512)S(1)}, f32[512,8192]{1,0:T(8,128)S(1)}) fusion(pred[8192]{0:T(1024)(128)(4,1)S(1)} %dynamic-slice_reduce_fusion.2, bf16[2,8192,128]{2,1,0:T(8,128)(2,1)} %get-tuple-element.365, s32[]{:T(128)S(6)} %copy.95, bf16[2,512,128]{2,1,0:T(8,128)(2,1)S(1)} %get-tuple-element.364), kind=kOutput, calls=%fused_computation.37.clone.1 | convolution fusion | flops 1086324224 | bytes 19016704 | tf_op jit(solution)/shard_map/cond/branch_1_fun/while/body/eval_jaxpr/jwt,jrt->jwr/dot_general | solution.py:49
  185.8 5.2 %fusion.129 = f32[512]{0:T(512)S(1)} fusion(f32[512,8192]{1,0:T(8,128)S(1)} %get-tuple-element.327, f32[512]{0:T(512)S(1)} %max.45, pred[8192]{0:T(1024)(128)(4,1)S(1)} %dynamic-slice_reduce_fusion.2), kind=kLoop, calls=%fused_computation.39.clone.1 | loop fusion | flops 20971008 | bytes 16789504 | tf_op jit(solution)/shard_map/cond/branch_1_fun/while/body/eval_jaxpr/reduce_sum | solution.py:63
  191.2 3.4 %fusion.131 = f32[512,128]{1,0:T(8,128)S(1)} fusion(f32[512,8192]{1,0:T(8,128)S(1)} %get-tuple-element.327, f32[512]{0:T(512)S(1)} %max.45, pred[8192]{0:T(1024)(128)(4,1)S(1)} %dynamic-slice_reduce_fusion.2, bf16[2,8192,128]{2,1,0:T(8,128)(2,1)S(1)} %copy-done.1, s32[]{:T(128)S(6)} %copy.95), kind=kOutput, calls=%fused_computation.40.clone.1 | convolution fusion | flops 1094713344 | bytes 19146756 | tf_op jit(solution)/shard_map/cond/branch_1_fun/while/body/eval_jaxpr/ciz,czm->cim/dot_general | solution.py:64
  194.6 1.0 fusion.132
  196.6 1.1 convert_element_type.68
  199.3 1.9 fusion.83
  201.3 5.4 %convolution_convert_fusion = bf16[256,8192]{1,0:T(8,128)(2,1)} fusion(bf16[256,8192]{1,0:T(8,128)(2,1)} %param.15, bf16[32,8,2,128]{3,2,1,0:T(2,128)(2,1)S(1)} %bitcast.141), kind=kOutput, calls=%fused_computation.87 | convolution fusion | flops 1075838976 | bytes 8519680 | tf_op jit(solution)/shard_map/dot_general | solution.py:204
  207.7 9.0 %all_to_all.5 = bf16[8,4,8,256]{3,2,1,0:T(8,128)(2,1)S(1)} all-to-all(bf16[8,4,8,256]{3,2,1,0:T(8,128)(2,1)S(1)} %bitcast.144), channel_id=1, replica_groups=mesh['group'=8,'tp'=16] {'group'}, dimensions={0} | all-to-all | bytes 262144 | tf_op jit(solution)/shard_map/all_to_all | solution.py:229
  217.3 65.6 %reduce-scatter.2.cloned.1.call-done = bf16[256,512]{1,0:T(8,128)(2,1)} async-done(((bf16[256,8192]{1,0:T(8,128)(2,1)}), bf16[256,512]{1,0:T(8,128)(2,1)}) %reduce-scatter.2.cloned.1.call-update) | async-done | bytes 262160 | tf_op jit(solution)/shard_map/reduce_scatter | solution.py:203
  (80 shorter events, 9.4 us)
Async XLA Ops:
  7.2 62.2 %copy-start = (bf16[8192,128]{1,0:T(8,128)(2,1)S(1)}, bf16[8192,128]{1,0:T(8,128)(2,1)}, u32[]{:S(2)}) copy-start(bf16[8192,128]{1,0:T(8,128)(2,1)} %param.14) | copy-start | bytes 6291460
  7.2 62.2 %all-gather.9.cloned.1.call-start = ((), (), s32[]{:S(2)}) async-start(), calls=%async_computation.5 | async-start | bytes 4456448 | tf_op jit(solution)/shard_map/all_gather | solution.py:111
  7.9 108.8 %all-gather.7.cloned.1.call-start = ((), (), s32[]{:S(2)}) async-start(), calls=%async_computation.3 | async-start | bytes 1114112 | tf_op jit(solution)/shard_map/all_gather | solution.py:129
  74.1 91.2 %all-gather.5.cloned.1.call-start = ((), (), s32[]{:S(2)}) async-start(), calls=%async_computation.2 | async-start | bytes 2228224 | tf_op jit(solution)/shard_map/all_gather | solution.py:128
  74.4 6.2 %copy-start.3 = (s32[1,64]{1,0:T(1,128)S(1)}, s32[1,64]{1,0:T(1,128)}, u32[]{:S(2)}) copy-start(s32[1,64]{1,0:T(1,128)} %param.18) | copy-start | bytes 772
  80.5 202.4 %reduce-scatter.2.cloned.1.call-start = ((), (), s32[]{:S(2)}) async-start(), calls=%async_computation.4 | async-start | bytes 4456448 | tf_op jit(solution)/shard_map/reduce_scatter | solution.py:203
  171.5 5.4 %copy-start.1 = (bf16[2,8192,128]{2,1,0:T(8,128)(2,1)S(1)}, bf16[2,8192,128]{2,1,0:T(8,128)(2,1)}, u32[]{:S(2)}) copy-start(bf16[2,8192,128]{2,1,0:T(8,128)(2,1)} %get-tuple-element.367) | copy-start | bytes 12582916 | tf_op jit(solution)/shard_map/cond/branch_1_fun/while
  185.8 5.4 %copy-start.1 = (bf16[2,8192,128]{2,1,0:T(8,128)(2,1)S(1)}, bf16[2,8192,128]{2,1,0:T(8,128)(2,1)}, u32[]{:S(2)}) copy-start(bf16[2,8192,128]{2,1,0:T(8,128)(2,1)} %get-tuple-element.367) | copy-start | bytes 12582916 | tf_op jit(solution)/shard_map/cond/branch_1_fun/while
  196.0 2.0 collective-permute-start.2
  196.3 1.7 collective-permute-start
  197.7 1.6 collective-permute-start.1
  206.6 0.7 copy-start.4
Sparse Core Ops, SparseCore 0:
  10.3 59.0 all-gather.8
  74.2 42.4 all-gather.6
  119.6 45.6 all-gather.4
  206.8 76.0 reduce-scatter.1
where the time goes:
time: 290 us; the launch traced here: 289 us
  waiting for transfers between devices  209 us (72%)
  matrix products  32 us (11%)
  other arithmetic  17.4 us (6%)
  between operations  14 us (5%)
  blocking collectives  8.97 us (3%)
  local copies, waits for them, and re-layouts  6.49 us (2%)
    reduce_scatter x1, waiting for transfers between devices, on_device(): lax.psum_scatter(jnp.dot(own_heads, out_weight, preferred_element_type=jn...  65.6 us
    all_gather x1, waiting for transfers between devices, on_device(): piece = lax.all_gather(tokens, 'tp', axis=1, tiled=True)  58.5 us
    all_gather x1, waiting for transfers between devices, on_device(): lax.all_gather(query_local, 'tp', axis=1, tiled=True)  47.6 us
    all_gather x1, waiting for transfers between devices, on_device(): lax.all_gather(pair_local, 'tp', axis=1, tiled=True)  36 us
    reduce_sum x4, other arithmetic, partial_block(): summed = jnp.sum(cached_weights, axis=2) + jnp.sum(recent_weights, axis=2)  10.7 us
    all_to_all x1, blocking collectives, on_device(): lax.all_to_all(outgoing_blocks, 'group', split_axis=0, concat_axis=0, til...  8.97 us
    dot_general x2, matrix products, partial_block(): jnp.einsum('jwt,jrt->jwr', query_vectors, key_row_block, preferred_elemen...  8.39 us
    dot_general x2, matrix products, partial_block(): jnp.einsum('ciz,czm->cim', cached_weights.astype(jnp.bfloat16), value_row...  6.8 us
  transfers between devices with their start and end apart: 7, of which 5 were waited for; matrix products, arithmetic and copies ran while one was open for 4% of the time, Pallas kernels for 0%

commit v1 on v0

v1 whole, which is shorter than its diff:
```python
import jax
import jax.numpy as jnp
from jax import lax
from jax.experimental import pallas as pl
from jax.experimental.pallas import tpu as pltpu
from jax.sharding import PartitionSpec as P

HD = 128
KVH = 8
STEPS = 4
NPR = 2
BS = 16
R = 64
GQ = 4
TOK = 256
CH = 128
RP = 32


NEG_FILL = -1e30


def tp_index(x_hi, y, core):
    return x_hi * 8 + (y % 4) * 2 + core


def moved(shard, x_flip, y_step, core_flip):
    pairs = []
    for x_hi in range(2):
        for y in range(4):
            for core in range(2):
                pairs.append(
                    (
                        tp_index(x_hi, y, core),
                        tp_index(x_hi ^ x_flip, y + y_step, core ^ core_flip),
                    )
                )
    return lax.ppermute(shard, "tp", pairs)


def core_swap(shard):
    return moved(shard, 0, 0, 1)


def turns(positions):
    midpoint = HD // 2
    frequency = jnp.exp(
        -jnp.log(500000.0) * jnp.arange(midpoint, dtype=jnp.float32) * 2.0 / HD
    )
    angles = positions.astype(jnp.float32)[:, None] * frequency[None, :]
    cosine = jnp.cos(angles)
    sine = jnp.sin(angles)
    return (
        jnp.concatenate([cosine, cosine], axis=1),
        jnp.concatenate([-sine, sine], axis=1),
    )


SPAN = 256
CHIPS = 8
SHARD = 512
HALF = TOK // 2
PREFILL_CHUNK = 4096
ROWS_AT_ONCE = 4
LOG2_E = 1.4426950408889634
NT = (((1,), (1,)), ((), ()))


def stacked_heads(queries):
    return jnp.concatenate([queries[:, j * HD : (j + 1) * HD] for j in range(GQ)], axis=0)


def weights_of(scores, largest):
    return jnp.exp2((scores - largest) * (HD**-0.5 * LOG2_E)).astype(jnp.bfloat16)


def with_ones(values):
    return jnp.concatenate([values, jnp.ones_like(values)], axis=1)


def write_heads(mixed_ref, level_ref, rows, mixed, largest):
    count = mixed.shape[0] // GQ
    total = mixed[:, HD : HD + 1]
    normal = (mixed[:, :HD] / total).astype(jnp.bfloat16)
    level = largest * HD**-0.5 + jnp.log(total)
    lane = lax.broadcasted_iota(jnp.int32, (count, GQ), 1)
    levels = jnp.zeros((count, GQ), jnp.float32)
    for j in range(GQ):
        part = slice(j * count, (j + 1) * count)
        mixed_ref[rows, j * HD : (j + 1) * HD] = normal[part]
        levels = jnp.where(lane == j, level[part], levels)
    level_ref[rows, :] = levels


def prefill_kernel(
    query_ref, key_ref, value_ref, bias_ref, mixed_ref, level_ref, keys, values, score_ref, sems
):
    rows = PREFILL_CHUNK // SPAN
    chunks = RP // rows

    def fetches(prompt, step):
        part = pl.ds(prompt * RP + step * rows, rows)
        index = prompt * chunks + step
        return (
            pltpu.make_async_copy(key_ref.at[part], keys.at[part], sems.at[0, index]),
            pltpu.make_async_copy(value_ref.at[part], values.at[part], sems.at[1, index]),
        )

    for prompt in range(NPR):
        for kind in range(2):
            for step in range(chunks):
                fetches(prompt, step)[kind].start()

    def one_prompt(prompt, carry):
        tokens = pl.ds(pl.multiple_of(prompt * CH, CH), CH)
        queries = stacked_heads(query_ref[tokens, :])

        def score_step(step, peak):
            fetches(prompt, step)[0].wait()
            part = keys[pl.ds(prompt * RP + step * rows, rows)].reshape(PREFILL_CHUNK, HD)
            scores = lax.dot_general(queries, part, NT, preferred_element_type=jnp.float32)
            scores = scores + bias_ref[prompt, pl.ds(step, 1), :]
            score_ref[step] = scores
            for lanes in range(PREFILL_CHUNK // HD):
                peak = jnp.maximum(peak, scores[:, lanes * HD : (lanes + 1) * HD])
            return peak

        peak = lax.fori_loop(
            0, chunks, score_step, jnp.full((GQ * CH, HD), NEG_FILL, jnp.float32)
        )
        largest = jnp.max(peak, axis=1, keepdims=True)
        level = jnp.broadcast_to(largest, (GQ * CH, HD))

        def mix_step(step, mixed):
            fetches(prompt, step)[1].wait()
            weights = jnp.concatenate(
                [
                    weights_of(score_ref[step, :, lanes * HD : (lanes + 1) * HD], level)
                    for lanes in range(PREFILL_CHUNK // HD)
                ],
                axis=1,
            )
            part = values[pl.ds(prompt * RP + step * rows, rows)].reshape(PREFILL_CHUNK, HD)
            return mixed + jnp.dot(weights, with_ones(part), preferred_element_type=jnp.float32)

        mixed = lax.fori_loop(0, chunks, mix_step, jnp.zeros((GQ * CH, 2 * HD), jnp.float32))
        write_heads(mixed_ref, level_ref, tokens, mixed, largest)
        return carry

    lax.fori_loop(0, NPR, one_prompt, 0)


def decode_kernel(query_ref, key_ref, value_ref, bias_ref, mixed_ref, level_ref):
    width = ROWS_AT_ONCE * SPAN
    tokens = ROWS_AT_ONCE * STEPS
    owner = lax.broadcasted_iota(jnp.int32, (GQ * tokens, width), 0) % tokens // STEPS
    holder = lax.broadcasted_iota(jnp.int32, (GQ * tokens, width), 1) // SPAN
    for part in range(query_ref.shape[0] // tokens):
        rows = slice(part * tokens, (part + 1) * tokens)
        cached = slice(part * ROWS_AT_ONCE, (part + 1) * ROWS_AT_ONCE)
        queries = stacked_heads(query_ref[rows, :])
        keys = key_ref[cached].reshape(width, HD)
        values = value_ref[cached].reshape(width, HD)
        scores = lax.dot_general(queries, keys, NT, preferred_element_type=jnp.float32)
        scores = jnp.where(owner == holder, scores + bias_ref[part : part + 1, :], NEG_FILL)
        largest = jnp.max(scores, axis=1, keepdims=True)
        mixed = jnp.dot(
            weights_of(scores, largest), with_ones(values), preferred_element_type=jnp.float32
        )
        write_heads(mixed_ref, level_ref, rows, mixed, largest)


def recent_kernel(prefill_ref, query_ref, key_ref, value_ref, mixed_ref, level_ref):
    is_prefill = prefill_ref[0] != 0
    row = lax.broadcasted_iota(jnp.int32, (TOK, TOK), 0)
    column = lax.broadcasted_iota(jnp.int32, (TOK, TOK), 1)
    together = jnp.where(is_prefill, row // CH - column // CH, row % R - column % R) == 0
    allowed = together & (column <= row)
    values = with_ones(value_ref[...])
    lane = lax.broadcasted_iota(jnp.int32, (TOK, GQ), 1)
    levels = jnp.zeros((TOK, GQ), jnp.float32)
    for j in range(GQ):
        head = slice(j * HD, (j + 1) * HD)
        scores = lax.dot_general(
            query_ref[:, head], key_ref[...], NT, preferred_element_type=jnp.float32
        )
        scores = jnp.where(allowed, scores, NEG_FILL)
        largest = jnp.max(scores, axis=1, keepdims=True)
        mixed = jnp.dot(weights_of(scores, largest), values, preferred_element_type=jnp.float32)
        total = mixed[:, HD : HD + 1]
        mixed_ref[:, head] = mixed[:, :HD] / total
        levels = jnp.where(lane == j, largest * HD**-0.5 + jnp.log(total), levels)
    level_ref[...] = levels


def merged(parts, levels):
    top = jnp.maximum(jnp.maximum(levels[0], levels[1]), levels[2])
    shares = [jnp.exp(level - top) for level in levels]
    total = shares[0] + shares[1] + shares[2]
    shares = [share / total for share in shares]
    heads = []
    for j in range(GQ):
        head = slice(j * HD, (j + 1) * HD)
        mixed = jnp.zeros((TOK, HD), jnp.float32)
        for part, share in zip(parts, shares):
            mixed = mixed + part[:, head].astype(jnp.float32) * share[:, j : j + 1]
        heads.append(mixed.astype(jnp.bfloat16))
    return jnp.concatenate(heads, axis=1)


def merge_out_kernel(
    place_ref,
    weight_ref,
    swapped_ref,
    own_ref,
    own_level,
    other_ref,
    other_level,
    recent_ref,
    recent_level,
    plus,
    minus,
    up,
    down,
    next_ref,
    last_ref,
    partner_ref,
    here_ref,
    attention_ref,
    held_ref,
    sems,
):
    core = place_ref[0]
    rows = weight_ref.shape[0]
    copies = []
    for index in range(CHIPS):
        chip = place_ref[1 + index]
        own = pl.ds(pl.multiple_of((2 * chip + core) * SHARD, SHARD), SHARD)
        other = pl.ds(pl.multiple_of(chip * SHARD, SHARD), SHARD)
        pair = (
            pltpu.make_async_copy(
                weight_ref.at[:, own], held_ref.at[index, :rows], sems.at[0, index]
            ),
            pltpu.make_async_copy(
                swapped_ref.at[:, other], held_ref.at[index, rows:], sems.at[1, index]
            ),
        )
        for copy in pair:
            copy.start()
        copies.append(pair)
    attention_ref[...] = merged(
        (own_ref, other_ref, recent_ref), (own_level[...], other_level[...], recent_level[...])
    )
    own = attention_ref[:, pl.ds(pl.multiple_of(core * rows, rows), rows)]
    other = attention_ref[:, pl.ds(pl.multiple_of((1 - core) * rows, rows), rows)]
    joined = jnp.concatenate([own, other], axis=1)

    def product(index):
        for copy in copies[index]:
            copy.wait()
        total = jnp.dot(joined, held_ref[index], preferred_element_type=jnp.float32)
        return total.astype(jnp.bfloat16)

    plus[:TOK] = product(0)
    minus[:TOK] = product(1)
    far = product(2)
    plus[TOK:] = far[:HALF]
    minus[TOK:] = far[HALF:]
    far = product(3)
    up[...] = far[:HALF]
    down[...] = far[HALF:]
    for index, ref in ((4, next_ref), (5, last_ref), (6, partner_ref), (7, here_ref)):
        ref[...] = product(index)


def total_of(*parts):
    total = parts[0].astype(jnp.float32)
    for part in parts[1:]:
        total = total + part.astype(jnp.float32)
    return total.astype(jnp.bfloat16)


def second_message_kernel(
    next_ref, last_ref, partner_ref, from_last, from_next, up, down, plus, minus, partner
):
    plus[:HALF] = total_of(next_ref[:HALF], from_last[TOK:], up[...])
    plus[HALF:] = next_ref[HALF:]
    minus[:HALF] = last_ref[:HALF]
    minus[HALF:] = total_of(last_ref[HALF:], from_next[TOK:], down[...])
    partner[...] = total_of(partner_ref[...], from_last[:TOK], from_next[:TOK])


def total_kernel(here_ref, from_last, from_next, from_partner, out_ref):
    out_ref[...] = total_of(here_ref[...], from_last[...], from_next[...], from_partner[...])


def join_kernel(token_ref, partner_ref, last_ref, next_ref, plus, minus, up, down):
    plus[:TOK] = partner_ref[...]
    plus[TOK:] = last_ref[:HALF]
    minus[:TOK] = partner_ref[...]
    minus[TOK:] = next_ref[HALF:]
    up[...] = last_ref[HALF:]
    down[...] = next_ref[:HALF]


def far_join_kernel(from_last, from_next, upper_ref, lower_ref, far):
    far[:HALF] = upper_ref[...]
    far[HALF:] = lower_ref[...]


def projected_parts(row_ref, shards, query_weight, pair_weight):
    joined = jnp.concatenate(shards, axis=1)
    rows = [
        pl.ds(pl.multiple_of(row_ref[index], SHARD), SHARD) for index in range(len(shards))
    ]
    return [
        jnp.dot(
            joined,
            jnp.concatenate([weight[part, :] for part in rows], axis=0),
            preferred_element_type=jnp.float32,
        )
        for weight in (query_weight, pair_weight)
    ]


def near_kernel(row_ref, query_weight, pair_weight, *refs):
    *shards, query, pair = refs
    query[...], pair[...] = projected_parts(
        row_ref, [ref[...] for ref in shards], query_weight, pair_weight
    )


def far_shards(last_ref, next_ref, far_ref):
    far = jnp.concatenate([last_ref[TOK:], next_ref[TOK:]], axis=0)
    return [last_ref[:TOK], next_ref[:TOK], far, far_ref[...]]


def last_kernel(row_ref, query_weight, pair_weight, query_in, pair_in, *refs):
    *sides, cosine_ref, sine_ref, query_out, pair_out = refs
    shards = far_shards(*sides[:3]) + far_shards(*sides[3:])
    sums = projected_parts(row_ref, shards, query_weight, pair_weight)
    query = query_in[...] + sums[0]
    pair = pair_in[...] + sums[1]
    cosine = cosine_ref[...]
    sine = sine_ref[...]

    def rotated(values):
        return values * cosine + pltpu.roll(values, HD // 2, 1) * sine

    for head in range(query.shape[1] // HD):
        part = slice(head * HD, (head + 1) * HD)
        query_out[:, part] = rotated(query[:, part]).astype(jnp.bfloat16)
    is_key = row_ref[len(shards)] != 0
    pair_out[...] = jnp.where(is_key, rotated(pair), pair).astype(jnp.bfloat16)


def blocks_kernel(cell_ref, key_ref, value_ref, out_ref):
    sliver = out_ref.shape[1]
    out_ref[...] = jnp.zeros_like(out_ref)

    @pl.when(cell_ref[0] != 0)
    def _():
        for block in range(TOK // BS):
            start = pl.multiple_of(cell_ref[1] * sliver, sliver) + block * BS
            cell = cell_ref[2 + block]
            out_ref[cell, :, :HD] = key_ref[pl.ds(start, sliver), :]
            out_ref[cell, :, HD:] = value_ref[pl.ds(start, sliver), :]


def called(kernel, shapes, scalars, *arrays, streamed=(), scratch=(), flops=0, grant=12):
    whole = pl.BlockSpec(memory_space=pltpu.VMEM)
    specs = [pl.BlockSpec(memory_space=pl.ANY)] * len(streamed) + [whole] * len(arrays)
    arrays = tuple(streamed) + arrays
    if scalars is not None:
        specs = [pl.BlockSpec(memory_space=pltpu.SMEM)] + specs
        arrays = (scalars,) + arrays
    return pl.pallas_call(
        kernel,
        in_specs=specs,
        out_specs=tuple(whole for _ in shapes),
        out_shape=tuple(jax.ShapeDtypeStruct(shape, kind) for shape, kind in shapes),
        scratch_shapes=scratch,
        compiler_params=pltpu.CompilerParams(vmem_limit_bytes=grant * 2**20),
        cost_estimate=pl.CostEstimate(flops=flops, transcendentals=0, bytes_accessed=2**21),
    )(*arrays)


def outputs_of(kind):
    return (
        jax.ShapeDtypeStruct((TOK, GQ * HD), kind),
        jax.ShapeDtypeStruct((TOK, GQ), jnp.float32),
    )


def prefill_part(queries, keys, values, bias):
    chunks = RP * SPAN // PREFILL_CHUNK
    whole = pl.BlockSpec(memory_space=pltpu.VMEM)
    there = pl.BlockSpec(memory_space=pl.ANY)
    return pl.pallas_call(
        prefill_kernel,
        in_specs=[whole, there, there, whole],
        out_specs=(whole, whole),
        out_shape=outputs_of(jnp.bfloat16),
        scratch_shapes=[
            pltpu.VMEM((R, SPAN, HD), jnp.bfloat16),
            pltpu.VMEM((R, SPAN, HD), jnp.bfloat16),
            pltpu.VMEM((chunks, GQ * CH, PREFILL_CHUNK), jnp.float32),
            pltpu.SemaphoreType.DMA((2, NPR * chunks)),
        ],
        compiler_params=pltpu.CompilerParams(vmem_limit_bytes=44 * 2**20),
    )(queries, keys, values, bias.reshape(NPR, chunks, PREFILL_CHUNK))


def decode_part(queries, keys, values, bias):
    def by_row(array):
        return array.reshape(STEPS, R, -1).transpose(1, 0, 2).reshape(TOK, -1)

    def by_step(array):
        return array.reshape(R, STEPS, -1).transpose(1, 0, 2).reshape(TOK, -1)

    rows = 8 * ROWS_AT_ONCE
    mixed, level = pl.pallas_call(
        decode_kernel,
        grid=(R // rows,),
        in_specs=[
            pl.BlockSpec((rows * STEPS, GQ * HD), lambda i: (i, 0)),
            pl.BlockSpec((rows, SPAN, HD), lambda i: (i, 0, 0)),
            pl.BlockSpec((rows, SPAN, HD), lambda i: (i, 0, 0)),
            pl.BlockSpec((rows // ROWS_AT_ONCE, ROWS_AT_ONCE * SPAN), lambda i: (i, 0)),
        ],
        out_specs=(
            pl.BlockSpec((rows * STEPS, GQ * HD), lambda i: (i, 0)),
            pl.BlockSpec((rows * STEPS, GQ), lambda i: (i, 0)),
        ),
        out_shape=outputs_of(jnp.bfloat16),
        compiler_params=pltpu.CompilerParams(vmem_limit_bytes=40 * 2**20),
    )(by_row(queries), keys, values, bias.reshape(R // ROWS_AT_ONCE, ROWS_AT_ONCE * SPAN))
    return by_step(mixed), by_step(level)


def recent_part(is_prefill, queries, keys, values):
    whole = pl.BlockSpec(memory_space=pltpu.VMEM)
    return pl.pallas_call(
        recent_kernel,
        in_specs=[pl.BlockSpec(memory_space=pltpu.SMEM), whole, whole, whole],
        out_specs=(whole, whole),
        out_shape=outputs_of(jnp.float32),
        compiler_params=pltpu.CompilerParams(vmem_limit_bytes=16 * 2**20),
    )(is_prefill.astype(jnp.int32).reshape(1), queries, keys, values)


def cut_kernel(core_ref, weight_ref, out_ref, held_ref, in_sems, out_sems):
    fetches = []
    stores = []
    for chip in range(CHIPS):
        columns = pl.ds(pl.multiple_of((2 * chip + 1 - core_ref[0]) * SHARD, SHARD), SHARD)
        fetches.append(
            pltpu.make_async_copy(weight_ref.at[:, columns], held_ref.at[chip], in_sems.at[chip])
        )
        stores.append(
            pltpu.make_async_copy(
                held_ref.at[chip],
                out_ref.at[:, chip * SHARD : (chip + 1) * SHARD],
                out_sems.at[chip],
            )
        )
    for fetch in fetches:
        fetch.start()
    for fetch, store in zip(fetches, stores):
        fetch.wait()
        store.start()
    for store in stores:
        store.wait()


def cut_columns(out_weight, core):
    return pl.pallas_call(
        cut_kernel,
        in_specs=[
            pl.BlockSpec(memory_space=pltpu.SMEM),
            pl.BlockSpec(memory_space=pl.ANY),
        ],
        out_specs=pl.BlockSpec(memory_space=pl.ANY),
        out_shape=jax.ShapeDtypeStruct((out_weight.shape[0], CHIPS * SHARD), jnp.bfloat16),
        scratch_shapes=[
            pltpu.VMEM((CHIPS, out_weight.shape[0], SHARD), jnp.bfloat16),
            pltpu.SemaphoreType.DMA((CHIPS,)),
            pltpu.SemaphoreType.DMA((CHIPS,)),
        ],
        compiler_params=pltpu.CompilerParams(vmem_limit_bytes=12 * 2**20),
    )(core.reshape(1), out_weight)


def on_device(
    layer_input, query_weight, kv_weight, out_weight, cache_keys, cache_values, lengths, placement
):
    group_count = lax.axis_size("group")
    splits = 2
    tp_rank = lax.axis_index("tp")
    group_rank = lax.axis_index("group")
    core = tp_rank % 2
    y = (tp_rank // 2) % 4
    x_hi = tp_rank // 8
    block_index = core
    last_block = block_index == splits - 1
    is_prefill = group_rank == 0
    tokens = layer_input[0]
    row_lengths = lengths[0]
    prefix = jnp.sum(row_lengths.reshape(NPR, RP), axis=1)
    prompt_positions = (prefix[:, None] + jnp.arange(CH, dtype=jnp.int32)[None, :]).reshape(TOK)
    decode_step_positions = (
        row_lengths[None, :] + jnp.arange(STEPS, dtype=jnp.int32)[:, None]
    ).reshape(TOK)
    positions = jnp.where(is_prefill, prompt_positions, decode_step_positions)

    cosine, sine = turns(positions)

    cut_out = cut_columns(out_weight, core)

    wide = ((TOK + HALF, SHARD), jnp.bfloat16)
    half = ((HALF, SHARD), jnp.bfloat16)
    shard = ((TOK, SHARD), jnp.bfloat16)
    weights = (query_weight, kv_weight)
    sums = (((TOK, query_weight.shape[1]), jnp.float32), ((TOK, kv_weight.shape[1]), jnp.float32))

    def rows_of(*owners):
        firsts = [tp_index(x_hi ^ flip, y + step, core) for flip, step in owners]
        return jnp.stack(firsts + [first ^ 1 for first in firsts]).astype(jnp.int32) * SHARD

    last_tokens, next_tokens = moved(tokens, 0, 1, 0), moved(tokens, 0, 3, 0)
    partner_tokens = moved(tokens, 1, 0, 0)
    token, *_ = lax.optimization_barrier((tp_rank.reshape(1), cut_out, cosine, sine))
    swapped_out = core_swap(cut_out)
    near = (tokens, last_tokens, next_tokens, partner_tokens)
    plus, minus, up, down = called(
        join_kernel, (wide, wide, half, half), token, partner_tokens, last_tokens, next_tokens
    )
    from_last, from_next = moved(plus, 0, 1, 0), moved(minus, 0, 3, 0)
    (far,) = called(
        far_join_kernel,
        (shard,),
        None,
        moved(down, 1, 3, 0),
        moved(up, 1, 1, 0),
        streamed=(from_last, from_next),
    )
    sides = (from_last, from_next, far)
    part = called(
        near_kernel,
        sums,
        rows_of((0, 0), (0, 3), (0, 1), (1, 0)),
        *weights,
        *near,
        *[core_swap(source) for source in near],
        flops=2 * TOK * 8 * SHARD * 3 * HD,
    )
    query_local, pair_local = called(
        last_kernel,
        tuple((shape, jnp.bfloat16) for shape, _ in sums),
        jnp.concatenate(
            [
                rows_of((1, 3), (1, 1), (0, 2), (1, 2)),
                (tp_rank < KVH).astype(jnp.int32)[None],
            ]
        ),
        *weights,
        *part,
        *sides,
        *[core_swap(source) for source in sides],
        cosine,
        sine,
        flops=2 * TOK * 8 * SHARD * 3 * HD,
    )
    query_other = core_swap(query_local)
    pair_held = lax.ppermute(
        pair_local, "tp", [(t, 2 * t if t < KVH else 2 * (t - KVH) + 1) for t in range(2 * KVH)]
    )
    my_queries = jnp.concatenate(
        [jnp.where(core == 0, query_local, query_other), jnp.where(core == 0, query_other, query_local)],
        axis=1,
    )
    present = (block_index * SPAN + jnp.arange(SPAN, dtype=jnp.int32))[None, :] < row_lengths[
        :, None
    ]
    bias = jnp.where(present, 0.0, NEG_FILL).astype(jnp.float32)
    cached = lax.cond(
        is_prefill, prefill_part, decode_part, my_queries, cache_keys[0], cache_values[0], bias
    )
    _, pair_held = lax.optimization_barrier((cached[1], pair_held))
    pair_other = core_swap(pair_held)
    my_keys = jnp.where(core == 0, pair_held, pair_other)
    my_values = jnp.where(core == 0, pair_other, pair_held)
    other_cached = (core_swap(cached[0]), core_swap(cached[1]))
    recent = recent_part(is_prefill, my_queries, my_keys, my_values)

    places = ((1, 1), (1, 3), (0, 2), (1, 2), (0, 1), (0, 3), (1, 0), (0, 0))
    place = jnp.stack(
        [core] + [(x_hi ^ flip) * 4 + (y + step) % 4 for flip, step in places]
    ).astype(jnp.int32)
    plus, minus, up, down, next_part, last_part, partner_part, here_part = called(
        merge_out_kernel,
        (wide, wide, half, half, shard, shard, shard, shard),
        place,
        *cached,
        *other_cached,
        *recent,
        streamed=(out_weight, swapped_out),
        scratch=(
            pltpu.VMEM((TOK, GQ * HD), jnp.bfloat16),
            pltpu.VMEM((CHIPS, GQ * HD, SHARD), jnp.bfloat16),
            pltpu.SemaphoreType.DMA((2, CHIPS)),
        ),
        flops=2 * TOK * CHIPS * SHARD * GQ * HD,
        grant=24,
    )
    from_last, from_next = moved(plus, 0, 1, 0), moved(minus, 0, 3, 0)
    up, down = moved(up, 1, 1, 0), moved(down, 1, 3, 0)

    block_count = TOK // BS
    slot_count = 2 * block_count // (group_count - 1)
    cells = placement[:, 0] * slot_count + placement[:, 1]
    sender = jnp.stack([is_prefill.astype(jnp.int32), core.astype(jnp.int32)])
    (blocks,) = called(
        blocks_kernel,
        (((group_count * slot_count, BS // splits, 2 * HD), jnp.bfloat16),),
        jnp.concatenate([sender, cells]),
        my_keys,
        my_values,
    )
    _, blocks = lax.optimization_barrier((here_part, blocks))
    blocks = blocks.reshape(2, 4, slot_count, BS // splits, 2 * HD)
    arrived = lax.ppermute(blocks, "group", [(0, 4)])
    plus, minus, partner = called(
        second_message_kernel,
        (shard, shard, shard),
        None,
        next_part,
        last_part,
        partner_part,
        from_last,
        from_next,
        up,
        down,
    )
    from_last, from_next = moved(plus, 0, 1, 0), moved(minus, 0, 3, 0)
    from_partner = moved(partner, 1, 0, 0)
    _, arrived = lax.optimization_barrier((partner, arrived))
    sent = lax.ppermute(arrived[:, 2:], "group", [(4, 6)])
    arrived = jnp.where(group_rank == 6, sent, arrived[:, :2])
    sent = lax.ppermute(arrived[:, 1:], "group", [(4, 5), (6, 7)])
    arrived = jnp.where(group_rank % 2 == 1, sent, arrived[:, :1])
    sent = lax.ppermute(arrived[0], "group", [(5, 1), (6, 2), (7, 3)])
    incoming = jnp.where(group_rank >= 4, arrived[1], sent)
    (projected,) = called(
        total_kernel, (shard,), None, here_part, from_last, from_next, from_partner
    )
    return (projected[None], incoming)


def solution(mesh):
    in_specs = (
        P("group", None, "tp"),
        P(None, "tp"),
        P(None, "tp"),
        P("tp", None),
        P("group", None, "tp", None),
        P("group", None, "tp", None),
        P("group", None),
        P(),
    )
    out_specs = (P("group", None, "tp"), P("group", None, "tp", None))
    return jax.shard_map(
        on_device, mesh=mesh, in_specs=in_specs, out_specs=out_specs, check_vma=False
    )
```

time: 290 us -> 105 us (0.36)
  the two profiles are of different devices: /device:TPU:0 before, /device:TPU:64 now
where the time goes in v1:
time: 105 us; the launch traced here: 104 us
  starting transfers between devices  36.6 us (35%)
  waiting for transfers between devices  29.3 us (28%)
  Pallas kernels  22.3 us (21%)
  local copies, waits for them, and re-layouts  11.5 us (11%)
  other arithmetic  3.13 us (3%)
    ppermute x26, starting transfers between devices, moved(): return lax.ppermute(shard, 'tp', pairs)  31.8 us
    ppermute x26, waiting for transfers between devices, moved(): return lax.ppermute(shard, 'tp', pairs)  18 us
    pallas_call x8, Pallas kernels, called(): pl.pallas_call(kernel, in_specs=specs, out_specs=tuple((whole for _ in sh...  13.3 us
    ppermute x1, waiting for transfers between devices, on_device(): sent = lax.ppermute(arrived[0], 'group', [(5, 1), (6, 2), (7, 3)])  11.4 us
    unnamed x27, local copies, waits for them, and re-layouts  10.6 us
    pallas_call x1, Pallas kernels, decode_part(): pl.pallas_call(decode_kernel, grid=(R // rows,), in_specs=[pl.BlockSpec((...  6.09 us
  transfers between devices with their start and end apart: 31, of which 11 were waited for; matrix products, arithmetic and copies ran while one was open for 4% of the time, Pallas kernels for 17%

profile of v1, /device:TPU:64, one launch (start us, length us, event | category | flops | bytes accessed | tf_op | source)
XLA Modules:
  0.0 104.1 jit_solution(6803806328860654333)
XLA Ops:
  0.7 3.1 %collective-permute-start.3 = (bf16[256,512]{1,0:T(8,128)(2,1)}, bf16[256,512]{1,0:T(8,128)(2,1)S(1)}, u32[]{:S(2)}, u32[]{:S(2)}) collective-permute-start(bf16[256,512]{1,0:T(8,128)(2,1)} %bitcast.57), channel_id=1, source_target_pairs={{0,8},{1,9},{2,10},{3,11},{4,12},{5,13},{6,14},{7,15},{8,0},{9,1},... | collective-permute-start | bytes 786440 | tf_op jit(solution)/shard_map/ppermute | solution.py:38
  3.8 3.0 %collective-permute-start.2 = (bf16[256,512]{1,0:T(8,128)(2,1)}, bf16[256,512]{1,0:T(8,128)(2,1)S(1)}, u32[]{:S(2)}, u32[]{:S(2)}) collective-permute-start(bf16[256,512]{1,0:T(8,128)(2,1)} %bitcast.58), channel_id=1, source_target_pairs={{0,6},{1,7},{2,0},{3,1},{4,2},{5,3},{6,4},{7,5},{8,14},{9,15},{10,... | collective-permute-start | bytes 786440 | tf_op jit(solution)/shard_map/ppermute | solution.py:38
  6.9 2.2 %copy-done.2 = bf16[256,8192]{1,0:T(8,128)(2,1)S(1)} copy-done((bf16[256,8192]{1,0:T(8,128)(2,1)S(1)}, bf16[256,8192]{1,0:T(8,128)(2,1)}, u32[]{:S(2)}) %copy-start.2) | copy-done | bytes 4194328
  9.0 1.6 %shard_map.95 = bf16[256,4096]{1,0:T(8,128)(2,1)} custom-call(s32[1]{0:T(128)} %bitcast.8.core_ref, bf16[256,8192]{1,0:T(8,128)(2,1)S(1)} %copy-done.2), custom_call_target="tpu_custom_call" | custom-call | tf_op jit(solution)/shard_map/pallas_call | solution.py:477
  13.7 2.6 %collective-permute-done.1.refs_1_.last_ref = bf16[256,512]{1,0:T(8,128)(2,1)S(1)} collective-permute-done((bf16[256,512]{1,0:T(8,128)(2,1)}, bf16[256,512]{1,0:T(8,128)(2,1)S(1)}, u32[]{:S(2)}, u32[]{:S(2)}) %collective-permute-start.1) | collective-permute-done | bytes 262176 | tf_op jit(solution)/shard_map/ppermute | solution.py:38
  17.9 3.9 %collective-permute-start.11 = (bf16[128,512]{1,0:T(8,128)(2,1)}, bf16[128,512]{1,0:T(8,128)(2,1)}, u32[]{:S(2)}, u32[]{:S(2)}) collective-permute-start(bf16[128,512]{1,0:T(8,128)(2,1)} %get-tuple-element.61), channel_id=1, source_target_pairs={{0,10},{1,11},{2,12},{3,13},{4,14},{5,15},{6,8},{7,9},{8,2},{9,3},... | collective-permute-start | bytes 393224 | tf_op jit(solution)/shard_map/ppermute | solution.py:38
  22.5 3.2 %collective-permute-start.9 = (bf16[384,512]{1,0:T(8,128)(2,1)}, bf16[384,512]{1,0:T(8,128)(2,1)S(1)}, u32[]{:S(2)}, u32[]{:S(2)}) collective-permute-start(bf16[384,512]{1,0:T(8,128)(2,1)} %get-tuple-element.59), channel_id=1, source_target_pairs={{0,6},{1,7},{2,0},{3,1},{4,2},{5,3},{6,4},{7,5},{8,14},{9,15},{10,... | collective-permute-start | bytes 1179656 | tf_op jit(solution)/shard_map/ppermute | solution.py:38
  26.0 1.5 %collective-permute-done.11.lower_ref = bf16[128,512]{1,0:T(8,128)(2,1)} collective-permute-done((bf16[128,512]{1,0:T(8,128)(2,1)}, bf16[128,512]{1,0:T(8,128)(2,1)}, u32[]{:S(2)}, u32[]{:S(2)}) %collective-permute-start.11) | collective-permute-done | bytes 131104 | tf_op jit(solution)/shard_map/ppermute | solution.py:38
  28.2 7.6 %collective-permute-done.8.from_last.refs_0_ = bf16[384,512]{1,0:T(8,128)(2,1)S(1)} collective-permute-done((bf16[384,512]{1,0:T(8,128)(2,1)}, bf16[384,512]{1,0:T(8,128)(2,1)S(1)}, u32[]{:S(2)}, u32[]{:S(2)}) %collective-permute-start.8) | collective-permute-done | bytes 393248 | tf_op jit(solution)/shard_map/ppermute | solution.py:38
  37.6 2.2 %copy-done = bf16[8192,256]{1,0:T(8,128)(2,1)S(1)} copy-done((bf16[8192,256]{1,0:T(8,128)(2,1)S(1)}, bf16[8192,256]{1,0:T(8,128)(2,1)}, u32[]{:S(2)}) %copy-start) | copy-done | bytes 4194328
  42.6 2.5 %shard_map.96 = (f32[256,256]{1,0:T(8,128)S(1)}, f32[256,128]{1,0:T(8,128)S(1)}) custom-call(s32[8]{0:T(128)S(1)} %broadcast_multiply_fusion.row_ref, bf16[8192,256]{1,0:T(8,128)(2,1)S(1)} %copy-done, bf16[8192,128]{1,0:T(8,128)(2,1)S(1)} %copy-done.4, bf16[256,512]{1,0:T(8,128)(2,1)S(1)} %bitcast.60, bf16[256,512]{1,0:T(8,128)(2,1)S(1)} %copy-done.6, ...), custom_call_target="tpu_custom_call" | custom-call | flops 805306368 | bytes 2097152 | tf_op jit(solution)/shard_map/pallas_call | solution.py:377
  45.2 3.1 %shard_map.99 = (bf16[256,256]{1,0:T(8,128)(2,1)S(1)}, bf16[256,128]{1,0:T(8,128)(2,1)}) custom-call(s32[9]{0:T(128)S(1)} %pad_add_fusion.row_ref, bf16[8192,256]{1,0:T(8,128)(2,1)S(1)} %copy-done.1, bf16[8192,128]{1,0:T(8,128)(2,1)S(1)} %copy-done.4, f32[256,256]{1,0:T(8,128)S(1)} %get-tuple-element.55.query_in, f32[256,128]{1,0:T(8,128)S(1)} %get-tuple-element.56.pair_in, ...), custom_call_target="tpu_custom_call" | custom-call | flops 805306368 | bytes 2097152 | tf_op jit(solution)/shard_map/pallas_call | solution.py:377
  48.9 1.5 %collective-permute-start.18 = (bf16[256,128]{1,0:T(8,128)(2,1)}, bf16[256,128]{1,0:T(8,128)(2,1)S(1)}, u32[]{:S(2)}, u32[]{:S(2)}) collective-permute-start(bf16[256,128]{1,0:T(8,128)(2,1)} %get-tuple-element.65), channel_id=1, source_target_pairs={{0,0},{1,2},{2,4},{3,6},{4,8},{5,10},{6,12},{7,14},{8,1},{9,3},{10... | collective-permute-start | bytes 196616 | tf_op jit(solution)/shard_map/ppermute | solution.py:575
  50.4 6.8 %conditional.1 = ((bf16[256,512]{1,0:T(8,128)(2,1)S(1)}, f32[256,4]{1,0:T(8,128)S(1)})) conditional(s32[]{:T(128)} %convert_element_type.13, (bf16[256,512]{1,0:T(8,128)(2,1)S(1)}, f32[64,256]{1,0:T(8,128)S(1)}, bf16[64,256,128]{2,1,0:T(8,128)(2,1)}, bf16[64,256,128]{2,1,0:T(8,128)(2,1)}) %tuple.37, (f32[64,256]{1,0:T(8,128)S(1)}, ...), branch_computations={%region_1.2_spmd, %region_2.3_spmd} | conditional | bytes 2236440 | solution.py:586
  50.8 6.1 %branch_0_fun.1 = (bf16[256,512]{1,0:T(8,128)(2,1)S(1)}, f32[256,4]{1,0:T(8,128)S(1)}) custom-call(bf16[256,512]{1,0:T(8,128)(2,1)S(1)} %reshape.70.query_ref, bf16[64,256,128]{2,1,0:T(8,128)(2,1)} %get-tuple-element.17.key_ref, bf16[64,256,128]{2,1,0:T(8,128)(2,1)} %get-tuple-element.18.value_ref, f32[16,1024]{1,0:T(8,128)S(1)} %reshape.71.bias_ref), custom_call_target="tpu_custom_call" | custom-call | tf_op jit(solution)/shard_map/cond/branch_0_fun/pallas_call | solution.py:422
  60.0 2.2 %copy-done.3 = bf16[256,8192]{1,0:T(8,128)(2,1)S(1)} copy-done((bf16[256,8192]{1,0:T(8,128)(2,1)S(1)}, bf16[256,8192]{1,0:T(8,128)(2,1)}, u32[]{:S(2)}) %copy-start.3) | copy-done | bytes 4194328
  62.1 4.1 %shard_map.101 = (bf16[384,512]{1,0:T(8,128)(2,1)S(1)}, bf16[384,512]{1,0:T(8,128)(2,1)S(1)}, bf16[128,512]{1,0:T(8,128)(2,1)S(1)}, bf16[128,512]{1,0:T(8,128)(2...) custom-call(s32[9]{0:T(128)S(1)} %stack.95.place_ref, ...), custom_call_target="tpu_custom_call" | custom-call | flops 1073741824 | bytes 2097152 | tf_op jit(solution)/shard_map/pallas_call | solution.py:377
  67.7 1.9 %collective-permute-start.21 = (bf16[384,512]{1,0:T(8,128)(2,1)S(1)}, bf16[384,512]{1,0:T(8,128)(2,1)S(1)}, u32[]{:S(2)}, u32[]{:S(2)}) collective-permute-start(bf16[384,512]{1,0:T(8,128)(2,1)S(1)} %get-tuple-element.74), channel_id=1, source_target_pairs={{0,6},{1,7},{2,0},{3,1},{4,2},{5,3},{6,4},{7,5},{8,14},{9,15},{10,... | collective-permute-start | bytes 1179656 | tf_op jit(solution)/shard_map/ppermute | solution.py:38
  69.6 2.6 %collective-permute-start.22 = (bf16[128,512]{1,0:T(8,128)(2,1)S(1)}, bf16[128,512]{1,0:T(8,128)(2,1)S(1)}, u32[]{:S(2)}, u32[]{:S(2)}) collective-permute-start(bf16[128,512]{1,0:T(8,128)(2,1)S(1)} %get-tuple-element.75), channel_id=1, source_target_pairs={{0,10},{1,11},{2,12},{3,13},{4,14},{5,15},{6,8},{7,9},{8,2},{9,3},... | collective-permute-start | bytes 393224 | tf_op jit(solution)/shard_map/ppermute | solution.py:38
  72.3 3.0 %collective-permute-start.23 = (bf16[128,512]{1,0:T(8,128)(2,1)S(1)}, bf16[128,512]{1,0:T(8,128)(2,1)S(1)}, u32[]{:S(2)}, u32[]{:S(2)}) collective-permute-start(bf16[128,512]{1,0:T(8,128)(2,1)S(1)} %get-tuple-element.76), channel_id=1, source_target_pairs={{0,14},{1,15},{2,8},{3,9},{4,10},{5,11},{6,12},{7,13},{8,6},{9,7},... | collective-permute-start | bytes 393224 | tf_op jit(solution)/shard_map/ppermute | solution.py:38
  76.5 3.1 %collective-permute-done.22.up = bf16[128,512]{1,0:T(8,128)(2,1)S(1)} collective-permute-done((bf16[128,512]{1,0:T(8,128)(2,1)S(1)}, bf16[128,512]{1,0:T(8,128)(2,1)S(1)}, u32[]{:S(2)}, u32[]{:S(2)}) %collective-permute-start.22) | collective-permute-done | bytes 131104 | tf_op jit(solution)/shard_map/ppermute | solution.py:38
  83.7 2.9 %collective-permute-start.26 = (bf16[256,512]{1,0:T(8,128)(2,1)S(1)}, bf16[256,512]{1,0:T(8,128)(2,1)S(1)}, u32[]{:S(2)}, u32[]{:S(2)}) collective-permute-start(bf16[256,512]{1,0:T(8,128)(2,1)S(1)} %get-tuple-element.79), channel_id=1, source_target_pairs={{0,8},{1,9},{2,10},{3,11},{4,12},{5,13},{6,14},{7,15},{8,0},{9,1},... | collective-permute-start | bytes 786440 | tf_op jit(solution)/shard_map/ppermute | solution.py:38
  86.7 3.2 %collective-permute-start.25 = (bf16[256,512]{1,0:T(8,128)(2,1)S(1)}, bf16[256,512]{1,0:T(8,128)(2,1)S(1)}, u32[]{:S(2)}, u32[]{:S(2)}) collective-permute-start(bf16[256,512]{1,0:T(8,128)(2,1)S(1)} %get-tuple-element.78), channel_id=1, source_target_pairs={{0,6},{1,7},{2,0},{3,1},{4,2},{5,3},{6,4},{7,5},{8,14},{9,15},{10,... | collective-permute-start | bytes 786440 | tf_op jit(solution)/shard_map/ppermute | solution.py:38
  91.2 11.4 %collective-permute-done.30 = bf16[1,4,8,256]{3,2,1,0:T(8,128)(2,1)S(1)} collective-permute-done((bf16[1,4,8,256]{3,2,1,0:T(8,128)(2,1)S(1)}, bf16[1,4,8,256]{3,2,1,0:T(8,128)(2,1)S(1)}, u32[]{:S(2)}, u32[]{:S(2)}) %collective-permute-start.30) | collective-permute-done | bytes 16416 | tf_op jit(solution)/shard_map/ppermute | solution.py:652
  (111 shorter events, 24.1 us)
Async XLA Ops:
  0.6 21.2 %collective-permute-start.4 = (bf16[256,512]{1,0:T(8,128)(2,1)}, bf16[256,512]{1,0:T(8,128)(2,1)S(1)}, u32[]{:S(2)}, u32[]{:S(2)}) collective-permute-start(bf16[256,512]{1,0:T(8,128)(2,1)} %bitcast.56), channel_id=1, source_target_pairs={{0,1},{1,0},{2,3},{3,2},{4,5},{5,4},{6,7},{7,6},{8,9},{9,8},{10,11... | collective-permute-start | bytes 786440 | tf_op jit(solution)/shard_map/ppermute | solution.py:38
  0.7 13.0 %collective-permute-start.3 = (bf16[256,512]{1,0:T(8,128)(2,1)}, bf16[256,512]{1,0:T(8,128)(2,1)S(1)}, u32[]{:S(2)}, u32[]{:S(2)}) collective-permute-start(bf16[256,512]{1,0:T(8,128)(2,1)} %bitcast.57), channel_id=1, source_target_pairs={{0,8},{1,9},{2,10},{3,11},{4,12},{5,13},{6,14},{7,15},{8,0},{9,1},... | collective-permute-start | bytes 786440 | tf_op jit(solution)/shard_map/ppermute | solution.py:38
  3.8 9.9 %collective-permute-start.2 = (bf16[256,512]{1,0:T(8,128)(2,1)}, bf16[256,512]{1,0:T(8,128)(2,1)S(1)}, u32[]{:S(2)}, u32[]{:S(2)}) collective-permute-start(bf16[256,512]{1,0:T(8,128)(2,1)} %bitcast.58), channel_id=1, source_target_pairs={{0,6},{1,7},{2,0},{3,1},{4,2},{5,3},{6,4},{7,5},{8,14},{9,15},{10,... | collective-permute-start | bytes 786440 | tf_op jit(solution)/shard_map/ppermute | solution.py:38
  6.9 9.5 %collective-permute-start.1 = (bf16[256,512]{1,0:T(8,128)(2,1)}, bf16[256,512]{1,0:T(8,128)(2,1)S(1)}, u32[]{:S(2)}, u32[]{:S(2)}) collective-permute-start(bf16[256,512]{1,0:T(8,128)(2,1)} %bitcast.59), channel_id=1, source_target_pairs={{0,2},{1,3},{2,4},{3,5},{4,6},{5,7},{6,0},{7,1},{8,10},{9,11},{10,... | collective-permute-start | bytes 786440 | tf_op jit(solution)/shard_map/ppermute | solution.py:38
  10.7 49.2 %collective-permute-start = (bf16[256,4096]{1,0:T(8,128)(2,1)}, bf16[256,4096]{1,0:T(8,128)(2,1)}, u32[]{:S(2)}, u32[]{:S(2)}) collective-permute-start(bf16[256,4096]{1,0:T(8,128)(2,1)} %shard_map.95), channel_id=1, source_target_pairs={{0,1},{1,0},{2,3},{3,2},{4,5},{5,4},{6,7},{7,6},{8,9},{9,8},{10,11... | collective-permute-start | bytes 6291464 | tf_op jit(solution)/shard_map/ppermute | solution.py:38
  17.4 8.6 %collective-permute-start.10 = (bf16[128,512]{1,0:T(8,128)(2,1)}, bf16[128,512]{1,0:T(8,128)(2,1)}, u32[]{:S(2)}, u32[]{:S(2)}) collective-permute-start(bf16[128,512]{1,0:T(8,128)(2,1)} %get-tuple-element.60), channel_id=1, source_target_pairs={{0,14},{1,15},{2,8},{3,9},{4,10},{5,11},{6,12},{7,13},{8,6},{9,7},... | collective-permute-start | bytes 393224 | tf_op jit(solution)/shard_map/ppermute | solution.py:38
  17.9 9.6 %collective-permute-start.11 = (bf16[128,512]{1,0:T(8,128)(2,1)}, bf16[128,512]{1,0:T(8,128)(2,1)}, u32[]{:S(2)}, u32[]{:S(2)}) collective-permute-start(bf16[128,512]{1,0:T(8,128)(2,1)} %get-tuple-element.61), channel_id=1, source_target_pairs={{0,10},{1,11},{2,12},{3,13},{4,14},{5,15},{6,8},{7,9},{8,2},{9,3},... | collective-permute-start | bytes 393224 | tf_op jit(solution)/shard_map/ppermute | solution.py:38
  21.8 14.0 %collective-permute-start.8 = (bf16[384,512]{1,0:T(8,128)(2,1)}, bf16[384,512]{1,0:T(8,128)(2,1)S(1)}, u32[]{:S(2)}, u32[]{:S(2)}) collective-permute-start(bf16[384,512]{1,0:T(8,128)(2,1)} %get-tuple-element.58), channel_id=1, source_target_pairs={{0,2},{1,3},{2,4},{3,5},{4,6},{5,7},{6,0},{7,1},{8,10},{9,11},{10,... | collective-permute-start | bytes 1179656 | tf_op jit(solution)/shard_map/ppermute | solution.py:38
  22.5 13.3 %collective-permute-start.9 = (bf16[384,512]{1,0:T(8,128)(2,1)}, bf16[384,512]{1,0:T(8,128)(2,1)S(1)}, u32[]{:S(2)}, u32[]{:S(2)}) collective-permute-start(bf16[384,512]{1,0:T(8,128)(2,1)} %get-tuple-element.59), channel_id=1, source_target_pairs={{0,6},{1,7},{2,0},{3,1},{4,2},{5,3},{6,4},{7,5},{8,14},{9,15},{10,... | collective-permute-start | bytes 1179656 | tf_op jit(solution)/shard_map/ppermute | solution.py:38
  27.6 9.9 %collective-permute-start.6 = (bf16[256,512]{1,0:T(8,128)(2,1)S(1)}, bf16[256,512]{1,0:T(8,128)(2,1)}, u32[]{:S(2)}, u32[]{:S(2)}) collective-permute-start(bf16[256,512]{1,0:T(8,128)(2,1)S(1)} %collective-permute-done.2.refs_2_.next_ref), channel_id=1, source_target_pairs={{0,1},{1,0},{2,3},{3,2},{4,5},{5,4},{6,7},{7,6},{8,9},{9,8},{10,11... | collective-permute-start | bytes 786440 | tf_op jit(solution)/shard_map/ppermute | solution.py:38
  27.7 9.9 %collective-permute-start.5 = (bf16[256,512]{1,0:T(8,128)(2,1)}, bf16[256,512]{1,0:T(8,128)(2,1)}, u32[]{:S(2)}, u32[]{:S(2)}) collective-permute-start(bf16[256,512]{1,0:T(8,128)(2,1)} %copy-done.5), channel_id=1, source_target_pairs={{0,1},{1,0},{2,3},{3,2},{4,5},{5,4},{6,7},{7,6},{8,9},{9,8},{10,11... | collective-permute-start | bytes 786440 | tf_op jit(solution)/shard_map/ppermute | solution.py:38
  35.8 9.4 %collective-permute-start.12 = (bf16[384,512]{1,0:T(8,128)(2,1)S(1)}, bf16[384,512]{1,0:T(8,128)(2,1)}, u32[]{:S(2)}, u32[]{:S(2)}) collective-permute-start(bf16[384,512]{1,0:T(8,128)(2,1)S(1)} %collective-permute-done.8.from_last.refs_0_), channel_id=1, source_target_pairs={{0,1},{1,0},{2,3},{3,2},{4,5},{5,4},{6,7},{7,6},{8,9},{9,8},{10,11... | collective-permute-start | bytes 1179656 | tf_op jit(solution)/shard_map/ppermute | solution.py:38
  35.8 9.4 %collective-permute-start.13 = (bf16[384,512]{1,0:T(8,128)(2,1)S(1)}, bf16[384,512]{1,0:T(8,128)(2,1)}, u32[]{:S(2)}, u32[]{:S(2)}) collective-permute-start(bf16[384,512]{1,0:T(8,128)(2,1)S(1)} %collective-permute-done.9.from_next.refs_1_), channel_id=1, source_target_pairs={{0,1},{1,0},{2,3},{3,2},{4,5},{5,4},{6,7},{7,6},{8,9},{9,8},{10,11... | collective-permute-start | bytes 1179656 | tf_op jit(solution)/shard_map/ppermute | solution.py:38
  37.5 7.7 %collective-permute-start.14 = (bf16[256,512]{1,0:T(8,128)(2,1)S(1)}, bf16[256,512]{1,0:T(8,128)(2,1)S(1)}, u32[]{:S(2)}, u32[]{:S(2)}) collective-permute-start(bf16[256,512]{1,0:T(8,128)(2,1)S(1)} %shard_map.98.refs_2_), channel_id=1, source_target_pairs={{0,1},{1,0},{2,3},{3,2},{4,5},{5,4},{6,7},{7,6},{8,9},{9,8},{10,11... | collective-permute-start | bytes 786440 | tf_op jit(solution)/shard_map/ppermute | solution.py:38
  48.9 8.3 %collective-permute-start.18 = (bf16[256,128]{1,0:T(8,128)(2,1)}, bf16[256,128]{1,0:T(8,128)(2,1)S(1)}, u32[]{:S(2)}, u32[]{:S(2)}) collective-permute-start(bf16[256,128]{1,0:T(8,128)(2,1)} %get-tuple-element.65), channel_id=1, source_target_pairs={{0,0},{1,2},{2,4},{3,6},{4,8},{5,10},{6,12},{7,14},{8,1},{9,3},{10... | collective-permute-start | bytes 196616 | tf_op jit(solution)/shard_map/ppermute | solution.py:575
  66.2 15.5 %collective-permute-start.20 = (bf16[384,512]{1,0:T(8,128)(2,1)S(1)}, bf16[384,512]{1,0:T(8,128)(2,1)S(1)}, u32[]{:S(2)}, u32[]{:S(2)}) collective-permute-start(bf16[384,512]{1,0:T(8,128)(2,1)S(1)} %get-tuple-element.73), channel_id=1, source_target_pairs={{0,2},{1,3},{2,4},{3,5},{4,6},{5,7},{6,0},{7,1},{8,10},{9,11},{10,... | collective-permute-start | bytes 1179656 | tf_op jit(solution)/shard_map/ppermute | solution.py:38
  67.7 14.4 %collective-permute-start.21 = (bf16[384,512]{1,0:T(8,128)(2,1)S(1)}, bf16[384,512]{1,0:T(8,128)(2,1)S(1)}, u32[]{:S(2)}, u32[]{:S(2)}) collective-permute-start(bf16[384,512]{1,0:T(8,128)(2,1)S(1)} %get-tuple-element.74), channel_id=1, source_target_pairs={{0,6},{1,7},{2,0},{3,1},{4,2},{5,3},{6,4},{7,5},{8,14},{9,15},{10,... | collective-permute-start | bytes 1179656 | tf_op jit(solution)/shard_map/ppermute | solution.py:38
  69.6 10.0 %collective-permute-start.22 = (bf16[128,512]{1,0:T(8,128)(2,1)S(1)}, bf16[128,512]{1,0:T(8,128)(2,1)S(1)}, u32[]{:S(2)}, u32[]{:S(2)}) collective-permute-start(bf16[128,512]{1,0:T(8,128)(2,1)S(1)} %get-tuple-element.75), channel_id=1, source_target_pairs={{0,10},{1,11},{2,12},{3,13},{4,14},{5,15},{6,8},{7,9},{8,2},{9,3},... | collective-permute-start | bytes 393224 | tf_op jit(solution)/shard_map/ppermute | solution.py:38
  72.3 8.2 %collective-permute-start.23 = (bf16[128,512]{1,0:T(8,128)(2,1)S(1)}, bf16[128,512]{1,0:T(8,128)(2,1)S(1)}, u32[]{:S(2)}, u32[]{:S(2)}) collective-permute-start(bf16[128,512]{1,0:T(8,128)(2,1)S(1)} %get-tuple-element.76), channel_id=1, source_target_pairs={{0,14},{1,15},{2,8},{3,9},{4,10},{5,11},{6,12},{7,13},{8,6},{9,7},... | collective-permute-start | bytes 393224 | tf_op jit(solution)/shard_map/ppermute | solution.py:38
  83.1 6.9 %collective-permute-start.29 = (bf16[2,1,4,8,256]{4,3,2,1,0:T(8,128)(2,1)S(1)}, bf16[2,1,4,8,256]{4,3,2,1,0:T(8,128)(2,1)S(1)}, u32[]{:S(2)}, u32[]{:S(2)}) collective-permute-start(bf16[2,1,4,8,256]{4,3,2,1,0:T(8,128)(2,1)S(1)} %slice.32), channel_id=1, source_target_pairs={{64,80},{96,112},{65,81},{97,113},{66,82},{98,114},{67,83},{99,115... | collective-permute-start | bytes 98312 | tf_op jit(solution)/shard_map/ppermute | solution.py:650
  83.7 19.5 %collective-permute-start.26 = (bf16[256,512]{1,0:T(8,128)(2,1)S(1)}, bf16[256,512]{1,0:T(8,128)(2,1)S(1)}, u32[]{:S(2)}, u32[]{:S(2)}) collective-permute-start(bf16[256,512]{1,0:T(8,128)(2,1)S(1)} %get-tuple-element.79), channel_id=1, source_target_pairs={{0,8},{1,9},{2,10},{3,11},{4,12},{5,13},{6,14},{7,15},{8,0},{9,1},... | collective-permute-start | bytes 786440 | tf_op jit(solution)/shard_map/ppermute | solution.py:38
  86.7 16.5 %collective-permute-start.24 = (bf16[256,512]{1,0:T(8,128)(2,1)S(1)}, bf16[256,512]{1,0:T(8,128)(2,1)S(1)}, u32[]{:S(2)}, u32[]{:S(2)}) collective-permute-start(bf16[256,512]{1,0:T(8,128)(2,1)S(1)} %get-tuple-element.77), channel_id=1, source_target_pairs={{0,2},{1,3},{2,4},{3,5},{4,6},{5,7},{6,0},{7,1},{8,10},{9,11},{10,... | collective-permute-start | bytes 786440 | tf_op jit(solution)/shard_map/ppermute | solution.py:38
  86.7 16.5 %collective-permute-start.25 = (bf16[256,512]{1,0:T(8,128)(2,1)S(1)}, bf16[256,512]{1,0:T(8,128)(2,1)S(1)}, u32[]{:S(2)}, u32[]{:S(2)}) collective-permute-start(bf16[256,512]{1,0:T(8,128)(2,1)S(1)} %get-tuple-element.78), channel_id=1, source_target_pairs={{0,6},{1,7},{2,0},{3,1},{4,2},{5,3},{6,4},{7,5},{8,14},{9,15},{10,... | collective-permute-start | bytes 786440 | tf_op jit(solution)/shard_map/ppermute | solution.py:38
  89.9 12.7 %collective-permute-start.30 = (bf16[1,4,8,256]{3,2,1,0:T(8,128)(2,1)S(1)}, bf16[1,4,8,256]{3,2,1,0:T(8,128)(2,1)S(1)}, u32[]{:S(2)}, u32[]{:S(2)}) collective-permute-start(bf16[1,4,8,256]{3,2,1,0:T(8,128)(2,1)S(1)} %slice_bitcast_fusion), channel_id=1, source_target_pairs={{80,16},{96,32},{112,48},{81,17},{97,33},{113,49},{82,18},{98,34},... | collective-permute-start | bytes 49160 | tf_op jit(solution)/shard_map/ppermute | solution.py:652
  (20 other events, 88.1 us)

commit v2 on v1

--- a/solution.py
+++ b/solution.py
@@ -1,3 +1,5 @@
+import functools
+
 import jax
 import jax.numpy as jnp
 from jax import lax
@@ -65,9 +67,22 @@
 LOG2_E = 1.4426950408889634
 NT = (((1,), (1,)), ((), ()))
 
-
-def stacked_heads(queries):
-    return jnp.concatenate([queries[:, j * HD : (j + 1) * HD] for j in range(GQ)], axis=0)
+CORE, IS_PREFILL, IS_KEY, NEAR_ROWS, FAR_ROWS, PLACE, CELLS, PICKS = 0, 1, 2, 3, 11, 19, 27, 43
+
+
+def stacked_heads(*parts):
+    return jnp.concatenate(
+        [part[:, j * HD : (j + 1) * HD] for part in parts for j in range(part.shape[1] // HD)],
+        axis=0,
+    )
+
+
+def length_bias(scalar_ref, length_ref, first, count):
+    place = lax.broadcasted_iota(jnp.int32, (1, SPAN), 1) + scalar_ref[CORE] * SPAN
+    return jnp.concatenate(
+        [jnp.where(place < length_ref[first + row], 0.0, NEG_FILL) for row in range(count)],
+        axis=1,
+    )
 
 
 def weights_of(scores, largest):
@@ -93,7 +108,18 @@
 
 
 def prefill_kernel(
-    query_ref, key_ref, value_ref, bias_ref, mixed_ref, level_ref, keys, values, score_ref, sems
+    scalar_ref,
+    length_ref,
+    own_ref,
+    other_ref,
+    key_ref,
+    value_ref,
+    mixed_ref,
+    level_ref,
+    keys,
+    values,
+    score_ref,
+    sems,
 ):
     rows = PREFILL_CHUNK // SPAN
     chunks = RP // rows
@@ -113,13 +139,13 @@
 
     def one_prompt(prompt, carry):
         tokens = pl.ds(pl.multiple_of(prompt * CH, CH), CH)
-        queries = stacked_heads(query_ref[tokens, :])
+        queries = stacked_heads(own_ref[tokens, :], other_ref[tokens, :])
 
         def score_step(step, peak):
             fetches(prompt, step)[0].wait()
             part = keys[pl.ds(prompt * RP + step * rows, rows)].reshape(PREFILL_CHUNK, HD)
             scores = lax.dot_general(queries, part, NT, preferred_element_type=jnp.float32)
-            scores = scores + bias_ref[prompt, pl.ds(step, 1), :]
+            scores = scores + length_bias(scalar_ref, length_ref, prompt * RP + step * rows, rows)
             score_ref[step] = scores
             for lanes in range(PREFILL_CHUNK // HD):
                 peak = jnp.maximum(peak, scores[:, lanes * HD : (lanes + 1) * HD])
@@ -150,7 +176,9 @@
     lax.fori_loop(0, NPR, one_prompt, 0)
 
 
-def decode_kernel(query_ref, key_ref, value_ref, bias_ref, mixed_ref, level_ref):
+def decode_kernel(
+    scalar_ref, length_ref, query_ref, key_ref, value_ref, mixed_ref, level_ref
+):
     width = ROWS_AT_ONCE * SPAN
     tokens = ROWS_AT_ONCE * STEPS
     owner = lax.broadcasted_iota(jnp.int32, (GQ * tokens, width), 0) % tokens // STEPS
@@ -162,7 +190,9 @@
         keys = key_ref[cached].reshape(width, HD)
         values = value_ref[cached].reshape(width, HD)
         scores = lax.dot_general(queries, keys, NT, preferred_element_type=jnp.float32)
-        scores = jnp.where(owner == holder, scores + bias_ref[part : part + 1, :], NEG_FILL)
+        first = (pl.program_id(0) * (query_ref.shape[0] // tokens) + part) * ROWS_AT_ONCE
+        bias = length_bias(scalar_ref, length_ref, first, ROWS_AT_ONCE)
+        scores = jnp.where(owner == holder, scores + bias, NEG_FILL)
         largest = jnp.max(scores, axis=1, keepdims=True)
         mixed = jnp.dot(
             weights_of(scores, largest), with_ones(values), preferred_element_type=jnp.float32
@@ -170,20 +200,26 @@
         write_heads(mixed_ref, level_ref, rows, mixed, largest)
 
 
-def recent_kernel(prefill_ref, query_ref, key_ref, value_ref, mixed_ref, level_ref):
-    is_prefill = prefill_ref[0] != 0
+def pair_of(scalar_ref, held_ref, other_ref):
+    first = scalar_ref[CORE] == 0
+    held, other = held_ref[...], other_ref[...]
+    return jnp.where(first, held, other), jnp.where(first, other, held)
+
+
+def recent_kernel(scalar_ref, own_ref, other_ref, held_ref, swapped_ref, mixed_ref, level_ref):
+    is_prefill = scalar_ref[IS_PREFILL] != 0
+    keys, values = pair_of(scalar_ref, held_ref, swapped_ref)
     row = lax.broadcasted_iota(jnp.int32, (TOK, TOK), 0)
     column = lax.broadcasted_iota(jnp.int32, (TOK, TOK), 1)
     together = jnp.where(is_prefill, row // CH - column // CH, row % R - column % R) == 0
     allowed = together & (column <= row)
-    values = with_ones(value_ref[...])
+    values = with_ones(values)
+    queries = [ref[:, j * HD : (j + 1) * HD] for ref in (own_ref, other_ref) for j in range(2)]
     lane = lax.broadcasted_iota(jnp.int32, (TOK, GQ), 1)
     levels = jnp.zeros((TOK, GQ), jnp.float32)
     for j in range(GQ):
         head = slice(j * HD, (j + 1) * HD)
-        scores = lax.dot_general(
-            query_ref[:, head], key_ref[...], NT, preferred_element_type=jnp.float32
-        )
+        scores = lax.dot_general(queries[j], keys, NT, preferred_element_type=jnp.float32)
         scores = jnp.where(allowed, scores, NEG_FILL)
         largest = jnp.max(scores, axis=1, keepdims=True)
         mixed = jnp.dot(weights_of(scores, largest), values, preferred_element_type=jnp.float32)
@@ -194,22 +230,23 @@
 
 
 def merged(parts, levels):
-    top = jnp.maximum(jnp.maximum(levels[0], levels[1]), levels[2])
-    shares = [jnp.exp(level - top) for level in levels]
-    total = shares[0] + shares[1] + shares[2]
-    shares = [share / total for share in shares]
     heads = []
     for j in range(GQ):
-        head = slice(j * HD, (j + 1) * HD)
+        places = (j, (j + GQ // 2) % GQ, j)
+        columns = [level[:, place : place + 1] for level, place in zip(levels, places)]
+        top = jnp.maximum(jnp.maximum(columns[0], columns[1]), columns[2])
+        shares = [jnp.exp(column - top) for column in columns]
+        total = shares[0] + shares[1] + shares[2]
         mixed = jnp.zeros((TOK, HD), jnp.float32)
-        for part, share in zip(parts, shares):
-            mixed = mixed + part[:, head].astype(jnp.float32) * share[:, j : j + 1]
+        for part, share, place in zip(parts, shares, places):
+            values = part[:, place * HD : (place + 1) * HD].astype(jnp.float32)
+            mixed = mixed + values * (share / total)
         heads.append(mixed.astype(jnp.bfloat16))
     return jnp.concatenate(heads, axis=1)
 
 
 def merge_out_kernel(
-    place_ref,
+    scalar_ref,
     weight_ref,
     swapped_ref,
     own_ref,
@@ -226,15 +263,14 @@
     last_ref,
     partner_ref,
     here_ref,
-    attention_ref,
     held_ref,
     sems,
 ):
-    core = place_ref[0]
+    core = scalar_ref[CORE]
     rows = weight_ref.shape[0]
     copies = []
     for index in range(CHIPS):
-        chip = place_ref[1 + index]
+        chip = scalar_ref[PLACE + index]
         own = pl.ds(pl.multiple_of((2 * chip + core) * SHARD, SHARD), SHARD)
         other = pl.ds(pl.multiple_of(chip * SHARD, SHARD), SHARD)
         pair = (
@@ -248,12 +284,9 @@
         for copy in pair:
             copy.start()
         copies.append(pair)
-    attention_ref[...] = merged(
+    joined = merged(
         (own_ref, other_ref, recent_ref), (own_level[...], other_level[...], recent_level[...])
     )
-    own = attention_ref[:, pl.ds(pl.multiple_of(core * rows, rows), rows)]
-    other = attention_ref[:, pl.ds(pl.multiple_of((1 - core) * rows, rows), rows)]
-    joined = jnp.concatenate([own, other], axis=1)
 
     def product(index):
         for copy in copies[index]:
@@ -294,24 +327,21 @@
     out_ref[...] = total_of(here_ref[...], from_last[...], from_next[...], from_partner[...])
 
 
-def join_kernel(token_ref, partner_ref, last_ref, next_ref, plus, minus, up, down):
+def join_kernel(scalar_ref, partner_ref, last_ref, next_ref, plus, minus, near):
     plus[:TOK] = partner_ref[...]
     plus[TOK:] = last_ref[:HALF]
     minus[:TOK] = partner_ref[...]
     minus[TOK:] = next_ref[HALF:]
-    up[...] = last_ref[HALF:]
-    down[...] = next_ref[:HALF]
-
-
-def far_join_kernel(from_last, from_next, upper_ref, lower_ref, far):
-    far[:HALF] = upper_ref[...]
-    far[HALF:] = lower_ref[...]
-
-
-def projected_parts(row_ref, shards, query_weight, pair_weight):
+    near[:TOK] = last_ref[...]
+    near[TOK : 2 * TOK] = next_ref[...]
+    near[2 * TOK :] = partner_ref[...]
+
+
+def projected_parts(scalar_ref, first, shards, query_weight, pair_weight):
     joined = jnp.concatenate(shards, axis=1)
     rows = [
-        pl.ds(pl.multiple_of(row_ref[index], SHARD), SHARD) for index in range(len(shards))
+        pl.ds(pl.multiple_of(scalar_ref[first + index], SHARD), SHARD)
+        for index in range(len(shards))
     ]
     return [
         jnp.dot(
@@ -323,22 +353,28 @@
     ]
 
 
-def near_kernel(row_ref, query_weight, pair_weight, *refs):
-    *shards, query, pair = refs
+def near_kernel(scalar_ref, query_weight, pair_weight, *refs):
+    *sources, query, pair, mark = refs
+    mark[...] = jnp.zeros_like(mark)
+    shards = []
+    for own_ref, near_ref in (sources[:2], sources[2:]):
+        shards.append(own_ref[...])
+        shards.extend(near_ref[index * TOK : (index + 1) * TOK] for index in range(3))
     query[...], pair[...] = projected_parts(
-        row_ref, [ref[...] for ref in shards], query_weight, pair_weight
-    )
-
-
-def far_shards(last_ref, next_ref, far_ref):
-    far = jnp.concatenate([last_ref[TOK:], next_ref[TOK:]], axis=0)
-    return [last_ref[:TOK], next_ref[:TOK], far, far_ref[...]]
-
-
-def last_kernel(row_ref, query_weight, pair_weight, query_in, pair_in, *refs):
+        scalar_ref, NEAR_ROWS, shards, query_weight, pair_weight
+    )
+
+
+def far_shards(last_ref, next_ref, upper_ref, lower_ref):
+    middle = jnp.concatenate([last_ref[TOK:], next_ref[TOK:]], axis=0)
+    far = jnp.concatenate([upper_ref[...], lower_ref[...]], axis=0)
+    return [last_ref[:TOK], next_ref[:TOK], middle, far]
+
+
+def last_kernel(scalar_ref, query_weight, pair_weight, query_in, pair_in, *refs):
     *sides, cosine_ref, sine_ref, query_out, pair_out = refs
-    shards = far_shards(*sides[:3]) + far_shards(*sides[3:])
-    sums = projected_parts(row_ref, shards, query_weight, pair_weight)
+    shards = far_shards(*sides[:4]) + far_shards(*sides[4:])
+    sums = projected_parts(scalar_ref, FAR_ROWS, shards, query_weight, pair_weight)
     query = query_in[...] + sums[0]
     pair = pair_in[...] + sums[1]
     cosine = cosine_ref[...]
@@ -350,21 +386,29 @@
     for head in range(query.shape[1] // HD):
         part = slice(head * HD, (head + 1) * HD)
         query_out[:, part] = rotated(query[:, part]).astype(jnp.bfloat16)
-    is_key = row_ref[len(shards)] != 0
+    is_key = scalar_ref[IS_KEY] != 0
     pair_out[...] = jnp.where(is_key, rotated(pair), pair).astype(jnp.bfloat16)
 
 
-def blocks_kernel(cell_ref, key_ref, value_ref, out_ref):
+def blocks_kernel(scalar_ref, held_ref, swapped_ref, out_ref, pair_ref):
     sliver = out_ref.shape[1]
     out_ref[...] = jnp.zeros_like(out_ref)
 
-    @pl.when(cell_ref[0] != 0)
+    @pl.when(scalar_ref[IS_PREFILL] != 0)
     def _():
+        keys, values = pair_of(scalar_ref, held_ref, swapped_ref)
+        pair_ref[:, :HD] = keys.astype(jnp.float32)
+        pair_ref[:, HD:] = values.astype(jnp.float32)
         for block in range(TOK // BS):
-            start = pl.multiple_of(cell_ref[1] * sliver, sliver) + block * BS
-            cell = cell_ref[2 + block]
-            out_ref[cell, :, :HD] = key_ref[pl.ds(start, sliver), :]
-            out_ref[cell, :, HD:] = value_ref[pl.ds(start, sliver), :]
+            start = pl.multiple_of(scalar_ref[CORE] * sliver, sliver) + block * BS
+            out_ref[scalar_ref[CELLS + block]] = pair_ref[pl.ds(start, sliver), :].astype(
+                jnp.bfloat16
+            )
+
+
+def pick_kernel(pick, scalar_ref, sent_ref, kept_ref, out_ref):
+    chosen = scalar_ref[PICKS + pick] != 0
+    out_ref[...] = jnp.where(chosen, sent_ref[...], kept_ref[...])
 
 
 def called(kernel, shapes, scalars, *arrays, streamed=(), scratch=(), flops=0, grant=12):
@@ -392,13 +436,14 @@
     )
 
 
-def prefill_part(queries, keys, values, bias):
+def prefill_part(scalars, lengths, own, other, keys, values):
     chunks = RP * SPAN // PREFILL_CHUNK
     whole = pl.BlockSpec(memory_space=pltpu.VMEM)
     there = pl.BlockSpec(memory_space=pl.ANY)
+    small = pl.BlockSpec(memory_space=pltpu.SMEM)
     return pl.pallas_call(
         prefill_kernel,
-        in_specs=[whole, there, there, whole],
+        in_specs=[small, small, whole, whole, there, there],
         out_specs=(whole, whole),
         out_shape=outputs_of(jnp.bfloat16),
         scratch_shapes=[
@@ -408,10 +453,10 @@
             pltpu.SemaphoreType.DMA((2, NPR * chunks)),
         ],
         compiler_params=pltpu.CompilerParams(vmem_limit_bytes=44 * 2**20),
-    )(queries, keys, values, bias.reshape(NPR, chunks, PREFILL_CHUNK))
-
-
-def decode_part(queries, keys, values, bias):
+    )(scalars, lengths, own, other, keys, values)
+
+
+def decode_part(scalars, lengths, own, other, keys, values):
     def by_row(array):
         return array.reshape(STEPS, R, -1).transpose(1, 0, 2).reshape(TOK, -1)
 
@@ -423,10 +468,11 @@
         decode_kernel,
         grid=(R // rows,),
         in_specs=[
+            pl.BlockSpec(memory_space=pltpu.SMEM),
+            pl.BlockSpec(memory_space=pltpu.SMEM),
             pl.BlockSpec((rows * STEPS, GQ * HD), lambda i: (i, 0)),
             pl.BlockSpec((rows, SPAN, HD), lambda i: (i, 0, 0)),
             pl.BlockSpec((rows, SPAN, HD), lambda i: (i, 0, 0)),
-            pl.BlockSpec((rows // ROWS_AT_ONCE, ROWS_AT_ONCE * SPAN), lambda i: (i, 0)),
         ],
         out_specs=(
             pl.BlockSpec((rows * STEPS, GQ * HD), lambda i: (i, 0)),
@@ -434,26 +480,15 @@
         ),
         out_shape=outputs_of(jnp.bfloat16),
         compiler_params=pltpu.CompilerParams(vmem_limit_bytes=40 * 2**20),
-    )(by_row(queries), keys, values, bias.reshape(R // ROWS_AT_ONCE, ROWS_AT_ONCE * SPAN))
+    )(scalars, lengths, by_row(jnp.concatenate([own, other], axis=1)), keys, values)
     return by_step(mixed), by_step(level)
 
 
-def recent_part(is_prefill, queries, keys, values):
-    whole = pl.BlockSpec(memory_space=pltpu.VMEM)
-    return pl.pallas_call(
-        recent_kernel,
-        in_specs=[pl.BlockSpec(memory_space=pltpu.SMEM), whole, whole, whole],
-        out_specs=(whole, whole),
-        out_shape=outputs_of(jnp.float32),
-        compiler_params=pltpu.CompilerParams(vmem_limit_bytes=16 * 2**20),
-    )(is_prefill.astype(jnp.int32).reshape(1), queries, keys, values)
-
-
-def cut_kernel(core_ref, weight_ref, out_ref, held_ref, in_sems, out_sems):
+def cut_kernel(scalar_ref, weight_ref, out_ref, held_ref, in_sems, out_sems):
     fetches = []
     stores = []
     for chip in range(CHIPS):
-        columns = pl.ds(pl.multiple_of((2 * chip + 1 - core_ref[0]) * SHARD, SHARD), SHARD)
+        columns = pl.ds(pl.multiple_of((2 * chip + 1 - scalar_ref[CORE]) * SHARD, SHARD), SHARD)
         fetches.append(
             pltpu.make_async_copy(weight_ref.at[:, columns], held_ref.at[chip], in_sems.at[chip])
         )
@@ -473,7 +508,7 @@
         store.wait()
 
 
-def cut_columns(out_weight, core):
+def cut_columns(scalars, out_weight):
     return pl.pallas_call(
         cut_kernel,
         in_specs=[
@@ -488,85 +523,93 @@
             pltpu.SemaphoreType.DMA((CHIPS,)),
         ],
         compiler_params=pltpu.CompilerParams(vmem_limit_bytes=12 * 2**20),
-    )(core.reshape(1), out_weight)
+    )(scalars, out_weight)
 
 
 def on_device(
     layer_input, query_weight, kv_weight, out_weight, cache_keys, cache_values, lengths, placement
 ):
     group_count = lax.axis_size("group")
-    splits = 2
     tp_rank = lax.axis_index("tp")
     group_rank = lax.axis_index("group")
     core = tp_rank % 2
     y = (tp_rank // 2) % 4
     x_hi = tp_rank // 8
-    block_index = core
-    last_block = block_index == splits - 1
     is_prefill = group_rank == 0
     tokens = layer_input[0]
     row_lengths = lengths[0]
+    slot_count = 2 * (TOK // BS) // (group_count - 1)
+
+    def rows_of(*owners):
+        firsts = [tp_index(x_hi ^ flip, y + step, core) for flip, step in owners]
+        return [first * SHARD for first in firsts] + [(first ^ 1) * SHARD for first in firsts]
+
+    places = ((1, 1), (1, 3), (0, 2), (1, 2), (0, 1), (0, 3), (1, 0), (0, 0))
+    single = (
+        [core, is_prefill, tp_rank < KVH]
+        + rows_of((0, 0), (0, 3), (0, 1), (1, 0))
+        + rows_of((1, 3), (1, 1), (0, 2), (1, 2))
+        + [(x_hi ^ flip) * 4 + (y + step) % 4 for flip, step in places]
+    )
+    picks = [group_rank == 6, group_rank % 2 == 1, group_rank < 4]
+    scalars = jnp.concatenate(
+        [
+            jnp.stack([jnp.asarray(one, jnp.int32) for one in single]),
+            placement[:, 0] * slot_count + placement[:, 1],
+            jnp.stack([jnp.asarray(one, jnp.int32) for one in picks]),
+        ]
+    )
     prefix = jnp.sum(row_lengths.reshape(NPR, RP), axis=1)
     prompt_positions = (prefix[:, None] + jnp.arange(CH, dtype=jnp.int32)[None, :]).reshape(TOK)
     decode_step_positions = (
         row_lengths[None, :] + jnp.arange(STEPS, dtype=jnp.int32)[:, None]
     ).reshape(TOK)
     positions = jnp.where(is_prefill, prompt_positions, decode_step_positions)
-
     cosine, sine = turns(positions)
 
-    cut_out = cut_columns(out_weight, core)
+    cut_out = cut_columns(scalars, out_weight)
 
     wide = ((TOK + HALF, SHARD), jnp.bfloat16)
     half = ((HALF, SHARD), jnp.bfloat16)
     shard = ((TOK, SHARD), jnp.bfloat16)
+    triple = ((3 * TOK, SHARD), jnp.bfloat16)
     weights = (query_weight, kv_weight)
     sums = (((TOK, query_weight.shape[1]), jnp.float32), ((TOK, kv_weight.shape[1]), jnp.float32))
-
-    def rows_of(*owners):
-        firsts = [tp_index(x_hi ^ flip, y + step, core) for flip, step in owners]
-        return jnp.stack(firsts + [first ^ 1 for first in firsts]).astype(jnp.int32) * SHARD
-
+    partner_tokens = moved(tokens, 1, 0, 0)
     last_tokens, next_tokens = moved(tokens, 0, 1, 0), moved(tokens, 0, 3, 0)
-    partner_tokens = moved(tokens, 1, 0, 0)
-    token, *_ = lax.optimization_barrier((tp_rank.reshape(1), cut_out, cosine, sine))
-    swapped_out = core_swap(cut_out)
-    near = (tokens, last_tokens, next_tokens, partner_tokens)
-    plus, minus, up, down = called(
-        join_kernel, (wide, wide, half, half), token, partner_tokens, last_tokens, next_tokens
+    other_tokens = core_swap(tokens)
+    scalars, *_ = lax.optimization_barrier((scalars, cut_out, cosine, sine))
+    plus, minus, near = called(
+        join_kernel,
+        (wide, wide, triple),
+        scalars,
+        partner_tokens,
+        last_tokens,
+        next_tokens,
     )
     from_last, from_next = moved(plus, 0, 1, 0), moved(minus, 0, 3, 0)
-    (far,) = called(
-        far_join_kernel,
-        (shard,),
-        None,
-        moved(down, 1, 3, 0),
-        moved(up, 1, 1, 0),
-        streamed=(from_last, from_next),
-    )
-    sides = (from_last, from_next, far)
-    part = called(
+    far_upper, far_lower = moved(from_last[:HALF], 0, 1, 0), moved(from_next[HALF:TOK], 0, 3, 0)
+    *part, mark = called(
         near_kernel,
-        sums,
-        rows_of((0, 0), (0, 3), (0, 1), (1, 0)),
+        sums + (((8, HD), jnp.float32),),
+        scalars,
         *weights,
-        *near,
-        *[core_swap(source) for source in near],
+        tokens,
+        near,
+        other_tokens,
+        core_swap(near),
         flops=2 * TOK * 8 * SHARD * 3 * HD,
     )
+    sides = (from_last, from_next, far_upper, far_lower)
+    _, *ready = lax.optimization_barrier((mark, far_upper, far_lower))
     query_local, pair_local = called(
         last_kernel,
         tuple((shape, jnp.bfloat16) for shape, _ in sums),
-        jnp.concatenate(
-            [
-                rows_of((1, 3), (1, 1), (0, 2), (1, 2)),
-                (tp_rank < KVH).astype(jnp.int32)[None],
-            ]
-        ),
+        scalars,
         *weights,
         *part,
         *sides,
-        *[core_swap(source) for source in sides],
+        *[core_swap(source) for source in (from_last, from_next, *ready)],
         cosine,
         sine,
         flops=2 * TOK * 8 * SHARD * 3 * HD,
@@ -575,61 +618,63 @@
     pair_held = lax.ppermute(
         pair_local, "tp", [(t, 2 * t if t < KVH else 2 * (t - KVH) + 1) for t in range(2 * KVH)]
     )
-    my_queries = jnp.concatenate(
-        [jnp.where(core == 0, query_local, query_other), jnp.where(core == 0, query_other, query_local)],
-        axis=1,
-    )
-    present = (block_index * SPAN + jnp.arange(SPAN, dtype=jnp.int32))[None, :] < row_lengths[
-        :, None
-    ]
-    bias = jnp.where(present, 0.0, NEG_FILL).astype(jnp.float32)
+    _, cut_out = lax.optimization_barrier((query_local, cut_out))
+    _, row_lengths = lax.optimization_barrier((pair_held, row_lengths))
+    swapped_out = core_swap(cut_out)
     cached = lax.cond(
-        is_prefill, prefill_part, decode_part, my_queries, cache_keys[0], cache_values[0], bias
-    )
-    _, pair_held = lax.optimization_barrier((cached[1], pair_held))
+        is_prefill,
+        prefill_part,
+        decode_part,
+        scalars,
+        row_lengths,
+        query_local,
+        query_other,
+        cache_keys[0],
+        cache_values[0],
+    )
     pair_other = core_swap(pair_held)
-    my_keys = jnp.where(core == 0, pair_held, pair_other)
-    my_values = jnp.where(core == 0, pair_other, pair_held)
     other_cached = (core_swap(cached[0]), core_swap(cached[1]))
-    recent = recent_part(is_prefill, my_queries, my_keys, my_values)
-
-    places = ((1, 1), (1, 3), (0, 2), (1, 2), (0, 1), (0, 3), (1, 0), (0, 0))
-    place = jnp.stack(
-        [core] + [(x_hi ^ flip) * 4 + (y + step) % 4 for flip, step in places]
-    ).astype(jnp.int32)
+    recent = called(
+        recent_kernel,
+        (((TOK, GQ * HD), jnp.float32), ((TOK, GQ), jnp.float32)),
+        scalars,
+        query_local,
+        query_other,
+        pair_held,
+        pair_other,
+        flops=4 * GQ * TOK * TOK * HD,
+    )
+
     plus, minus, up, down, next_part, last_part, partner_part, here_part = called(
         merge_out_kernel,
         (wide, wide, half, half, shard, shard, shard, shard),
-        place,
+        scalars,
         *cached,
         *other_cached,
         *recent,
         streamed=(out_weight, swapped_out),
         scratch=(
-            pltpu.VMEM((TOK, GQ * HD), jnp.bfloat16),
             pltpu.VMEM((CHIPS, GQ * HD, SHARD), jnp.bfloat16),
             pltpu.SemaphoreType.DMA((2, CHIPS)),
         ),
         flops=2 * TOK * CHIPS * SHARD * GQ * HD,
-        grant=24,
+        grant=16,
     )
     from_last, from_next = moved(plus, 0, 1, 0), moved(minus, 0, 3, 0)
     up, down = moved(up, 1, 1, 0), moved(down, 1, 3, 0)
 
-    block_count = TOK // BS
-    slot_count = 2 * block_count // (group_count - 1)
-    cells = placement[:, 0] * slot_count + placement[:, 1]
-    sender = jnp.stack([is_prefill.astype(jnp.int32), core.astype(jnp.int32)])
     (blocks,) = called(
         blocks_kernel,
-        (((group_count * slot_count, BS // splits, 2 * HD), jnp.bfloat16),),
-        jnp.concatenate([sender, cells]),
-        my_keys,
-        my_values,
+        (((group_count * slot_count, BS // 2, 2 * HD), jnp.bfloat16),),
+        scalars,
+        pair_held,
+        pair_other,
+        scratch=(pltpu.VMEM((TOK, 2 * HD), jnp.float32),),
     )
     _, blocks = lax.optimization_barrier((here_part, blocks))
-    blocks = blocks.reshape(2, 4, slot_count, BS // splits, 2 * HD)
+    blocks = blocks.reshape(2, 4, slot_count, BS // 2, 2 * HD)
     arrived = lax.ppermute(blocks, "group", [(0, 4)])
+
     plus, minus, partner = called(
         second_message_kernel,
         (shard, shard, shard),
@@ -644,13 +689,18 @@
     )
     from_last, from_next = moved(plus, 0, 1, 0), moved(minus, 0, 3, 0)
     from_partner = moved(partner, 1, 0, 0)
+
+    def picked(pick, sent, kept):
+        kernel = functools.partial(pick_kernel, pick)
+        return called(kernel, ((sent.shape, sent.dtype),), scalars, sent, kept)[0]
+
     _, arrived = lax.optimization_barrier((partner, arrived))
     sent = lax.ppermute(arrived[:, 2:], "group", [(4, 6)])
-    arrived = jnp.where(group_rank == 6, sent, arrived[:, :2])
+    arrived = picked(0, sent, arrived[:, :2])
     sent = lax.ppermute(arrived[:, 1:], "group", [(4, 5), (6, 7)])
-    arrived = jnp.where(group_rank % 2 == 1, sent, arrived[:, :1])
+    arrived = picked(1, sent, arrived[:, :1])
     sent = lax.ppermute(arrived[0], "group", [(5, 1), (6, 2), (7, 3)])
-    incoming = jnp.where(group_rank >= 4, arrived[1], sent)
+    incoming = picked(2, sent, arrived[1])
     (projected,) = called(
         total_kernel, (shard,), None, here_part, from_last, from_next, from_partner
     )

time: 105 us -> 110 us (1.048)
  waiting for transfers between devices: 29.3 us -> 41.4 us
  local copies, waits for them, and re-layouts: 11.5 us -> 5.64 us
  starting transfers between devices: 36.6 us -> 35.5 us
    ppermute x26 -> x25, waiting for transfers between devices: 18 us -> 28.9 us  [moved(): return lax.ppermute(shard, 'tp', pairs)]
    unnamed x27 -> x13, local copies, waits for them, and re-layouts: 10.6 us -> 4.92 us
    pallas_call x8 -> x11, Pallas kernels: 13.3 us -> 15 us  [called(): pl.pallas_call(kernel, in_specs=specs, out_specs=tuple((whole for _ in sh...]
    pallas_call x2 -> x1, Pallas kernels: 7.32 us -> 6.13 us  [decode_part(): pl.pallas_call(decode_kernel, grid=(R // rows,), in_specs=[pl.BlockSpec(m...]
    ppermute x26 -> x25, starting transfers between devices: 31.8 us -> 31.6 us  [moved(): return lax.ppermute(shard, 'tp', pairs)]
  transfers between devices with their start and end apart: 31 -> 30, of which waited for: 11 -> 9; matrix products, arithmetic and copies ran while one was open for 4% -> 4% of each run, Pallas kernels for 17% -> 12%
where the time goes in v2:
time: 110 us; the launch traced here: 109 us
  waiting for transfers between devices  41.4 us (38%)
  starting transfers between devices  35.5 us (32%)
  Pallas kernels  22.1 us (20%)
  local copies, waits for them, and re-layouts  5.64 us (5%)
  other arithmetic  3.62 us (3%)
    ppermute x25, starting transfers between devices, moved(): return lax.ppermute(shard, 'tp', pairs)  31.6 us
    ppermute x25, waiting for transfers between devices, moved(): return lax.ppermute(shard, 'tp', pairs)  28.9 us
    pallas_call x11, Pallas kernels, called(): pl.pallas_call(kernel, in_specs=specs, out_specs=tuple((whole for _ in sh...  15 us
    ppermute x1, waiting for transfers between devices, on_device(): sent = lax.ppermute(arrived[0], 'group', [(5, 1), (6, 2), (7, 3)])  12.5 us
    pallas_call x1, Pallas kernels, decode_part(): pl.pallas_call(decode_kernel, grid=(R // rows,), in_specs=[pl.BlockSpec(m...  6.13 us
    unnamed x13, local copies, waits for them, and re-layouts  4.92 us
  transfers between devices with their start and end apart: 30, of which 9 were waited for; matrix products, arithmetic and copies ran while one was open for 4% of the time, Pallas kernels for 12%

profile of v2, /device:TPU:64, one launch (start us, length us, event | category | flops | bytes accessed | tf_op | source)
XLA Modules:
  0.0 109.5 jit_solution(3475632151388891161)
XLA Ops:
  0.6 3.1 %collective-permute-start = (bf16[256,512]{1,0:T(8,128)(2,1)}, bf16[256,512]{1,0:T(8,128)(2,1)S(1)}, u32[]{:S(2)}, u32[]{:S(2)}) collective-permute-start(bf16[256,512]{1,0:T(8,128)(2,1)} %bitcast.56), channel_id=1, source_target_pairs={{0,8},{1,9},{2,10},{3,11},{4,12},{5,13},{6,14},{7,15},{8,0},{9,1},... | collective-permute-start | bytes 786440 | tf_op jit(solution)/shard_map/ppermute | solution.py:40
  5.3 1.7 %collective-permute-start.2 = (bf16[256,512]{1,0:T(8,128)(2,1)}, bf16[256,512]{1,0:T(8,128)(2,1)S(1)}, u32[]{:S(2)}, u32[]{:S(2)}) collective-permute-start(bf16[256,512]{1,0:T(8,128)(2,1)} %bitcast.58), channel_id=1, source_target_pairs={{0,6},{1,7},{2,0},{3,1},{4,2},{5,3},{6,4},{7,5},{8,14},{9,15},{10,... | collective-permute-start | bytes 786440 | tf_op jit(solution)/shard_map/ppermute | solution.py:40
  10.7 2.2 %copy-done.1 = bf16[256,8192]{1,0:T(8,128)(2,1)S(1)} copy-done((bf16[256,8192]{1,0:T(8,128)(2,1)S(1)}, bf16[256,8192]{1,0:T(8,128)(2,1)}, u32[]{:S(2)}) %copy-start.1) | copy-done | bytes 4194328
  15.9 2.9 %collective-permute-start.6 = (bf16[384,512]{1,0:T(8,128)(2,1)S(1)}, bf16[384,512]{1,0:T(8,128)(2,1)S(1)}, u32[]{:S(2)}, u32[]{:S(2)}) collective-permute-start(bf16[384,512]{1,0:T(8,128)(2,1)S(1)} %get-tuple-element.74), channel_id=1, source_target_pairs={{0,6},{1,7},{2,0},{3,1},{4,2},{5,3},{6,4},{7,5},{8,14},{9,15},{10,... | collective-permute-start | bytes 1179656 | tf_op jit(solution)/shard_map/ppermute | solution.py:40
  18.7 9.4 %collective-permute-done.5.refs_0_ = bf16[384,512]{1,0:T(8,128)(2,1)S(1)} collective-permute-done((bf16[384,512]{1,0:T(8,128)(2,1)S(1)}, bf16[384,512]{1,0:T(8,128)(2,1)S(1)}, u32[]{:S(2)}, u32[]{:S(2)}) %collective-permute-start.5) | collective-permute-done | bytes 393248 | tf_op jit(solution)/shard_map/ppermute | solution.py:40
  29.0 5.5 %collective-permute-done.7.refs_2_ = bf16[128,512]{1,0:T(8,128)(2,1)S(1)} collective-permute-done((bf16[128,512]{1,0:T(8,128)(2,1)S(1)}, bf16[128,512]{1,0:T(8,128)(2,1)S(1)}, u32[]{:S(2)}, u32[]{:S(2)}) %collective-permute-start.7) | collective-permute-done | bytes 131104 | tf_op jit(solution)/shard_map/ppermute | solution.py:40
  34.5 5.0 %collective-permute-done.8.refs_3_ = bf16[128,512]{1,0:T(8,128)(2,1)S(1)} collective-permute-done((bf16[128,512]{1,0:T(8,128)(2,1)S(1)}, bf16[128,512]{1,0:T(8,128)(2,1)S(1)}, u32[]{:S(2)}, u32[]{:S(2)}) %collective-permute-start.8) | collective-permute-done | bytes 131104 | tf_op jit(solution)/shard_map/ppermute | solution.py:40
  40.0 2.3 %shard_map.97 = (f32[256,256]{1,0:T(8,128)S(1)}, f32[256,128]{1,0:T(8,128)S(1)}, f32[8,128]{1,0:T(8,128)}) custom-call(s32[46]{0:T(128)S(1)} %concatenate.12.scalar_ref, bf16[8192,256]{1,0:T(8,128)(2,1)S(1)} %copy-done, bf16[8192,128]{1,0:T(8,128)(2,1)S(1)} %copy-done.3, bf16[256,512]{1,0:T(8,128)(2,1)S(1)} %bitcast.60, ...), custom_call_target="tpu_custom_call" | custom-call | flops 805306368 | bytes 2097152 | tf_op jit(solution)/shard_map/pallas_call | solution.py:421
  42.4 1.9 %shard_map.98 = (bf16[256,256]{1,0:T(8,128)(2,1)S(1)}, bf16[256,128]{1,0:T(8,128)(2,1)S(1)}) custom-call(s32[46]{0:T(128)S(1)} %concatenate.12.scalar_ref, bf16[8192,256]{1,0:T(8,128)(2,1)S(1)} %copy-done, bf16[8192,128]{1,0:T(8,128)(2,1)S(1)} %copy-done.3, f32[256,256]{1,0:T(8,128)S(1)} %get-tuple-element.71.query_in, ...), custom_call_target="tpu_custom_call" | custom-call | flops 805306368 | bytes 2097152 | tf_op jit(solution)/shard_map/pallas_call | solution.py:421
  45.5 2.8 %collective-permute-done.14.other_ref = bf16[256,256]{1,0:T(8,128)(2,1)S(1)} collective-permute-done((bf16[256,256]{1,0:T(8,128)(2,1)S(1)}, bf16[256,256]{1,0:T(8,128)(2,1)S(1)}, u32[]{:S(2)}, u32[]{:S(2)}) %collective-permute-start.14) | collective-permute-done | bytes 131104 | tf_op jit(solution)/shard_map/ppermute | solution.py:40
  48.3 6.8 %conditional.1 = ((bf16[256,512]{1,0:T(8,128)(2,1)S(1)}, f32[256,4]{1,0:T(8,128)S(1)})) conditional(s32[]{:T(128)} %convert_element_type.15, (bf16[256,256]{1,0:T(8,128)(2,1)S(1)}, bf16[256,256]{1,0:T(8,128)(2,1)S(1)}, s32[46]{0:T(128)S(1)}, s32[64]{0:T(128)S(1)}, bf16[64,256,128]{2,1,0:T(8,128)(2,1)}, ...), branch_computations={%region_1.2_spmd, %region_2.3_spmd} | conditional | flops 524288 | bytes 2629656 | solution.py:624
  48.6 6.1 %branch_0_fun.1 = (bf16[256,512]{1,0:T(8,128)(2,1)S(1)}, f32[256,4]{1,0:T(8,128)S(1)}) custom-call(s32[46]{0:T(128)S(1)} %get-tuple-element.24.scalar_ref, s32[64]{0:T(128)S(1)} %get-tuple-element.25.length_ref, bf16[256,512]{1,0:T(8,128)(2,1)S(1)} %reshape.56.query_ref, bf16[64,256,128]{2,1,0:T(8,128)(2,1)} %get-tuple-element.28.key_ref, ...), custom_call_target="tpu_custom_call" | custom-call | tf_op jit(solution)/shard_map/cond/branch_0_fun/pallas_call | solution.py:467
  55.1 3.8 %collective-permute-start.16 = (bf16[256,512]{1,0:T(8,128)(2,1)S(1)}, bf16[256,512]{1,0:T(8,128)(2,1)S(1)}, u32[]{:S(2)}, u32[]{:S(2)}) collective-permute-start(bf16[256,512]{1,0:T(8,128)(2,1)S(1)} %get-tuple-element.81.own_ref), channel_id=1, source_target_pairs={{0,1},{1,0},{2,3},{3,2},{4,5},{5,4},{6,7},{7,6},{8,9},{9,8},{10,11... | collective-permute-start | bytes 786440 | tf_op jit(solution)/shard_map/ppermute | solution.py:40
  60.2 1.8 %shard_map.99 = (f32[256,512]{1,0:T(8,128)S(1)}, f32[256,4]{1,0:T(8,128)S(1)}) custom-call(s32[46]{0:T(128)S(1)} %concatenate.12.scalar_ref, bf16[256,256]{1,0:T(8,128)(2,1)S(1)} %get-tuple-element.77.own_ref, bf16[256,256]{1,0:T(8,128)(2,1)S(1)} %collective-permute-done.14.other_ref, bf16[256,128]{1,0:T(8,128)(2,1)S(1)} %collective-permute-done.15.held_ref, ...), custom_call_target="tpu_custom_call" | custom-call | flops 134217728 | bytes 2097152 | tf_op jit(solution)/shard_map/pallas_call | solution.py:421
  62.0 2.2 %copy-done.2 = bf16[256,8192]{1,0:T(8,128)(2,1)S(1)} copy-done((bf16[256,8192]{1,0:T(8,128)(2,1)S(1)}, bf16[256,8192]{1,0:T(8,128)(2,1)}, u32[]{:S(2)}) %copy-start.2) | copy-done | bytes 4194328
  64.1 4.5 %shard_map.100 = (bf16[384,512]{1,0:T(8,128)(2,1)S(1)}, bf16[384,512]{1,0:T(8,128)(2,1)S(1)}, bf16[128,512]{1,0:T(8,128)(2,1)S(1)}, bf16[128,512]{1,0:T(8,128)(2...) custom-call(s32[46]{0:T(128)S(1)} %concatenate.12.scalar_ref, ...), custom_call_target="tpu_custom_call" | custom-call | flops 1073741824 | bytes 2097152 | tf_op jit(solution)/shard_map/pallas_call | solution.py:421
  68.8 3.2 %collective-permute-start.20 = (bf16[384,512]{1,0:T(8,128)(2,1)S(1)}, bf16[384,512]{1,0:T(8,128)(2,1)S(1)}, u32[]{:S(2)}, u32[]{:S(2)}) collective-permute-start(bf16[384,512]{1,0:T(8,128)(2,1)S(1)} %get-tuple-element.90), channel_id=1, source_target_pairs={{0,6},{1,7},{2,0},{3,1},{4,2},{5,3},{6,4},{7,5},{8,14},{9,15},{10,... | collective-permute-start | bytes 1179656 | tf_op jit(solution)/shard_map/ppermute | solution.py:40
  72.0 2.1 %collective-permute-start.21 = (bf16[128,512]{1,0:T(8,128)(2,1)S(1)}, bf16[128,512]{1,0:T(8,128)(2,1)S(1)}, u32[]{:S(2)}, u32[]{:S(2)}) collective-permute-start(bf16[128,512]{1,0:T(8,128)(2,1)S(1)} %get-tuple-element.91), channel_id=1, source_target_pairs={{0,10},{1,11},{2,12},{3,13},{4,14},{5,15},{6,8},{7,9},{8,2},{9,3},... | collective-permute-start | bytes 393224 | tf_op jit(solution)/shard_map/ppermute | solution.py:40
  74.0 3.6 %collective-permute-start.22 = (bf16[128,512]{1,0:T(8,128)(2,1)S(1)}, bf16[128,512]{1,0:T(8,128)(2,1)S(1)}, u32[]{:S(2)}, u32[]{:S(2)}) collective-permute-start(bf16[128,512]{1,0:T(8,128)(2,1)S(1)} %get-tuple-element.92), channel_id=1, source_target_pairs={{0,14},{1,15},{2,8},{3,9},{4,10},{5,11},{6,12},{7,13},{8,6},{9,7},... | collective-permute-start | bytes 393224 | tf_op jit(solution)/shard_map/ppermute | solution.py:40
  78.9 3.1 %collective-permute-done.21.up = bf16[128,512]{1,0:T(8,128)(2,1)S(1)} collective-permute-done((bf16[128,512]{1,0:T(8,128)(2,1)S(1)}, bf16[128,512]{1,0:T(8,128)(2,1)S(1)}, u32[]{:S(2)}, u32[]{:S(2)}) %collective-permute-start.21) | collective-permute-done | bytes 131104 | tf_op jit(solution)/shard_map/ppermute | solution.py:40
  82.0 2.2 %collective-permute-done.19.from_last = bf16[384,512]{1,0:T(8,128)(2,1)S(1)} collective-permute-done((bf16[384,512]{1,0:T(8,128)(2,1)S(1)}, bf16[384,512]{1,0:T(8,128)(2,1)S(1)}, u32[]{:S(2)}, u32[]{:S(2)}) %collective-permute-start.19) | collective-permute-done | bytes 393248 | tf_op jit(solution)/shard_map/ppermute | solution.py:40
  87.6 2.1 %collective-permute-start.24 = (bf16[256,512]{1,0:T(8,128)(2,1)S(1)}, bf16[256,512]{1,0:T(8,128)(2,1)S(1)}, u32[]{:S(2)}, u32[]{:S(2)}) collective-permute-start(bf16[256,512]{1,0:T(8,128)(2,1)S(1)} %get-tuple-element.94), channel_id=1, source_target_pairs={{0,6},{1,7},{2,0},{3,1},{4,2},{5,3},{6,4},{7,5},{8,14},{9,15},{10,... | collective-permute-start | bytes 786440 | tf_op jit(solution)/shard_map/ppermute | solution.py:40
  89.7 3.4 %collective-permute-start.25 = (bf16[256,512]{1,0:T(8,128)(2,1)S(1)}, bf16[256,512]{1,0:T(8,128)(2,1)S(1)}, u32[]{:S(2)}, u32[]{:S(2)}) collective-permute-start(bf16[256,512]{1,0:T(8,128)(2,1)S(1)} %get-tuple-element.95), channel_id=1, source_target_pairs={{0,8},{1,9},{2,10},{3,11},{4,12},{5,13},{6,14},{7,15},{8,0},{9,1},... | collective-permute-start | bytes 786440 | tf_op jit(solution)/shard_map/ppermute | solution.py:40
  95.0 12.5 %collective-permute-done.29.sent_ref = bf16[1,4,8,256]{3,2,1,0:T(8,128)(2,1)S(1)} collective-permute-done((bf16[1,4,8,256]{3,2,1,0:T(8,128)(2,1)S(1)}, bf16[1,4,8,256]{3,2,1,0:T(8,128)(2,1)S(1)}, u32[]{:S(2)}, u32[]{:S(2)}) %collective-permute-start.29) | collective-permute-done | bytes 16416 | tf_op jit(solution)/shard_map/ppermute | solution.py:702
  (85 shorter events, 21.0 us)
Async XLA Ops:
  0.6 14.0 %collective-permute-start = (bf16[256,512]{1,0:T(8,128)(2,1)}, bf16[256,512]{1,0:T(8,128)(2,1)S(1)}, u32[]{:S(2)}, u32[]{:S(2)}) collective-permute-start(bf16[256,512]{1,0:T(8,128)(2,1)} %bitcast.56), channel_id=1, source_target_pairs={{0,8},{1,9},{2,10},{3,11},{4,12},{5,13},{6,14},{7,15},{8,0},{9,1},... | collective-permute-start | bytes 786440 | tf_op jit(solution)/shard_map/ppermute | solution.py:40
  3.7 10.9 %collective-permute-start.1 = (bf16[256,512]{1,0:T(8,128)(2,1)}, bf16[256,512]{1,0:T(8,128)(2,1)S(1)}, u32[]{:S(2)}, u32[]{:S(2)}) collective-permute-start(bf16[256,512]{1,0:T(8,128)(2,1)} %bitcast.57), channel_id=1, source_target_pairs={{0,2},{1,3},{2,4},{3,5},{4,6},{5,7},{6,0},{7,1},{8,10},{9,11},{10,... | collective-permute-start | bytes 786440 | tf_op jit(solution)/shard_map/ppermute | solution.py:40
  5.3 9.4 %collective-permute-start.2 = (bf16[256,512]{1,0:T(8,128)(2,1)}, bf16[256,512]{1,0:T(8,128)(2,1)S(1)}, u32[]{:S(2)}, u32[]{:S(2)}) collective-permute-start(bf16[256,512]{1,0:T(8,128)(2,1)} %bitcast.58), channel_id=1, source_target_pairs={{0,6},{1,7},{2,0},{3,1},{4,2},{5,3},{6,4},{7,5},{8,14},{9,15},{10,... | collective-permute-start | bytes 786440 | tf_op jit(solution)/shard_map/ppermute | solution.py:40
  15.3 24.7 %collective-permute-start.4 = (bf16[768,512]{1,0:T(8,128)(2,1)S(1)}, bf16[768,512]{1,0:T(8,128)(2,1)S(1)}, u32[]{:S(2)}, u32[]{:S(2)}) collective-permute-start(bf16[768,512]{1,0:T(8,128)(2,1)S(1)} %get-tuple-element.70.refs_1_), channel_id=1, source_target_pairs={{0,1},{1,0},{2,3},{3,2},{4,5},{5,4},{6,7},{7,6},{8,9},{9,8},{10,11... | collective-permute-start | bytes 2359304 | tf_op jit(solution)/shard_map/ppermute | solution.py:40
  15.4 12.7 %collective-permute-start.5 = (bf16[384,512]{1,0:T(8,128)(2,1)S(1)}, bf16[384,512]{1,0:T(8,128)(2,1)S(1)}, u32[]{:S(2)}, u32[]{:S(2)}) collective-permute-start(bf16[384,512]{1,0:T(8,128)(2,1)S(1)} %get-tuple-element.73), channel_id=1, source_target_pairs={{0,2},{1,3},{2,4},{3,5},{4,6},{5,7},{6,0},{7,1},{8,10},{9,11},{10,... | collective-permute-start | bytes 1179656 | tf_op jit(solution)/shard_map/ppermute | solution.py:40
  15.9 13.0 %collective-permute-start.6 = (bf16[384,512]{1,0:T(8,128)(2,1)S(1)}, bf16[384,512]{1,0:T(8,128)(2,1)S(1)}, u32[]{:S(2)}, u32[]{:S(2)}) collective-permute-start(bf16[384,512]{1,0:T(8,128)(2,1)S(1)} %get-tuple-element.74), channel_id=1, source_target_pairs={{0,6},{1,7},{2,0},{3,1},{4,2},{5,3},{6,4},{7,5},{8,14},{9,15},{10,... | collective-permute-start | bytes 1179656 | tf_op jit(solution)/shard_map/ppermute | solution.py:40
  28.2 6.3 %collective-permute-start.7 = (bf16[128,512]{1,0:T(8,128)(2,1)S(1)}, bf16[128,512]{1,0:T(8,128)(2,1)S(1)}, u32[]{:S(2)}, u32[]{:S(2)}) collective-permute-start(bf16[128,512]{1,0:T(8,128)(2,1)S(1)} %slice.40), channel_id=1, source_target_pairs={{0,2},{1,3},{2,4},{3,5},{4,6},{5,7},{6,0},{7,1},{8,10},{9,11},{10,... | collective-permute-start | bytes 393224 | tf_op jit(solution)/shard_map/ppermute | solution.py:40
  28.3 11.2 %collective-permute-start.3 = (bf16[256,512]{1,0:T(8,128)(2,1)S(1)}, bf16[256,512]{1,0:T(8,128)(2,1)S(1)}, u32[]{:S(2)}, u32[]{:S(2)}) collective-permute-start(bf16[256,512]{1,0:T(8,128)(2,1)S(1)} %bitcast.59), channel_id=1, source_target_pairs={{0,1},{1,0},{2,3},{3,2},{4,5},{5,4},{6,7},{7,6},{8,9},{9,8},{10,11... | collective-permute-start | bytes 786440 | tf_op jit(solution)/shard_map/ppermute | solution.py:40
  28.4 14.0 %collective-permute-start.9 = (bf16[384,512]{1,0:T(8,128)(2,1)S(1)}, bf16[384,512]{1,0:T(8,128)(2,1)S(1)}, u32[]{:S(2)}, u32[]{:S(2)}) collective-permute-start(bf16[384,512]{1,0:T(8,128)(2,1)S(1)} %collective-permute-done.5.refs_0_), channel_id=1, source_target_pairs={{0,1},{1,0},{2,3},{3,2},{4,5},{5,4},{6,7},{7,6},{8,9},{9,8},{10,11... | collective-permute-start | bytes 1179656 | tf_op jit(solution)/shard_map/ppermute | solution.py:40
  28.9 13.5 %collective-permute-start.10 = (bf16[384,512]{1,0:T(8,128)(2,1)S(1)}, bf16[384,512]{1,0:T(8,128)(2,1)S(1)}, u32[]{:S(2)}, u32[]{:S(2)}) collective-permute-start(bf16[384,512]{1,0:T(8,128)(2,1)S(1)} %collective-permute-done.6.refs_1_), channel_id=1, source_target_pairs={{0,1},{1,0},{2,3},{3,2},{4,5},{5,4},{6,7},{7,6},{8,9},{9,8},{10,11... | collective-permute-start | bytes 1179656 | tf_op jit(solution)/shard_map/ppermute | solution.py:40
  34.5 5.0 %collective-permute-start.8 = (bf16[128,512]{1,0:T(8,128)(2,1)S(1)}, bf16[128,512]{1,0:T(8,128)(2,1)S(1)}, u32[]{:S(2)}, u32[]{:S(2)}) collective-permute-start(bf16[128,512]{1,0:T(8,128)(2,1)S(1)} %slice.41), channel_id=1, source_target_pairs={{0,6},{1,7},{2,0},{3,1},{4,2},{5,3},{6,4},{7,5},{8,14},{9,15},{10,... | collective-permute-start | bytes 393224 | tf_op jit(solution)/shard_map/ppermute | solution.py:40
  44.3 17.7 %collective-permute-start.13 = (bf16[256,4096]{1,0:T(8,128)(2,1)S(1)}, bf16[256,4096]{1,0:T(8,128)(2,1)}, u32[]{:S(2)}, u32[]{:S(2)}) collective-permute-start(bf16[256,4096]{1,0:T(8,128)(2,1)S(1)} %shard_map.95), channel_id=1, source_target_pairs={{0,1},{1,0},{2,3},{3,2},{4,5},{5,4},{6,7},{7,6},{8,9},{9,8},{10,11... | collective-permute-start | bytes 6291464 | tf_op jit(solution)/shard_map/ppermute | solution.py:40
  44.4 4.0 %collective-permute-start.14 = (bf16[256,256]{1,0:T(8,128)(2,1)S(1)}, bf16[256,256]{1,0:T(8,128)(2,1)S(1)}, u32[]{:S(2)}, u32[]{:S(2)}) collective-permute-start(bf16[256,256]{1,0:T(8,128)(2,1)S(1)} %get-tuple-element.77.own_ref), channel_id=1, source_target_pairs={{0,1},{1,0},{2,3},{3,2},{4,5},{5,4},{6,7},{7,6},{8,9},{9,8},{10,11... | collective-permute-start | bytes 393224 | tf_op jit(solution)/shard_map/ppermute | solution.py:40
  55.1 6.8 %collective-permute-start.16 = (bf16[256,512]{1,0:T(8,128)(2,1)S(1)}, bf16[256,512]{1,0:T(8,128)(2,1)S(1)}, u32[]{:S(2)}, u32[]{:S(2)}) collective-permute-start(bf16[256,512]{1,0:T(8,128)(2,1)S(1)} %get-tuple-element.81.own_ref), channel_id=1, source_target_pairs={{0,1},{1,0},{2,3},{3,2},{4,5},{5,4},{6,7},{7,6},{8,9},{9,8},{10,11... | collective-permute-start | bytes 786440 | tf_op jit(solution)/shard_map/ppermute | solution.py:40
  68.7 15.6 %collective-permute-start.19 = (bf16[384,512]{1,0:T(8,128)(2,1)S(1)}, bf16[384,512]{1,0:T(8,128)(2,1)S(1)}, u32[]{:S(2)}, u32[]{:S(2)}) collective-permute-start(bf16[384,512]{1,0:T(8,128)(2,1)S(1)} %get-tuple-element.89), channel_id=1, source_target_pairs={{0,2},{1,3},{2,4},{3,5},{4,6},{5,7},{6,0},{7,1},{8,10},{9,11},{10,... | collective-permute-start | bytes 1179656 | tf_op jit(solution)/shard_map/ppermute | solution.py:40
  68.8 15.5 %collective-permute-start.20 = (bf16[384,512]{1,0:T(8,128)(2,1)S(1)}, bf16[384,512]{1,0:T(8,128)(2,1)S(1)}, u32[]{:S(2)}, u32[]{:S(2)}) collective-permute-start(bf16[384,512]{1,0:T(8,128)(2,1)S(1)} %get-tuple-element.90), channel_id=1, source_target_pairs={{0,6},{1,7},{2,0},{3,1},{4,2},{5,3},{6,4},{7,5},{8,14},{9,15},{10,... | collective-permute-start | bytes 1179656 | tf_op jit(solution)/shard_map/ppermute | solution.py:40
  72.0 10.0 %collective-permute-start.21 = (bf16[128,512]{1,0:T(8,128)(2,1)S(1)}, bf16[128,512]{1,0:T(8,128)(2,1)S(1)}, u32[]{:S(2)}, u32[]{:S(2)}) collective-permute-start(bf16[128,512]{1,0:T(8,128)(2,1)S(1)} %get-tuple-element.91), channel_id=1, source_target_pairs={{0,10},{1,11},{2,12},{3,13},{4,14},{5,15},{6,8},{7,9},{8,2},{9,3},... | collective-permute-start | bytes 393224 | tf_op jit(solution)/shard_map/ppermute | solution.py:40
  74.0 8.0 %collective-permute-start.22 = (bf16[128,512]{1,0:T(8,128)(2,1)S(1)}, bf16[128,512]{1,0:T(8,128)(2,1)S(1)}, u32[]{:S(2)}, u32[]{:S(2)}) collective-permute-start(bf16[128,512]{1,0:T(8,128)(2,1)S(1)} %get-tuple-element.92), channel_id=1, source_target_pairs={{0,14},{1,15},{2,8},{3,9},{4,10},{5,11},{6,12},{7,13},{8,6},{9,7},... | collective-permute-start | bytes 393224 | tf_op jit(solution)/shard_map/ppermute | solution.py:40
  78.2 6.3 %collective-permute-start.26 = (bf16[2,4,4,8,256]{4,3,2,1,0:T(8,128)(2,1)S(1)}, bf16[2,4,4,8,256]{4,3,2,1,0:T(8,128)(2,1)S(1)}, u32[]{:S(2)}, u32[]{:S(2)}) collective-permute-start(bf16[2,4,4,8,256]{4,3,2,1,0:T(8,128)(2,1)S(1)} %bitcast.61), channel_id=1, source_target_pairs={{0,64},{1,65},{2,66},{3,67},{4,68},{5,69},{6,70},{7,71},{8,72},{9,... | collective-permute-start | bytes 393224 | tf_op jit(solution)/shard_map/ppermute | solution.py:676
  85.7 7.4 %collective-permute-start.28 = (bf16[2,1,4,8,256]{4,3,2,1,0:T(8,128)(2,1)S(1)}, bf16[2,1,4,8,256]{4,3,2,1,0:T(8,128)(2,1)S(1)}, u32[]{:S(2)}, u32[]{:S(2)}) collective-permute-start(bf16[2,1,4,8,256]{4,3,2,1,0:T(8,128)(2,1)S(1)} %get-tuple-element.101), channel_id=1, source_target_pairs={{64,80},{96,112},{65,81},{97,113},{66,82},{98,114},{67,83},{99,115... | collective-permute-start | bytes 98312 | tf_op jit(solution)/shard_map/ppermute | solution.py:700
  86.4 22.2 %collective-permute-start.23 = (bf16[256,512]{1,0:T(8,128)(2,1)S(1)}, bf16[256,512]{1,0:T(8,128)(2,1)S(1)}, u32[]{:S(2)}, u32[]{:S(2)}) collective-permute-start(bf16[256,512]{1,0:T(8,128)(2,1)S(1)} %get-tuple-element.93), channel_id=1, source_target_pairs={{0,2},{1,3},{2,4},{3,5},{4,6},{5,7},{6,0},{7,1},{8,10},{9,11},{10,... | collective-permute-start | bytes 786440 | tf_op jit(solution)/shard_map/ppermute | solution.py:40
  87.6 21.0 %collective-permute-start.24 = (bf16[256,512]{1,0:T(8,128)(2,1)S(1)}, bf16[256,512]{1,0:T(8,128)(2,1)S(1)}, u32[]{:S(2)}, u32[]{:S(2)}) collective-permute-start(bf16[256,512]{1,0:T(8,128)(2,1)S(1)} %get-tuple-element.94), channel_id=1, source_target_pairs={{0,6},{1,7},{2,0},{3,1},{4,2},{5,3},{6,4},{7,5},{8,14},{9,15},{10,... | collective-permute-start | bytes 786440 | tf_op jit(solution)/shard_map/ppermute | solution.py:40
  89.7 18.9 %collective-permute-start.25 = (bf16[256,512]{1,0:T(8,128)(2,1)S(1)}, bf16[256,512]{1,0:T(8,128)(2,1)S(1)}, u32[]{:S(2)}, u32[]{:S(2)}) collective-permute-start(bf16[256,512]{1,0:T(8,128)(2,1)S(1)} %get-tuple-element.95), channel_id=1, source_target_pairs={{0,8},{1,9},{2,10},{3,11},{4,12},{5,13},{6,14},{7,15},{8,0},{9,1},... | collective-permute-start | bytes 786440 | tf_op jit(solution)/shard_map/ppermute | solution.py:40
  93.7 13.8 %collective-permute-start.29 = (bf16[1,4,8,256]{3,2,1,0:T(8,128)(2,1)S(1)}, bf16[1,4,8,256]{3,2,1,0:T(8,128)(2,1)S(1)}, u32[]{:S(2)}, u32[]{:S(2)}) collective-permute-start(bf16[1,4,8,256]{3,2,1,0:T(8,128)(2,1)S(1)} %get-tuple-element.103), channel_id=1, source_target_pairs={{80,16},{96,32},{112,48},{81,17},{97,33},{113,49},{82,18},{98,34},... | collective-permute-start | bytes 49160 | tf_op jit(solution)/shard_map/ppermute | solution.py:702
  (12 other events, 91.3 us)

commit v3 on v2

--- a/solution.py
+++ b/solution.py
@@ -1,5 +1,3 @@
-import functools
-
 import jax
 import jax.numpy as jnp
 from jax import lax
@@ -66,8 +64,9 @@
 ROWS_AT_ONCE = 4
 LOG2_E = 1.4426950408889634
 NT = (((1,), (1,)), ((), ()))
-
-CORE, IS_PREFILL, IS_KEY, NEAR_ROWS, FAR_ROWS, PLACE, CELLS, PICKS = 0, 1, 2, 3, 11, 19, 27, 43
+LONG = 6 * 10**9
+
+CORE, IS_PREFILL, IS_KEY, NEAR_ROWS, FAR_ROWS, PLACE, CELLS = 0, 1, 2, 3, 11, 19, 27
 
 
 def stacked_heads(*parts):
@@ -200,55 +199,97 @@
         write_heads(mixed_ref, level_ref, rows, mixed, largest)
 
 
-def pair_of(scalar_ref, held_ref, other_ref):
-    first = scalar_ref[CORE] == 0
-    held, other = held_ref[...], other_ref[...]
-    return jnp.where(first, held, other), jnp.where(first, other, held)
+def sort_pair(scalar_ref, held_ref, swapped_ref, keys, values):
+    @pl.when(scalar_ref[CORE] == 0)
+    def _():
+        keys[...] = held_ref[...].astype(keys.dtype)
+        values[...] = swapped_ref[...].astype(values.dtype)
+
+    @pl.when(scalar_ref[CORE] != 0)
+    def _():
+        keys[...] = swapped_ref[...].astype(keys.dtype)
+        values[...] = held_ref[...].astype(values.dtype)
 
 
 def recent_kernel(scalar_ref, own_ref, other_ref, held_ref, swapped_ref, mixed_ref, level_ref):
-    is_prefill = scalar_ref[IS_PREFILL] != 0
-    keys, values = pair_of(scalar_ref, held_ref, swapped_ref)
     row = lax.broadcasted_iota(jnp.int32, (TOK, TOK), 0)
     column = lax.broadcasted_iota(jnp.int32, (TOK, TOK), 1)
+    is_prefill = scalar_ref[IS_PREFILL] != 0
     together = jnp.where(is_prefill, row // CH - column // CH, row % R - column % R) == 0
     allowed = together & (column <= row)
-    values = with_ones(values)
-    queries = [ref[:, j * HD : (j + 1) * HD] for ref in (own_ref, other_ref) for j in range(2)]
     lane = lax.broadcasted_iota(jnp.int32, (TOK, GQ), 1)
-    levels = jnp.zeros((TOK, GQ), jnp.float32)
-    for j in range(GQ):
-        head = slice(j * HD, (j + 1) * HD)
-        scores = lax.dot_general(queries[j], keys, NT, preferred_element_type=jnp.float32)
-        scores = jnp.where(allowed, scores, NEG_FILL)
-        largest = jnp.max(scores, axis=1, keepdims=True)
-        mixed = jnp.dot(weights_of(scores, largest), values, preferred_element_type=jnp.float32)
-        total = mixed[:, HD : HD + 1]
-        mixed_ref[:, head] = mixed[:, :HD] / total
-        levels = jnp.where(lane == j, largest * HD**-0.5 + jnp.log(total), levels)
-    level_ref[...] = levels
+
+    def attend(key_ref, value_ref):
+        values = with_ones(value_ref[...])
+        levels = jnp.zeros((TOK, GQ), jnp.float32)
+        for j in range(GQ):
+            source = own_ref if j < GQ // 2 else other_ref
+            part = slice(j % (GQ // 2) * HD, (j % (GQ // 2) + 1) * HD)
+            scores = lax.dot_general(
+                source[:, part], key_ref[...], NT, preferred_element_type=jnp.float32
+            )
+            scores = jnp.where(allowed, scores, NEG_FILL)
+            largest = jnp.max(scores, axis=1, keepdims=True)
+            mixed = jnp.dot(
+                weights_of(scores, largest), values, preferred_element_type=jnp.float32
+            )
+            total = mixed[:, HD : HD + 1]
+            mixed_ref[:, j * HD : (j + 1) * HD] = (mixed[:, :HD] / total).astype(mixed_ref.dtype)
+            levels = jnp.where(lane == j, largest * HD**-0.5 + jnp.log(total), levels)
+        level_ref[...] = levels
+
+    @pl.when(scalar_ref[CORE] == 0)
+    def _():
+        attend(held_ref, swapped_ref)
+
+    @pl.when(scalar_ref[CORE] != 0)
+    def _():
+        attend(swapped_ref, held_ref)
 
 
 def merged(parts, levels):
+    half = GQ // 2
+    turned = jnp.concatenate([levels[1][:, half:], levels[1][:, :half]], axis=1)
+    levels = [levels[0], turned, levels[2]]
+    top = jnp.maximum(jnp.maximum(levels[0], levels[1]), levels[2])
+    shares = [jnp.exp(level - top) for level in levels]
+    total = shares[0] + shares[1] + shares[2]
+    shares = [share / total for share in shares]
     heads = []
     for j in range(GQ):
-        places = (j, (j + GQ // 2) % GQ, j)
-        columns = [level[:, place : place + 1] for level, place in zip(levels, places)]
-        top = jnp.maximum(jnp.maximum(columns[0], columns[1]), columns[2])
-        shares = [jnp.exp(column - top) for column in columns]
-        total = shares[0] + shares[1] + shares[2]
         mixed = jnp.zeros((TOK, HD), jnp.float32)
-        for part, share, place in zip(parts, shares, places):
+        for part, share, place in zip(parts, shares, (j, (j + half) % GQ, j)):
             values = part[:, place * HD : (place + 1) * HD].astype(jnp.float32)
-            mixed = mixed + values * (share / total)
+            mixed = mixed + values * share[:, j : j + 1]
         heads.append(mixed.astype(jnp.bfloat16))
     return jnp.concatenate(heads, axis=1)
 
 
+def swapped_copies(scalar_ref, first, swapped_ref, held_ref, sems):
+    copies = []
+    for index in range(4):
+        columns = pl.ds(pl.multiple_of(scalar_ref[PLACE + first + index] * SHARD, SHARD), SHARD)
+        copies.append(
+            pltpu.make_async_copy(
+                swapped_ref.at[:, columns], held_ref.at[index], sems.at[index]
+            )
+        )
+        copies[-1].start()
+    return copies
+
+
+def product(scalar_ref, chip, joined, copy, weight_ref, held_ref, index):
+    column = 2 * scalar_ref[PLACE + chip] + scalar_ref[CORE]
+    own = weight_ref[:, pl.ds(pl.multiple_of(column * SHARD, SHARD), SHARD)]
+    copy.wait()
+    weights = jnp.concatenate([own, held_ref[index]], axis=0)
+    return jnp.dot(joined, weights, preferred_element_type=jnp.float32).astype(jnp.bfloat16)
+
+
 def merge_out_kernel(
     scalar_ref,
+    swapped_ref,
     weight_ref,
-    swapped_ref,
     own_ref,
     own_level,
     other_ref,
@@ -259,51 +300,35 @@
     minus,
     up,
     down,
-    next_ref,
-    last_ref,
-    partner_ref,
-    here_ref,
+    attention,
     held_ref,
     sems,
 ):
-    core = scalar_ref[CORE]
-    rows = weight_ref.shape[0]
-    copies = []
-    for index in range(CHIPS):
-        chip = scalar_ref[PLACE + index]
-        own = pl.ds(pl.multiple_of((2 * chip + core) * SHARD, SHARD), SHARD)
-        other = pl.ds(pl.multiple_of(chip * SHARD, SHARD), SHARD)
-        pair = (
-            pltpu.make_async_copy(
-                weight_ref.at[:, own], held_ref.at[index, :rows], sems.at[0, index]
-            ),
-            pltpu.make_async_copy(
-                swapped_ref.at[:, other], held_ref.at[index, rows:], sems.at[1, index]
-            ),
-        )
-        for copy in pair:
-            copy.start()
-        copies.append(pair)
+    copies = swapped_copies(scalar_ref, 0, swapped_ref, held_ref, sems)
     joined = merged(
         (own_ref, other_ref, recent_ref), (own_level[...], other_level[...], recent_level[...])
     )
-
-    def product(index):
-        for copy in copies[index]:
-            copy.wait()
-        total = jnp.dot(joined, held_ref[index], preferred_element_type=jnp.float32)
-        return total.astype(jnp.bfloat16)
-
-    plus[:TOK] = product(0)
-    minus[:TOK] = product(1)
-    far = product(2)
-    plus[TOK:] = far[:HALF]
-    minus[TOK:] = far[HALF:]
-    far = product(3)
-    up[...] = far[:HALF]
-    down[...] = far[HALF:]
-    for index, ref in ((4, next_ref), (5, last_ref), (6, partner_ref), (7, here_ref)):
-        ref[...] = product(index)
+    attention[...] = joined
+    parts = [
+        product(scalar_ref, index, joined, copies[index], weight_ref, held_ref, index)
+        for index in range(4)
+    ]
+    plus[:TOK] = parts[0]
+    minus[:TOK] = parts[1]
+    plus[TOK:] = parts[2][:HALF]
+    minus[TOK:] = parts[2][HALF:]
+    up[...] = parts[3][:HALF]
+    down[...] = parts[3][HALF:]
+
+
+def out_kernel(scalar_ref, swapped_ref, weight_ref, attention, *refs):
+    *out_refs, held_ref, sems = refs
+    copies = swapped_copies(scalar_ref, 4, swapped_ref, held_ref, sems)
+    joined = attention[...]
+    for index, ref in enumerate(out_refs):
+        ref[...] = product(
+            scalar_ref, 4 + index, joined, copies[index], weight_ref, held_ref, index
+        )
 
 
 def total_of(*parts):
@@ -314,7 +339,17 @@
 
 
 def second_message_kernel(
-    next_ref, last_ref, partner_ref, from_last, from_next, up, down, plus, minus, partner
+    arrived_ref,
+    next_ref,
+    last_ref,
+    partner_ref,
+    from_last,
+    from_next,
+    up,
+    down,
+    plus,
+    minus,
+    partner,
 ):
     plus[:HALF] = total_of(next_ref[:HALF], from_last[TOK:], up[...])
     plus[HALF:] = next_ref[HALF:]
@@ -327,14 +362,29 @@
     out_ref[...] = total_of(here_ref[...], from_last[...], from_next[...], from_partner[...])
 
 
-def join_kernel(scalar_ref, partner_ref, last_ref, next_ref, plus, minus, near):
+def join_kernel(
+    scalar_ref, own_ref, partner_ref, last_ref, next_ref, plus, minus, up, down, near, sem
+):
+    own = pltpu.make_async_copy(own_ref, near.at[:TOK], sem)
+    own.start()
     plus[:TOK] = partner_ref[...]
     plus[TOK:] = last_ref[:HALF]
     minus[:TOK] = partner_ref[...]
     minus[TOK:] = next_ref[HALF:]
-    near[:TOK] = last_ref[...]
-    near[TOK : 2 * TOK] = next_ref[...]
-    near[2 * TOK :] = partner_ref[...]
+    up[...] = last_ref[HALF:]
+    down[...] = next_ref[:HALF]
+    for index, ref in enumerate((last_ref, next_ref, partner_ref)):
+        near[(index + 1) * TOK : (index + 2) * TOK] = ref[...]
+    own.wait()
+
+
+def sides_kernel(mark_ref, last_ref, next_ref, upper_ref, lower_ref, sides):
+    sides[:TOK] = last_ref[:TOK]
+    sides[TOK : 2 * TOK] = next_ref[:TOK]
+    sides[2 * TOK : 2 * TOK + HALF] = last_ref[TOK:]
+    sides[2 * TOK + HALF : 3 * TOK] = next_ref[TOK:]
+    sides[3 * TOK : 3 * TOK + HALF] = upper_ref[...]
+    sides[3 * TOK + HALF :] = lower_ref[...]
 
 
 def projected_parts(scalar_ref, first, shards, query_weight, pair_weight):
@@ -353,28 +403,42 @@
     ]
 
 
-def near_kernel(scalar_ref, query_weight, pair_weight, *refs):
-    *sources, query, pair, mark = refs
+def four_shards(ref):
+    return [ref[index * TOK : (index + 1) * TOK] for index in range(4)]
+
+
+def near_kernel(scalar_ref, query_weight, pair_weight, near_ref, other_ref, query, pair, mark):
     mark[...] = jnp.zeros_like(mark)
-    shards = []
-    for own_ref, near_ref in (sources[:2], sources[2:]):
-        shards.append(own_ref[...])
-        shards.extend(near_ref[index * TOK : (index + 1) * TOK] for index in range(3))
     query[...], pair[...] = projected_parts(
-        scalar_ref, NEAR_ROWS, shards, query_weight, pair_weight
-    )
-
-
-def far_shards(last_ref, next_ref, upper_ref, lower_ref):
-    middle = jnp.concatenate([last_ref[TOK:], next_ref[TOK:]], axis=0)
-    far = jnp.concatenate([upper_ref[...], lower_ref[...]], axis=0)
-    return [last_ref[:TOK], next_ref[:TOK], middle, far]
-
-
-def last_kernel(scalar_ref, query_weight, pair_weight, query_in, pair_in, *refs):
-    *sides, cosine_ref, sine_ref, query_out, pair_out = refs
-    shards = far_shards(*sides[:4]) + far_shards(*sides[4:])
-    sums = projected_parts(scalar_ref, FAR_ROWS, shards, query_weight, pair_weight)
+        scalar_ref,
+        NEAR_ROWS,
+        four_shards(near_ref) + four_shards(other_ref),
+        query_weight,
+        pair_weight,
+    )
+
+
+def far_kernel(scalar_ref, query_weight, pair_weight, query_in, pair_in, far_ref, query, pair):
+    sums = projected_parts(scalar_ref, FAR_ROWS, four_shards(far_ref), query_weight, pair_weight)
+    query[...] = query_in[...] + sums[0]
+    pair[...] = pair_in[...] + sums[1]
+
+
+def last_kernel(
+    scalar_ref,
+    query_weight,
+    pair_weight,
+    query_in,
+    pair_in,
+    far_ref,
+    cosine_ref,
+    sine_ref,
+    query_out,
+    pair_out,
+):
+    sums = projected_parts(
+        scalar_ref, FAR_ROWS + 4, four_shards(far_ref), query_weight, pair_weight
+    )
     query = query_in[...] + sums[0]
     pair = pair_in[...] + sums[1]
     cosine = cosine_ref[...]
@@ -390,25 +454,18 @@
     pair_out[...] = jnp.where(is_key, rotated(pair), pair).astype(jnp.bfloat16)
 
 
-def blocks_kernel(scalar_ref, held_ref, swapped_ref, out_ref, pair_ref):
+def blocks_kernel(scalar_ref, held_ref, swapped_ref, out_ref, keys, values):
     sliver = out_ref.shape[1]
     out_ref[...] = jnp.zeros_like(out_ref)
 
     @pl.when(scalar_ref[IS_PREFILL] != 0)
     def _():
-        keys, values = pair_of(scalar_ref, held_ref, swapped_ref)
-        pair_ref[:, :HD] = keys.astype(jnp.float32)
-        pair_ref[:, HD:] = values.astype(jnp.float32)
+        sort_pair(scalar_ref, held_ref, swapped_ref, keys, values)
         for block in range(TOK // BS):
             start = pl.multiple_of(scalar_ref[CORE] * sliver, sliver) + block * BS
-            out_ref[scalar_ref[CELLS + block]] = pair_ref[pl.ds(start, sliver), :].astype(
-                jnp.bfloat16
-            )
-
-
-def pick_kernel(pick, scalar_ref, sent_ref, kept_ref, out_ref):
-    chosen = scalar_ref[PICKS + pick] != 0
-    out_ref[...] = jnp.where(chosen, sent_ref[...], kept_ref[...])
+            cell = scalar_ref[CELLS + block]
+            out_ref[cell, :, :HD] = keys[pl.ds(start, sliver), :].astype(jnp.bfloat16)
+            out_ref[cell, :, HD:] = values[pl.ds(start, sliver), :].astype(jnp.bfloat16)
 
 
 def called(kernel, shapes, scalars, *arrays, streamed=(), scratch=(), flops=0, grant=12):
@@ -551,12 +608,11 @@
         + rows_of((1, 3), (1, 1), (0, 2), (1, 2))
         + [(x_hi ^ flip) * 4 + (y + step) % 4 for flip, step in places]
     )
-    picks = [group_rank == 6, group_rank % 2 == 1, group_rank < 4]
+    picks = [group_rank >= 4, group_rank // 2 % 2 == 1, group_rank % 2 == 1]
     scalars = jnp.concatenate(
         [
             jnp.stack([jnp.asarray(one, jnp.int32) for one in single]),
             placement[:, 0] * slot_count + placement[:, 1],
-            jnp.stack([jnp.asarray(one, jnp.int32) for one in picks]),
         ]
     )
     prefix = jnp.sum(row_lengths.reshape(NPR, RP), axis=1)
@@ -565,61 +621,78 @@
         row_lengths[None, :] + jnp.arange(STEPS, dtype=jnp.int32)[:, None]
     ).reshape(TOK)
     positions = jnp.where(is_prefill, prompt_positions, decode_step_positions)
-    cosine, sine = turns(positions)
 
     cut_out = cut_columns(scalars, out_weight)
 
     wide = ((TOK + HALF, SHARD), jnp.bfloat16)
     half = ((HALF, SHARD), jnp.bfloat16)
     shard = ((TOK, SHARD), jnp.bfloat16)
-    triple = ((3 * TOK, SHARD), jnp.bfloat16)
+    four = ((4 * TOK, SHARD), jnp.bfloat16)
     weights = (query_weight, kv_weight)
     sums = (((TOK, query_weight.shape[1]), jnp.float32), ((TOK, kv_weight.shape[1]), jnp.float32))
     partner_tokens = moved(tokens, 1, 0, 0)
     last_tokens, next_tokens = moved(tokens, 0, 1, 0), moved(tokens, 0, 3, 0)
-    other_tokens = core_swap(tokens)
-    scalars, *_ = lax.optimization_barrier((scalars, cut_out, cosine, sine))
-    plus, minus, near = called(
+    scalars, picks, positions = lax.optimization_barrier((scalars, picks, positions))
+    cosine, sine = turns(positions)
+    plus, minus, up, down, near = called(
         join_kernel,
-        (wide, wide, triple),
+        (wide, wide, half, half, four),
         scalars,
         partner_tokens,
         last_tokens,
         next_tokens,
+        streamed=(tokens,),
+        scratch=(pltpu.SemaphoreType.DMA(()),),
+        flops=LONG,
     )
     from_last, from_next = moved(plus, 0, 1, 0), moved(minus, 0, 3, 0)
-    far_upper, far_lower = moved(from_last[:HALF], 0, 1, 0), moved(from_next[HALF:TOK], 0, 3, 0)
+    far_upper, far_lower = moved(down, 1, 3, 0), moved(up, 1, 1, 0)
+    scalars, cut_out = lax.optimization_barrier((scalars, cut_out))
     *part, mark = called(
         near_kernel,
         sums + (((8, HD), jnp.float32),),
         scalars,
         *weights,
-        tokens,
         near,
-        other_tokens,
         core_swap(near),
         flops=2 * TOK * 8 * SHARD * 3 * HD,
     )
-    sides = (from_last, from_next, far_upper, far_lower)
-    _, *ready = lax.optimization_barrier((mark, far_upper, far_lower))
+    (sides,) = called(
+        sides_kernel,
+        (four,),
+        None,
+        from_last,
+        from_next,
+        far_upper,
+        far_lower,
+        streamed=(mark,),
+    )
+    other_sides = core_swap(sides)
+    part = called(
+        far_kernel,
+        sums,
+        scalars,
+        *weights,
+        *part,
+        sides,
+        flops=2 * TOK * 4 * SHARD * 3 * HD,
+    )
     query_local, pair_local = called(
         last_kernel,
         tuple((shape, jnp.bfloat16) for shape, _ in sums),
         scalars,
         *weights,
         *part,
-        *sides,
-        *[core_swap(source) for source in (from_last, from_next, *ready)],
+        other_sides,
         cosine,
         sine,
-        flops=2 * TOK * 8 * SHARD * 3 * HD,
-    )
+        flops=2 * TOK * 4 * SHARD * 3 * HD,
+    )
+    pair_local, cut_out = lax.optimization_barrier((pair_local, cut_out))
     query_other = core_swap(query_local)
     pair_held = lax.ppermute(
         pair_local, "tp", [(t, 2 * t if t < KVH else 2 * (t - KVH) + 1) for t in range(2 * KVH)]
     )
-    _, cut_out = lax.optimization_barrier((query_local, cut_out))
-    _, row_lengths = lax.optimization_barrier((pair_held, row_lengths))
     swapped_out = core_swap(cut_out)
     cached = lax.cond(
         is_prefill,
@@ -632,48 +705,60 @@
         cache_keys[0],
         cache_values[0],
     )
+    cached, pair_held = lax.optimization_barrier((cached, pair_held))
     pair_other = core_swap(pair_held)
     other_cached = (core_swap(cached[0]), core_swap(cached[1]))
     recent = called(
         recent_kernel,
-        (((TOK, GQ * HD), jnp.float32), ((TOK, GQ), jnp.float32)),
+        (((TOK, GQ * HD), jnp.bfloat16), ((TOK, GQ), jnp.float32)),
         scalars,
         query_local,
         query_other,
         pair_held,
         pair_other,
-        flops=4 * GQ * TOK * TOK * HD,
-    )
-
-    plus, minus, up, down, next_part, last_part, partner_part, here_part = called(
+        flops=LONG,
+    )
+
+    product_scratch = (
+        pltpu.VMEM((4, out_weight.shape[0], SHARD), jnp.bfloat16),
+        pltpu.SemaphoreType.DMA((4,)),
+    )
+    plus, minus, up, down, attention = called(
         merge_out_kernel,
-        (wide, wide, half, half, shard, shard, shard, shard),
+        (wide, wide, half, half, ((TOK, GQ * HD), jnp.bfloat16)),
         scalars,
+        out_weight,
         *cached,
         *other_cached,
         *recent,
-        streamed=(out_weight, swapped_out),
-        scratch=(
-            pltpu.VMEM((CHIPS, GQ * HD, SHARD), jnp.bfloat16),
-            pltpu.SemaphoreType.DMA((2, CHIPS)),
-        ),
-        flops=2 * TOK * CHIPS * SHARD * GQ * HD,
-        grant=16,
+        streamed=(swapped_out,),
+        scratch=product_scratch,
+        flops=2 * TOK * 4 * SHARD * GQ * HD,
+    )
+    next_part, last_part, partner_part, here_part = called(
+        out_kernel,
+        (shard,) * 4,
+        scalars,
+        out_weight,
+        attention,
+        streamed=(swapped_out,),
+        scratch=product_scratch,
+        flops=2 * TOK * 4 * SHARD * GQ * HD,
     )
     from_last, from_next = moved(plus, 0, 1, 0), moved(minus, 0, 3, 0)
     up, down = moved(up, 1, 1, 0), moved(down, 1, 3, 0)
 
+    _, late_scalars = lax.optimization_barrier((attention, scalars))
     (blocks,) = called(
         blocks_kernel,
         (((group_count * slot_count, BS // 2, 2 * HD), jnp.bfloat16),),
-        scalars,
+        late_scalars,
         pair_held,
         pair_other,
-        scratch=(pltpu.VMEM((TOK, 2 * HD), jnp.float32),),
-    )
-    _, blocks = lax.optimization_barrier((here_part, blocks))
-    blocks = blocks.reshape(2, 4, slot_count, BS // 2, 2 * HD)
-    arrived = lax.ppermute(blocks, "group", [(0, 4)])
+        scratch=(pltpu.VMEM((TOK, HD), jnp.float32),) * 2,
+    )
+    blocks = blocks.reshape(group_count, slot_count, BS // 2, 2 * HD)
+    arrived = lax.ppermute(blocks[4:], "group", [(0, 4)])
 
     plus, minus, partner = called(
         second_message_kernel,
@@ -686,21 +771,16 @@
         from_next,
         up,
         down,
+        streamed=(arrived,),
     )
     from_last, from_next = moved(plus, 0, 1, 0), moved(minus, 0, 3, 0)
     from_partner = moved(partner, 1, 0, 0)
 
-    def picked(pick, sent, kept):
-        kernel = functools.partial(pick_kernel, pick)
-        return called(kernel, ((sent.shape, sent.dtype),), scalars, sent, kept)[0]
-
-    _, arrived = lax.optimization_barrier((partner, arrived))
-    sent = lax.ppermute(arrived[:, 2:], "group", [(4, 6)])
-    arrived = picked(0, sent, arrived[:, :2])
-    sent = lax.ppermute(arrived[:, 1:], "group", [(4, 5), (6, 7)])
-    arrived = picked(1, sent, arrived[:, :1])
-    sent = lax.ppermute(arrived[0], "group", [(5, 1), (6, 2), (7, 3)])
-    incoming = picked(2, sent, arrived[1])
+    blocks = jnp.where(picks[0], arrived, blocks[:4])
+    sent = lax.ppermute(blocks[2:], "group", [(0, 2), (4, 6)])
+    blocks = jnp.where(picks[1], sent, blocks[:2])
+    sent = lax.ppermute(blocks[1:], "group", [(0, 1), (2, 3), (4, 5), (6, 7)])
+    incoming = jnp.where(picks[2], sent, blocks[:1])
     (projected,) = called(
         total_kernel, (shard,), None, here_part, from_last, from_next, from_partner
     )

time: 110 us -> 86.3 us (0.78)
  the two profiles are of different devices: /device:TPU:64 before, /device:TPU:0 now
where the time goes in v3:
time: 86.3 us; the launch traced here: 86 us
  starting transfers between devices  35.4 us (41%)
  Pallas kernels  28.2 us (33%)
  waiting for transfers between devices  15.4 us (18%)
  other arithmetic  4.22 us (5%)
  local copies, waits for them, and re-layouts  1.85 us (2%)
  between operations  0.94 us (1%)
    ppermute x21, starting transfers between devices, moved(): return lax.ppermute(shard, 'tp', pairs)  30.9 us
    ppermute x21, waiting for transfers between devices, moved(): return lax.ppermute(shard, 'tp', pairs)  13.9 us
    pallas_call x11, Pallas kernels, called(): pl.pallas_call(kernel, in_specs=specs, out_specs=tuple((whole for _ in sh...  13.1 us
    pallas_call x1, Pallas kernels, prefill_part(): pl.pallas_call(prefill_kernel, in_specs=[small, small, whole, whole, ther...  12.9 us
    pallas_call x1, Pallas kernels, cut_columns(): pl.pallas_call(cut_kernel, in_specs=[pl.BlockSpec(memory_space=pltpu.SMEM...  2.22 us
  transfers between devices with their start and end apart: 25, of which 12 were waited for; matrix products, arithmetic and copies ran while one was open for 6% of the time, Pallas kernels for 26%

profile of v3, /device:TPU:0, one launch (start us, length us, event | category | flops | bytes accessed | tf_op | source)
XLA Modules:
  0.0 86.0 jit_solution(12432757083762229514)
XLA Ops:
  0.6 3.2 %collective-permute-start = (bf16[256,512]{1,0:T(8,128)(2,1)}, bf16[256,512]{1,0:T(8,128)(2,1)S(1)}, u32[]{:S(2)}, u32[]{:S(2)}) collective-permute-start(bf16[256,512]{1,0:T(8,128)(2,1)} %bitcast.49), channel_id=1, source_target_pairs={{0,8},{1,9},{2,10},{3,11},{4,12},{5,13},{6,14},{7,15},{8,0},{9,1},... | collective-permute-start | bytes 786440 | tf_op jit(solution)/shard_map/ppermute | solution.py:38
  3.8 1.6 %collective-permute-start.1 = (bf16[256,512]{1,0:T(8,128)(2,1)}, bf16[256,512]{1,0:T(8,128)(2,1)S(1)}, u32[]{:S(2)}, u32[]{:S(2)}) collective-permute-start(bf16[256,512]{1,0:T(8,128)(2,1)} %bitcast.50), channel_id=1, source_target_pairs={{0,2},{1,3},{2,4},{3,5},{4,6},{5,7},{6,0},{7,1},{8,10},{9,11},{10,... | collective-permute-start | bytes 786440 | tf_op jit(solution)/shard_map/ppermute | solution.py:38
  5.4 1.7 %collective-permute-start.2 = (bf16[256,512]{1,0:T(8,128)(2,1)}, bf16[256,512]{1,0:T(8,128)(2,1)S(1)}, u32[]{:S(2)}, u32[]{:S(2)}) collective-permute-start(bf16[256,512]{1,0:T(8,128)(2,1)} %bitcast.51), channel_id=1, source_target_pairs={{0,6},{1,7},{2,0},{3,1},{4,2},{5,3},{6,4},{7,5},{8,14},{9,15},{10,... | collective-permute-start | bytes 786440 | tf_op jit(solution)/shard_map/ppermute | solution.py:38
  10.8 2.3 %collective-permute-done.1.last_ref = bf16[256,512]{1,0:T(8,128)(2,1)S(1)} collective-permute-done((bf16[256,512]{1,0:T(8,128)(2,1)}, bf16[256,512]{1,0:T(8,128)(2,1)S(1)}, u32[]{:S(2)}, u32[]{:S(2)}) %collective-permute-start.1) | collective-permute-done | bytes 262176 | tf_op jit(solution)/shard_map/ppermute | solution.py:38
  14.9 1.6 %collective-permute-start.4 = (bf16[384,512]{1,0:T(8,128)(2,1)S(1)}, bf16[384,512]{1,0:T(8,128)(2,1)S(1)}, u32[]{:S(2)}, u32[]{:S(2)}) collective-permute-start(bf16[384,512]{1,0:T(8,128)(2,1)S(1)} %get-tuple-element.87), channel_id=1, source_target_pairs={{0,2},{1,3},{2,4},{3,5},{4,6},{5,7},{6,0},{7,1},{8,10},{9,11},{10,... | collective-permute-start | bytes 1179656 | tf_op jit(solution)/shard_map/ppermute | solution.py:38
  16.5 1.7 %collective-permute-start.5 = (bf16[384,512]{1,0:T(8,128)(2,1)S(1)}, bf16[384,512]{1,0:T(8,128)(2,1)S(1)}, u32[]{:S(2)}, u32[]{:S(2)}) collective-permute-start(bf16[384,512]{1,0:T(8,128)(2,1)S(1)} %get-tuple-element.88), channel_id=1, source_target_pairs={{0,6},{1,7},{2,0},{3,1},{4,2},{5,3},{6,4},{7,5},{8,14},{9,15},{10,... | collective-permute-start | bytes 1179656 | tf_op jit(solution)/shard_map/ppermute | solution.py:38
  18.2 1.7 %collective-permute-start.6 = (bf16[128,512]{1,0:T(8,128)(2,1)S(1)}, bf16[128,512]{1,0:T(8,128)(2,1)S(1)}, u32[]{:S(2)}, u32[]{:S(2)}) collective-permute-start(bf16[128,512]{1,0:T(8,128)(2,1)S(1)} %get-tuple-element.89), channel_id=1, source_target_pairs={{0,14},{1,15},{2,8},{3,9},{4,10},{5,11},{6,12},{7,13},{8,6},{9,7},... | collective-permute-start | bytes 393224 | tf_op jit(solution)/shard_map/ppermute | solution.py:38
  19.9 2.7 %collective-permute-start.7 = (bf16[128,512]{1,0:T(8,128)(2,1)S(1)}, bf16[128,512]{1,0:T(8,128)(2,1)S(1)}, u32[]{:S(2)}, u32[]{:S(2)}) collective-permute-start(bf16[128,512]{1,0:T(8,128)(2,1)S(1)} %get-tuple-element.90), channel_id=1, source_target_pairs={{0,10},{1,11},{2,12},{3,13},{4,14},{5,15},{6,8},{7,9},{8,2},{9,3},... | collective-permute-start | bytes 393224 | tf_op jit(solution)/shard_map/ppermute | solution.py:38
  22.6 2.2 %shard_map.95 = bf16[256,4096]{1,0:T(8,128)(2,1)} custom-call(s32[43]{0:T(128)S(1)} %concatenate.12.scalar_ref, bf16[256,8192]{1,0:T(8,128)(2,1)S(1)} %copy-done.1), custom_call_target="tpu_custom_call" | custom-call | tf_op jit(solution)/shard_map/pallas_call | solution.py:569
  24.9 1.8 %shard_map.97 = (f32[256,256]{1,0:T(8,128)S(1)}, f32[256,128]{1,0:T(8,128)S(1)}, f32[8,128]{1,0:T(8,128)S(1)}) custom-call(s32[43]{0:T(128)S(1)} %concatenate.12.scalar_ref, bf16[8192,256]{1,0:T(8,128)(2,1)S(1)} %copy-done, bf16[8192,128]{1,0:T(8,128)(2,1)S(1)} %copy-done.3, bf16[1024,512]{1,0:T(8,128)(2,1)S(1)} %get-tuple-element.83.near_ref, ...), custom_call_target="tpu_custom_call" | custom-call | flops 805306368 | bytes 2097152 | tf_op jit(solution)/shard_map/pallas_call | solution.py:478
  27.0 2.1 %collective-permute-done.7.lower_ref = bf16[128,512]{1,0:T(8,128)(2,1)S(1)} collective-permute-done((bf16[128,512]{1,0:T(8,128)(2,1)S(1)}, bf16[128,512]{1,0:T(8,128)(2,1)S(1)}, u32[]{:S(2)}, u32[]{:S(2)}) %collective-permute-start.7) | collective-permute-done | bytes 131104 | tf_op jit(solution)/shard_map/ppermute | solution.py:38
  35.9 2.9 %collective-permute-done.10.other_ref = bf16[256,256]{1,0:T(8,128)(2,1)S(1)} collective-permute-done((bf16[256,256]{1,0:T(8,128)(2,1)S(1)}, bf16[256,256]{1,0:T(8,128)(2,1)S(1)}, u32[]{:S(2)}, u32[]{:S(2)}) %collective-permute-start.10) | collective-permute-done | bytes 131104 | tf_op jit(solution)/shard_map/ppermute | solution.py:38
  38.9 12.9 %conditional.1 = ((bf16[256,512]{1,0:T(8,128)(2,1)S(1)}, f32[256,4]{1,0:T(8,128)S(1)})) conditional(s32[]{:T(128)} %convert_element_type.8, (bf16[256,256]{1,0:T(8,128)(2,1)S(1)}, bf16[256,256]{1,0:T(8,128)(2,1)S(1)}, s32[43]{0:T(128)S(1)}, s32[64]{0:T(128)S(1)}, bf16[64,256,128]{2,1,0:T(8,128)(2,1)}, ...), branch_computations={%region_1.2_spmd, %region_2.3_spmd} | conditional | flops 524288 | bytes 2629656 | solution.py:697
  38.9 12.9 %branch_1_fun.1 = (bf16[256,512]{1,0:T(8,128)(2,1)S(1)}, f32[256,4]{1,0:T(8,128)S(1)}) custom-call(s32[43]{0:T(128)S(1)} %get-tuple-element.32.scalar_ref, s32[64]{0:T(128)S(1)} %get-tuple-element.33.length_ref, bf16[256,256]{1,0:T(8,128)(2,1)S(1)} %get-tuple-element.34.own_ref, bf16[256,256]{1,0:T(8,128)(2,1)S(1)} %get-tuple-element.35.other_ref, ...), custom_call_target="tpu_custom_call" | custom-call | tf_op jit(solution)/shard_map/cond/branch_1_fun/pallas_call | solution.py:501
  53.1 1.8 %shard_map.101 = (bf16[256,512]{1,0:T(8,128)(2,1)S(1)}, f32[256,4]{1,0:T(8,128)S(1)}) custom-call(s32[43]{0:T(128)S(1)} %concatenate.12.scalar_ref, bf16[256,256]{1,0:T(8,128)(2,1)S(1)} %get-tuple-element.97.own_ref, bf16[256,256]{1,0:T(8,128)(2,1)S(1)} %collective-permute-done.10.other_ref, bf16[256,128]{1,0:T(8,128)(2,1)S(1)} %collective-permute-done.11.held_ref, ...), custom_call_target="tpu_custom_call" | custom-call | flops 6000000000 | bytes 2097152 | tf_op jit(solution)/shard_map/pallas_call | solution.py:478
  55.0 2.6 %shard_map.102 = (bf16[384,512]{1,0:T(8,128)(2,1)S(1)}, bf16[384,512]{1,0:T(8,128)(2,1)S(1)}, bf16[128,512]{1,0:T(8,128)(2,1)S(1)}, bf16[128,512]{1,0:T(8,128)(2,1)S(1)}, bf16[256,512]{1,0:T(8,128)(2,1)S(1)}) custom-call(s32[43]{0:T(128)S(1)} %concatenate.12.scalar_ref, bf16[256,4096]{1,0:T(8,128)(2,1)S(1)} %collective-permute-done.9.swapped_ref, ...), custom_call_target="tpu_custom_call" | custom-call | flops 536870912 | bytes 2097152 | tf_op jit(solution)/shard_map/pallas_call | solution.py:478
  57.6 2.1 %collective-permute-start.16 = (bf16[384,512]{1,0:T(8,128)(2,1)S(1)}, bf16[384,512]{1,0:T(8,128)(2,1)S(1)}, u32[]{:S(2)}, u32[]{:S(2)}) collective-permute-start(bf16[384,512]{1,0:T(8,128)(2,1)S(1)} %get-tuple-element.112), channel_id=1, source_target_pairs={{0,2},{1,3},{2,4},{3,5},{4,6},{5,7},{6,0},{7,1},{8,10},{9,11},{10,... | collective-permute-start | bytes 1179656 | tf_op jit(solution)/shard_map/ppermute | solution.py:38
  62.8 3.0 %collective-permute-start.18 = (bf16[128,512]{1,0:T(8,128)(2,1)S(1)}, bf16[128,512]{1,0:T(8,128)(2,1)S(1)}, u32[]{:S(2)}, u32[]{:S(2)}) collective-permute-start(bf16[128,512]{1,0:T(8,128)(2,1)S(1)} %get-tuple-element.114), channel_id=1, source_target_pairs={{0,10},{1,11},{2,12},{3,13},{4,14},{5,15},{6,8},{7,9},{8,2},{9,3},... | collective-permute-start | bytes 393224 | tf_op jit(solution)/shard_map/ppermute | solution.py:38
  65.9 2.7 %collective-permute-start.19 = (bf16[128,512]{1,0:T(8,128)(2,1)S(1)}, bf16[128,512]{1,0:T(8,128)(2,1)S(1)}, u32[]{:S(2)}, u32[]{:S(2)}) collective-permute-start(bf16[128,512]{1,0:T(8,128)(2,1)S(1)} %get-tuple-element.115), channel_id=1, source_target_pairs={{0,14},{1,15},{2,8},{3,9},{4,10},{5,11},{6,12},{7,13},{8,6},{9,7},... | collective-permute-start | bytes 393224 | tf_op jit(solution)/shard_map/ppermute | solution.py:38
  69.9 1.9 %shard_map.103 = (bf16[256,512]{1,0:T(8,128)(2,1)S(1)}, bf16[256,512]{1,0:T(8,128)(2,1)S(1)}, bf16[256,512]{1,0:T(8,128)(2,1)S(1)}, bf16[256,512]{1,0:T(8,128)(2,1)S(1)}) custom-call(s32[43]{0:T(128)S(1)} %concatenate.12.scalar_ref, bf16[256,4096]{1,0:T(8,128)(2,1)S(1)} %collective-permute-done.9.swapped_ref, bf16[256,8192]{1,0:T(8,128)(2,1)S(1)} %copy-done.2, ...), custom_call_target="tpu_custom_call" | custom-call | flops 536870912 | bytes 2097152 | tf_op jit(solution)/shard_map/pallas_call | solution.py:478
  74.7 2.4 %collective-permute-start.21 = (bf16[256,512]{1,0:T(8,128)(2,1)S(1)}, bf16[256,512]{1,0:T(8,128)(2,1)S(1)}, u32[]{:S(2)}, u32[]{:S(2)}) collective-permute-start(bf16[256,512]{1,0:T(8,128)(2,1)S(1)} %get-tuple-element.117), channel_id=1, source_target_pairs={{0,6},{1,7},{2,0},{3,1},{4,2},{5,3},{6,4},{7,5},{8,14},{9,15},{10,... | collective-permute-start | bytes 786440 | tf_op jit(solution)/shard_map/ppermute | solution.py:38
  77.1 2.7 %collective-permute-start.22 = (bf16[256,512]{1,0:T(8,128)(2,1)S(1)}, bf16[256,512]{1,0:T(8,128)(2,1)S(1)}, u32[]{:S(2)}, u32[]{:S(2)}) collective-permute-start(bf16[256,512]{1,0:T(8,128)(2,1)S(1)} %get-tuple-element.118), channel_id=1, source_target_pairs={{0,8},{1,9},{2,10},{3,11},{4,12},{5,13},{6,14},{7,15},{8,0},{9,1},... | collective-permute-start | bytes 786440 | tf_op jit(solution)/shard_map/ppermute | solution.py:38
  81.1 1.4 %collective-permute-done.24 = bf16[1,4,8,256]{3,2,1,0:T(8,128)(2,1)S(1)} collective-permute-done((bf16[1,4,8,256]{3,2,1,0:T(8,128)(2,1)S(1)}, bf16[1,4,8,256]{3,2,1,0:T(8,128)(2,1)S(1)}, u32[]{:S(2)}, u32[]{:S(2)}) %collective-permute-start.24) | collective-permute-done | bytes 16416 | tf_op jit(solution)/shard_map/ppermute | solution.py:782
  83.2 2.0 %collective-permute-done.22.from_partner = bf16[256,512]{1,0:T(8,128)(2,1)S(1)} collective-permute-done((bf16[256,512]{1,0:T(8,128)(2,1)S(1)}, bf16[256,512]{1,0:T(8,128)(2,1)S(1)}, u32[]{:S(2)}, u32[]{:S(2)}) %collective-permute-start.22) | collective-permute-done | bytes 262176 | tf_op jit(solution)/shard_map/ppermute | solution.py:38
  (71 shorter events, 24.0 us)
Async XLA Ops:
  0.6 10.2 %collective-permute-start = (bf16[256,512]{1,0:T(8,128)(2,1)}, bf16[256,512]{1,0:T(8,128)(2,1)S(1)}, u32[]{:S(2)}, u32[]{:S(2)}) collective-permute-start(bf16[256,512]{1,0:T(8,128)(2,1)} %bitcast.49), channel_id=1, source_target_pairs={{0,8},{1,9},{2,10},{3,11},{4,12},{5,13},{6,14},{7,15},{8,0},{9,1},... | collective-permute-start | bytes 786440 | tf_op jit(solution)/shard_map/ppermute | solution.py:38
  3.8 9.3 %collective-permute-start.1 = (bf16[256,512]{1,0:T(8,128)(2,1)}, bf16[256,512]{1,0:T(8,128)(2,1)S(1)}, u32[]{:S(2)}, u32[]{:S(2)}) collective-permute-start(bf16[256,512]{1,0:T(8,128)(2,1)} %bitcast.50), channel_id=1, source_target_pairs={{0,2},{1,3},{2,4},{3,5},{4,6},{5,7},{6,0},{7,1},{8,10},{9,11},{10,... | collective-permute-start | bytes 786440 | tf_op jit(solution)/shard_map/ppermute | solution.py:38
  5.4 7.7 %collective-permute-start.2 = (bf16[256,512]{1,0:T(8,128)(2,1)}, bf16[256,512]{1,0:T(8,128)(2,1)S(1)}, u32[]{:S(2)}, u32[]{:S(2)}) collective-permute-start(bf16[256,512]{1,0:T(8,128)(2,1)} %bitcast.51), channel_id=1, source_target_pairs={{0,6},{1,7},{2,0},{3,1},{4,2},{5,3},{6,4},{7,5},{8,14},{9,15},{10,... | collective-permute-start | bytes 786440 | tf_op jit(solution)/shard_map/ppermute | solution.py:38
  14.8 10.1 %collective-permute-start.3 = (bf16[1024,512]{1,0:T(8,128)(2,1)S(1)}, bf16[1024,512]{1,0:T(8,128)(2,1)S(1)}, u32[]{:S(2)}, u32[]{:S(2)}) collective-permute-start(bf16[1024,512]{1,0:T(8,128)(2,1)S(1)} %get-tuple-element.83.near_ref), channel_id=1, source_target_pairs={{0,1},{1,0},{2,3},{3,2},{4,5},{5,4},{6,7},{7,6},{8,9},{9,8},{10,11... | collective-permute-start | bytes 3145736 | tf_op jit(solution)/shard_map/ppermute | solution.py:38
  14.9 15.6 %collective-permute-start.4 = (bf16[384,512]{1,0:T(8,128)(2,1)S(1)}, bf16[384,512]{1,0:T(8,128)(2,1)S(1)}, u32[]{:S(2)}, u32[]{:S(2)}) collective-permute-start(bf16[384,512]{1,0:T(8,128)(2,1)S(1)} %get-tuple-element.87), channel_id=1, source_target_pairs={{0,2},{1,3},{2,4},{3,5},{4,6},{5,7},{6,0},{7,1},{8,10},{9,11},{10,... | collective-permute-start | bytes 1179656 | tf_op jit(solution)/shard_map/ppermute | solution.py:38
  16.5 14.0 %collective-permute-start.5 = (bf16[384,512]{1,0:T(8,128)(2,1)S(1)}, bf16[384,512]{1,0:T(8,128)(2,1)S(1)}, u32[]{:S(2)}, u32[]{:S(2)}) collective-permute-start(bf16[384,512]{1,0:T(8,128)(2,1)S(1)} %get-tuple-element.88), channel_id=1, source_target_pairs={{0,6},{1,7},{2,0},{3,1},{4,2},{5,3},{6,4},{7,5},{8,14},{9,15},{10,... | collective-permute-start | bytes 1179656 | tf_op jit(solution)/shard_map/ppermute | solution.py:38
  18.2 8.8 %collective-permute-start.6 = (bf16[128,512]{1,0:T(8,128)(2,1)S(1)}, bf16[128,512]{1,0:T(8,128)(2,1)S(1)}, u32[]{:S(2)}, u32[]{:S(2)}) collective-permute-start(bf16[128,512]{1,0:T(8,128)(2,1)S(1)} %get-tuple-element.89), channel_id=1, source_target_pairs={{0,14},{1,15},{2,8},{3,9},{4,10},{5,11},{6,12},{7,13},{8,6},{9,7},... | collective-permute-start | bytes 393224 | tf_op jit(solution)/shard_map/ppermute | solution.py:38
  19.9 9.1 %collective-permute-start.7 = (bf16[128,512]{1,0:T(8,128)(2,1)S(1)}, bf16[128,512]{1,0:T(8,128)(2,1)S(1)}, u32[]{:S(2)}, u32[]{:S(2)}) collective-permute-start(bf16[128,512]{1,0:T(8,128)(2,1)S(1)} %get-tuple-element.90), channel_id=1, source_target_pairs={{0,10},{1,11},{2,12},{3,13},{4,14},{5,15},{6,8},{7,9},{8,2},{9,3},... | collective-permute-start | bytes 393224 | tf_op jit(solution)/shard_map/ppermute | solution.py:38
  30.6 2.7 %collective-permute-start.8 = (bf16[1024,512]{1,0:T(8,128)(2,1)S(1)}, bf16[1024,512]{1,0:T(8,128)(2,1)S(1)}, u32[]{:S(2)}, u32[]{:S(2)}) collective-permute-start(bf16[1024,512]{1,0:T(8,128)(2,1)S(1)} %shard_map.98.far_ref), channel_id=1, source_target_pairs={{0,1},{1,0},{2,3},{3,2},{4,5},{5,4},{6,7},{7,6},{8,9},{9,8},{10,11... | collective-permute-start | bytes 3145736 | tf_op jit(solution)/shard_map/ppermute | solution.py:38
  34.7 20.3 %collective-permute-start.9 = (bf16[256,4096]{1,0:T(8,128)(2,1)}, bf16[256,4096]{1,0:T(8,128)(2,1)S(1)}, u32[]{:S(2)}, u32[]{:S(2)}) collective-permute-start(bf16[256,4096]{1,0:T(8,128)(2,1)} %shard_map.95), channel_id=1, source_target_pairs={{0,1},{1,0},{2,3},{3,2},{4,5},{5,4},{6,7},{7,6},{8,9},{9,8},{10,11... | collective-permute-start | bytes 6291464 | tf_op jit(solution)/shard_map/ppermute | solution.py:38
  34.9 4.0 %collective-permute-start.10 = (bf16[256,256]{1,0:T(8,128)(2,1)S(1)}, bf16[256,256]{1,0:T(8,128)(2,1)S(1)}, u32[]{:S(2)}, u32[]{:S(2)}) collective-permute-start(bf16[256,256]{1,0:T(8,128)(2,1)S(1)} %get-tuple-element.97.own_ref), channel_id=1, source_target_pairs={{0,1},{1,0},{2,3},{3,2},{4,5},{5,4},{6,7},{7,6},{8,9},{9,8},{10,11... | collective-permute-start | bytes 393224 | tf_op jit(solution)/shard_map/ppermute | solution.py:38
  35.2 16.5 %collective-permute-start.11 = (bf16[256,128]{1,0:T(8,128)(2,1)S(1)}, bf16[256,128]{1,0:T(8,128)(2,1)S(1)}, u32[]{:S(2)}, u32[]{:S(2)}) collective-permute-start(bf16[256,128]{1,0:T(8,128)(2,1)S(1)} %get-tuple-element.100), channel_id=1, source_target_pairs={{0,0},{1,2},{2,4},{3,6},{4,8},{5,10},{6,12},{7,14},{8,1},{9,3},{10... | collective-permute-start | bytes 196616 | tf_op jit(solution)/shard_map/ppermute | solution.py:693
  52.2 2.7 %collective-permute-start.12 = (bf16[256,512]{1,0:T(8,128)(2,1)S(1)}, bf16[256,512]{1,0:T(8,128)(2,1)S(1)}, u32[]{:S(2)}, u32[]{:S(2)}) collective-permute-start(bf16[256,512]{1,0:T(8,128)(2,1)S(1)} %get-tuple-element.101.own_ref), channel_id=1, source_target_pairs={{0,1},{1,0},{2,3},{3,2},{4,5},{5,4},{6,7},{7,6},{8,9},{9,8},{10,11... | collective-permute-start | bytes 786440 | tf_op jit(solution)/shard_map/ppermute | solution.py:38
  52.4 2.6 %collective-permute-start.13 = (f32[256,4]{1,0:T(8,128)S(1)}, f32[256,4]{1,0:T(8,128)S(1)}, u32[]{:S(2)}, u32[]{:S(2)}) collective-permute-start(f32[256,4]{1,0:T(8,128)S(1)} %get-tuple-element.102.own_level), channel_id=1, source_target_pairs={{0,1},{1,0},{2,3},{3,2},{4,5},{5,4},{6,7},{7,6},{8,9},{9,8},{10,11... | collective-permute-start | bytes 12296 | tf_op jit(solution)/shard_map/ppermute | solution.py:38
  57.6 16.0 %collective-permute-start.16 = (bf16[384,512]{1,0:T(8,128)(2,1)S(1)}, bf16[384,512]{1,0:T(8,128)(2,1)S(1)}, u32[]{:S(2)}, u32[]{:S(2)}) collective-permute-start(bf16[384,512]{1,0:T(8,128)(2,1)S(1)} %get-tuple-element.112), channel_id=1, source_target_pairs={{0,2},{1,3},{2,4},{3,5},{4,6},{5,7},{6,0},{7,1},{8,10},{9,11},{10,... | collective-permute-start | bytes 1179656 | tf_op jit(solution)/shard_map/ppermute | solution.py:38
  59.7 13.9 %collective-permute-start.17 = (bf16[384,512]{1,0:T(8,128)(2,1)S(1)}, bf16[384,512]{1,0:T(8,128)(2,1)S(1)}, u32[]{:S(2)}, u32[]{:S(2)}) collective-permute-start(bf16[384,512]{1,0:T(8,128)(2,1)S(1)} %get-tuple-element.113), channel_id=1, source_target_pairs={{0,6},{1,7},{2,0},{3,1},{4,2},{5,3},{6,4},{7,5},{8,14},{9,15},{10,... | collective-permute-start | bytes 1179656 | tf_op jit(solution)/shard_map/ppermute | solution.py:38
  61.5 7.0 %collective-permute-start.15 = (bf16[4,4,8,256]{3,2,1,0:T(8,128)(2,1)S(1)}, bf16[4,4,8,256]{3,2,1,0:T(8,128)(2,1)S(1)}, u32[]{:S(2)}, u32[]{:S(2)}) collective-permute-start(bf16[4,4,8,256]{3,2,1,0:T(8,128)(2,1)S(1)} %bitcast.64), channel_id=1, source_target_pairs={{0,64},{1,65},{2,66},{3,67},{4,68},{5,69},{6,70},{7,71},{8,72},{9,... | collective-permute-start | bytes 196616 | tf_op jit(solution)/shard_map/ppermute | solution.py:761
  62.8 10.1 %collective-permute-start.18 = (bf16[128,512]{1,0:T(8,128)(2,1)S(1)}, bf16[128,512]{1,0:T(8,128)(2,1)S(1)}, u32[]{:S(2)}, u32[]{:S(2)}) collective-permute-start(bf16[128,512]{1,0:T(8,128)(2,1)S(1)} %get-tuple-element.114), channel_id=1, source_target_pairs={{0,10},{1,11},{2,12},{3,13},{4,14},{5,15},{6,8},{7,9},{8,2},{9,3},... | collective-permute-start | bytes 393224 | tf_op jit(solution)/shard_map/ppermute | solution.py:38
  65.9 7.7 %collective-permute-start.19 = (bf16[128,512]{1,0:T(8,128)(2,1)S(1)}, bf16[128,512]{1,0:T(8,128)(2,1)S(1)}, u32[]{:S(2)}, u32[]{:S(2)}) collective-permute-start(bf16[128,512]{1,0:T(8,128)(2,1)S(1)} %get-tuple-element.115), channel_id=1, source_target_pairs={{0,14},{1,15},{2,8},{3,9},{4,10},{5,11},{6,12},{7,13},{8,6},{9,7},... | collective-permute-start | bytes 393224 | tf_op jit(solution)/shard_map/ppermute | solution.py:38
  68.6 11.2 %collective-permute-start.23 = (bf16[2,4,8,256]{3,2,1,0:T(8,128)(2,1)S(1)}, bf16[2,4,8,256]{3,2,1,0:T(8,128)(2,1)S(1)}, u32[]{:S(2)}, u32[]{:S(2)}) collective-permute-start(bf16[2,4,8,256]{3,2,1,0:T(8,128)(2,1)S(1)} %slice.42), channel_id=1, source_target_pairs={{0,32},{64,96},{1,33},{65,97},{2,34},{66,98},{3,35},{67,99},{4,36}... | collective-permute-start | bytes 98312 | tf_op jit(solution)/shard_map/ppermute | solution.py:780
  73.8 9.4 %collective-permute-start.20 = (bf16[256,512]{1,0:T(8,128)(2,1)S(1)}, bf16[256,512]{1,0:T(8,128)(2,1)S(1)}, u32[]{:S(2)}, u32[]{:S(2)}) collective-permute-start(bf16[256,512]{1,0:T(8,128)(2,1)S(1)} %get-tuple-element.116), channel_id=1, source_target_pairs={{0,2},{1,3},{2,4},{3,5},{4,6},{5,7},{6,0},{7,1},{8,10},{9,11},{10,... | collective-permute-start | bytes 786440 | tf_op jit(solution)/shard_map/ppermute | solution.py:38
  74.7 8.5 %collective-permute-start.21 = (bf16[256,512]{1,0:T(8,128)(2,1)S(1)}, bf16[256,512]{1,0:T(8,128)(2,1)S(1)}, u32[]{:S(2)}, u32[]{:S(2)}) collective-permute-start(bf16[256,512]{1,0:T(8,128)(2,1)S(1)} %get-tuple-element.117), channel_id=1, source_target_pairs={{0,6},{1,7},{2,0},{3,1},{4,2},{5,3},{6,4},{7,5},{8,14},{9,15},{10,... | collective-permute-start | bytes 786440 | tf_op jit(solution)/shard_map/ppermute | solution.py:38
  77.1 8.1 %collective-permute-start.22 = (bf16[256,512]{1,0:T(8,128)(2,1)S(1)}, bf16[256,512]{1,0:T(8,128)(2,1)S(1)}, u32[]{:S(2)}, u32[]{:S(2)}) collective-permute-start(bf16[256,512]{1,0:T(8,128)(2,1)S(1)} %get-tuple-element.118), channel_id=1, source_target_pairs={{0,8},{1,9},{2,10},{3,11},{4,12},{5,13},{6,14},{7,15},{8,0},{9,1},... | collective-permute-start | bytes 786440 | tf_op jit(solution)/shard_map/ppermute | solution.py:38
  79.8 2.7 %collective-permute-start.24 = (bf16[1,4,8,256]{3,2,1,0:T(8,128)(2,1)S(1)}, bf16[1,4,8,256]{3,2,1,0:T(8,128)(2,1)S(1)}, u32[]{:S(2)}, u32[]{:S(2)}) collective-permute-start(bf16[1,4,8,256]{3,2,1,0:T(8,128)(2,1)S(1)} %slice.44), channel_id=1, source_target_pairs={{0,16},{32,48},{64,80},{96,112},{1,17},{33,49},{65,81},{97,113},{2... | collective-permute-start | bytes 49160 | tf_op jit(solution)/shard_map/ppermute | solution.py:782
  (7 other events, 43.7 us)

commit v4 on v3

--- a/solution.py
+++ b/solution.py
@@ -219,32 +219,27 @@
     allowed = together & (column <= row)
     lane = lax.broadcasted_iota(jnp.int32, (TOK, GQ), 1)
 
-    def attend(key_ref, value_ref):
-        values = with_ones(value_ref[...])
-        levels = jnp.zeros((TOK, GQ), jnp.float32)
-        for j in range(GQ):
-            source = own_ref if j < GQ // 2 else other_ref
-            part = slice(j % (GQ // 2) * HD, (j % (GQ // 2) + 1) * HD)
-            scores = lax.dot_general(
-                source[:, part], key_ref[...], NT, preferred_element_type=jnp.float32
-            )
-            scores = jnp.where(allowed, scores, NEG_FILL)
-            largest = jnp.max(scores, axis=1, keepdims=True)
-            mixed = jnp.dot(
-                weights_of(scores, largest), values, preferred_element_type=jnp.float32
-            )
-            total = mixed[:, HD : HD + 1]
-            mixed_ref[:, j * HD : (j + 1) * HD] = (mixed[:, :HD] / total).astype(mixed_ref.dtype)
-            levels = jnp.where(lane == j, largest * HD**-0.5 + jnp.log(total), levels)
-        level_ref[...] = levels
-
-    @pl.when(scalar_ref[CORE] == 0)
-    def _():
-        attend(held_ref, swapped_ref)
-
-    @pl.when(scalar_ref[CORE] != 0)
-    def _():
-        attend(swapped_ref, held_ref)
+    held = held_ref[...].astype(jnp.float32)
+    swapped = swapped_ref[...].astype(jnp.float32)
+    first = scalar_ref[CORE] == 0
+    keys = jnp.where(first, held, swapped).astype(jnp.bfloat16)
+    values = with_ones(jnp.where(first, swapped, held).astype(jnp.bfloat16))
+    levels = jnp.zeros((TOK, GQ), jnp.float32)
+    for j in range(GQ):
+        source = own_ref if j < GQ // 2 else other_ref
+        part = slice(j % (GQ // 2) * HD, (j % (GQ // 2) + 1) * HD)
+        scores = lax.dot_general(
+            source[:, part], keys, NT, preferred_element_type=jnp.float32
+        )
+        scores = jnp.where(allowed, scores, NEG_FILL)
+        largest = jnp.max(scores, axis=1, keepdims=True)
+        mixed = jnp.dot(
+            weights_of(scores, largest), values, preferred_element_type=jnp.float32
+        )
+        total = mixed[:, HD : HD + 1]
+        mixed_ref[:, j * HD : (j + 1) * HD] = (mixed[:, :HD] / total).astype(mixed_ref.dtype)
+        levels = jnp.where(lane == j, largest * HD**-0.5 + jnp.log(total), levels)
+    level_ref[...] = levels
 
 
 def merged(parts, levels):
@@ -363,10 +358,8 @@
 
 
 def join_kernel(
-    scalar_ref, own_ref, partner_ref, last_ref, next_ref, plus, minus, up, down, near, sem
+    scalar_ref, swapped_ref, partner_ref, last_ref, next_ref, plus, minus, up, down, near
 ):
-    own = pltpu.make_async_copy(own_ref, near.at[:TOK], sem)
-    own.start()
     plus[:TOK] = partner_ref[...]
     plus[TOK:] = last_ref[:HALF]
     minus[:TOK] = partner_ref[...]
@@ -374,8 +367,7 @@
     up[...] = last_ref[HALF:]
     down[...] = next_ref[:HALF]
     for index, ref in enumerate((last_ref, next_ref, partner_ref)):
-        near[(index + 1) * TOK : (index + 2) * TOK] = ref[...]
-    own.wait()
+        near[index * TOK : (index + 1) * TOK] = ref[...]
 
 
 def sides_kernel(mark_ref, last_ref, next_ref, upper_ref, lower_ref, sides):
@@ -403,23 +395,32 @@
     ]
 
 
-def four_shards(ref):
-    return [ref[index * TOK : (index + 1) * TOK] for index in range(4)]
-
-
-def near_kernel(scalar_ref, query_weight, pair_weight, near_ref, other_ref, query, pair, mark):
+def shards_of(ref):
+    return [ref[index * TOK : (index + 1) * TOK] for index in range(ref.shape[0] // TOK)]
+
+
+def near_kernel(
+    scalar_ref,
+    query_weight,
+    pair_weight,
+    own_ref,
+    near_ref,
+    other_ref,
+    other_near_ref,
+    query,
+    pair,
+    mark,
+):
     mark[...] = jnp.zeros_like(mark)
+    sources = (own_ref, near_ref, other_ref, other_near_ref)
+    shards = [shard for ref in sources for shard in shards_of(ref)]
     query[...], pair[...] = projected_parts(
-        scalar_ref,
-        NEAR_ROWS,
-        four_shards(near_ref) + four_shards(other_ref),
-        query_weight,
-        pair_weight,
+        scalar_ref, NEAR_ROWS, shards, query_weight, pair_weight
     )
 
 
 def far_kernel(scalar_ref, query_weight, pair_weight, query_in, pair_in, far_ref, query, pair):
-    sums = projected_parts(scalar_ref, FAR_ROWS, four_shards(far_ref), query_weight, pair_weight)
+    sums = projected_parts(scalar_ref, FAR_ROWS, shards_of(far_ref), query_weight, pair_weight)
     query[...] = query_in[...] + sums[0]
     pair[...] = pair_in[...] + sums[1]
 
@@ -437,7 +438,7 @@
     pair_out,
 ):
     sums = projected_parts(
-        scalar_ref, FAR_ROWS + 4, four_shards(far_ref), query_weight, pair_weight
+        scalar_ref, FAR_ROWS + 4, shards_of(far_ref), query_weight, pair_weight
     )
     query = query_in[...] + sums[0]
     pair = pair_in[...] + sums[1]
@@ -627,33 +628,37 @@
     wide = ((TOK + HALF, SHARD), jnp.bfloat16)
     half = ((HALF, SHARD), jnp.bfloat16)
     shard = ((TOK, SHARD), jnp.bfloat16)
+    triple = ((3 * TOK, SHARD), jnp.bfloat16)
     four = ((4 * TOK, SHARD), jnp.bfloat16)
     weights = (query_weight, kv_weight)
     sums = (((TOK, query_weight.shape[1]), jnp.float32), ((TOK, kv_weight.shape[1]), jnp.float32))
     partner_tokens = moved(tokens, 1, 0, 0)
     last_tokens, next_tokens = moved(tokens, 0, 1, 0), moved(tokens, 0, 3, 0)
+    other_tokens = core_swap(tokens)
     scalars, picks, positions = lax.optimization_barrier((scalars, picks, positions))
     cosine, sine = turns(positions)
     plus, minus, up, down, near = called(
         join_kernel,
-        (wide, wide, half, half, four),
+        (wide, wide, half, half, triple),
         scalars,
         partner_tokens,
         last_tokens,
         next_tokens,
-        streamed=(tokens,),
-        scratch=(pltpu.SemaphoreType.DMA(()),),
+        streamed=(other_tokens,),
         flops=LONG,
     )
     from_last, from_next = moved(plus, 0, 1, 0), moved(minus, 0, 3, 0)
     far_upper, far_lower = moved(down, 1, 3, 0), moved(up, 1, 1, 0)
     scalars, cut_out = lax.optimization_barrier((scalars, cut_out))
+    swapped_out = core_swap(cut_out)
     *part, mark = called(
         near_kernel,
         sums + (((8, HD), jnp.float32),),
         scalars,
         *weights,
+        tokens,
         near,
+        other_tokens,
         core_swap(near),
         flops=2 * TOK * 8 * SHARD * 3 * HD,
     )
@@ -688,12 +693,10 @@
         sine,
         flops=2 * TOK * 4 * SHARD * 3 * HD,
     )
-    pair_local, cut_out = lax.optimization_barrier((pair_local, cut_out))
     query_other = core_swap(query_local)
     pair_held = lax.ppermute(
         pair_local, "tp", [(t, 2 * t if t < KVH else 2 * (t - KVH) + 1) for t in range(2 * KVH)]
     )
-    swapped_out = core_swap(cut_out)
     cached = lax.cond(
         is_prefill,
         prefill_part,

time: 86.3 us -> 88.5 us (1.025)
  Pallas kernels: 28.2 us -> 29.7 us
  local copies, waits for them, and re-layouts: 1.85 us -> 0.9 us
  starting transfers between devices: 35.4 us -> 36.3 us
    pallas_call x11, Pallas kernels: 13.1 us -> 14.1 us  [called(): pl.pallas_call(kernel, in_specs=specs, out_specs=tuple((whole for _ in sh...]
    unnamed x13, local copies, waits for them, and re-layouts: 1.55 us -> 0.61 us
    ppermute x21 -> x22, waiting for transfers between devices: 13.9 us -> 14.8 us  [moved(): return lax.ppermute(shard, 'tp', pairs)]
    ppermute x21 -> x22, starting transfers between devices: 30.9 us -> 31.7 us  [moved(): return lax.ppermute(shard, 'tp', pairs)]
  transfers between devices with their start and end apart: 25 -> 26, of which waited for: 12 -> 11; matrix products, arithmetic and copies ran while one was open for 6% -> 6% of each run, Pallas kernels for 26% -> 29%
where the time goes in v4:
time: 88.5 us; the launch traced here: 88.2 us
  starting transfers between devices  36.3 us (41%)
  Pallas kernels  29.7 us (34%)
  waiting for transfers between devices  16.2 us (18%)
  other arithmetic  4.22 us (5%)
  between operations  0.93 us (1%)
  local copies, waits for them, and re-layouts  0.9 us (1%)
    ppermute x22, starting transfers between devices, moved(): return lax.ppermute(shard, 'tp', pairs)  31.7 us
    ppermute x22, waiting for transfers between devices, moved(): return lax.ppermute(shard, 'tp', pairs)  14.8 us
    pallas_call x11, Pallas kernels, called(): pl.pallas_call(kernel, in_specs=specs, out_specs=tuple((whole for _ in sh...  14.1 us
    pallas_call x1, Pallas kernels, prefill_part(): pl.pallas_call(prefill_kernel, in_specs=[small, small, whole, whole, ther...  13.3 us
    pallas_call x1, Pallas kernels, cut_columns(): pl.pallas_call(cut_kernel, in_specs=[pl.BlockSpec(memory_space=pltpu.SMEM...  2.21 us
  transfers between devices with their start and end apart: 26, of which 11 were waited for; matrix products, arithmetic and copies ran while one was open for 6% of the time, Pallas kernels for 29%

profile of v4, /device:TPU:0, one launch (start us, length us, event | category | flops | bytes accessed | tf_op | source)
XLA Modules:
  0.0 88.2 jit_solution(14263205083461645389)
XLA Ops:
  0.7 3.2 %collective-permute-start.2 = (bf16[256,512]{1,0:T(8,128)(2,1)}, bf16[256,512]{1,0:T(8,128)(2,1)S(1)}, u32[]{:S(2)}, u32[]{:S(2)}) collective-permute-start(bf16[256,512]{1,0:T(8,128)(2,1)} %bitcast.49), channel_id=1, source_target_pairs={{0,8},{1,9},{2,10},{3,11},{4,12},{5,13},{6,14},{7,15},{8,0},{9,1},... | collective-permute-start | bytes 786440 | tf_op jit(solution)/shard_map/ppermute | solution.py:38
  5.5 1.7 %collective-permute-start.4 = (bf16[256,512]{1,0:T(8,128)(2,1)}, bf16[256,512]{1,0:T(8,128)(2,1)S(1)}, u32[]{:S(2)}, u32[]{:S(2)}) collective-permute-start(bf16[256,512]{1,0:T(8,128)(2,1)} %bitcast.51), channel_id=1, source_target_pairs={{0,6},{1,7},{2,0},{3,1},{4,2},{5,3},{6,4},{7,5},{8,14},{9,15},{10,... | collective-permute-start | bytes 786440 | tf_op jit(solution)/shard_map/ppermute | solution.py:38
  11.2 2.6 %collective-permute-done.3.last_ref = bf16[256,512]{1,0:T(8,128)(2,1)S(1)} collective-permute-done((bf16[256,512]{1,0:T(8,128)(2,1)}, bf16[256,512]{1,0:T(8,128)(2,1)S(1)}, u32[]{:S(2)}, u32[]{:S(2)}) %collective-permute-start.3) | collective-permute-done | bytes 262176 | tf_op jit(solution)/shard_map/ppermute | solution.py:38
  14.6 1.6 %collective-permute-start.6 = (bf16[384,512]{1,0:T(8,128)(2,1)S(1)}, bf16[384,512]{1,0:T(8,128)(2,1)S(1)}, u32[]{:S(2)}, u32[]{:S(2)}) collective-permute-start(bf16[384,512]{1,0:T(8,128)(2,1)S(1)} %get-tuple-element.86), channel_id=1, source_target_pairs={{0,2},{1,3},{2,4},{3,5},{4,6},{5,7},{6,0},{7,1},{8,10},{9,11},{10,... | collective-permute-start | bytes 1179656 | tf_op jit(solution)/shard_map/ppermute | solution.py:38
  16.2 1.7 %collective-permute-start.7 = (bf16[384,512]{1,0:T(8,128)(2,1)S(1)}, bf16[384,512]{1,0:T(8,128)(2,1)S(1)}, u32[]{:S(2)}, u32[]{:S(2)}) collective-permute-start(bf16[384,512]{1,0:T(8,128)(2,1)S(1)} %get-tuple-element.87), channel_id=1, source_target_pairs={{0,6},{1,7},{2,0},{3,1},{4,2},{5,3},{6,4},{7,5},{8,14},{9,15},{10,... | collective-permute-start | bytes 1179656 | tf_op jit(solution)/shard_map/ppermute | solution.py:38
  17.9 2.2 %shard_map.95 = bf16[256,4096]{1,0:T(8,128)(2,1)} custom-call(s32[43]{0:T(128)S(1)} %concatenate.12.scalar_ref, bf16[256,8192]{1,0:T(8,128)(2,1)S(1)} %copy-done.1), custom_call_target="tpu_custom_call" | custom-call | tf_op jit(solution)/shard_map/pallas_call | solution.py:570
  20.2 1.8 %collective-permute-start.8 = (bf16[128,512]{1,0:T(8,128)(2,1)S(1)}, bf16[128,512]{1,0:T(8,128)(2,1)S(1)}, u32[]{:S(2)}, u32[]{:S(2)}) collective-permute-start(bf16[128,512]{1,0:T(8,128)(2,1)S(1)} %get-tuple-element.88), channel_id=1, source_target_pairs={{0,14},{1,15},{2,8},{3,9},{4,10},{5,11},{6,12},{7,13},{8,6},{9,7},... | collective-permute-start | bytes 393224 | tf_op jit(solution)/shard_map/ppermute | solution.py:38
  22.0 2.7 %collective-permute-start.9 = (bf16[128,512]{1,0:T(8,128)(2,1)S(1)}, bf16[128,512]{1,0:T(8,128)(2,1)S(1)}, u32[]{:S(2)}, u32[]{:S(2)}) collective-permute-start(bf16[128,512]{1,0:T(8,128)(2,1)S(1)} %get-tuple-element.89), channel_id=1, source_target_pairs={{0,10},{1,11},{2,12},{3,13},{4,14},{5,15},{6,8},{7,9},{8,2},{9,3},... | collective-permute-start | bytes 393224 | tf_op jit(solution)/shard_map/ppermute | solution.py:38
  24.7 1.8 %shard_map.97 = (f32[256,256]{1,0:T(8,128)S(1)}, f32[256,128]{1,0:T(8,128)S(1)}, f32[8,128]{1,0:T(8,128)S(1)}) custom-call(s32[43]{0:T(128)S(1)} %concatenate.12.scalar_ref, bf16[8192,256]{1,0:T(8,128)(2,1)S(1)} %copy-done, bf16[8192,128]{1,0:T(8,128)(2,1)S(1)} %copy-done.3, bf16[256,512]{1,0:T(8,128)(2,1)S(1)} %bitcast.52, ...), custom_call_target="tpu_custom_call" | custom-call | flops 805306368 | bytes 2097152 | tf_op jit(solution)/shard_map/pallas_call | solution.py:479
  26.5 2.5 %collective-permute-done.8.upper_ref = bf16[128,512]{1,0:T(8,128)(2,1)S(1)} collective-permute-done((bf16[128,512]{1,0:T(8,128)(2,1)S(1)}, bf16[128,512]{1,0:T(8,128)(2,1)S(1)}, u32[]{:S(2)}, u32[]{:S(2)}) %collective-permute-start.8) | collective-permute-done | bytes 131104 | tf_op jit(solution)/shard_map/ppermute | solution.py:38
  29.0 2.6 %collective-permute-done.9.lower_ref = bf16[128,512]{1,0:T(8,128)(2,1)S(1)} collective-permute-done((bf16[128,512]{1,0:T(8,128)(2,1)S(1)}, bf16[128,512]{1,0:T(8,128)(2,1)S(1)}, u32[]{:S(2)}, u32[]{:S(2)}) %collective-permute-start.9) | collective-permute-done | bytes 131104 | tf_op jit(solution)/shard_map/ppermute | solution.py:38
  34.4 2.0 %shard_map.100 = (bf16[256,256]{1,0:T(8,128)(2,1)}, bf16[256,128]{1,0:T(8,128)(2,1)S(1)}) custom-call(s32[43]{0:T(128)S(1)} %concatenate.12.scalar_ref, bf16[8192,256]{1,0:T(8,128)(2,1)S(1)} %copy-done, bf16[8192,128]{1,0:T(8,128)(2,1)S(1)} %copy-done.3, f32[256,256]{1,0:T(8,128)S(1)} %get-tuple-element.90.query_in, ...), custom_call_target="tpu_custom_call" | custom-call | flops 402653184 | bytes 2097152 | tf_op jit(solution)/shard_map/pallas_call | solution.py:479
  38.1 13.3 %conditional.1 = ((bf16[256,512]{1,0:T(8,128)(2,1)S(1)}, f32[256,4]{1,0:T(8,128)S(1)})) conditional(s32[]{:T(128)} %convert_element_type.8, (bf16[256,256]{1,0:T(8,128)(2,1)}, bf16[256,256]{1,0:T(8,128)(2,1)}, s32[43]{0:T(128)S(1)}, s32[64]{0:T(128)S(1)}, bf16[64,256,128]{2,1,0:T(8,128)(2,1)}, /*index=5*/bf16[64,256,128]{2,1,0:T(8,128)(2,1)}) %tuple.40, ...), branch_computations={%region_1.2_spmd, %region_2.3_spmd} | conditional | flops 524288 | bytes 2629656 | solution.py:700
  38.1 13.3 %branch_1_fun.1 = (bf16[256,512]{1,0:T(8,128)(2,1)S(1)}, f32[256,4]{1,0:T(8,128)S(1)}) custom-call(s32[43]{0:T(128)S(1)} %get-tuple-element.32.scalar_ref, s32[64]{0:T(128)S(1)} %get-tuple-element.33.length_ref, bf16[256,256]{1,0:T(8,128)(2,1)} %get-tuple-element.34.own_ref, bf16[256,256]{1,0:T(8,128)(2,1)} %get-tuple-element.35.other_ref, ...), custom_call_target="tpu_custom_call" | custom-call | tf_op jit(solution)/shard_map/cond/branch_1_fun/pallas_call | solution.py:502
  51.5 2.3 %collective-permute-start.15 = (bf16[256,128]{1,0:T(8,128)(2,1)S(1)}, bf16[256,128]{1,0:T(8,128)(2,1)S(1)}, u32[]{:S(2)}, u32[]{:S(2)}) collective-permute-start(bf16[256,128]{1,0:T(8,128)(2,1)S(1)} %collective-permute-done.12.held_ref), channel_id=1, source_target_pairs={{0,1},{1,0},{2,3},{3,2},{4,5},{5,4},{6,7},{7,6},{8,9},{9,8},{10,11... | collective-permute-start | bytes 196616 | tf_op jit(solution)/shard_map/ppermute | solution.py:38
  54.6 2.2 %shard_map.101 = (bf16[256,512]{1,0:T(8,128)(2,1)S(1)}, f32[256,4]{1,0:T(8,128)S(1)}) custom-call(s32[43]{0:T(128)S(1)} %concatenate.12.scalar_ref, bf16[256,256]{1,0:T(8,128)(2,1)} %get-tuple-element.93.own_ref, bf16[256,256]{1,0:T(8,128)(2,1)} %collective-permute-done.11.other_ref, bf16[256,128]{1,0:T(8,128)(2,1)S(1)} %collective-permute-done.12.held_ref, ...), custom_call_target="tpu_custom_call" | custom-call | flops 6000000000 | bytes 2097152 | tf_op jit(solution)/shard_map/pallas_call | solution.py:479
  56.9 2.6 %shard_map.102 = (bf16[384,512]{1,0:T(8,128)(2,1)S(1)}, bf16[384,512]{1,0:T(8,128)(2,1)S(1)}, bf16[128,512]{1,0:T(8,128)(2,1)S(1)}, bf16[128,512]{1,0:T(8,128)(2,1)S(1)}, bf16[256,512]{1,0:T(8,128)(2,1)S(1)}) custom-call(s32[43]{0:T(128)S(1)} %concatenate.12.scalar_ref, bf16[256,4096]{1,0:T(8,128)(2,1)S(1)} %collective-permute-done.swapped_ref, ...), custom_call_target="tpu_custom_call" | custom-call | flops 536870912 | bytes 2097152 | tf_op jit(solution)/shard_map/pallas_call | solution.py:479
  60.4 2.4 %collective-permute-start.18 = (bf16[384,512]{1,0:T(8,128)(2,1)S(1)}, bf16[384,512]{1,0:T(8,128)(2,1)S(1)}, u32[]{:S(2)}, u32[]{:S(2)}) collective-permute-start(bf16[384,512]{1,0:T(8,128)(2,1)S(1)} %get-tuple-element.109), channel_id=1, source_target_pairs={{0,6},{1,7},{2,0},{3,1},{4,2},{5,3},{6,4},{7,5},{8,14},{9,15},{10,... | collective-permute-start | bytes 1179656 | tf_op jit(solution)/shard_map/ppermute | solution.py:38
  64.7 2.1 %collective-permute-start.19 = (bf16[128,512]{1,0:T(8,128)(2,1)S(1)}, bf16[128,512]{1,0:T(8,128)(2,1)S(1)}, u32[]{:S(2)}, u32[]{:S(2)}) collective-permute-start(bf16[128,512]{1,0:T(8,128)(2,1)S(1)} %get-tuple-element.110), channel_id=1, source_target_pairs={{0,10},{1,11},{2,12},{3,13},{4,14},{5,15},{6,8},{7,9},{8,2},{9,3},... | collective-permute-start | bytes 393224 | tf_op jit(solution)/shard_map/ppermute | solution.py:38
  66.8 3.6 %collective-permute-start.20 = (bf16[128,512]{1,0:T(8,128)(2,1)S(1)}, bf16[128,512]{1,0:T(8,128)(2,1)S(1)}, u32[]{:S(2)}, u32[]{:S(2)}) collective-permute-start(bf16[128,512]{1,0:T(8,128)(2,1)S(1)} %get-tuple-element.111), channel_id=1, source_target_pairs={{0,14},{1,15},{2,8},{3,9},{4,10},{5,11},{6,12},{7,13},{8,6},{9,7},... | collective-permute-start | bytes 393224 | tf_op jit(solution)/shard_map/ppermute | solution.py:38
  71.8 1.9 %shard_map.103 = (bf16[256,512]{1,0:T(8,128)(2,1)S(1)}, bf16[256,512]{1,0:T(8,128)(2,1)S(1)}, bf16[256,512]{1,0:T(8,128)(2,1)S(1)}, bf16[256,512]{1,0:T(8,128)(2,1)S(1)}) custom-call(s32[43]{0:T(128)S(1)} %concatenate.12.scalar_ref, bf16[256,4096]{1,0:T(8,128)(2,1)S(1)} %collective-permute-done.swapped_ref, bf16[256,8192]{1,0:T(8,128)(2,1)S(1)} %copy-done.2, ...), custom_call_target="tpu_custom_call" | custom-call | flops 536870912 | bytes 2097152 | tf_op jit(solution)/shard_map/pallas_call | solution.py:479
  77.8 1.7 %collective-permute-start.22 = (bf16[256,512]{1,0:T(8,128)(2,1)S(1)}, bf16[256,512]{1,0:T(8,128)(2,1)S(1)}, u32[]{:S(2)}, u32[]{:S(2)}) collective-permute-start(bf16[256,512]{1,0:T(8,128)(2,1)S(1)} %get-tuple-element.113), channel_id=1, source_target_pairs={{0,6},{1,7},{2,0},{3,1},{4,2},{5,3},{6,4},{7,5},{8,14},{9,15},{10,... | collective-permute-start | bytes 786440 | tf_op jit(solution)/shard_map/ppermute | solution.py:38
  79.5 1.9 %collective-permute-start.23 = (bf16[256,512]{1,0:T(8,128)(2,1)S(1)}, bf16[256,512]{1,0:T(8,128)(2,1)S(1)}, u32[]{:S(2)}, u32[]{:S(2)}) collective-permute-start(bf16[256,512]{1,0:T(8,128)(2,1)S(1)} %get-tuple-element.114), channel_id=1, source_target_pairs={{0,8},{1,9},{2,10},{3,11},{4,12},{5,13},{6,14},{7,15},{8,0},{9,1},... | collective-permute-start | bytes 786440 | tf_op jit(solution)/shard_map/ppermute | solution.py:38
  84.8 2.6 %collective-permute-done.23.from_partner = bf16[256,512]{1,0:T(8,128)(2,1)S(1)} collective-permute-done((bf16[256,512]{1,0:T(8,128)(2,1)S(1)}, bf16[256,512]{1,0:T(8,128)(2,1)S(1)}, u32[]{:S(2)}, u32[]{:S(2)}) %collective-permute-start.23) | collective-permute-done | bytes 262176 | tf_op jit(solution)/shard_map/ppermute | solution.py:38
  (73 shorter events, 24.2 us)
Async XLA Ops:
  0.6 10.3 %collective-permute-start.1 = (bf16[256,512]{1,0:T(8,128)(2,1)}, bf16[256,512]{1,0:T(8,128)(2,1)S(1)}, u32[]{:S(2)}, u32[]{:S(2)}) collective-permute-start(bf16[256,512]{1,0:T(8,128)(2,1)} %bitcast.48), channel_id=1, source_target_pairs={{0,1},{1,0},{2,3},{3,2},{4,5},{5,4},{6,7},{7,6},{8,9},{9,8},{10,11... | collective-permute-start | bytes 786440 | tf_op jit(solution)/shard_map/ppermute | solution.py:38
  0.7 10.4 %collective-permute-start.2 = (bf16[256,512]{1,0:T(8,128)(2,1)}, bf16[256,512]{1,0:T(8,128)(2,1)S(1)}, u32[]{:S(2)}, u32[]{:S(2)}) collective-permute-start(bf16[256,512]{1,0:T(8,128)(2,1)} %bitcast.49), channel_id=1, source_target_pairs={{0,8},{1,9},{2,10},{3,11},{4,12},{5,13},{6,14},{7,15},{8,0},{9,1},... | collective-permute-start | bytes 786440 | tf_op jit(solution)/shard_map/ppermute | solution.py:38
  3.9 9.9 %collective-permute-start.3 = (bf16[256,512]{1,0:T(8,128)(2,1)}, bf16[256,512]{1,0:T(8,128)(2,1)S(1)}, u32[]{:S(2)}, u32[]{:S(2)}) collective-permute-start(bf16[256,512]{1,0:T(8,128)(2,1)} %bitcast.50), channel_id=1, source_target_pairs={{0,2},{1,3},{2,4},{3,5},{4,6},{5,7},{6,0},{7,1},{8,10},{9,11},{10,... | collective-permute-start | bytes 786440 | tf_op jit(solution)/shard_map/ppermute | solution.py:38
  5.5 8.3 %collective-permute-start.4 = (bf16[256,512]{1,0:T(8,128)(2,1)}, bf16[256,512]{1,0:T(8,128)(2,1)S(1)}, u32[]{:S(2)}, u32[]{:S(2)}) collective-permute-start(bf16[256,512]{1,0:T(8,128)(2,1)} %bitcast.51), channel_id=1, source_target_pairs={{0,6},{1,7},{2,0},{3,1},{4,2},{5,3},{6,4},{7,5},{8,14},{9,15},{10,... | collective-permute-start | bytes 786440 | tf_op jit(solution)/shard_map/ppermute | solution.py:38
  14.5 7.5 %collective-permute-start.5 = (bf16[768,512]{1,0:T(8,128)(2,1)S(1)}, bf16[768,512]{1,0:T(8,128)(2,1)S(1)}, u32[]{:S(2)}, u32[]{:S(2)}) collective-permute-start(bf16[768,512]{1,0:T(8,128)(2,1)S(1)} %get-tuple-element.82.near_ref), channel_id=1, source_target_pairs={{0,1},{1,0},{2,3},{3,2},{4,5},{5,4},{6,7},{7,6},{8,9},{9,8},{10,11... | collective-permute-start | bytes 2359304 | tf_op jit(solution)/shard_map/ppermute | solution.py:38
  14.6 17.0 %collective-permute-start.6 = (bf16[384,512]{1,0:T(8,128)(2,1)S(1)}, bf16[384,512]{1,0:T(8,128)(2,1)S(1)}, u32[]{:S(2)}, u32[]{:S(2)}) collective-permute-start(bf16[384,512]{1,0:T(8,128)(2,1)S(1)} %get-tuple-element.86), channel_id=1, source_target_pairs={{0,2},{1,3},{2,4},{3,5},{4,6},{5,7},{6,0},{7,1},{8,10},{9,11},{10,... | collective-permute-start | bytes 1179656 | tf_op jit(solution)/shard_map/ppermute | solution.py:38
  16.2 15.4 %collective-permute-start.7 = (bf16[384,512]{1,0:T(8,128)(2,1)S(1)}, bf16[384,512]{1,0:T(8,128)(2,1)S(1)}, u32[]{:S(2)}, u32[]{:S(2)}) collective-permute-start(bf16[384,512]{1,0:T(8,128)(2,1)S(1)} %get-tuple-element.87), channel_id=1, source_target_pairs={{0,6},{1,7},{2,0},{3,1},{4,2},{5,3},{6,4},{7,5},{8,14},{9,15},{10,... | collective-permute-start | bytes 1179656 | tf_op jit(solution)/shard_map/ppermute | solution.py:38
  20.1 36.7 %collective-permute-start = (bf16[256,4096]{1,0:T(8,128)(2,1)}, bf16[256,4096]{1,0:T(8,128)(2,1)S(1)}, u32[]{:S(2)}, u32[]{:S(2)}) collective-permute-start(bf16[256,4096]{1,0:T(8,128)(2,1)} %shard_map.95), channel_id=1, source_target_pairs={{0,1},{1,0},{2,3},{3,2},{4,5},{5,4},{6,7},{7,6},{8,9},{9,8},{10,11... | collective-permute-start | bytes 6291464 | tf_op jit(solution)/shard_map/ppermute | solution.py:38
  20.2 8.8 %collective-permute-start.8 = (bf16[128,512]{1,0:T(8,128)(2,1)S(1)}, bf16[128,512]{1,0:T(8,128)(2,1)S(1)}, u32[]{:S(2)}, u32[]{:S(2)}) collective-permute-start(bf16[128,512]{1,0:T(8,128)(2,1)S(1)} %get-tuple-element.88), channel_id=1, source_target_pairs={{0,14},{1,15},{2,8},{3,9},{4,10},{5,11},{6,12},{7,13},{8,6},{9,7},... | collective-permute-start | bytes 393224 | tf_op jit(solution)/shard_map/ppermute | solution.py:38
  22.0 9.6 %collective-permute-start.9 = (bf16[128,512]{1,0:T(8,128)(2,1)S(1)}, bf16[128,512]{1,0:T(8,128)(2,1)S(1)}, u32[]{:S(2)}, u32[]{:S(2)}) collective-permute-start(bf16[128,512]{1,0:T(8,128)(2,1)S(1)} %get-tuple-element.89), channel_id=1, source_target_pairs={{0,10},{1,11},{2,12},{3,13},{4,14},{5,15},{6,8},{7,9},{8,2},{9,3},... | collective-permute-start | bytes 393224 | tf_op jit(solution)/shard_map/ppermute | solution.py:38
  31.7 2.7 %collective-permute-start.10 = (bf16[1024,512]{1,0:T(8,128)(2,1)S(1)}, bf16[1024,512]{1,0:T(8,128)(2,1)S(1)}, u32[]{:S(2)}, u32[]{:S(2)}) collective-permute-start(bf16[1024,512]{1,0:T(8,128)(2,1)S(1)} %shard_map.98.far_ref), channel_id=1, source_target_pairs={{0,1},{1,0},{2,3},{3,2},{4,5},{5,4},{6,7},{7,6},{8,9},{9,8},{10,11... | collective-permute-start | bytes 3145736 | tf_op jit(solution)/shard_map/ppermute | solution.py:38
  36.5 14.9 %collective-permute-start.12 = (bf16[256,128]{1,0:T(8,128)(2,1)S(1)}, bf16[256,128]{1,0:T(8,128)(2,1)S(1)}, u32[]{:S(2)}, u32[]{:S(2)}) collective-permute-start(bf16[256,128]{1,0:T(8,128)(2,1)S(1)} %get-tuple-element.96), channel_id=1, source_target_pairs={{0,0},{1,2},{2,4},{3,6},{4,8},{5,10},{6,12},{7,14},{8,1},{9,3},{10... | collective-permute-start | bytes 196616 | tf_op jit(solution)/shard_map/ppermute | solution.py:697
  51.5 3.2 %collective-permute-start.15 = (bf16[256,128]{1,0:T(8,128)(2,1)S(1)}, bf16[256,128]{1,0:T(8,128)(2,1)S(1)}, u32[]{:S(2)}, u32[]{:S(2)}) collective-permute-start(bf16[256,128]{1,0:T(8,128)(2,1)S(1)} %collective-permute-done.12.held_ref), channel_id=1, source_target_pairs={{0,1},{1,0},{2,3},{3,2},{4,5},{5,4},{6,7},{7,6},{8,9},{9,8},{10,11... | collective-permute-start | bytes 196616 | tf_op jit(solution)/shard_map/ppermute | solution.py:38
  53.7 3.1 %collective-permute-start.13 = (bf16[256,512]{1,0:T(8,128)(2,1)S(1)}, bf16[256,512]{1,0:T(8,128)(2,1)S(1)}, u32[]{:S(2)}, u32[]{:S(2)}) collective-permute-start(bf16[256,512]{1,0:T(8,128)(2,1)S(1)} %get-tuple-element.97.own_ref), channel_id=1, source_target_pairs={{0,1},{1,0},{2,3},{3,2},{4,5},{5,4},{6,7},{7,6},{8,9},{9,8},{10,11... | collective-permute-start | bytes 786440 | tf_op jit(solution)/shard_map/ppermute | solution.py:38
  53.8 3.0 %collective-permute-start.14 = (f32[256,4]{1,0:T(8,128)S(1)}, f32[256,4]{1,0:T(8,128)S(1)}, u32[]{:S(2)}, u32[]{:S(2)}) collective-permute-start(f32[256,4]{1,0:T(8,128)S(1)} %get-tuple-element.98.own_level), channel_id=1, source_target_pairs={{0,1},{1,0},{2,3},{3,2},{4,5},{5,4},{6,7},{7,6},{8,9},{9,8},{10,11... | collective-permute-start | bytes 12296 | tf_op jit(solution)/shard_map/ppermute | solution.py:38
  59.5 16.5 %collective-permute-start.17 = (bf16[384,512]{1,0:T(8,128)(2,1)S(1)}, bf16[384,512]{1,0:T(8,128)(2,1)S(1)}, u32[]{:S(2)}, u32[]{:S(2)}) collective-permute-start(bf16[384,512]{1,0:T(8,128)(2,1)S(1)} %get-tuple-element.108), channel_id=1, source_target_pairs={{0,2},{1,3},{2,4},{3,5},{4,6},{5,7},{6,0},{7,1},{8,10},{9,11},{10,... | collective-permute-start | bytes 1179656 | tf_op jit(solution)/shard_map/ppermute | solution.py:38
  60.4 15.6 %collective-permute-start.18 = (bf16[384,512]{1,0:T(8,128)(2,1)S(1)}, bf16[384,512]{1,0:T(8,128)(2,1)S(1)}, u32[]{:S(2)}, u32[]{:S(2)}) collective-permute-start(bf16[384,512]{1,0:T(8,128)(2,1)S(1)} %get-tuple-element.109), channel_id=1, source_target_pairs={{0,6},{1,7},{2,0},{3,1},{4,2},{5,3},{6,4},{7,5},{8,14},{9,15},{10,... | collective-permute-start | bytes 1179656 | tf_op jit(solution)/shard_map/ppermute | solution.py:38
  63.4 7.0 %collective-permute-start.16 = (bf16[4,4,8,256]{3,2,1,0:T(8,128)(2,1)S(1)}, bf16[4,4,8,256]{3,2,1,0:T(8,128)(2,1)S(1)}, u32[]{:S(2)}, u32[]{:S(2)}) collective-permute-start(bf16[4,4,8,256]{3,2,1,0:T(8,128)(2,1)S(1)} %bitcast.65), channel_id=1, source_target_pairs={{0,64},{1,65},{2,66},{3,67},{4,68},{5,69},{6,70},{7,71},{8,72},{9,... | collective-permute-start | bytes 196616 | tf_op jit(solution)/shard_map/ppermute | solution.py:764
  64.7 10.1 %collective-permute-start.19 = (bf16[128,512]{1,0:T(8,128)(2,1)S(1)}, bf16[128,512]{1,0:T(8,128)(2,1)S(1)}, u32[]{:S(2)}, u32[]{:S(2)}) collective-permute-start(bf16[128,512]{1,0:T(8,128)(2,1)S(1)} %get-tuple-element.110), channel_id=1, source_target_pairs={{0,10},{1,11},{2,12},{3,13},{4,14},{5,15},{6,8},{7,9},{8,2},{9,3},... | collective-permute-start | bytes 393224 | tf_op jit(solution)/shard_map/ppermute | solution.py:38
  66.8 9.2 %collective-permute-start.20 = (bf16[128,512]{1,0:T(8,128)(2,1)S(1)}, bf16[128,512]{1,0:T(8,128)(2,1)S(1)}, u32[]{:S(2)}, u32[]{:S(2)}) collective-permute-start(bf16[128,512]{1,0:T(8,128)(2,1)S(1)} %get-tuple-element.111), channel_id=1, source_target_pairs={{0,14},{1,15},{2,8},{3,9},{4,10},{5,11},{6,12},{7,13},{8,6},{9,7},... | collective-permute-start | bytes 393224 | tf_op jit(solution)/shard_map/ppermute | solution.py:38
  70.5 10.9 %collective-permute-start.24 = (bf16[2,4,8,256]{3,2,1,0:T(8,128)(2,1)S(1)}, bf16[2,4,8,256]{3,2,1,0:T(8,128)(2,1)S(1)}, u32[]{:S(2)}, u32[]{:S(2)}) collective-permute-start(bf16[2,4,8,256]{3,2,1,0:T(8,128)(2,1)S(1)} %slice.42), channel_id=1, source_target_pairs={{0,32},{64,96},{1,33},{65,97},{2,34},{66,98},{3,35},{67,99},{4,36}... | collective-permute-start | bytes 98312 | tf_op jit(solution)/shard_map/ppermute | solution.py:783
  76.2 8.6 %collective-permute-start.21 = (bf16[256,512]{1,0:T(8,128)(2,1)S(1)}, bf16[256,512]{1,0:T(8,128)(2,1)S(1)}, u32[]{:S(2)}, u32[]{:S(2)}) collective-permute-start(bf16[256,512]{1,0:T(8,128)(2,1)S(1)} %get-tuple-element.112), channel_id=1, source_target_pairs={{0,2},{1,3},{2,4},{3,5},{4,6},{5,7},{6,0},{7,1},{8,10},{9,11},{10,... | collective-permute-start | bytes 786440 | tf_op jit(solution)/shard_map/ppermute | solution.py:38
  77.8 7.0 %collective-permute-start.22 = (bf16[256,512]{1,0:T(8,128)(2,1)S(1)}, bf16[256,512]{1,0:T(8,128)(2,1)S(1)}, u32[]{:S(2)}, u32[]{:S(2)}) collective-permute-start(bf16[256,512]{1,0:T(8,128)(2,1)S(1)} %get-tuple-element.113), channel_id=1, source_target_pairs={{0,6},{1,7},{2,0},{3,1},{4,2},{5,3},{6,4},{7,5},{8,14},{9,15},{10,... | collective-permute-start | bytes 786440 | tf_op jit(solution)/shard_map/ppermute | solution.py:38
  79.5 7.9 %collective-permute-start.23 = (bf16[256,512]{1,0:T(8,128)(2,1)S(1)}, bf16[256,512]{1,0:T(8,128)(2,1)S(1)}, u32[]{:S(2)}, u32[]{:S(2)}) collective-permute-start(bf16[256,512]{1,0:T(8,128)(2,1)S(1)} %get-tuple-element.114), channel_id=1, source_target_pairs={{0,8},{1,9},{2,10},{3,11},{4,12},{5,13},{6,14},{7,15},{8,0},{9,1},... | collective-permute-start | bytes 786440 | tf_op jit(solution)/shard_map/ppermute | solution.py:38
  (8 other events, 52.6 us)

commit v5 on v3

--- a/solution.py
+++ b/solution.py
@@ -64,6 +64,7 @@
 ROWS_AT_ONCE = 4
 LOG2_E = 1.4426950408889634
 NT = (((1,), (1,)), ((), ()))
+TN = (((0,), (0,)), ((), ()))
 LONG = 6 * 10**9
 
 CORE, IS_PREFILL, IS_KEY, NEAR_ROWS, FAR_ROWS, PLACE, CELLS = 0, 1, 2, 3, 11, 19, 27
@@ -136,40 +137,63 @@
             for step in range(chunks):
                 fetches(prompt, step)[kind].start()
 
+    position = lax.broadcasted_iota(jnp.int32, (SPAN, GQ * CH), 0) + scalar_ref[CORE] * SPAN
+    folded = (PREFILL_CHUNK // 8, 8, GQ * CH)
+
     def one_prompt(prompt, carry):
         tokens = pl.ds(pl.multiple_of(prompt * CH, CH), CH)
         queries = stacked_heads(own_ref[tokens, :], other_ref[tokens, :])
 
         def score_step(step, peak):
             fetches(prompt, step)[0].wait()
-            part = keys[pl.ds(prompt * RP + step * rows, rows)].reshape(PREFILL_CHUNK, HD)
-            scores = lax.dot_general(queries, part, NT, preferred_element_type=jnp.float32)
-            scores = scores + length_bias(scalar_ref, length_ref, prompt * RP + step * rows, rows)
+            first = prompt * RP + step * rows
+            part = keys[pl.ds(first, rows)].reshape(PREFILL_CHUNK, HD)
+            scores = lax.dot_general(part, queries, NT, preferred_element_type=jnp.float32)
+            scores = jnp.concatenate(
+                [
+                    jnp.where(
+                        position < length_ref[first + row],
+                        scores[row * SPAN : (row + 1) * SPAN],
+                        NEG_FILL,
+                    )
+                    for row in range(rows)
+                ],
+                axis=0,
+            )
             score_ref[step] = scores
-            for lanes in range(PREFILL_CHUNK // HD):
-                peak = jnp.maximum(peak, scores[:, lanes * HD : (lanes + 1) * HD])
-            return peak
-
-        peak = lax.fori_loop(
-            0, chunks, score_step, jnp.full((GQ * CH, HD), NEG_FILL, jnp.float32)
-        )
-        largest = jnp.max(peak, axis=1, keepdims=True)
-        level = jnp.broadcast_to(largest, (GQ * CH, HD))
-
-        def mix_step(step, mixed):
+            return jnp.maximum(peak, jnp.max(scores.reshape(folded), axis=0))
+
+        peak = lax.fori_loop(0, chunks, score_step, jnp.full((8, GQ * CH), NEG_FILL, jnp.float32))
+        largest = jnp.max(peak, axis=0, keepdims=True)
+
+        def mix_step(step, sums):
+            mixed, total = sums
             fetches(prompt, step)[1].wait()
-            weights = jnp.concatenate(
-                [
-                    weights_of(score_ref[step, :, lanes * HD : (lanes + 1) * HD], level)
-                    for lanes in range(PREFILL_CHUNK // HD)
-                ],
-                axis=1,
+            weights = jnp.exp2((score_ref[step] - largest) * (HD**-0.5 * LOG2_E))
+            total = total + jnp.sum(weights.reshape(folded), axis=0)
+            part = values[pl.ds(prompt * RP + step * rows, rows)].reshape(PREFILL_CHUNK, HD)
+            mixed = mixed + lax.dot_general(
+                part, weights.astype(jnp.bfloat16), TN, preferred_element_type=jnp.float32
             )
-            part = values[pl.ds(prompt * RP + step * rows, rows)].reshape(PREFILL_CHUNK, HD)
-            return mixed + jnp.dot(weights, with_ones(part), preferred_element_type=jnp.float32)
-
-        mixed = lax.fori_loop(0, chunks, mix_step, jnp.zeros((GQ * CH, 2 * HD), jnp.float32))
-        write_heads(mixed_ref, level_ref, tokens, mixed, largest)
+            return mixed, total
+
+        mixed, total = lax.fori_loop(
+            0,
+            chunks,
+            mix_step,
+            (jnp.zeros((HD, GQ * CH), jnp.float32), jnp.zeros((8, GQ * CH), jnp.float32)),
+        )
+        total = jnp.sum(total, axis=0, keepdims=True)
+        normal = mixed / total
+        level = jnp.broadcast_to(largest * HD**-0.5 + jnp.log(total), (8, GQ * CH))
+        lane = lax.broadcasted_iota(jnp.int32, (CH, GQ), 1)
+        levels = jnp.zeros((CH, GQ), jnp.float32)
+        for j in range(GQ):
+            head = slice(j * HD, (j + 1) * HD)
+            mixed_ref[tokens, head] = normal[:, j * CH : (j + 1) * CH].T.astype(jnp.bfloat16)
+            column = level[:, j * CH : (j + 1) * CH].T
+            levels = jnp.where(lane == j, column[:, :1], levels)
+        level_ref[tokens, :] = levels
         return carry
 
     lax.fori_loop(0, NPR, one_prompt, 0)
@@ -219,32 +243,27 @@
     allowed = together & (column <= row)
     lane = lax.broadcasted_iota(jnp.int32, (TOK, GQ), 1)
 
-    def attend(key_ref, value_ref):
-        values = with_ones(value_ref[...])
-        levels = jnp.zeros((TOK, GQ), jnp.float32)
-        for j in range(GQ):
-            source = own_ref if j < GQ // 2 else other_ref
-            part = slice(j % (GQ // 2) * HD, (j % (GQ // 2) + 1) * HD)
-            scores = lax.dot_general(
-                source[:, part], key_ref[...], NT, preferred_element_type=jnp.float32
-            )
-            scores = jnp.where(allowed, scores, NEG_FILL)
-            largest = jnp.max(scores, axis=1, keepdims=True)
-            mixed = jnp.dot(
-                weights_of(scores, largest), values, preferred_element_type=jnp.float32
-            )
-            total = mixed[:, HD : HD + 1]
-            mixed_ref[:, j * HD : (j + 1) * HD] = (mixed[:, :HD] / total).astype(mixed_ref.dtype)
-            levels = jnp.where(lane == j, largest * HD**-0.5 + jnp.log(total), levels)
-        level_ref[...] = levels
-
-    @pl.when(scalar_ref[CORE] == 0)
-    def _():
-        attend(held_ref, swapped_ref)
-
-    @pl.when(scalar_ref[CORE] != 0)
-    def _():
-        attend(swapped_ref, held_ref)
+    held = held_ref[...].astype(jnp.float32)
+    swapped = swapped_ref[...].astype(jnp.float32)
+    first = scalar_ref[CORE] == 0
+    keys = jnp.where(first, held, swapped).astype(jnp.bfloat16)
+    values = with_ones(jnp.where(first, swapped, held).astype(jnp.bfloat16))
+    levels = jnp.zeros((TOK, GQ), jnp.float32)
+    for j in range(GQ):
+        source = own_ref if j < GQ // 2 else other_ref
+        part = slice(j % (GQ // 2) * HD, (j % (GQ // 2) + 1) * HD)
+        scores = lax.dot_general(
+            source[:, part], keys, NT, preferred_element_type=jnp.float32
+        )
+        scores = jnp.where(allowed, scores, NEG_FILL)
+        largest = jnp.max(scores, axis=1, keepdims=True)
+        mixed = jnp.dot(
+            weights_of(scores, largest), values, preferred_element_type=jnp.float32
+        )
+        total = mixed[:, HD : HD + 1]
+        mixed_ref[:, j * HD : (j + 1) * HD] = (mixed[:, :HD] / total).astype(mixed_ref.dtype)
+        levels = jnp.where(lane == j, largest * HD**-0.5 + jnp.log(total), levels)
+    level_ref[...] = levels
 
 
 def merged(parts, levels):
@@ -506,7 +525,7 @@
         scratch_shapes=[
             pltpu.VMEM((R, SPAN, HD), jnp.bfloat16),
             pltpu.VMEM((R, SPAN, HD), jnp.bfloat16),
-            pltpu.VMEM((chunks, GQ * CH, PREFILL_CHUNK), jnp.float32),
+            pltpu.VMEM((chunks, PREFILL_CHUNK, GQ * CH), jnp.float32),
             pltpu.SemaphoreType.DMA((2, NPR * chunks)),
         ],
         compiler_params=pltpu.CompilerParams(vmem_limit_bytes=44 * 2**20),

time: 86.3 us -> 87.7 us (1.016)
  Pallas kernels: 28.2 us -> 29.6 us
    pallas_call x1, Pallas kernels: 12.9 us -> 14.3 us  [prefill_part(): pl.pallas_call(prefill_kernel, in_specs=[small, small, whole, whole, ther...]
  transfers between devices with their start and end apart: 25 -> 25, of which waited for: 12 -> 12; matrix products, arithmetic and copies ran while one was open for 6% -> 6% of each run, Pallas kernels for 26% -> 28%
where the time goes in v5:
time: 87.7 us; the launch traced here: 87.4 us
  starting transfers between devices  35.4 us (40%)
  Pallas kernels  29.6 us (34%)
  waiting for transfers between devices  15.4 us (18%)
  other arithmetic  4.22 us (5%)
  local copies, waits for them, and re-layouts  1.85 us (2%)
  between operations  0.94 us (1%)
    ppermute x21, starting transfers between devices, moved(): return lax.ppermute(shard, 'tp', pairs)  30.9 us
    pallas_call x1, Pallas kernels, prefill_part(): pl.pallas_call(prefill_kernel, in_specs=[small, small, whole, whole, ther...  14.3 us
    ppermute x21, waiting for transfers between devices, moved(): return lax.ppermute(shard, 'tp', pairs)  13.9 us
    pallas_call x11, Pallas kernels, called(): pl.pallas_call(kernel, in_specs=specs, out_specs=tuple((whole for _ in sh...  13.1 us
    pallas_call x1, Pallas kernels, cut_columns(): pl.pallas_call(cut_kernel, in_specs=[pl.BlockSpec(memory_space=pltpu.SMEM...  2.22 us
  transfers between devices with their start and end apart: 25, of which 12 were waited for; matrix products, arithmetic and copies ran while one was open for 6% of the time, Pallas kernels for 28%

profile of v5, /device:TPU:0, one launch (start us, length us, event | category | flops | bytes accessed | tf_op | source)
XLA Modules:
  0.0 87.4 jit_solution(16254412984650981938)
XLA Ops:
  0.6 3.2 %collective-permute-start = (bf16[256,512]{1,0:T(8,128)(2,1)}, bf16[256,512]{1,0:T(8,128)(2,1)S(1)}, u32[]{:S(2)}, u32[]{:S(2)}) collective-permute-start(bf16[256,512]{1,0:T(8,128)(2,1)} %bitcast.49), channel_id=1, source_target_pairs={{0,8},{1,9},{2,10},{3,11},{4,12},{5,13},{6,14},{7,15},{8,0},{9,1},... | collective-permute-start | bytes 786440 | tf_op jit(solution)/shard_map/ppermute | solution.py:38
  3.8 1.6 %collective-permute-start.1 = (bf16[256,512]{1,0:T(8,128)(2,1)}, bf16[256,512]{1,0:T(8,128)(2,1)S(1)}, u32[]{:S(2)}, u32[]{:S(2)}) collective-permute-start(bf16[256,512]{1,0:T(8,128)(2,1)} %bitcast.50), channel_id=1, source_target_pairs={{0,2},{1,3},{2,4},{3,5},{4,6},{5,7},{6,0},{7,1},{8,10},{9,11},{10,... | collective-permute-start | bytes 786440 | tf_op jit(solution)/shard_map/ppermute | solution.py:38
  5.4 1.7 %collective-permute-start.2 = (bf16[256,512]{1,0:T(8,128)(2,1)}, bf16[256,512]{1,0:T(8,128)(2,1)S(1)}, u32[]{:S(2)}, u32[]{:S(2)}) collective-permute-start(bf16[256,512]{1,0:T(8,128)(2,1)} %bitcast.51), channel_id=1, source_target_pairs={{0,6},{1,7},{2,0},{3,1},{4,2},{5,3},{6,4},{7,5},{8,14},{9,15},{10,... | collective-permute-start | bytes 786440 | tf_op jit(solution)/shard_map/ppermute | solution.py:38
  10.8 2.3 %collective-permute-done.1.last_ref = bf16[256,512]{1,0:T(8,128)(2,1)S(1)} collective-permute-done((bf16[256,512]{1,0:T(8,128)(2,1)}, bf16[256,512]{1,0:T(8,128)(2,1)S(1)}, u32[]{:S(2)}, u32[]{:S(2)}) %collective-permute-start.1) | collective-permute-done | bytes 262176 | tf_op jit(solution)/shard_map/ppermute | solution.py:38
  14.9 1.6 %collective-permute-start.4 = (bf16[384,512]{1,0:T(8,128)(2,1)S(1)}, bf16[384,512]{1,0:T(8,128)(2,1)S(1)}, u32[]{:S(2)}, u32[]{:S(2)}) collective-permute-start(bf16[384,512]{1,0:T(8,128)(2,1)S(1)} %get-tuple-element.87), channel_id=1, source_target_pairs={{0,2},{1,3},{2,4},{3,5},{4,6},{5,7},{6,0},{7,1},{8,10},{9,11},{10,... | collective-permute-start | bytes 1179656 | tf_op jit(solution)/shard_map/ppermute | solution.py:38
  16.5 1.7 %collective-permute-start.5 = (bf16[384,512]{1,0:T(8,128)(2,1)S(1)}, bf16[384,512]{1,0:T(8,128)(2,1)S(1)}, u32[]{:S(2)}, u32[]{:S(2)}) collective-permute-start(bf16[384,512]{1,0:T(8,128)(2,1)S(1)} %get-tuple-element.88), channel_id=1, source_target_pairs={{0,6},{1,7},{2,0},{3,1},{4,2},{5,3},{6,4},{7,5},{8,14},{9,15},{10,... | collective-permute-start | bytes 1179656 | tf_op jit(solution)/shard_map/ppermute | solution.py:38
  18.2 1.7 %collective-permute-start.6 = (bf16[128,512]{1,0:T(8,128)(2,1)S(1)}, bf16[128,512]{1,0:T(8,128)(2,1)S(1)}, u32[]{:S(2)}, u32[]{:S(2)}) collective-permute-start(bf16[128,512]{1,0:T(8,128)(2,1)S(1)} %get-tuple-element.89), channel_id=1, source_target_pairs={{0,14},{1,15},{2,8},{3,9},{4,10},{5,11},{6,12},{7,13},{8,6},{9,7},... | collective-permute-start | bytes 393224 | tf_op jit(solution)/shard_map/ppermute | solution.py:38
  19.9 2.7 %collective-permute-start.7 = (bf16[128,512]{1,0:T(8,128)(2,1)S(1)}, bf16[128,512]{1,0:T(8,128)(2,1)S(1)}, u32[]{:S(2)}, u32[]{:S(2)}) collective-permute-start(bf16[128,512]{1,0:T(8,128)(2,1)S(1)} %get-tuple-element.90), channel_id=1, source_target_pairs={{0,10},{1,11},{2,12},{3,13},{4,14},{5,15},{6,8},{7,9},{8,2},{9,3},... | collective-permute-start | bytes 393224 | tf_op jit(solution)/shard_map/ppermute | solution.py:38
  22.6 2.2 %shard_map.95 = bf16[256,4096]{1,0:T(8,128)(2,1)} custom-call(s32[43]{0:T(128)S(1)} %concatenate.12.scalar_ref, bf16[256,8192]{1,0:T(8,128)(2,1)S(1)} %copy-done.1), custom_call_target="tpu_custom_call" | custom-call | tf_op jit(solution)/shard_map/pallas_call | solution.py:588
  24.9 1.8 %shard_map.97 = (f32[256,256]{1,0:T(8,128)S(1)}, f32[256,128]{1,0:T(8,128)S(1)}, f32[8,128]{1,0:T(8,128)S(1)}) custom-call(s32[43]{0:T(128)S(1)} %concatenate.12.scalar_ref, bf16[8192,256]{1,0:T(8,128)(2,1)S(1)} %copy-done, bf16[8192,128]{1,0:T(8,128)(2,1)S(1)} %copy-done.3, bf16[1024,512]{1,0:T(8,128)(2,1)S(1)} %get-tuple-element.83.near_ref, ...), custom_call_target="tpu_custom_call" | custom-call | flops 805306368 | bytes 2097152 | tf_op jit(solution)/shard_map/pallas_call | solution.py:497
  27.0 2.1 %collective-permute-done.7.lower_ref = bf16[128,512]{1,0:T(8,128)(2,1)S(1)} collective-permute-done((bf16[128,512]{1,0:T(8,128)(2,1)S(1)}, bf16[128,512]{1,0:T(8,128)(2,1)S(1)}, u32[]{:S(2)}, u32[]{:S(2)}) %collective-permute-start.7) | collective-permute-done | bytes 131104 | tf_op jit(solution)/shard_map/ppermute | solution.py:38
  35.9 2.9 %collective-permute-done.10.other_ref = bf16[256,256]{1,0:T(8,128)(2,1)S(1)} collective-permute-done((bf16[256,256]{1,0:T(8,128)(2,1)S(1)}, bf16[256,256]{1,0:T(8,128)(2,1)S(1)}, u32[]{:S(2)}, u32[]{:S(2)}) %collective-permute-start.10) | collective-permute-done | bytes 131104 | tf_op jit(solution)/shard_map/ppermute | solution.py:38
  38.9 14.3 %conditional.1 = ((bf16[256,512]{1,0:T(8,128)(2,1)S(1)}, f32[256,4]{1,0:T(8,128)S(1)})) conditional(s32[]{:T(128)} %convert_element_type.8, (bf16[256,256]{1,0:T(8,128)(2,1)S(1)}, bf16[256,256]{1,0:T(8,128)(2,1)S(1)}, s32[43]{0:T(128)S(1)}, s32[64]{0:T(128)S(1)}, bf16[64,256,128]{2,1,0:T(8,128)(2,1)}, ...), branch_computations={%region_1.2_spmd, %region_2.3_spmd} | conditional | flops 524288 | bytes 2629656 | solution.py:716
  38.9 14.3 %branch_1_fun.1 = (bf16[256,512]{1,0:T(8,128)(2,1)S(1)}, f32[256,4]{1,0:T(8,128)S(1)}) custom-call(s32[43]{0:T(128)S(1)} %get-tuple-element.32.scalar_ref, s32[64]{0:T(128)S(1)} %get-tuple-element.33.length_ref, bf16[256,256]{1,0:T(8,128)(2,1)S(1)} %get-tuple-element.34.own_ref, bf16[256,256]{1,0:T(8,128)(2,1)S(1)} %get-tuple-element.35.other_ref, ...), custom_call_target="tpu_custom_call" | custom-call | tf_op jit(solution)/shard_map/cond/branch_1_fun/pallas_call | solution.py:520
  54.6 1.8 %shard_map.101 = (bf16[256,512]{1,0:T(8,128)(2,1)S(1)}, f32[256,4]{1,0:T(8,128)S(1)}) custom-call(s32[43]{0:T(128)S(1)} %concatenate.12.scalar_ref, bf16[256,256]{1,0:T(8,128)(2,1)S(1)} %get-tuple-element.97.own_ref, bf16[256,256]{1,0:T(8,128)(2,1)S(1)} %collective-permute-done.10.other_ref, bf16[256,128]{1,0:T(8,128)(2,1)S(1)} %collective-permute-done.11.held_ref, ...), custom_call_target="tpu_custom_call" | custom-call | flops 6000000000 | bytes 2097152 | tf_op jit(solution)/shard_map/pallas_call | solution.py:497
  56.4 2.6 %shard_map.102 = (bf16[384,512]{1,0:T(8,128)(2,1)S(1)}, bf16[384,512]{1,0:T(8,128)(2,1)S(1)}, bf16[128,512]{1,0:T(8,128)(2,1)S(1)}, bf16[128,512]{1,0:T(8,128)(2,1)S(1)}, bf16[256,512]{1,0:T(8,128)(2,1)S(1)}) custom-call(s32[43]{0:T(128)S(1)} %concatenate.12.scalar_ref, bf16[256,4096]{1,0:T(8,128)(2,1)S(1)} %collective-permute-done.9.swapped_ref, ...), custom_call_target="tpu_custom_call" | custom-call | flops 536870912 | bytes 2097152 | tf_op jit(solution)/shard_map/pallas_call | solution.py:497
  59.0 2.1 %collective-permute-start.16 = (bf16[384,512]{1,0:T(8,128)(2,1)S(1)}, bf16[384,512]{1,0:T(8,128)(2,1)S(1)}, u32[]{:S(2)}, u32[]{:S(2)}) collective-permute-start(bf16[384,512]{1,0:T(8,128)(2,1)S(1)} %get-tuple-element.112), channel_id=1, source_target_pairs={{0,2},{1,3},{2,4},{3,5},{4,6},{5,7},{6,0},{7,1},{8,10},{9,11},{10,... | collective-permute-start | bytes 1179656 | tf_op jit(solution)/shard_map/ppermute | solution.py:38
  64.2 3.0 %collective-permute-start.18 = (bf16[128,512]{1,0:T(8,128)(2,1)S(1)}, bf16[128,512]{1,0:T(8,128)(2,1)S(1)}, u32[]{:S(2)}, u32[]{:S(2)}) collective-permute-start(bf16[128,512]{1,0:T(8,128)(2,1)S(1)} %get-tuple-element.114), channel_id=1, source_target_pairs={{0,10},{1,11},{2,12},{3,13},{4,14},{5,15},{6,8},{7,9},{8,2},{9,3},... | collective-permute-start | bytes 393224 | tf_op jit(solution)/shard_map/ppermute | solution.py:38
  67.2 2.7 %collective-permute-start.19 = (bf16[128,512]{1,0:T(8,128)(2,1)S(1)}, bf16[128,512]{1,0:T(8,128)(2,1)S(1)}, u32[]{:S(2)}, u32[]{:S(2)}) collective-permute-start(bf16[128,512]{1,0:T(8,128)(2,1)S(1)} %get-tuple-element.115), channel_id=1, source_target_pairs={{0,14},{1,15},{2,8},{3,9},{4,10},{5,11},{6,12},{7,13},{8,6},{9,7},... | collective-permute-start | bytes 393224 | tf_op jit(solution)/shard_map/ppermute | solution.py:38
  71.3 1.9 %shard_map.103 = (bf16[256,512]{1,0:T(8,128)(2,1)S(1)}, bf16[256,512]{1,0:T(8,128)(2,1)S(1)}, bf16[256,512]{1,0:T(8,128)(2,1)S(1)}, bf16[256,512]{1,0:T(8,128)(2,1)S(1)}) custom-call(s32[43]{0:T(128)S(1)} %concatenate.12.scalar_ref, bf16[256,4096]{1,0:T(8,128)(2,1)S(1)} %collective-permute-done.9.swapped_ref, bf16[256,8192]{1,0:T(8,128)(2,1)S(1)} %copy-done.2, ...), custom_call_target="tpu_custom_call" | custom-call | flops 536870912 | bytes 2097152 | tf_op jit(solution)/shard_map/pallas_call | solution.py:497
  76.0 2.5 %collective-permute-start.21 = (bf16[256,512]{1,0:T(8,128)(2,1)S(1)}, bf16[256,512]{1,0:T(8,128)(2,1)S(1)}, u32[]{:S(2)}, u32[]{:S(2)}) collective-permute-start(bf16[256,512]{1,0:T(8,128)(2,1)S(1)} %get-tuple-element.117), channel_id=1, source_target_pairs={{0,6},{1,7},{2,0},{3,1},{4,2},{5,3},{6,4},{7,5},{8,14},{9,15},{10,... | collective-permute-start | bytes 786440 | tf_op jit(solution)/shard_map/ppermute | solution.py:38
  78.5 2.7 %collective-permute-start.22 = (bf16[256,512]{1,0:T(8,128)(2,1)S(1)}, bf16[256,512]{1,0:T(8,128)(2,1)S(1)}, u32[]{:S(2)}, u32[]{:S(2)}) collective-permute-start(bf16[256,512]{1,0:T(8,128)(2,1)S(1)} %get-tuple-element.118), channel_id=1, source_target_pairs={{0,8},{1,9},{2,10},{3,11},{4,12},{5,13},{6,14},{7,15},{8,0},{9,1},... | collective-permute-start | bytes 786440 | tf_op jit(solution)/shard_map/ppermute | solution.py:38
  82.5 1.4 %collective-permute-done.24 = bf16[1,4,8,256]{3,2,1,0:T(8,128)(2,1)S(1)} collective-permute-done((bf16[1,4,8,256]{3,2,1,0:T(8,128)(2,1)S(1)}, bf16[1,4,8,256]{3,2,1,0:T(8,128)(2,1)S(1)}, u32[]{:S(2)}, u32[]{:S(2)}) %collective-permute-start.24) | collective-permute-done | bytes 16416 | tf_op jit(solution)/shard_map/ppermute | solution.py:801
  84.5 2.0 %collective-permute-done.22.from_partner = bf16[256,512]{1,0:T(8,128)(2,1)S(1)} collective-permute-done((bf16[256,512]{1,0:T(8,128)(2,1)S(1)}, bf16[256,512]{1,0:T(8,128)(2,1)S(1)}, u32[]{:S(2)}, u32[]{:S(2)}) %collective-permute-start.22) | collective-permute-done | bytes 262176 | tf_op jit(solution)/shard_map/ppermute | solution.py:38
  (71 shorter events, 24.0 us)
Async XLA Ops:
  0.6 10.2 %collective-permute-start = (bf16[256,512]{1,0:T(8,128)(2,1)}, bf16[256,512]{1,0:T(8,128)(2,1)S(1)}, u32[]{:S(2)}, u32[]{:S(2)}) collective-permute-start(bf16[256,512]{1,0:T(8,128)(2,1)} %bitcast.49), channel_id=1, source_target_pairs={{0,8},{1,9},{2,10},{3,11},{4,12},{5,13},{6,14},{7,15},{8,0},{9,1},... | collective-permute-start | bytes 786440 | tf_op jit(solution)/shard_map/ppermute | solution.py:38
  3.8 9.3 %collective-permute-start.1 = (bf16[256,512]{1,0:T(8,128)(2,1)}, bf16[256,512]{1,0:T(8,128)(2,1)S(1)}, u32[]{:S(2)}, u32[]{:S(2)}) collective-permute-start(bf16[256,512]{1,0:T(8,128)(2,1)} %bitcast.50), channel_id=1, source_target_pairs={{0,2},{1,3},{2,4},{3,5},{4,6},{5,7},{6,0},{7,1},{8,10},{9,11},{10,... | collective-permute-start | bytes 786440 | tf_op jit(solution)/shard_map/ppermute | solution.py:38
  5.4 7.7 %collective-permute-start.2 = (bf16[256,512]{1,0:T(8,128)(2,1)}, bf16[256,512]{1,0:T(8,128)(2,1)S(1)}, u32[]{:S(2)}, u32[]{:S(2)}) collective-permute-start(bf16[256,512]{1,0:T(8,128)(2,1)} %bitcast.51), channel_id=1, source_target_pairs={{0,6},{1,7},{2,0},{3,1},{4,2},{5,3},{6,4},{7,5},{8,14},{9,15},{10,... | collective-permute-start | bytes 786440 | tf_op jit(solution)/shard_map/ppermute | solution.py:38
  14.8 10.1 %collective-permute-start.3 = (bf16[1024,512]{1,0:T(8,128)(2,1)S(1)}, bf16[1024,512]{1,0:T(8,128)(2,1)S(1)}, u32[]{:S(2)}, u32[]{:S(2)}) collective-permute-start(bf16[1024,512]{1,0:T(8,128)(2,1)S(1)} %get-tuple-element.83.near_ref), channel_id=1, source_target_pairs={{0,1},{1,0},{2,3},{3,2},{4,5},{5,4},{6,7},{7,6},{8,9},{9,8},{10,11... | collective-permute-start | bytes 3145736 | tf_op jit(solution)/shard_map/ppermute | solution.py:38
  14.9 15.6 %collective-permute-start.4 = (bf16[384,512]{1,0:T(8,128)(2,1)S(1)}, bf16[384,512]{1,0:T(8,128)(2,1)S(1)}, u32[]{:S(2)}, u32[]{:S(2)}) collective-permute-start(bf16[384,512]{1,0:T(8,128)(2,1)S(1)} %get-tuple-element.87), channel_id=1, source_target_pairs={{0,2},{1,3},{2,4},{3,5},{4,6},{5,7},{6,0},{7,1},{8,10},{9,11},{10,... | collective-permute-start | bytes 1179656 | tf_op jit(solution)/shard_map/ppermute | solution.py:38
  16.5 14.0 %collective-permute-start.5 = (bf16[384,512]{1,0:T(8,128)(2,1)S(1)}, bf16[384,512]{1,0:T(8,128)(2,1)S(1)}, u32[]{:S(2)}, u32[]{:S(2)}) collective-permute-start(bf16[384,512]{1,0:T(8,128)(2,1)S(1)} %get-tuple-element.88), channel_id=1, source_target_pairs={{0,6},{1,7},{2,0},{3,1},{4,2},{5,3},{6,4},{7,5},{8,14},{9,15},{10,... | collective-permute-start | bytes 1179656 | tf_op jit(solution)/shard_map/ppermute | solution.py:38
  18.2 8.8 %collective-permute-start.6 = (bf16[128,512]{1,0:T(8,128)(2,1)S(1)}, bf16[128,512]{1,0:T(8,128)(2,1)S(1)}, u32[]{:S(2)}, u32[]{:S(2)}) collective-permute-start(bf16[128,512]{1,0:T(8,128)(2,1)S(1)} %get-tuple-element.89), channel_id=1, source_target_pairs={{0,14},{1,15},{2,8},{3,9},{4,10},{5,11},{6,12},{7,13},{8,6},{9,7},... | collective-permute-start | bytes 393224 | tf_op jit(solution)/shard_map/ppermute | solution.py:38
  19.9 9.1 %collective-permute-start.7 = (bf16[128,512]{1,0:T(8,128)(2,1)S(1)}, bf16[128,512]{1,0:T(8,128)(2,1)S(1)}, u32[]{:S(2)}, u32[]{:S(2)}) collective-permute-start(bf16[128,512]{1,0:T(8,128)(2,1)S(1)} %get-tuple-element.90), channel_id=1, source_target_pairs={{0,10},{1,11},{2,12},{3,13},{4,14},{5,15},{6,8},{7,9},{8,2},{9,3},... | collective-permute-start | bytes 393224 | tf_op jit(solution)/shard_map/ppermute | solution.py:38
  30.6 2.7 %collective-permute-start.8 = (bf16[1024,512]{1,0:T(8,128)(2,1)S(1)}, bf16[1024,512]{1,0:T(8,128)(2,1)S(1)}, u32[]{:S(2)}, u32[]{:S(2)}) collective-permute-start(bf16[1024,512]{1,0:T(8,128)(2,1)S(1)} %shard_map.98.far_ref), channel_id=1, source_target_pairs={{0,1},{1,0},{2,3},{3,2},{4,5},{5,4},{6,7},{7,6},{8,9},{9,8},{10,11... | collective-permute-start | bytes 3145736 | tf_op jit(solution)/shard_map/ppermute | solution.py:38
  34.7 21.7 %collective-permute-start.9 = (bf16[256,4096]{1,0:T(8,128)(2,1)}, bf16[256,4096]{1,0:T(8,128)(2,1)S(1)}, u32[]{:S(2)}, u32[]{:S(2)}) collective-permute-start(bf16[256,4096]{1,0:T(8,128)(2,1)} %shard_map.95), channel_id=1, source_target_pairs={{0,1},{1,0},{2,3},{3,2},{4,5},{5,4},{6,7},{7,6},{8,9},{9,8},{10,11... | collective-permute-start | bytes 6291464 | tf_op jit(solution)/shard_map/ppermute | solution.py:38
  34.9 4.0 %collective-permute-start.10 = (bf16[256,256]{1,0:T(8,128)(2,1)S(1)}, bf16[256,256]{1,0:T(8,128)(2,1)S(1)}, u32[]{:S(2)}, u32[]{:S(2)}) collective-permute-start(bf16[256,256]{1,0:T(8,128)(2,1)S(1)} %get-tuple-element.97.own_ref), channel_id=1, source_target_pairs={{0,1},{1,0},{2,3},{3,2},{4,5},{5,4},{6,7},{7,6},{8,9},{9,8},{10,11... | collective-permute-start | bytes 393224 | tf_op jit(solution)/shard_map/ppermute | solution.py:38
  35.2 17.9 %collective-permute-start.11 = (bf16[256,128]{1,0:T(8,128)(2,1)S(1)}, bf16[256,128]{1,0:T(8,128)(2,1)S(1)}, u32[]{:S(2)}, u32[]{:S(2)}) collective-permute-start(bf16[256,128]{1,0:T(8,128)(2,1)S(1)} %get-tuple-element.100), channel_id=1, source_target_pairs={{0,0},{1,2},{2,4},{3,6},{4,8},{5,10},{6,12},{7,14},{8,1},{9,3},{10... | collective-permute-start | bytes 196616 | tf_op jit(solution)/shard_map/ppermute | solution.py:712
  53.7 2.7 %collective-permute-start.12 = (bf16[256,512]{1,0:T(8,128)(2,1)S(1)}, bf16[256,512]{1,0:T(8,128)(2,1)S(1)}, u32[]{:S(2)}, u32[]{:S(2)}) collective-permute-start(bf16[256,512]{1,0:T(8,128)(2,1)S(1)} %get-tuple-element.101.own_ref), channel_id=1, source_target_pairs={{0,1},{1,0},{2,3},{3,2},{4,5},{5,4},{6,7},{7,6},{8,9},{9,8},{10,11... | collective-permute-start | bytes 786440 | tf_op jit(solution)/shard_map/ppermute | solution.py:38
  53.8 2.5 %collective-permute-start.13 = (f32[256,4]{1,0:T(8,128)S(1)}, f32[256,4]{1,0:T(8,128)S(1)}, u32[]{:S(2)}, u32[]{:S(2)}) collective-permute-start(f32[256,4]{1,0:T(8,128)S(1)} %get-tuple-element.102.own_level), channel_id=1, source_target_pairs={{0,1},{1,0},{2,3},{3,2},{4,5},{5,4},{6,7},{7,6},{8,9},{9,8},{10,11... | collective-permute-start | bytes 12296 | tf_op jit(solution)/shard_map/ppermute | solution.py:38
  59.0 16.0 %collective-permute-start.16 = (bf16[384,512]{1,0:T(8,128)(2,1)S(1)}, bf16[384,512]{1,0:T(8,128)(2,1)S(1)}, u32[]{:S(2)}, u32[]{:S(2)}) collective-permute-start(bf16[384,512]{1,0:T(8,128)(2,1)S(1)} %get-tuple-element.112), channel_id=1, source_target_pairs={{0,2},{1,3},{2,4},{3,5},{4,6},{5,7},{6,0},{7,1},{8,10},{9,11},{10,... | collective-permute-start | bytes 1179656 | tf_op jit(solution)/shard_map/ppermute | solution.py:38
  61.1 13.9 %collective-permute-start.17 = (bf16[384,512]{1,0:T(8,128)(2,1)S(1)}, bf16[384,512]{1,0:T(8,128)(2,1)S(1)}, u32[]{:S(2)}, u32[]{:S(2)}) collective-permute-start(bf16[384,512]{1,0:T(8,128)(2,1)S(1)} %get-tuple-element.113), channel_id=1, source_target_pairs={{0,6},{1,7},{2,0},{3,1},{4,2},{5,3},{6,4},{7,5},{8,14},{9,15},{10,... | collective-permute-start | bytes 1179656 | tf_op jit(solution)/shard_map/ppermute | solution.py:38
  62.9 7.0 %collective-permute-start.15 = (bf16[4,4,8,256]{3,2,1,0:T(8,128)(2,1)S(1)}, bf16[4,4,8,256]{3,2,1,0:T(8,128)(2,1)S(1)}, u32[]{:S(2)}, u32[]{:S(2)}) collective-permute-start(bf16[4,4,8,256]{3,2,1,0:T(8,128)(2,1)S(1)} %bitcast.64), channel_id=1, source_target_pairs={{0,64},{1,65},{2,66},{3,67},{4,68},{5,69},{6,70},{7,71},{8,72},{9,... | collective-permute-start | bytes 196616 | tf_op jit(solution)/shard_map/ppermute | solution.py:780
  64.2 10.1 %collective-permute-start.18 = (bf16[128,512]{1,0:T(8,128)(2,1)S(1)}, bf16[128,512]{1,0:T(8,128)(2,1)S(1)}, u32[]{:S(2)}, u32[]{:S(2)}) collective-permute-start(bf16[128,512]{1,0:T(8,128)(2,1)S(1)} %get-tuple-element.114), channel_id=1, source_target_pairs={{0,10},{1,11},{2,12},{3,13},{4,14},{5,15},{6,8},{7,9},{8,2},{9,3},... | collective-permute-start | bytes 393224 | tf_op jit(solution)/shard_map/ppermute | solution.py:38
  67.2 7.8 %collective-permute-start.19 = (bf16[128,512]{1,0:T(8,128)(2,1)S(1)}, bf16[128,512]{1,0:T(8,128)(2,1)S(1)}, u32[]{:S(2)}, u32[]{:S(2)}) collective-permute-start(bf16[128,512]{1,0:T(8,128)(2,1)S(1)} %get-tuple-element.115), channel_id=1, source_target_pairs={{0,14},{1,15},{2,8},{3,9},{4,10},{5,11},{6,12},{7,13},{8,6},{9,7},... | collective-permute-start | bytes 393224 | tf_op jit(solution)/shard_map/ppermute | solution.py:38
  70.0 11.2 %collective-permute-start.23 = (bf16[2,4,8,256]{3,2,1,0:T(8,128)(2,1)S(1)}, bf16[2,4,8,256]{3,2,1,0:T(8,128)(2,1)S(1)}, u32[]{:S(2)}, u32[]{:S(2)}) collective-permute-start(bf16[2,4,8,256]{3,2,1,0:T(8,128)(2,1)S(1)} %slice.42), channel_id=1, source_target_pairs={{0,32},{64,96},{1,33},{65,97},{2,34},{66,98},{3,35},{67,99},{4,36}... | collective-permute-start | bytes 98312 | tf_op jit(solution)/shard_map/ppermute | solution.py:799
  75.2 9.4 %collective-permute-start.20 = (bf16[256,512]{1,0:T(8,128)(2,1)S(1)}, bf16[256,512]{1,0:T(8,128)(2,1)S(1)}, u32[]{:S(2)}, u32[]{:S(2)}) collective-permute-start(bf16[256,512]{1,0:T(8,128)(2,1)S(1)} %get-tuple-element.116), channel_id=1, source_target_pairs={{0,2},{1,3},{2,4},{3,5},{4,6},{5,7},{6,0},{7,1},{8,10},{9,11},{10,... | collective-permute-start | bytes 786440 | tf_op jit(solution)/shard_map/ppermute | solution.py:38
  76.0 8.5 %collective-permute-start.21 = (bf16[256,512]{1,0:T(8,128)(2,1)S(1)}, bf16[256,512]{1,0:T(8,128)(2,1)S(1)}, u32[]{:S(2)}, u32[]{:S(2)}) collective-permute-start(bf16[256,512]{1,0:T(8,128)(2,1)S(1)} %get-tuple-element.117), channel_id=1, source_target_pairs={{0,6},{1,7},{2,0},{3,1},{4,2},{5,3},{6,4},{7,5},{8,14},{9,15},{10,... | collective-permute-start | bytes 786440 | tf_op jit(solution)/shard_map/ppermute | solution.py:38
  78.5 8.1 %collective-permute-start.22 = (bf16[256,512]{1,0:T(8,128)(2,1)S(1)}, bf16[256,512]{1,0:T(8,128)(2,1)S(1)}, u32[]{:S(2)}, u32[]{:S(2)}) collective-permute-start(bf16[256,512]{1,0:T(8,128)(2,1)S(1)} %get-tuple-element.118), channel_id=1, source_target_pairs={{0,8},{1,9},{2,10},{3,11},{4,12},{5,13},{6,14},{7,15},{8,0},{9,1},... | collective-permute-start | bytes 786440 | tf_op jit(solution)/shard_map/ppermute | solution.py:38
  81.2 2.7 %collective-permute-start.24 = (bf16[1,4,8,256]{3,2,1,0:T(8,128)(2,1)S(1)}, bf16[1,4,8,256]{3,2,1,0:T(8,128)(2,1)S(1)}, u32[]{:S(2)}, u32[]{:S(2)}) collective-permute-start(bf16[1,4,8,256]{3,2,1,0:T(8,128)(2,1)S(1)} %slice.44), channel_id=1, source_target_pairs={{0,16},{32,48},{64,80},{96,112},{1,17},{33,49},{65,81},{97,113},{2... | collective-permute-start | bytes 49160 | tf_op jit(solution)/shard_map/ppermute | solution.py:801
  (7 other events, 43.7 us)

commit v6 on v3

--- a/solution.py
+++ b/solution.py
@@ -60,7 +60,7 @@
 CHIPS = 8
 SHARD = 512
 HALF = TOK // 2
-PREFILL_CHUNK = 4096
+PREFILL_CHUNK = 8192
 ROWS_AT_ONCE = 4
 LOG2_E = 1.4426950408889634
 NT = (((1,), (1,)), ((), ()))
@@ -219,32 +219,27 @@
     allowed = together & (column <= row)
     lane = lax.broadcasted_iota(jnp.int32, (TOK, GQ), 1)
 
-    def attend(key_ref, value_ref):
-        values = with_ones(value_ref[...])
-        levels = jnp.zeros((TOK, GQ), jnp.float32)
-        for j in range(GQ):
-            source = own_ref if j < GQ // 2 else other_ref
-            part = slice(j % (GQ // 2) * HD, (j % (GQ // 2) + 1) * HD)
-            scores = lax.dot_general(
-                source[:, part], key_ref[...], NT, preferred_element_type=jnp.float32
-            )
-            scores = jnp.where(allowed, scores, NEG_FILL)
-            largest = jnp.max(scores, axis=1, keepdims=True)
-            mixed = jnp.dot(
-                weights_of(scores, largest), values, preferred_element_type=jnp.float32
-            )
-            total = mixed[:, HD : HD + 1]
-            mixed_ref[:, j * HD : (j + 1) * HD] = (mixed[:, :HD] / total).astype(mixed_ref.dtype)
-            levels = jnp.where(lane == j, largest * HD**-0.5 + jnp.log(total), levels)
-        level_ref[...] = levels
-
-    @pl.when(scalar_ref[CORE] == 0)
-    def _():
-        attend(held_ref, swapped_ref)
-
-    @pl.when(scalar_ref[CORE] != 0)
-    def _():
-        attend(swapped_ref, held_ref)
+    held = held_ref[...].astype(jnp.float32)
+    swapped = swapped_ref[...].astype(jnp.float32)
+    first = scalar_ref[CORE] == 0
+    keys = jnp.where(first, held, swapped).astype(jnp.bfloat16)
+    values = with_ones(jnp.where(first, swapped, held).astype(jnp.bfloat16))
+    levels = jnp.zeros((TOK, GQ), jnp.float32)
+    for j in range(GQ):
+        source = own_ref if j < GQ // 2 else other_ref
+        part = slice(j % (GQ // 2) * HD, (j % (GQ // 2) + 1) * HD)
+        scores = lax.dot_general(
+            source[:, part], keys, NT, preferred_element_type=jnp.float32
+        )
+        scores = jnp.where(allowed, scores, NEG_FILL)
+        largest = jnp.max(scores, axis=1, keepdims=True)
+        mixed = jnp.dot(
+            weights_of(scores, largest), values, preferred_element_type=jnp.float32
+        )
+        total = mixed[:, HD : HD + 1]
+        mixed_ref[:, j * HD : (j + 1) * HD] = (mixed[:, :HD] / total).astype(mixed_ref.dtype)
+        levels = jnp.where(lane == j, largest * HD**-0.5 + jnp.log(total), levels)
+    level_ref[...] = levels
 
 
 def merged(parts, levels):
@@ -509,7 +504,7 @@
             pltpu.VMEM((chunks, GQ * CH, PREFILL_CHUNK), jnp.float32),
             pltpu.SemaphoreType.DMA((2, NPR * chunks)),
         ],
-        compiler_params=pltpu.CompilerParams(vmem_limit_bytes=44 * 2**20),
+        compiler_params=pltpu.CompilerParams(vmem_limit_bytes=58 * 2**20),
     )(scalars, lengths, own, other, keys, values)
 
 

time: 86.3 us -> 93.8 us (1.087)
  Pallas kernels: 28.2 us -> 35.7 us
    pallas_call x1, Pallas kernels: 12.9 us -> 20.4 us  [prefill_part(): pl.pallas_call(prefill_kernel, in_specs=[small, small, whole, whole, ther...]
  transfers between devices with their start and end apart: 25 -> 25, of which waited for: 12 -> 12; matrix products, arithmetic and copies ran while one was open for 6% -> 5% of each run, Pallas kernels for 26% -> 32%
where the time goes in v6:
time: 93.8 us; the launch traced here: 93.5 us
  Pallas kernels  35.7 us (38%)
  starting transfers between devices  35.4 us (38%)
  waiting for transfers between devices  15.4 us (16%)
  other arithmetic  4.22 us (4%)
  local copies, waits for them, and re-layouts  1.85 us (2%)
  between operations  0.94 us (1%)
    ppermute x21, starting transfers between devices, moved(): return lax.ppermute(shard, 'tp', pairs)  30.9 us
    pallas_call x1, Pallas kernels, prefill_part(): pl.pallas_call(prefill_kernel, in_specs=[small, small, whole, whole, ther...  20.4 us
    ppermute x21, waiting for transfers between devices, moved(): return lax.ppermute(shard, 'tp', pairs)  13.9 us
    pallas_call x11, Pallas kernels, called(): pl.pallas_call(kernel, in_specs=specs, out_specs=tuple((whole for _ in sh...  13.1 us
    pallas_call x1, Pallas kernels, cut_columns(): pl.pallas_call(cut_kernel, in_specs=[pl.BlockSpec(memory_space=pltpu.SMEM...  2.22 us
  transfers between devices with their start and end apart: 25, of which 12 were waited for; matrix products, arithmetic and copies ran while one was open for 5% of the time, Pallas kernels for 32%

profile of v6, /device:TPU:0, one launch (start us, length us, event | category | flops | bytes accessed | tf_op | source)
XLA Modules:
  0.0 93.5 jit_solution(4346742143889118245)
XLA Ops:
  0.6 3.2 %collective-permute-start = (bf16[256,512]{1,0:T(8,128)(2,1)}, bf16[256,512]{1,0:T(8,128)(2,1)S(1)}, u32[]{:S(2)}, u32[]{:S(2)}) collective-permute-start(bf16[256,512]{1,0:T(8,128)(2,1)} %bitcast.49), channel_id=1, source_target_pairs={{0,8},{1,9},{2,10},{3,11},{4,12},{5,13},{6,14},{7,15},{8,0},{9,1},... | collective-permute-start | bytes 786440 | tf_op jit(solution)/shard_map/ppermute | solution.py:38
  3.8 1.6 %collective-permute-start.1 = (bf16[256,512]{1,0:T(8,128)(2,1)}, bf16[256,512]{1,0:T(8,128)(2,1)S(1)}, u32[]{:S(2)}, u32[]{:S(2)}) collective-permute-start(bf16[256,512]{1,0:T(8,128)(2,1)} %bitcast.50), channel_id=1, source_target_pairs={{0,2},{1,3},{2,4},{3,5},{4,6},{5,7},{6,0},{7,1},{8,10},{9,11},{10,... | collective-permute-start | bytes 786440 | tf_op jit(solution)/shard_map/ppermute | solution.py:38
  5.4 1.7 %collective-permute-start.2 = (bf16[256,512]{1,0:T(8,128)(2,1)}, bf16[256,512]{1,0:T(8,128)(2,1)S(1)}, u32[]{:S(2)}, u32[]{:S(2)}) collective-permute-start(bf16[256,512]{1,0:T(8,128)(2,1)} %bitcast.51), channel_id=1, source_target_pairs={{0,6},{1,7},{2,0},{3,1},{4,2},{5,3},{6,4},{7,5},{8,14},{9,15},{10,... | collective-permute-start | bytes 786440 | tf_op jit(solution)/shard_map/ppermute | solution.py:38
  10.8 2.3 %collective-permute-done.1.last_ref = bf16[256,512]{1,0:T(8,128)(2,1)S(1)} collective-permute-done((bf16[256,512]{1,0:T(8,128)(2,1)}, bf16[256,512]{1,0:T(8,128)(2,1)S(1)}, u32[]{:S(2)}, u32[]{:S(2)}) %collective-permute-start.1) | collective-permute-done | bytes 262176 | tf_op jit(solution)/shard_map/ppermute | solution.py:38
  14.9 1.6 %collective-permute-start.4 = (bf16[384,512]{1,0:T(8,128)(2,1)S(1)}, bf16[384,512]{1,0:T(8,128)(2,1)S(1)}, u32[]{:S(2)}, u32[]{:S(2)}) collective-permute-start(bf16[384,512]{1,0:T(8,128)(2,1)S(1)} %get-tuple-element.87), channel_id=1, source_target_pairs={{0,2},{1,3},{2,4},{3,5},{4,6},{5,7},{6,0},{7,1},{8,10},{9,11},{10,... | collective-permute-start | bytes 1179656 | tf_op jit(solution)/shard_map/ppermute | solution.py:38
  16.5 1.7 %collective-permute-start.5 = (bf16[384,512]{1,0:T(8,128)(2,1)S(1)}, bf16[384,512]{1,0:T(8,128)(2,1)S(1)}, u32[]{:S(2)}, u32[]{:S(2)}) collective-permute-start(bf16[384,512]{1,0:T(8,128)(2,1)S(1)} %get-tuple-element.88), channel_id=1, source_target_pairs={{0,6},{1,7},{2,0},{3,1},{4,2},{5,3},{6,4},{7,5},{8,14},{9,15},{10,... | collective-permute-start | bytes 1179656 | tf_op jit(solution)/shard_map/ppermute | solution.py:38
  18.2 1.7 %collective-permute-start.6 = (bf16[128,512]{1,0:T(8,128)(2,1)S(1)}, bf16[128,512]{1,0:T(8,128)(2,1)S(1)}, u32[]{:S(2)}, u32[]{:S(2)}) collective-permute-start(bf16[128,512]{1,0:T(8,128)(2,1)S(1)} %get-tuple-element.89), channel_id=1, source_target_pairs={{0,14},{1,15},{2,8},{3,9},{4,10},{5,11},{6,12},{7,13},{8,6},{9,7},... | collective-permute-start | bytes 393224 | tf_op jit(solution)/shard_map/ppermute | solution.py:38
  19.9 2.7 %collective-permute-start.7 = (bf16[128,512]{1,0:T(8,128)(2,1)S(1)}, bf16[128,512]{1,0:T(8,128)(2,1)S(1)}, u32[]{:S(2)}, u32[]{:S(2)}) collective-permute-start(bf16[128,512]{1,0:T(8,128)(2,1)S(1)} %get-tuple-element.90), channel_id=1, source_target_pairs={{0,10},{1,11},{2,12},{3,13},{4,14},{5,15},{6,8},{7,9},{8,2},{9,3},... | collective-permute-start | bytes 393224 | tf_op jit(solution)/shard_map/ppermute | solution.py:38
  22.6 2.2 %shard_map.95 = bf16[256,4096]{1,0:T(8,128)(2,1)} custom-call(s32[43]{0:T(128)S(1)} %concatenate.12.scalar_ref, bf16[256,8192]{1,0:T(8,128)(2,1)S(1)} %copy-done.1), custom_call_target="tpu_custom_call" | custom-call | tf_op jit(solution)/shard_map/pallas_call | solution.py:564
  24.9 1.8 %shard_map.97 = (f32[256,256]{1,0:T(8,128)S(1)}, f32[256,128]{1,0:T(8,128)S(1)}, f32[8,128]{1,0:T(8,128)S(1)}) custom-call(s32[43]{0:T(128)S(1)} %concatenate.12.scalar_ref, bf16[8192,256]{1,0:T(8,128)(2,1)S(1)} %copy-done, bf16[8192,128]{1,0:T(8,128)(2,1)S(1)} %copy-done.3, bf16[1024,512]{1,0:T(8,128)(2,1)S(1)} %get-tuple-element.83.near_ref, ...), custom_call_target="tpu_custom_call" | custom-call | flops 805306368 | bytes 2097152 | tf_op jit(solution)/shard_map/pallas_call | solution.py:473
  27.0 2.1 %collective-permute-done.7.lower_ref = bf16[128,512]{1,0:T(8,128)(2,1)S(1)} collective-permute-done((bf16[128,512]{1,0:T(8,128)(2,1)S(1)}, bf16[128,512]{1,0:T(8,128)(2,1)S(1)}, u32[]{:S(2)}, u32[]{:S(2)}) %collective-permute-start.7) | collective-permute-done | bytes 131104 | tf_op jit(solution)/shard_map/ppermute | solution.py:38
  35.9 2.9 %collective-permute-done.10.other_ref = bf16[256,256]{1,0:T(8,128)(2,1)S(1)} collective-permute-done((bf16[256,256]{1,0:T(8,128)(2,1)S(1)}, bf16[256,256]{1,0:T(8,128)(2,1)S(1)}, u32[]{:S(2)}, u32[]{:S(2)}) %collective-permute-start.10) | collective-permute-done | bytes 131104 | tf_op jit(solution)/shard_map/ppermute | solution.py:38
  38.9 20.4 %conditional.1 = ((bf16[256,512]{1,0:T(8,128)(2,1)S(1)}, f32[256,4]{1,0:T(8,128)S(1)})) conditional(s32[]{:T(128)} %convert_element_type.8, (bf16[256,256]{1,0:T(8,128)(2,1)S(1)}, bf16[256,256]{1,0:T(8,128)(2,1)S(1)}, s32[43]{0:T(128)S(1)}, s32[64]{0:T(128)S(1)}, bf16[64,256,128]{2,1,0:T(8,128)(2,1)}, ...), branch_computations={%region_1.2_spmd, %region_2.3_spmd} | conditional | flops 524288 | bytes 2629656 | solution.py:692
  38.9 20.4 %branch_1_fun.1 = (bf16[256,512]{1,0:T(8,128)(2,1)S(1)}, f32[256,4]{1,0:T(8,128)S(1)}) custom-call(s32[43]{0:T(128)S(1)} %get-tuple-element.32.scalar_ref, s32[64]{0:T(128)S(1)} %get-tuple-element.33.length_ref, bf16[256,256]{1,0:T(8,128)(2,1)S(1)} %get-tuple-element.34.own_ref, bf16[256,256]{1,0:T(8,128)(2,1)S(1)} %get-tuple-element.35.other_ref, ...), custom_call_target="tpu_custom_call" | custom-call | tf_op jit(solution)/shard_map/cond/branch_1_fun/pallas_call | solution.py:496
  60.7 1.8 %shard_map.101 = (bf16[256,512]{1,0:T(8,128)(2,1)S(1)}, f32[256,4]{1,0:T(8,128)S(1)}) custom-call(s32[43]{0:T(128)S(1)} %concatenate.12.scalar_ref, bf16[256,256]{1,0:T(8,128)(2,1)S(1)} %get-tuple-element.97.own_ref, bf16[256,256]{1,0:T(8,128)(2,1)S(1)} %collective-permute-done.10.other_ref, bf16[256,128]{1,0:T(8,128)(2,1)S(1)} %collective-permute-done.11.held_ref, ...), custom_call_target="tpu_custom_call" | custom-call | flops 6000000000 | bytes 2097152 | tf_op jit(solution)/shard_map/pallas_call | solution.py:473
  62.5 2.6 %shard_map.102 = (bf16[384,512]{1,0:T(8,128)(2,1)S(1)}, bf16[384,512]{1,0:T(8,128)(2,1)S(1)}, bf16[128,512]{1,0:T(8,128)(2,1)S(1)}, bf16[128,512]{1,0:T(8,128)(2,1)S(1)}, bf16[256,512]{1,0:T(8,128)(2,1)S(1)}) custom-call(s32[43]{0:T(128)S(1)} %concatenate.12.scalar_ref, bf16[256,4096]{1,0:T(8,128)(2,1)S(1)} %collective-permute-done.9.swapped_ref, ...), custom_call_target="tpu_custom_call" | custom-call | flops 536870912 | bytes 2097152 | tf_op jit(solution)/shard_map/pallas_call | solution.py:473
  65.1 2.1 %collective-permute-start.16 = (bf16[384,512]{1,0:T(8,128)(2,1)S(1)}, bf16[384,512]{1,0:T(8,128)(2,1)S(1)}, u32[]{:S(2)}, u32[]{:S(2)}) collective-permute-start(bf16[384,512]{1,0:T(8,128)(2,1)S(1)} %get-tuple-element.112), channel_id=1, source_target_pairs={{0,2},{1,3},{2,4},{3,5},{4,6},{5,7},{6,0},{7,1},{8,10},{9,11},{10,... | collective-permute-start | bytes 1179656 | tf_op jit(solution)/shard_map/ppermute | solution.py:38
  70.3 3.0 %collective-permute-start.18 = (bf16[128,512]{1,0:T(8,128)(2,1)S(1)}, bf16[128,512]{1,0:T(8,128)(2,1)S(1)}, u32[]{:S(2)}, u32[]{:S(2)}) collective-permute-start(bf16[128,512]{1,0:T(8,128)(2,1)S(1)} %get-tuple-element.114), channel_id=1, source_target_pairs={{0,10},{1,11},{2,12},{3,13},{4,14},{5,15},{6,8},{7,9},{8,2},{9,3},... | collective-permute-start | bytes 393224 | tf_op jit(solution)/shard_map/ppermute | solution.py:38
  73.4 2.7 %collective-permute-start.19 = (bf16[128,512]{1,0:T(8,128)(2,1)S(1)}, bf16[128,512]{1,0:T(8,128)(2,1)S(1)}, u32[]{:S(2)}, u32[]{:S(2)}) collective-permute-start(bf16[128,512]{1,0:T(8,128)(2,1)S(1)} %get-tuple-element.115), channel_id=1, source_target_pairs={{0,14},{1,15},{2,8},{3,9},{4,10},{5,11},{6,12},{7,13},{8,6},{9,7},... | collective-permute-start | bytes 393224 | tf_op jit(solution)/shard_map/ppermute | solution.py:38
  77.4 1.9 %shard_map.103 = (bf16[256,512]{1,0:T(8,128)(2,1)S(1)}, bf16[256,512]{1,0:T(8,128)(2,1)S(1)}, bf16[256,512]{1,0:T(8,128)(2,1)S(1)}, bf16[256,512]{1,0:T(8,128)(2,1)S(1)}) custom-call(s32[43]{0:T(128)S(1)} %concatenate.12.scalar_ref, bf16[256,4096]{1,0:T(8,128)(2,1)S(1)} %collective-permute-done.9.swapped_ref, bf16[256,8192]{1,0:T(8,128)(2,1)S(1)} %copy-done.2, ...), custom_call_target="tpu_custom_call" | custom-call | flops 536870912 | bytes 2097152 | tf_op jit(solution)/shard_map/pallas_call | solution.py:473
  82.2 2.4 %collective-permute-start.21 = (bf16[256,512]{1,0:T(8,128)(2,1)S(1)}, bf16[256,512]{1,0:T(8,128)(2,1)S(1)}, u32[]{:S(2)}, u32[]{:S(2)}) collective-permute-start(bf16[256,512]{1,0:T(8,128)(2,1)S(1)} %get-tuple-element.117), channel_id=1, source_target_pairs={{0,6},{1,7},{2,0},{3,1},{4,2},{5,3},{6,4},{7,5},{8,14},{9,15},{10,... | collective-permute-start | bytes 786440 | tf_op jit(solution)/shard_map/ppermute | solution.py:38
  84.6 2.7 %collective-permute-start.22 = (bf16[256,512]{1,0:T(8,128)(2,1)S(1)}, bf16[256,512]{1,0:T(8,128)(2,1)S(1)}, u32[]{:S(2)}, u32[]{:S(2)}) collective-permute-start(bf16[256,512]{1,0:T(8,128)(2,1)S(1)} %get-tuple-element.118), channel_id=1, source_target_pairs={{0,8},{1,9},{2,10},{3,11},{4,12},{5,13},{6,14},{7,15},{8,0},{9,1},... | collective-permute-start | bytes 786440 | tf_op jit(solution)/shard_map/ppermute | solution.py:38
  88.6 1.4 %collective-permute-done.24 = bf16[1,4,8,256]{3,2,1,0:T(8,128)(2,1)S(1)} collective-permute-done((bf16[1,4,8,256]{3,2,1,0:T(8,128)(2,1)S(1)}, bf16[1,4,8,256]{3,2,1,0:T(8,128)(2,1)S(1)}, u32[]{:S(2)}, u32[]{:S(2)}) %collective-permute-start.24) | collective-permute-done | bytes 16416 | tf_op jit(solution)/shard_map/ppermute | solution.py:777
  90.7 2.0 %collective-permute-done.22.from_partner = bf16[256,512]{1,0:T(8,128)(2,1)S(1)} collective-permute-done((bf16[256,512]{1,0:T(8,128)(2,1)S(1)}, bf16[256,512]{1,0:T(8,128)(2,1)S(1)}, u32[]{:S(2)}, u32[]{:S(2)}) %collective-permute-start.22) | collective-permute-done | bytes 262176 | tf_op jit(solution)/shard_map/ppermute | solution.py:38
  (71 shorter events, 24.0 us)
Async XLA Ops:
  0.6 10.2 %collective-permute-start = (bf16[256,512]{1,0:T(8,128)(2,1)}, bf16[256,512]{1,0:T(8,128)(2,1)S(1)}, u32[]{:S(2)}, u32[]{:S(2)}) collective-permute-start(bf16[256,512]{1,0:T(8,128)(2,1)} %bitcast.49), channel_id=1, source_target_pairs={{0,8},{1,9},{2,10},{3,11},{4,12},{5,13},{6,14},{7,15},{8,0},{9,1},... | collective-permute-start | bytes 786440 | tf_op jit(solution)/shard_map/ppermute | solution.py:38
  3.8 9.3 %collective-permute-start.1 = (bf16[256,512]{1,0:T(8,128)(2,1)}, bf16[256,512]{1,0:T(8,128)(2,1)S(1)}, u32[]{:S(2)}, u32[]{:S(2)}) collective-permute-start(bf16[256,512]{1,0:T(8,128)(2,1)} %bitcast.50), channel_id=1, source_target_pairs={{0,2},{1,3},{2,4},{3,5},{4,6},{5,7},{6,0},{7,1},{8,10},{9,11},{10,... | collective-permute-start | bytes 786440 | tf_op jit(solution)/shard_map/ppermute | solution.py:38
  5.4 7.7 %collective-permute-start.2 = (bf16[256,512]{1,0:T(8,128)(2,1)}, bf16[256,512]{1,0:T(8,128)(2,1)S(1)}, u32[]{:S(2)}, u32[]{:S(2)}) collective-permute-start(bf16[256,512]{1,0:T(8,128)(2,1)} %bitcast.51), channel_id=1, source_target_pairs={{0,6},{1,7},{2,0},{3,1},{4,2},{5,3},{6,4},{7,5},{8,14},{9,15},{10,... | collective-permute-start | bytes 786440 | tf_op jit(solution)/shard_map/ppermute | solution.py:38
  14.8 10.1 %collective-permute-start.3 = (bf16[1024,512]{1,0:T(8,128)(2,1)S(1)}, bf16[1024,512]{1,0:T(8,128)(2,1)S(1)}, u32[]{:S(2)}, u32[]{:S(2)}) collective-permute-start(bf16[1024,512]{1,0:T(8,128)(2,1)S(1)} %get-tuple-element.83.near_ref), channel_id=1, source_target_pairs={{0,1},{1,0},{2,3},{3,2},{4,5},{5,4},{6,7},{7,6},{8,9},{9,8},{10,11... | collective-permute-start | bytes 3145736 | tf_op jit(solution)/shard_map/ppermute | solution.py:38
  14.9 15.6 %collective-permute-start.4 = (bf16[384,512]{1,0:T(8,128)(2,1)S(1)}, bf16[384,512]{1,0:T(8,128)(2,1)S(1)}, u32[]{:S(2)}, u32[]{:S(2)}) collective-permute-start(bf16[384,512]{1,0:T(8,128)(2,1)S(1)} %get-tuple-element.87), channel_id=1, source_target_pairs={{0,2},{1,3},{2,4},{3,5},{4,6},{5,7},{6,0},{7,1},{8,10},{9,11},{10,... | collective-permute-start | bytes 1179656 | tf_op jit(solution)/shard_map/ppermute | solution.py:38
  16.5 14.0 %collective-permute-start.5 = (bf16[384,512]{1,0:T(8,128)(2,1)S(1)}, bf16[384,512]{1,0:T(8,128)(2,1)S(1)}, u32[]{:S(2)}, u32[]{:S(2)}) collective-permute-start(bf16[384,512]{1,0:T(8,128)(2,1)S(1)} %get-tuple-element.88), channel_id=1, source_target_pairs={{0,6},{1,7},{2,0},{3,1},{4,2},{5,3},{6,4},{7,5},{8,14},{9,15},{10,... | collective-permute-start | bytes 1179656 | tf_op jit(solution)/shard_map/ppermute | solution.py:38
  18.2 8.8 %collective-permute-start.6 = (bf16[128,512]{1,0:T(8,128)(2,1)S(1)}, bf16[128,512]{1,0:T(8,128)(2,1)S(1)}, u32[]{:S(2)}, u32[]{:S(2)}) collective-permute-start(bf16[128,512]{1,0:T(8,128)(2,1)S(1)} %get-tuple-element.89), channel_id=1, source_target_pairs={{0,14},{1,15},{2,8},{3,9},{4,10},{5,11},{6,12},{7,13},{8,6},{9,7},... | collective-permute-start | bytes 393224 | tf_op jit(solution)/shard_map/ppermute | solution.py:38
  19.9 9.1 %collective-permute-start.7 = (bf16[128,512]{1,0:T(8,128)(2,1)S(1)}, bf16[128,512]{1,0:T(8,128)(2,1)S(1)}, u32[]{:S(2)}, u32[]{:S(2)}) collective-permute-start(bf16[128,512]{1,0:T(8,128)(2,1)S(1)} %get-tuple-element.90), channel_id=1, source_target_pairs={{0,10},{1,11},{2,12},{3,13},{4,14},{5,15},{6,8},{7,9},{8,2},{9,3},... | collective-permute-start | bytes 393224 | tf_op jit(solution)/shard_map/ppermute | solution.py:38
  30.6 2.7 %collective-permute-start.8 = (bf16[1024,512]{1,0:T(8,128)(2,1)S(1)}, bf16[1024,512]{1,0:T(8,128)(2,1)S(1)}, u32[]{:S(2)}, u32[]{:S(2)}) collective-permute-start(bf16[1024,512]{1,0:T(8,128)(2,1)S(1)} %shard_map.98.far_ref), channel_id=1, source_target_pairs={{0,1},{1,0},{2,3},{3,2},{4,5},{5,4},{6,7},{7,6},{8,9},{9,8},{10,11... | collective-permute-start | bytes 3145736 | tf_op jit(solution)/shard_map/ppermute | solution.py:38
  34.7 27.8 %collective-permute-start.9 = (bf16[256,4096]{1,0:T(8,128)(2,1)}, bf16[256,4096]{1,0:T(8,128)(2,1)S(1)}, u32[]{:S(2)}, u32[]{:S(2)}) collective-permute-start(bf16[256,4096]{1,0:T(8,128)(2,1)} %shard_map.95), channel_id=1, source_target_pairs={{0,1},{1,0},{2,3},{3,2},{4,5},{5,4},{6,7},{7,6},{8,9},{9,8},{10,11... | collective-permute-start | bytes 6291464 | tf_op jit(solution)/shard_map/ppermute | solution.py:38
  34.9 4.0 %collective-permute-start.10 = (bf16[256,256]{1,0:T(8,128)(2,1)S(1)}, bf16[256,256]{1,0:T(8,128)(2,1)S(1)}, u32[]{:S(2)}, u32[]{:S(2)}) collective-permute-start(bf16[256,256]{1,0:T(8,128)(2,1)S(1)} %get-tuple-element.97.own_ref), channel_id=1, source_target_pairs={{0,1},{1,0},{2,3},{3,2},{4,5},{5,4},{6,7},{7,6},{8,9},{9,8},{10,11... | collective-permute-start | bytes 393224 | tf_op jit(solution)/shard_map/ppermute | solution.py:38
  35.2 24.1 %collective-permute-start.11 = (bf16[256,128]{1,0:T(8,128)(2,1)S(1)}, bf16[256,128]{1,0:T(8,128)(2,1)S(1)}, u32[]{:S(2)}, u32[]{:S(2)}) collective-permute-start(bf16[256,128]{1,0:T(8,128)(2,1)S(1)} %get-tuple-element.100), channel_id=1, source_target_pairs={{0,0},{1,2},{2,4},{3,6},{4,8},{5,10},{6,12},{7,14},{8,1},{9,3},{10... | collective-permute-start | bytes 196616 | tf_op jit(solution)/shard_map/ppermute | solution.py:688
  59.8 2.7 %collective-permute-start.12 = (bf16[256,512]{1,0:T(8,128)(2,1)S(1)}, bf16[256,512]{1,0:T(8,128)(2,1)S(1)}, u32[]{:S(2)}, u32[]{:S(2)}) collective-permute-start(bf16[256,512]{1,0:T(8,128)(2,1)S(1)} %get-tuple-element.101.own_ref), channel_id=1, source_target_pairs={{0,1},{1,0},{2,3},{3,2},{4,5},{5,4},{6,7},{7,6},{8,9},{9,8},{10,11... | collective-permute-start | bytes 786440 | tf_op jit(solution)/shard_map/ppermute | solution.py:38
  59.9 2.5 %collective-permute-start.13 = (f32[256,4]{1,0:T(8,128)S(1)}, f32[256,4]{1,0:T(8,128)S(1)}, u32[]{:S(2)}, u32[]{:S(2)}) collective-permute-start(f32[256,4]{1,0:T(8,128)S(1)} %get-tuple-element.102.own_level), channel_id=1, source_target_pairs={{0,1},{1,0},{2,3},{3,2},{4,5},{5,4},{6,7},{7,6},{8,9},{9,8},{10,11... | collective-permute-start | bytes 12296 | tf_op jit(solution)/shard_map/ppermute | solution.py:38
  65.1 16.0 %collective-permute-start.16 = (bf16[384,512]{1,0:T(8,128)(2,1)S(1)}, bf16[384,512]{1,0:T(8,128)(2,1)S(1)}, u32[]{:S(2)}, u32[]{:S(2)}) collective-permute-start(bf16[384,512]{1,0:T(8,128)(2,1)S(1)} %get-tuple-element.112), channel_id=1, source_target_pairs={{0,2},{1,3},{2,4},{3,5},{4,6},{5,7},{6,0},{7,1},{8,10},{9,11},{10,... | collective-permute-start | bytes 1179656 | tf_op jit(solution)/shard_map/ppermute | solution.py:38
  67.2 13.9 %collective-permute-start.17 = (bf16[384,512]{1,0:T(8,128)(2,1)S(1)}, bf16[384,512]{1,0:T(8,128)(2,1)S(1)}, u32[]{:S(2)}, u32[]{:S(2)}) collective-permute-start(bf16[384,512]{1,0:T(8,128)(2,1)S(1)} %get-tuple-element.113), channel_id=1, source_target_pairs={{0,6},{1,7},{2,0},{3,1},{4,2},{5,3},{6,4},{7,5},{8,14},{9,15},{10,... | collective-permute-start | bytes 1179656 | tf_op jit(solution)/shard_map/ppermute | solution.py:38
  69.0 7.0 %collective-permute-start.15 = (bf16[4,4,8,256]{3,2,1,0:T(8,128)(2,1)S(1)}, bf16[4,4,8,256]{3,2,1,0:T(8,128)(2,1)S(1)}, u32[]{:S(2)}, u32[]{:S(2)}) collective-permute-start(bf16[4,4,8,256]{3,2,1,0:T(8,128)(2,1)S(1)} %bitcast.64), channel_id=1, source_target_pairs={{0,64},{1,65},{2,66},{3,67},{4,68},{5,69},{6,70},{7,71},{8,72},{9,... | collective-permute-start | bytes 196616 | tf_op jit(solution)/shard_map/ppermute | solution.py:756
  70.3 10.1 %collective-permute-start.18 = (bf16[128,512]{1,0:T(8,128)(2,1)S(1)}, bf16[128,512]{1,0:T(8,128)(2,1)S(1)}, u32[]{:S(2)}, u32[]{:S(2)}) collective-permute-start(bf16[128,512]{1,0:T(8,128)(2,1)S(1)} %get-tuple-element.114), channel_id=1, source_target_pairs={{0,10},{1,11},{2,12},{3,13},{4,14},{5,15},{6,8},{7,9},{8,2},{9,3},... | collective-permute-start | bytes 393224 | tf_op jit(solution)/shard_map/ppermute | solution.py:38
  73.4 7.7 %collective-permute-start.19 = (bf16[128,512]{1,0:T(8,128)(2,1)S(1)}, bf16[128,512]{1,0:T(8,128)(2,1)S(1)}, u32[]{:S(2)}, u32[]{:S(2)}) collective-permute-start(bf16[128,512]{1,0:T(8,128)(2,1)S(1)} %get-tuple-element.115), channel_id=1, source_target_pairs={{0,14},{1,15},{2,8},{3,9},{4,10},{5,11},{6,12},{7,13},{8,6},{9,7},... | collective-permute-start | bytes 393224 | tf_op jit(solution)/shard_map/ppermute | solution.py:38
  76.1 11.2 %collective-permute-start.23 = (bf16[2,4,8,256]{3,2,1,0:T(8,128)(2,1)S(1)}, bf16[2,4,8,256]{3,2,1,0:T(8,128)(2,1)S(1)}, u32[]{:S(2)}, u32[]{:S(2)}) collective-permute-start(bf16[2,4,8,256]{3,2,1,0:T(8,128)(2,1)S(1)} %slice.42), channel_id=1, source_target_pairs={{0,32},{64,96},{1,33},{65,97},{2,34},{66,98},{3,35},{67,99},{4,36}... | collective-permute-start | bytes 98312 | tf_op jit(solution)/shard_map/ppermute | solution.py:775
  81.3 9.4 %collective-permute-start.20 = (bf16[256,512]{1,0:T(8,128)(2,1)S(1)}, bf16[256,512]{1,0:T(8,128)(2,1)S(1)}, u32[]{:S(2)}, u32[]{:S(2)}) collective-permute-start(bf16[256,512]{1,0:T(8,128)(2,1)S(1)} %get-tuple-element.116), channel_id=1, source_target_pairs={{0,2},{1,3},{2,4},{3,5},{4,6},{5,7},{6,0},{7,1},{8,10},{9,11},{10,... | collective-permute-start | bytes 786440 | tf_op jit(solution)/shard_map/ppermute | solution.py:38
  82.2 8.5 %collective-permute-start.21 = (bf16[256,512]{1,0:T(8,128)(2,1)S(1)}, bf16[256,512]{1,0:T(8,128)(2,1)S(1)}, u32[]{:S(2)}, u32[]{:S(2)}) collective-permute-start(bf16[256,512]{1,0:T(8,128)(2,1)S(1)} %get-tuple-element.117), channel_id=1, source_target_pairs={{0,6},{1,7},{2,0},{3,1},{4,2},{5,3},{6,4},{7,5},{8,14},{9,15},{10,... | collective-permute-start | bytes 786440 | tf_op jit(solution)/shard_map/ppermute | solution.py:38
  84.6 8.1 %collective-permute-start.22 = (bf16[256,512]{1,0:T(8,128)(2,1)S(1)}, bf16[256,512]{1,0:T(8,128)(2,1)S(1)}, u32[]{:S(2)}, u32[]{:S(2)}) collective-permute-start(bf16[256,512]{1,0:T(8,128)(2,1)S(1)} %get-tuple-element.118), channel_id=1, source_target_pairs={{0,8},{1,9},{2,10},{3,11},{4,12},{5,13},{6,14},{7,15},{8,0},{9,1},... | collective-permute-start | bytes 786440 | tf_op jit(solution)/shard_map/ppermute | solution.py:38
  87.3 2.7 %collective-permute-start.24 = (bf16[1,4,8,256]{3,2,1,0:T(8,128)(2,1)S(1)}, bf16[1,4,8,256]{3,2,1,0:T(8,128)(2,1)S(1)}, u32[]{:S(2)}, u32[]{:S(2)}) collective-permute-start(bf16[1,4,8,256]{3,2,1,0:T(8,128)(2,1)S(1)} %slice.44), channel_id=1, source_target_pairs={{0,16},{32,48},{64,80},{96,112},{1,17},{33,49},{65,81},{97,113},{2... | collective-permute-start | bytes 49160 | tf_op jit(solution)/shard_map/ppermute | solution.py:777
  (7 other events, 43.7 us)

commit v7 on v6

--- a/solution.py
+++ b/solution.py
@@ -60,7 +60,7 @@
 CHIPS = 8
 SHARD = 512
 HALF = TOK // 2
-PREFILL_CHUNK = 8192
+PREFILL_CHUNK = 4096
 ROWS_AT_ONCE = 4
 LOG2_E = 1.4426950408889634
 NT = (((1,), (1,)), ((), ()))
@@ -413,7 +413,18 @@
     )
 
 
-def far_kernel(scalar_ref, query_weight, pair_weight, query_in, pair_in, far_ref, query, pair):
+def far_kernel(
+    scalar_ref,
+    cosine_ref,
+    sine_ref,
+    query_weight,
+    pair_weight,
+    query_in,
+    pair_in,
+    far_ref,
+    query,
+    pair,
+):
     sums = projected_parts(scalar_ref, FAR_ROWS, four_shards(far_ref), query_weight, pair_weight)
     query[...] = query_in[...] + sums[0]
     pair[...] = pair_in[...] + sums[1]
@@ -504,7 +515,7 @@
             pltpu.VMEM((chunks, GQ * CH, PREFILL_CHUNK), jnp.float32),
             pltpu.SemaphoreType.DMA((2, NPR * chunks)),
         ],
-        compiler_params=pltpu.CompilerParams(vmem_limit_bytes=58 * 2**20),
+        compiler_params=pltpu.CompilerParams(vmem_limit_bytes=44 * 2**20),
     )(scalars, lengths, own, other, keys, values)
 
 
@@ -670,8 +681,11 @@
         *weights,
         *part,
         sides,
+        streamed=(cosine, sine),
         flops=2 * TOK * 4 * SHARD * 3 * HD,
     )
+    _, _, cut_out = lax.optimization_barrier((other_sides, part[1], cut_out))
+    swapped_out = core_swap(cut_out)
     query_local, pair_local = called(
         last_kernel,
         tuple((shape, jnp.bfloat16) for shape, _ in sums),
@@ -683,12 +697,10 @@
         sine,
         flops=2 * TOK * 4 * SHARD * 3 * HD,
     )
-    pair_local, cut_out = lax.optimization_barrier((pair_local, cut_out))
     query_other = core_swap(query_local)
     pair_held = lax.ppermute(
         pair_local, "tp", [(t, 2 * t if t < KVH else 2 * (t - KVH) + 1) for t in range(2 * KVH)]
     )
-    swapped_out = core_swap(cut_out)
     cached = lax.cond(
         is_prefill,
         prefill_part,

time: 93.8 us -> 86.1 us (0.918)
  Pallas kernels: 35.7 us -> 28.2 us
  waiting for transfers between devices: 15.4 us -> 14.4 us
    pallas_call x1, Pallas kernels: 20.4 us -> 12.9 us  [prefill_part(): pl.pallas_call(prefill_kernel, in_specs=[small, small, whole, whole, ther...]
    ppermute x21, waiting for transfers between devices: 13.9 us -> 12.9 us  [moved(): return lax.ppermute(shard, 'tp', pairs)]
  transfers between devices with their start and end apart: 25 -> 25, of which waited for: 12 -> 13; matrix products, arithmetic and copies ran while one was open for 5% -> 6% of each run, Pallas kernels for 32% -> 28%
where the time goes in v7:
time: 86.1 us; the launch traced here: 85.8 us
  starting transfers between devices  36.2 us (42%)
  Pallas kernels  28.2 us (33%)
  waiting for transfers between devices  14.4 us (17%)
  other arithmetic  4.22 us (5%)
  local copies, waits for them, and re-layouts  1.85 us (2%)
  between operations  0.94 us (1%)
    ppermute x21, starting transfers between devices, moved(): return lax.ppermute(shard, 'tp', pairs)  31.7 us
    pallas_call x11, Pallas kernels, called(): pl.pallas_call(kernel, in_specs=specs, out_specs=tuple((whole for _ in sh...  13.1 us
    ppermute x21, waiting for transfers between devices, moved(): return lax.ppermute(shard, 'tp', pairs)  12.9 us
    pallas_call x1, Pallas kernels, prefill_part(): pl.pallas_call(prefill_kernel, in_specs=[small, small, whole, whole, ther...  12.9 us
    pallas_call x1, Pallas kernels, cut_columns(): pl.pallas_call(cut_kernel, in_specs=[pl.BlockSpec(memory_space=pltpu.SMEM...  2.22 us
  transfers between devices with their start and end apart: 25, of which 13 were waited for; matrix products, arithmetic and copies ran while one was open for 6% of the time, Pallas kernels for 28%

profile of v7, /device:TPU:0, one launch (start us, length us, event | category | flops | bytes accessed | tf_op | source)
XLA Modules:
  0.0 85.8 jit_solution(9900765059618315946)
XLA Ops:
  0.6 3.2 %collective-permute-start = (bf16[256,512]{1,0:T(8,128)(2,1)}, bf16[256,512]{1,0:T(8,128)(2,1)S(1)}, u32[]{:S(2)}, u32[]{:S(2)}) collective-permute-start(bf16[256,512]{1,0:T(8,128)(2,1)} %bitcast.49), channel_id=1, source_target_pairs={{0,8},{1,9},{2,10},{3,11},{4,12},{5,13},{6,14},{7,15},{8,0},{9,1},... | collective-permute-start | bytes 786440 | tf_op jit(solution)/shard_map/ppermute | solution.py:38
  3.8 1.6 %collective-permute-start.1 = (bf16[256,512]{1,0:T(8,128)(2,1)}, bf16[256,512]{1,0:T(8,128)(2,1)S(1)}, u32[]{:S(2)}, u32[]{:S(2)}) collective-permute-start(bf16[256,512]{1,0:T(8,128)(2,1)} %bitcast.50), channel_id=1, source_target_pairs={{0,2},{1,3},{2,4},{3,5},{4,6},{5,7},{6,0},{7,1},{8,10},{9,11},{10,... | collective-permute-start | bytes 786440 | tf_op jit(solution)/shard_map/ppermute | solution.py:38
  5.4 1.7 %collective-permute-start.2 = (bf16[256,512]{1,0:T(8,128)(2,1)}, bf16[256,512]{1,0:T(8,128)(2,1)S(1)}, u32[]{:S(2)}, u32[]{:S(2)}) collective-permute-start(bf16[256,512]{1,0:T(8,128)(2,1)} %bitcast.51), channel_id=1, source_target_pairs={{0,6},{1,7},{2,0},{3,1},{4,2},{5,3},{6,4},{7,5},{8,14},{9,15},{10,... | collective-permute-start | bytes 786440 | tf_op jit(solution)/shard_map/ppermute | solution.py:38
  10.8 2.3 %collective-permute-done.1.last_ref = bf16[256,512]{1,0:T(8,128)(2,1)S(1)} collective-permute-done((bf16[256,512]{1,0:T(8,128)(2,1)}, bf16[256,512]{1,0:T(8,128)(2,1)S(1)}, u32[]{:S(2)}, u32[]{:S(2)}) %collective-permute-start.1) | collective-permute-done | bytes 262176 | tf_op jit(solution)/shard_map/ppermute | solution.py:38
  14.9 1.6 %collective-permute-start.4 = (bf16[384,512]{1,0:T(8,128)(2,1)S(1)}, bf16[384,512]{1,0:T(8,128)(2,1)S(1)}, u32[]{:S(2)}, u32[]{:S(2)}) collective-permute-start(bf16[384,512]{1,0:T(8,128)(2,1)S(1)} %get-tuple-element.84), channel_id=1, source_target_pairs={{0,2},{1,3},{2,4},{3,5},{4,6},{5,7},{6,0},{7,1},{8,10},{9,11},{10,... | collective-permute-start | bytes 1179656 | tf_op jit(solution)/shard_map/ppermute | solution.py:38
  16.5 1.7 %collective-permute-start.5 = (bf16[384,512]{1,0:T(8,128)(2,1)S(1)}, bf16[384,512]{1,0:T(8,128)(2,1)S(1)}, u32[]{:S(2)}, u32[]{:S(2)}) collective-permute-start(bf16[384,512]{1,0:T(8,128)(2,1)S(1)} %get-tuple-element.85), channel_id=1, source_target_pairs={{0,6},{1,7},{2,0},{3,1},{4,2},{5,3},{6,4},{7,5},{8,14},{9,15},{10,... | collective-permute-start | bytes 1179656 | tf_op jit(solution)/shard_map/ppermute | solution.py:38
  18.2 1.7 %collective-permute-start.6 = (bf16[128,512]{1,0:T(8,128)(2,1)S(1)}, bf16[128,512]{1,0:T(8,128)(2,1)S(1)}, u32[]{:S(2)}, u32[]{:S(2)}) collective-permute-start(bf16[128,512]{1,0:T(8,128)(2,1)S(1)} %get-tuple-element.86), channel_id=1, source_target_pairs={{0,14},{1,15},{2,8},{3,9},{4,10},{5,11},{6,12},{7,13},{8,6},{9,7},... | collective-permute-start | bytes 393224 | tf_op jit(solution)/shard_map/ppermute | solution.py:38
  19.9 2.7 %collective-permute-start.7 = (bf16[128,512]{1,0:T(8,128)(2,1)S(1)}, bf16[128,512]{1,0:T(8,128)(2,1)S(1)}, u32[]{:S(2)}, u32[]{:S(2)}) collective-permute-start(bf16[128,512]{1,0:T(8,128)(2,1)S(1)} %get-tuple-element.87), channel_id=1, source_target_pairs={{0,10},{1,11},{2,12},{3,13},{4,14},{5,15},{6,8},{7,9},{8,2},{9,3},... | collective-permute-start | bytes 393224 | tf_op jit(solution)/shard_map/ppermute | solution.py:38
  22.6 2.2 %shard_map.95 = bf16[256,4096]{1,0:T(8,128)(2,1)} custom-call(s32[43]{0:T(128)S(1)} %concatenate.12.scalar_ref, bf16[256,8192]{1,0:T(8,128)(2,1)S(1)} %copy-done.1), custom_call_target="tpu_custom_call" | custom-call | tf_op jit(solution)/shard_map/pallas_call | solution.py:575
  24.9 1.8 %shard_map.97 = (f32[256,256]{1,0:T(8,128)S(1)}, f32[256,128]{1,0:T(8,128)S(1)}, f32[8,128]{1,0:T(8,128)S(1)}) custom-call(s32[43]{0:T(128)S(1)} %concatenate.12.scalar_ref, bf16[8192,256]{1,0:T(8,128)(2,1)S(1)} %copy-done, bf16[8192,128]{1,0:T(8,128)(2,1)S(1)} %copy-done.3, bf16[1024,512]{1,0:T(8,128)(2,1)S(1)} %get-tuple-element.82.near_ref, ...), custom_call_target="tpu_custom_call" | custom-call | flops 805306368 | bytes 2097152 | tf_op jit(solution)/shard_map/pallas_call | solution.py:484
  27.0 2.1 %collective-permute-done.7.lower_ref = bf16[128,512]{1,0:T(8,128)(2,1)S(1)} collective-permute-done((bf16[128,512]{1,0:T(8,128)(2,1)S(1)}, bf16[128,512]{1,0:T(8,128)(2,1)S(1)}, u32[]{:S(2)}, u32[]{:S(2)}) %collective-permute-start.7) | collective-permute-done | bytes 131104 | tf_op jit(solution)/shard_map/ppermute | solution.py:38
  35.9 1.7 %collective-permute-done.10.other_ref = bf16[256,256]{1,0:T(8,128)(2,1)S(1)} collective-permute-done((bf16[256,256]{1,0:T(8,128)(2,1)S(1)}, bf16[256,256]{1,0:T(8,128)(2,1)S(1)}, u32[]{:S(2)}, u32[]{:S(2)}) %collective-permute-start.10) | collective-permute-done | bytes 131104 | tf_op jit(solution)/shard_map/ppermute | solution.py:38
  37.7 12.9 %conditional.1 = ((bf16[256,512]{1,0:T(8,128)(2,1)S(1)}, f32[256,4]{1,0:T(8,128)S(1)})) conditional(s32[]{:T(128)} %convert_element_type.8, (bf16[256,256]{1,0:T(8,128)(2,1)S(1)}, bf16[256,256]{1,0:T(8,128)(2,1)S(1)}, s32[43]{0:T(128)S(1)}, s32[64]{0:T(128)S(1)}, bf16[64,256,128]{2,1,0:T(8,128)(2,1)}, ...), branch_computations={%region_1.2_spmd, %region_2.3_spmd} | conditional | flops 524288 | bytes 2629656 | solution.py:704
  37.7 12.9 %branch_1_fun.1 = (bf16[256,512]{1,0:T(8,128)(2,1)S(1)}, f32[256,4]{1,0:T(8,128)S(1)}) custom-call(s32[43]{0:T(128)S(1)} %get-tuple-element.32.scalar_ref, s32[64]{0:T(128)S(1)} %get-tuple-element.33.length_ref, bf16[256,256]{1,0:T(8,128)(2,1)S(1)} %get-tuple-element.34.own_ref, bf16[256,256]{1,0:T(8,128)(2,1)S(1)} %get-tuple-element.35.other_ref, ...), custom_call_target="tpu_custom_call" | custom-call | tf_op jit(solution)/shard_map/cond/branch_1_fun/pallas_call | solution.py:507
  52.7 1.8 %shard_map.101 = (bf16[256,512]{1,0:T(8,128)(2,1)S(1)}, f32[256,4]{1,0:T(8,128)S(1)}) custom-call(s32[43]{0:T(128)S(1)} %concatenate.12.scalar_ref, bf16[256,256]{1,0:T(8,128)(2,1)S(1)} %get-tuple-element.95.own_ref, bf16[256,256]{1,0:T(8,128)(2,1)S(1)} %collective-permute-done.10.other_ref, bf16[256,128]{1,0:T(8,128)(2,1)S(1)} %collective-permute-done.11.held_ref, ...), custom_call_target="tpu_custom_call" | custom-call | flops 6000000000 | bytes 2097152 | tf_op jit(solution)/shard_map/pallas_call | solution.py:484
  54.5 2.6 %shard_map.102 = (bf16[384,512]{1,0:T(8,128)(2,1)S(1)}, bf16[384,512]{1,0:T(8,128)(2,1)S(1)}, bf16[128,512]{1,0:T(8,128)(2,1)S(1)}, bf16[128,512]{1,0:T(8,128)(2,1)S(1)}, bf16[256,512]{1,0:T(8,128)(2,1)S(1)}) custom-call(s32[43]{0:T(128)S(1)} %concatenate.12.scalar_ref, bf16[256,4096]{1,0:T(8,128)(2,1)S(1)} %collective-permute-done.9.swapped_ref, ...), custom_call_target="tpu_custom_call" | custom-call | flops 536870912 | bytes 2097152 | tf_op jit(solution)/shard_map/pallas_call | solution.py:484
  57.1 2.5 %collective-permute-start.16 = (bf16[384,512]{1,0:T(8,128)(2,1)S(1)}, bf16[384,512]{1,0:T(8,128)(2,1)S(1)}, u32[]{:S(2)}, u32[]{:S(2)}) collective-permute-start(bf16[384,512]{1,0:T(8,128)(2,1)S(1)} %get-tuple-element.110), channel_id=1, source_target_pairs={{0,2},{1,3},{2,4},{3,5},{4,6},{5,7},{6,0},{7,1},{8,10},{9,11},{10,... | collective-permute-start | bytes 1179656 | tf_op jit(solution)/shard_map/ppermute | solution.py:38
  62.3 3.5 %collective-permute-start.18 = (bf16[128,512]{1,0:T(8,128)(2,1)S(1)}, bf16[128,512]{1,0:T(8,128)(2,1)S(1)}, u32[]{:S(2)}, u32[]{:S(2)}) collective-permute-start(bf16[128,512]{1,0:T(8,128)(2,1)S(1)} %get-tuple-element.112), channel_id=1, source_target_pairs={{0,10},{1,11},{2,12},{3,13},{4,14},{5,15},{6,8},{7,9},{8,2},{9,3},... | collective-permute-start | bytes 393224 | tf_op jit(solution)/shard_map/ppermute | solution.py:38
  65.8 2.2 %collective-permute-start.19 = (bf16[128,512]{1,0:T(8,128)(2,1)S(1)}, bf16[128,512]{1,0:T(8,128)(2,1)S(1)}, u32[]{:S(2)}, u32[]{:S(2)}) collective-permute-start(bf16[128,512]{1,0:T(8,128)(2,1)S(1)} %get-tuple-element.113), channel_id=1, source_target_pairs={{0,14},{1,15},{2,8},{3,9},{4,10},{5,11},{6,12},{7,13},{8,6},{9,7},... | collective-permute-start | bytes 393224 | tf_op jit(solution)/shard_map/ppermute | solution.py:38
  69.4 1.9 %shard_map.103 = (bf16[256,512]{1,0:T(8,128)(2,1)S(1)}, bf16[256,512]{1,0:T(8,128)(2,1)S(1)}, bf16[256,512]{1,0:T(8,128)(2,1)S(1)}, bf16[256,512]{1,0:T(8,128)(2,1)S(1)}) custom-call(s32[43]{0:T(128)S(1)} %concatenate.12.scalar_ref, bf16[256,4096]{1,0:T(8,128)(2,1)S(1)} %collective-permute-done.9.swapped_ref, bf16[256,8192]{1,0:T(8,128)(2,1)S(1)} %copy-done.2, ...), custom_call_target="tpu_custom_call" | custom-call | flops 536870912 | bytes 2097152 | tf_op jit(solution)/shard_map/pallas_call | solution.py:484
  74.2 2.9 %collective-permute-start.21 = (bf16[256,512]{1,0:T(8,128)(2,1)S(1)}, bf16[256,512]{1,0:T(8,128)(2,1)S(1)}, u32[]{:S(2)}, u32[]{:S(2)}) collective-permute-start(bf16[256,512]{1,0:T(8,128)(2,1)S(1)} %get-tuple-element.115), channel_id=1, source_target_pairs={{0,6},{1,7},{2,0},{3,1},{4,2},{5,3},{6,4},{7,5},{8,14},{9,15},{10,... | collective-permute-start | bytes 786440 | tf_op jit(solution)/shard_map/ppermute | solution.py:38
  77.0 2.7 %collective-permute-start.22 = (bf16[256,512]{1,0:T(8,128)(2,1)S(1)}, bf16[256,512]{1,0:T(8,128)(2,1)S(1)}, u32[]{:S(2)}, u32[]{:S(2)}) collective-permute-start(bf16[256,512]{1,0:T(8,128)(2,1)S(1)} %get-tuple-element.116), channel_id=1, source_target_pairs={{0,8},{1,9},{2,10},{3,11},{4,12},{5,13},{6,14},{7,15},{8,0},{9,1},... | collective-permute-start | bytes 786440 | tf_op jit(solution)/shard_map/ppermute | solution.py:38
  81.1 1.4 %collective-permute-done.24 = bf16[1,4,8,256]{3,2,1,0:T(8,128)(2,1)S(1)} collective-permute-done((bf16[1,4,8,256]{3,2,1,0:T(8,128)(2,1)S(1)}, bf16[1,4,8,256]{3,2,1,0:T(8,128)(2,1)S(1)}, u32[]{:S(2)}, u32[]{:S(2)}) %collective-permute-start.24) | collective-permute-done | bytes 16416 | tf_op jit(solution)/shard_map/ppermute | solution.py:789
  83.1 1.8 %collective-permute-done.22.from_partner = bf16[256,512]{1,0:T(8,128)(2,1)S(1)} collective-permute-done((bf16[256,512]{1,0:T(8,128)(2,1)S(1)}, bf16[256,512]{1,0:T(8,128)(2,1)S(1)}, u32[]{:S(2)}, u32[]{:S(2)}) %collective-permute-start.22) | collective-permute-done | bytes 262176 | tf_op jit(solution)/shard_map/ppermute | solution.py:38
  (71 shorter events, 24.3 us)
Async XLA Ops:
  0.6 10.2 %collective-permute-start = (bf16[256,512]{1,0:T(8,128)(2,1)}, bf16[256,512]{1,0:T(8,128)(2,1)S(1)}, u32[]{:S(2)}, u32[]{:S(2)}) collective-permute-start(bf16[256,512]{1,0:T(8,128)(2,1)} %bitcast.49), channel_id=1, source_target_pairs={{0,8},{1,9},{2,10},{3,11},{4,12},{5,13},{6,14},{7,15},{8,0},{9,1},... | collective-permute-start | bytes 786440 | tf_op jit(solution)/shard_map/ppermute | solution.py:38
  3.8 9.3 %collective-permute-start.1 = (bf16[256,512]{1,0:T(8,128)(2,1)}, bf16[256,512]{1,0:T(8,128)(2,1)S(1)}, u32[]{:S(2)}, u32[]{:S(2)}) collective-permute-start(bf16[256,512]{1,0:T(8,128)(2,1)} %bitcast.50), channel_id=1, source_target_pairs={{0,2},{1,3},{2,4},{3,5},{4,6},{5,7},{6,0},{7,1},{8,10},{9,11},{10,... | collective-permute-start | bytes 786440 | tf_op jit(solution)/shard_map/ppermute | solution.py:38
  5.4 7.7 %collective-permute-start.2 = (bf16[256,512]{1,0:T(8,128)(2,1)}, bf16[256,512]{1,0:T(8,128)(2,1)S(1)}, u32[]{:S(2)}, u32[]{:S(2)}) collective-permute-start(bf16[256,512]{1,0:T(8,128)(2,1)} %bitcast.51), channel_id=1, source_target_pairs={{0,6},{1,7},{2,0},{3,1},{4,2},{5,3},{6,4},{7,5},{8,14},{9,15},{10,... | collective-permute-start | bytes 786440 | tf_op jit(solution)/shard_map/ppermute | solution.py:38
  14.8 10.1 %collective-permute-start.3 = (bf16[1024,512]{1,0:T(8,128)(2,1)S(1)}, bf16[1024,512]{1,0:T(8,128)(2,1)S(1)}, u32[]{:S(2)}, u32[]{:S(2)}) collective-permute-start(bf16[1024,512]{1,0:T(8,128)(2,1)S(1)} %get-tuple-element.82.near_ref), channel_id=1, source_target_pairs={{0,1},{1,0},{2,3},{3,2},{4,5},{5,4},{6,7},{7,6},{8,9},{9,8},{10,11... | collective-permute-start | bytes 3145736 | tf_op jit(solution)/shard_map/ppermute | solution.py:38
  14.9 15.6 %collective-permute-start.4 = (bf16[384,512]{1,0:T(8,128)(2,1)S(1)}, bf16[384,512]{1,0:T(8,128)(2,1)S(1)}, u32[]{:S(2)}, u32[]{:S(2)}) collective-permute-start(bf16[384,512]{1,0:T(8,128)(2,1)S(1)} %get-tuple-element.84), channel_id=1, source_target_pairs={{0,2},{1,3},{2,4},{3,5},{4,6},{5,7},{6,0},{7,1},{8,10},{9,11},{10,... | collective-permute-start | bytes 1179656 | tf_op jit(solution)/shard_map/ppermute | solution.py:38
  16.5 14.0 %collective-permute-start.5 = (bf16[384,512]{1,0:T(8,128)(2,1)S(1)}, bf16[384,512]{1,0:T(8,128)(2,1)S(1)}, u32[]{:S(2)}, u32[]{:S(2)}) collective-permute-start(bf16[384,512]{1,0:T(8,128)(2,1)S(1)} %get-tuple-element.85), channel_id=1, source_target_pairs={{0,6},{1,7},{2,0},{3,1},{4,2},{5,3},{6,4},{7,5},{8,14},{9,15},{10,... | collective-permute-start | bytes 1179656 | tf_op jit(solution)/shard_map/ppermute | solution.py:38
  18.2 8.8 %collective-permute-start.6 = (bf16[128,512]{1,0:T(8,128)(2,1)S(1)}, bf16[128,512]{1,0:T(8,128)(2,1)S(1)}, u32[]{:S(2)}, u32[]{:S(2)}) collective-permute-start(bf16[128,512]{1,0:T(8,128)(2,1)S(1)} %get-tuple-element.86), channel_id=1, source_target_pairs={{0,14},{1,15},{2,8},{3,9},{4,10},{5,11},{6,12},{7,13},{8,6},{9,7},... | collective-permute-start | bytes 393224 | tf_op jit(solution)/shard_map/ppermute | solution.py:38
  19.9 9.1 %collective-permute-start.7 = (bf16[128,512]{1,0:T(8,128)(2,1)S(1)}, bf16[128,512]{1,0:T(8,128)(2,1)S(1)}, u32[]{:S(2)}, u32[]{:S(2)}) collective-permute-start(bf16[128,512]{1,0:T(8,128)(2,1)S(1)} %get-tuple-element.87), channel_id=1, source_target_pairs={{0,10},{1,11},{2,12},{3,13},{4,14},{5,15},{6,8},{7,9},{8,2},{9,3},... | collective-permute-start | bytes 393224 | tf_op jit(solution)/shard_map/ppermute | solution.py:38
  30.6 2.7 %collective-permute-start.8 = (bf16[1024,512]{1,0:T(8,128)(2,1)S(1)}, bf16[1024,512]{1,0:T(8,128)(2,1)S(1)}, u32[]{:S(2)}, u32[]{:S(2)}) collective-permute-start(bf16[1024,512]{1,0:T(8,128)(2,1)S(1)} %shard_map.98.far_ref), channel_id=1, source_target_pairs={{0,1},{1,0},{2,3},{3,2},{4,5},{5,4},{6,7},{7,6},{8,9},{9,8},{10,11... | collective-permute-start | bytes 3145736 | tf_op jit(solution)/shard_map/ppermute | solution.py:38
  33.3 21.2 %collective-permute-start.9 = (bf16[256,4096]{1,0:T(8,128)(2,1)}, bf16[256,4096]{1,0:T(8,128)(2,1)S(1)}, u32[]{:S(2)}, u32[]{:S(2)}) collective-permute-start(bf16[256,4096]{1,0:T(8,128)(2,1)} %shard_map.95), channel_id=1, source_target_pairs={{0,1},{1,0},{2,3},{3,2},{4,5},{5,4},{6,7},{7,6},{8,9},{9,8},{10,11... | collective-permute-start | bytes 6291464 | tf_op jit(solution)/shard_map/ppermute | solution.py:38
  34.8 2.9 %collective-permute-start.10 = (bf16[256,256]{1,0:T(8,128)(2,1)S(1)}, bf16[256,256]{1,0:T(8,128)(2,1)S(1)}, u32[]{:S(2)}, u32[]{:S(2)}) collective-permute-start(bf16[256,256]{1,0:T(8,128)(2,1)S(1)} %get-tuple-element.95.own_ref), channel_id=1, source_target_pairs={{0,1},{1,0},{2,3},{3,2},{4,5},{5,4},{6,7},{7,6},{8,9},{9,8},{10,11... | collective-permute-start | bytes 393224 | tf_op jit(solution)/shard_map/ppermute | solution.py:38
  35.2 15.3 %collective-permute-start.11 = (bf16[256,128]{1,0:T(8,128)(2,1)S(1)}, bf16[256,128]{1,0:T(8,128)(2,1)S(1)}, u32[]{:S(2)}, u32[]{:S(2)}) collective-permute-start(bf16[256,128]{1,0:T(8,128)(2,1)S(1)} %get-tuple-element.98), channel_id=1, source_target_pairs={{0,0},{1,2},{2,4},{3,6},{4,8},{5,10},{6,12},{7,14},{8,1},{9,3},{10... | collective-permute-start | bytes 196616 | tf_op jit(solution)/shard_map/ppermute | solution.py:701
  51.8 2.7 %collective-permute-start.12 = (bf16[256,512]{1,0:T(8,128)(2,1)S(1)}, bf16[256,512]{1,0:T(8,128)(2,1)S(1)}, u32[]{:S(2)}, u32[]{:S(2)}) collective-permute-start(bf16[256,512]{1,0:T(8,128)(2,1)S(1)} %get-tuple-element.99.own_ref), channel_id=1, source_target_pairs={{0,1},{1,0},{2,3},{3,2},{4,5},{5,4},{6,7},{7,6},{8,9},{9,8},{10,11... | collective-permute-start | bytes 786440 | tf_op jit(solution)/shard_map/ppermute | solution.py:38
  51.9 2.6 %collective-permute-start.13 = (f32[256,4]{1,0:T(8,128)S(1)}, f32[256,4]{1,0:T(8,128)S(1)}, u32[]{:S(2)}, u32[]{:S(2)}) collective-permute-start(f32[256,4]{1,0:T(8,128)S(1)} %get-tuple-element.100.own_level), channel_id=1, source_target_pairs={{0,1},{1,0},{2,3},{3,2},{4,5},{5,4},{6,7},{7,6},{8,9},{9,8},{10,11... | collective-permute-start | bytes 12296 | tf_op jit(solution)/shard_map/ppermute | solution.py:38
  57.1 16.4 %collective-permute-start.16 = (bf16[384,512]{1,0:T(8,128)(2,1)S(1)}, bf16[384,512]{1,0:T(8,128)(2,1)S(1)}, u32[]{:S(2)}, u32[]{:S(2)}) collective-permute-start(bf16[384,512]{1,0:T(8,128)(2,1)S(1)} %get-tuple-element.110), channel_id=1, source_target_pairs={{0,2},{1,3},{2,4},{3,5},{4,6},{5,7},{6,0},{7,1},{8,10},{9,11},{10,... | collective-permute-start | bytes 1179656 | tf_op jit(solution)/shard_map/ppermute | solution.py:38
  59.6 13.9 %collective-permute-start.17 = (bf16[384,512]{1,0:T(8,128)(2,1)S(1)}, bf16[384,512]{1,0:T(8,128)(2,1)S(1)}, u32[]{:S(2)}, u32[]{:S(2)}) collective-permute-start(bf16[384,512]{1,0:T(8,128)(2,1)S(1)} %get-tuple-element.111), channel_id=1, source_target_pairs={{0,6},{1,7},{2,0},{3,1},{4,2},{5,3},{6,4},{7,5},{8,14},{9,15},{10,... | collective-permute-start | bytes 1179656 | tf_op jit(solution)/shard_map/ppermute | solution.py:38
  61.0 7.0 %collective-permute-start.15 = (bf16[4,4,8,256]{3,2,1,0:T(8,128)(2,1)S(1)}, bf16[4,4,8,256]{3,2,1,0:T(8,128)(2,1)S(1)}, u32[]{:S(2)}, u32[]{:S(2)}) collective-permute-start(bf16[4,4,8,256]{3,2,1,0:T(8,128)(2,1)S(1)} %bitcast.64), channel_id=1, source_target_pairs={{0,64},{1,65},{2,66},{3,67},{4,68},{5,69},{6,70},{7,71},{8,72},{9,... | collective-permute-start | bytes 196616 | tf_op jit(solution)/shard_map/ppermute | solution.py:768
  62.3 10.1 %collective-permute-start.18 = (bf16[128,512]{1,0:T(8,128)(2,1)S(1)}, bf16[128,512]{1,0:T(8,128)(2,1)S(1)}, u32[]{:S(2)}, u32[]{:S(2)}) collective-permute-start(bf16[128,512]{1,0:T(8,128)(2,1)S(1)} %get-tuple-element.112), channel_id=1, source_target_pairs={{0,10},{1,11},{2,12},{3,13},{4,14},{5,15},{6,8},{7,9},{8,2},{9,3},... | collective-permute-start | bytes 393224 | tf_op jit(solution)/shard_map/ppermute | solution.py:38
  65.8 7.7 %collective-permute-start.19 = (bf16[128,512]{1,0:T(8,128)(2,1)S(1)}, bf16[128,512]{1,0:T(8,128)(2,1)S(1)}, u32[]{:S(2)}, u32[]{:S(2)}) collective-permute-start(bf16[128,512]{1,0:T(8,128)(2,1)S(1)} %get-tuple-element.113), channel_id=1, source_target_pairs={{0,14},{1,15},{2,8},{3,9},{4,10},{5,11},{6,12},{7,13},{8,6},{9,7},... | collective-permute-start | bytes 393224 | tf_op jit(solution)/shard_map/ppermute | solution.py:38
  68.1 11.7 %collective-permute-start.23 = (bf16[2,4,8,256]{3,2,1,0:T(8,128)(2,1)S(1)}, bf16[2,4,8,256]{3,2,1,0:T(8,128)(2,1)S(1)}, u32[]{:S(2)}, u32[]{:S(2)}) collective-permute-start(bf16[2,4,8,256]{3,2,1,0:T(8,128)(2,1)S(1)} %slice.42), channel_id=1, source_target_pairs={{0,32},{64,96},{1,33},{65,97},{2,34},{66,98},{3,35},{67,99},{4,36}... | collective-permute-start | bytes 98312 | tf_op jit(solution)/shard_map/ppermute | solution.py:787
  73.7 9.4 %collective-permute-start.20 = (bf16[256,512]{1,0:T(8,128)(2,1)S(1)}, bf16[256,512]{1,0:T(8,128)(2,1)S(1)}, u32[]{:S(2)}, u32[]{:S(2)}) collective-permute-start(bf16[256,512]{1,0:T(8,128)(2,1)S(1)} %get-tuple-element.114), channel_id=1, source_target_pairs={{0,2},{1,3},{2,4},{3,5},{4,6},{5,7},{6,0},{7,1},{8,10},{9,11},{10,... | collective-permute-start | bytes 786440 | tf_op jit(solution)/shard_map/ppermute | solution.py:38
  74.2 8.9 %collective-permute-start.21 = (bf16[256,512]{1,0:T(8,128)(2,1)S(1)}, bf16[256,512]{1,0:T(8,128)(2,1)S(1)}, u32[]{:S(2)}, u32[]{:S(2)}) collective-permute-start(bf16[256,512]{1,0:T(8,128)(2,1)S(1)} %get-tuple-element.115), channel_id=1, source_target_pairs={{0,6},{1,7},{2,0},{3,1},{4,2},{5,3},{6,4},{7,5},{8,14},{9,15},{10,... | collective-permute-start | bytes 786440 | tf_op jit(solution)/shard_map/ppermute | solution.py:38
  77.0 7.9 %collective-permute-start.22 = (bf16[256,512]{1,0:T(8,128)(2,1)S(1)}, bf16[256,512]{1,0:T(8,128)(2,1)S(1)}, u32[]{:S(2)}, u32[]{:S(2)}) collective-permute-start(bf16[256,512]{1,0:T(8,128)(2,1)S(1)} %get-tuple-element.116), channel_id=1, source_target_pairs={{0,8},{1,9},{2,10},{3,11},{4,12},{5,13},{6,14},{7,15},{8,0},{9,1},... | collective-permute-start | bytes 786440 | tf_op jit(solution)/shard_map/ppermute | solution.py:38
  79.8 2.7 %collective-permute-start.24 = (bf16[1,4,8,256]{3,2,1,0:T(8,128)(2,1)S(1)}, bf16[1,4,8,256]{3,2,1,0:T(8,128)(2,1)S(1)}, u32[]{:S(2)}, u32[]{:S(2)}) collective-permute-start(bf16[1,4,8,256]{3,2,1,0:T(8,128)(2,1)S(1)} %slice.44), channel_id=1, source_target_pairs={{0,16},{32,48},{64,80},{96,112},{1,17},{33,49},{65,81},{97,113},{2... | collective-permute-start | bytes 49160 | tf_op jit(solution)/shard_map/ppermute | solution.py:789
  (7 other events, 44.0 us)

commit v8 on v7

--- a/solution.py
+++ b/solution.py
@@ -357,20 +357,23 @@
     out_ref[...] = total_of(here_ref[...], from_last[...], from_next[...], from_partner[...])
 
 
+def fetch_kernel(source_ref, out_ref, sem):
+    copy = pltpu.make_async_copy(source_ref, out_ref, sem)
+    copy.start()
+    copy.wait()
+
+
 def join_kernel(
-    scalar_ref, own_ref, partner_ref, last_ref, next_ref, plus, minus, up, down, near, sem
+    scalar_ref, own_ref, partner_ref, last_ref, next_ref, plus, minus, up, down, near
 ):
-    own = pltpu.make_async_copy(own_ref, near.at[:TOK], sem)
-    own.start()
     plus[:TOK] = partner_ref[...]
     plus[TOK:] = last_ref[:HALF]
     minus[:TOK] = partner_ref[...]
     minus[TOK:] = next_ref[HALF:]
     up[...] = last_ref[HALF:]
     down[...] = next_ref[:HALF]
-    for index, ref in enumerate((last_ref, next_ref, partner_ref)):
-        near[(index + 1) * TOK : (index + 2) * TOK] = ref[...]
-    own.wait()
+    for index, ref in enumerate((own_ref, last_ref, next_ref, partner_ref)):
+        near[index * TOK : (index + 1) * TOK] = ref[...]
 
 
 def sides_kernel(mark_ref, last_ref, next_ref, upper_ref, lower_ref, sides):
@@ -640,15 +643,21 @@
     last_tokens, next_tokens = moved(tokens, 0, 1, 0), moved(tokens, 0, 3, 0)
     scalars, picks, positions = lax.optimization_barrier((scalars, picks, positions))
     cosine, sine = turns(positions)
+    (own_tokens,) = called(
+        fetch_kernel,
+        (shard,),
+        None,
+        streamed=(tokens,),
+        scratch=(pltpu.SemaphoreType.DMA(()),),
+    )
     plus, minus, up, down, near = called(
         join_kernel,
         (wide, wide, half, half, four),
         scalars,
+        own_tokens,
         partner_tokens,
         last_tokens,
         next_tokens,
-        streamed=(tokens,),
-        scratch=(pltpu.SemaphoreType.DMA(()),),
         flops=LONG,
     )
     from_last, from_next = moved(plus, 0, 1, 0), moved(minus, 0, 3, 0)

time: 86.1 us -> 85.1 us (0.988)
  waiting for transfers between devices: 14.4 us -> 13.3 us
    ppermute x21, waiting for transfers between devices: 12.9 us -> 11.9 us  [moved(): return lax.ppermute(shard, 'tp', pairs)]
    pallas_call x11 -> x12, Pallas kernels: 13.1 us -> 13.1 us  [called(): pl.pallas_call(kernel, in_specs=specs, out_specs=tuple((whole for _ in sh...]
where the time goes in v8:
time: 85.1 us; the launch traced here: 84.8 us
  starting transfers between devices  36.2 us (43%)
  Pallas kernels  28.2 us (33%)
  waiting for transfers between devices  13.3 us (16%)
  other arithmetic  4.22 us (5%)
  local copies, waits for them, and re-layouts  1.85 us (2%)
  between operations  1.01 us (1%)
    ppermute x21, starting transfers between devices, moved(): return lax.ppermute(shard, 'tp', pairs)  31.7 us
    pallas_call x12, Pallas kernels, called(): pl.pallas_call(kernel, in_specs=specs, out_specs=tuple((whole for _ in sh...  13.1 us
    pallas_call x1, Pallas kernels, prefill_part(): pl.pallas_call(prefill_kernel, in_specs=[small, small, whole, whole, ther...  12.9 us
    ppermute x21, waiting for transfers between devices, moved(): return lax.ppermute(shard, 'tp', pairs)  11.9 us
    pallas_call x1, Pallas kernels, cut_columns(): pl.pallas_call(cut_kernel, in_specs=[pl.BlockSpec(memory_space=pltpu.SMEM...  2.22 us
  transfers between devices with their start and end apart: 25, of which 13 were waited for; matrix products, arithmetic and copies ran while one was open for 6% of the time, Pallas kernels for 28%

profile of v8, /device:TPU:0, one launch (start us, length us, event | category | flops | bytes accessed | tf_op | source)
XLA Modules:
  0.0 84.8 jit_solution(18290611420661057526)
XLA Ops:
  0.6 3.2 %collective-permute-start = (bf16[256,512]{1,0:T(8,128)(2,1)}, bf16[256,512]{1,0:T(8,128)(2,1)S(1)}, u32[]{:S(2)}, u32[]{:S(2)}) collective-permute-start(bf16[256,512]{1,0:T(8,128)(2,1)} %bitcast.48), channel_id=1, source_target_pairs={{0,8},{1,9},{2,10},{3,11},{4,12},{5,13},{6,14},{7,15},{8,0},{9,1},... | collective-permute-start | bytes 786440 | tf_op jit(solution)/shard_map/ppermute | solution.py:38
  3.8 1.6 %collective-permute-start.1 = (bf16[256,512]{1,0:T(8,128)(2,1)}, bf16[256,512]{1,0:T(8,128)(2,1)S(1)}, u32[]{:S(2)}, u32[]{:S(2)}) collective-permute-start(bf16[256,512]{1,0:T(8,128)(2,1)} %bitcast.49), channel_id=1, source_target_pairs={{0,2},{1,3},{2,4},{3,5},{4,6},{5,7},{6,0},{7,1},{8,10},{9,11},{10,... | collective-permute-start | bytes 786440 | tf_op jit(solution)/shard_map/ppermute | solution.py:38
  5.4 1.7 %collective-permute-start.2 = (bf16[256,512]{1,0:T(8,128)(2,1)}, bf16[256,512]{1,0:T(8,128)(2,1)S(1)}, u32[]{:S(2)}, u32[]{:S(2)}) collective-permute-start(bf16[256,512]{1,0:T(8,128)(2,1)} %bitcast.50), channel_id=1, source_target_pairs={{0,6},{1,7},{2,0},{3,1},{4,2},{5,3},{6,4},{7,5},{8,14},{9,15},{10,... | collective-permute-start | bytes 786440 | tf_op jit(solution)/shard_map/ppermute | solution.py:38
  13.9 1.6 %collective-permute-start.4 = (bf16[384,512]{1,0:T(8,128)(2,1)S(1)}, bf16[384,512]{1,0:T(8,128)(2,1)S(1)}, u32[]{:S(2)}, u32[]{:S(2)}) collective-permute-start(bf16[384,512]{1,0:T(8,128)(2,1)S(1)} %get-tuple-element.84), channel_id=1, source_target_pairs={{0,2},{1,3},{2,4},{3,5},{4,6},{5,7},{6,0},{7,1},{8,10},{9,11},{10,... | collective-permute-start | bytes 1179656 | tf_op jit(solution)/shard_map/ppermute | solution.py:38
  15.5 1.7 %collective-permute-start.5 = (bf16[384,512]{1,0:T(8,128)(2,1)S(1)}, bf16[384,512]{1,0:T(8,128)(2,1)S(1)}, u32[]{:S(2)}, u32[]{:S(2)}) collective-permute-start(bf16[384,512]{1,0:T(8,128)(2,1)S(1)} %get-tuple-element.85), channel_id=1, source_target_pairs={{0,6},{1,7},{2,0},{3,1},{4,2},{5,3},{6,4},{7,5},{8,14},{9,15},{10,... | collective-permute-start | bytes 1179656 | tf_op jit(solution)/shard_map/ppermute | solution.py:38
  17.2 1.7 %collective-permute-start.6 = (bf16[128,512]{1,0:T(8,128)(2,1)S(1)}, bf16[128,512]{1,0:T(8,128)(2,1)S(1)}, u32[]{:S(2)}, u32[]{:S(2)}) collective-permute-start(bf16[128,512]{1,0:T(8,128)(2,1)S(1)} %get-tuple-element.86), channel_id=1, source_target_pairs={{0,14},{1,15},{2,8},{3,9},{4,10},{5,11},{6,12},{7,13},{8,6},{9,7},... | collective-permute-start | bytes 393224 | tf_op jit(solution)/shard_map/ppermute | solution.py:38
  18.9 2.7 %collective-permute-start.7 = (bf16[128,512]{1,0:T(8,128)(2,1)S(1)}, bf16[128,512]{1,0:T(8,128)(2,1)S(1)}, u32[]{:S(2)}, u32[]{:S(2)}) collective-permute-start(bf16[128,512]{1,0:T(8,128)(2,1)S(1)} %get-tuple-element.87), channel_id=1, source_target_pairs={{0,10},{1,11},{2,12},{3,13},{4,14},{5,15},{6,8},{7,9},{8,2},{9,3},... | collective-permute-start | bytes 393224 | tf_op jit(solution)/shard_map/ppermute | solution.py:38
  21.6 2.2 %shard_map.95 = bf16[256,4096]{1,0:T(8,128)(2,1)} custom-call(s32[43]{0:T(128)S(1)} %concatenate.12.scalar_ref, bf16[256,8192]{1,0:T(8,128)(2,1)S(1)} %copy-done.1), custom_call_target="tpu_custom_call" | custom-call | tf_op jit(solution)/shard_map/pallas_call | solution.py:578
  23.9 1.8 %shard_map.98 = (f32[256,256]{1,0:T(8,128)S(1)}, f32[256,128]{1,0:T(8,128)S(1)}, f32[8,128]{1,0:T(8,128)S(1)}) custom-call(s32[43]{0:T(128)S(1)} %concatenate.12.scalar_ref, bf16[8192,256]{1,0:T(8,128)(2,1)S(1)} %copy-done, bf16[8192,128]{1,0:T(8,128)(2,1)S(1)} %copy-done.3, bf16[1024,512]{1,0:T(8,128)(2,1)S(1)} %get-tuple-element.82.near_ref, ...), custom_call_target="tpu_custom_call" | custom-call | flops 805306368 | bytes 2097152 | tf_op jit(solution)/shard_map/pallas_call | solution.py:487
  26.0 2.1 %collective-permute-done.7.lower_ref = bf16[128,512]{1,0:T(8,128)(2,1)S(1)} collective-permute-done((bf16[128,512]{1,0:T(8,128)(2,1)S(1)}, bf16[128,512]{1,0:T(8,128)(2,1)S(1)}, u32[]{:S(2)}, u32[]{:S(2)}) %collective-permute-start.7) | collective-permute-done | bytes 131104 | tf_op jit(solution)/shard_map/ppermute | solution.py:38
  28.1 1.4 %collective-permute-done.4.last_ref = bf16[384,512]{1,0:T(8,128)(2,1)S(1)} collective-permute-done((bf16[384,512]{1,0:T(8,128)(2,1)S(1)}, bf16[384,512]{1,0:T(8,128)(2,1)S(1)}, u32[]{:S(2)}, u32[]{:S(2)}) %collective-permute-start.4) | collective-permute-done | bytes 393248 | tf_op jit(solution)/shard_map/ppermute | solution.py:38
  34.9 1.7 %collective-permute-done.10.other_ref = bf16[256,256]{1,0:T(8,128)(2,1)S(1)} collective-permute-done((bf16[256,256]{1,0:T(8,128)(2,1)S(1)}, bf16[256,256]{1,0:T(8,128)(2,1)S(1)}, u32[]{:S(2)}, u32[]{:S(2)}) %collective-permute-start.10) | collective-permute-done | bytes 131104 | tf_op jit(solution)/shard_map/ppermute | solution.py:38
  36.7 12.9 %conditional.1 = ((bf16[256,512]{1,0:T(8,128)(2,1)S(1)}, f32[256,4]{1,0:T(8,128)S(1)})) conditional(s32[]{:T(128)} %convert_element_type.8, (bf16[256,256]{1,0:T(8,128)(2,1)S(1)}, bf16[256,256]{1,0:T(8,128)(2,1)S(1)}, s32[43]{0:T(128)S(1)}, s32[64]{0:T(128)S(1)}, bf16[64,256,128]{2,1,0:T(8,128)(2,1)}, ...), branch_computations={%region_1.2_spmd, %region_2.3_spmd} | conditional | flops 524288 | bytes 2629656 | solution.py:713
  36.7 12.9 %branch_1_fun.1 = (bf16[256,512]{1,0:T(8,128)(2,1)S(1)}, f32[256,4]{1,0:T(8,128)S(1)}) custom-call(s32[43]{0:T(128)S(1)} %get-tuple-element.32.scalar_ref, s32[64]{0:T(128)S(1)} %get-tuple-element.33.length_ref, bf16[256,256]{1,0:T(8,128)(2,1)S(1)} %get-tuple-element.34.own_ref, bf16[256,256]{1,0:T(8,128)(2,1)S(1)} %get-tuple-element.35.other_ref, ...), custom_call_target="tpu_custom_call" | custom-call | tf_op jit(solution)/shard_map/cond/branch_1_fun/pallas_call | solution.py:510
  51.7 1.8 %shard_map.102 = (bf16[256,512]{1,0:T(8,128)(2,1)S(1)}, f32[256,4]{1,0:T(8,128)S(1)}) custom-call(s32[43]{0:T(128)S(1)} %concatenate.12.scalar_ref, bf16[256,256]{1,0:T(8,128)(2,1)S(1)} %get-tuple-element.95.own_ref, bf16[256,256]{1,0:T(8,128)(2,1)S(1)} %collective-permute-done.10.other_ref, bf16[256,128]{1,0:T(8,128)(2,1)S(1)} %collective-permute-done.11.held_ref, ...), custom_call_target="tpu_custom_call" | custom-call | flops 6000000000 | bytes 2097152 | tf_op jit(solution)/shard_map/pallas_call | solution.py:487
  53.5 2.6 %shard_map.103 = (bf16[384,512]{1,0:T(8,128)(2,1)S(1)}, bf16[384,512]{1,0:T(8,128)(2,1)S(1)}, bf16[128,512]{1,0:T(8,128)(2,1)S(1)}, bf16[128,512]{1,0:T(8,128)(2,1)S(1)}, bf16[256,512]{1,0:T(8,128)(2,1)S(1)}) custom-call(s32[43]{0:T(128)S(1)} %concatenate.12.scalar_ref, bf16[256,4096]{1,0:T(8,128)(2,1)S(1)} %collective-permute-done.9.swapped_ref, ...), custom_call_target="tpu_custom_call" | custom-call | flops 536870912 | bytes 2097152 | tf_op jit(solution)/shard_map/pallas_call | solution.py:487
  56.1 2.5 %collective-permute-start.16 = (bf16[384,512]{1,0:T(8,128)(2,1)S(1)}, bf16[384,512]{1,0:T(8,128)(2,1)S(1)}, u32[]{:S(2)}, u32[]{:S(2)}) collective-permute-start(bf16[384,512]{1,0:T(8,128)(2,1)S(1)} %get-tuple-element.110), channel_id=1, source_target_pairs={{0,2},{1,3},{2,4},{3,5},{4,6},{5,7},{6,0},{7,1},{8,10},{9,11},{10,... | collective-permute-start | bytes 1179656 | tf_op jit(solution)/shard_map/ppermute | solution.py:38
  61.4 3.5 %collective-permute-start.18 = (bf16[128,512]{1,0:T(8,128)(2,1)S(1)}, bf16[128,512]{1,0:T(8,128)(2,1)S(1)}, u32[]{:S(2)}, u32[]{:S(2)}) collective-permute-start(bf16[128,512]{1,0:T(8,128)(2,1)S(1)} %get-tuple-element.112), channel_id=1, source_target_pairs={{0,10},{1,11},{2,12},{3,13},{4,14},{5,15},{6,8},{7,9},{8,2},{9,3},... | collective-permute-start | bytes 393224 | tf_op jit(solution)/shard_map/ppermute | solution.py:38
  64.8 2.3 %collective-permute-start.19 = (bf16[128,512]{1,0:T(8,128)(2,1)S(1)}, bf16[128,512]{1,0:T(8,128)(2,1)S(1)}, u32[]{:S(2)}, u32[]{:S(2)}) collective-permute-start(bf16[128,512]{1,0:T(8,128)(2,1)S(1)} %get-tuple-element.113), channel_id=1, source_target_pairs={{0,14},{1,15},{2,8},{3,9},{4,10},{5,11},{6,12},{7,13},{8,6},{9,7},... | collective-permute-start | bytes 393224 | tf_op jit(solution)/shard_map/ppermute | solution.py:38
  68.4 1.9 %shard_map.104 = (bf16[256,512]{1,0:T(8,128)(2,1)S(1)}, bf16[256,512]{1,0:T(8,128)(2,1)S(1)}, bf16[256,512]{1,0:T(8,128)(2,1)S(1)}, bf16[256,512]{1,0:T(8,128)(2,1)S(1)}) custom-call(s32[43]{0:T(128)S(1)} %concatenate.12.scalar_ref, bf16[256,4096]{1,0:T(8,128)(2,1)S(1)} %collective-permute-done.9.swapped_ref, bf16[256,8192]{1,0:T(8,128)(2,1)S(1)} %copy-done.2, ...), custom_call_target="tpu_custom_call" | custom-call | flops 536870912 | bytes 2097152 | tf_op jit(solution)/shard_map/pallas_call | solution.py:487
  73.2 2.9 %collective-permute-start.21 = (bf16[256,512]{1,0:T(8,128)(2,1)S(1)}, bf16[256,512]{1,0:T(8,128)(2,1)S(1)}, u32[]{:S(2)}, u32[]{:S(2)}) collective-permute-start(bf16[256,512]{1,0:T(8,128)(2,1)S(1)} %get-tuple-element.115), channel_id=1, source_target_pairs={{0,6},{1,7},{2,0},{3,1},{4,2},{5,3},{6,4},{7,5},{8,14},{9,15},{10,... | collective-permute-start | bytes 786440 | tf_op jit(solution)/shard_map/ppermute | solution.py:38
  76.1 2.7 %collective-permute-start.22 = (bf16[256,512]{1,0:T(8,128)(2,1)S(1)}, bf16[256,512]{1,0:T(8,128)(2,1)S(1)}, u32[]{:S(2)}, u32[]{:S(2)}) collective-permute-start(bf16[256,512]{1,0:T(8,128)(2,1)S(1)} %get-tuple-element.116), channel_id=1, source_target_pairs={{0,8},{1,9},{2,10},{3,11},{4,12},{5,13},{6,14},{7,15},{8,0},{9,1},... | collective-permute-start | bytes 786440 | tf_op jit(solution)/shard_map/ppermute | solution.py:38
  80.1 1.4 %collective-permute-done.24 = bf16[1,4,8,256]{3,2,1,0:T(8,128)(2,1)S(1)} collective-permute-done((bf16[1,4,8,256]{3,2,1,0:T(8,128)(2,1)S(1)}, bf16[1,4,8,256]{3,2,1,0:T(8,128)(2,1)S(1)}, u32[]{:S(2)}, u32[]{:S(2)}) %collective-permute-start.24) | collective-permute-done | bytes 16416 | tf_op jit(solution)/shard_map/ppermute | solution.py:798
  82.2 1.8 %collective-permute-done.22.from_partner = bf16[256,512]{1,0:T(8,128)(2,1)S(1)} collective-permute-done((bf16[256,512]{1,0:T(8,128)(2,1)S(1)}, bf16[256,512]{1,0:T(8,128)(2,1)S(1)}, u32[]{:S(2)}, u32[]{:S(2)}) %collective-permute-start.22) | collective-permute-done | bytes 262176 | tf_op jit(solution)/shard_map/ppermute | solution.py:38
  (72 shorter events, 24.1 us)
Async XLA Ops:
  0.6 11.2 %collective-permute-start = (bf16[256,512]{1,0:T(8,128)(2,1)}, bf16[256,512]{1,0:T(8,128)(2,1)S(1)}, u32[]{:S(2)}, u32[]{:S(2)}) collective-permute-start(bf16[256,512]{1,0:T(8,128)(2,1)} %bitcast.48), channel_id=1, source_target_pairs={{0,8},{1,9},{2,10},{3,11},{4,12},{5,13},{6,14},{7,15},{8,0},{9,1},... | collective-permute-start | bytes 786440 | tf_op jit(solution)/shard_map/ppermute | solution.py:38
  3.8 9.3 %collective-permute-start.1 = (bf16[256,512]{1,0:T(8,128)(2,1)}, bf16[256,512]{1,0:T(8,128)(2,1)S(1)}, u32[]{:S(2)}, u32[]{:S(2)}) collective-permute-start(bf16[256,512]{1,0:T(8,128)(2,1)} %bitcast.49), channel_id=1, source_target_pairs={{0,2},{1,3},{2,4},{3,5},{4,6},{5,7},{6,0},{7,1},{8,10},{9,11},{10,... | collective-permute-start | bytes 786440 | tf_op jit(solution)/shard_map/ppermute | solution.py:38
  5.4 7.7 %collective-permute-start.2 = (bf16[256,512]{1,0:T(8,128)(2,1)}, bf16[256,512]{1,0:T(8,128)(2,1)S(1)}, u32[]{:S(2)}, u32[]{:S(2)}) collective-permute-start(bf16[256,512]{1,0:T(8,128)(2,1)} %bitcast.50), channel_id=1, source_target_pairs={{0,6},{1,7},{2,0},{3,1},{4,2},{5,3},{6,4},{7,5},{8,14},{9,15},{10,... | collective-permute-start | bytes 786440 | tf_op jit(solution)/shard_map/ppermute | solution.py:38
  13.8 10.1 %collective-permute-start.3 = (bf16[1024,512]{1,0:T(8,128)(2,1)S(1)}, bf16[1024,512]{1,0:T(8,128)(2,1)S(1)}, u32[]{:S(2)}, u32[]{:S(2)}) collective-permute-start(bf16[1024,512]{1,0:T(8,128)(2,1)S(1)} %get-tuple-element.82.near_ref), channel_id=1, source_target_pairs={{0,1},{1,0},{2,3},{3,2},{4,5},{5,4},{6,7},{7,6},{8,9},{9,8},{10,11... | collective-permute-start | bytes 3145736 | tf_op jit(solution)/shard_map/ppermute | solution.py:38
  13.9 15.6 %collective-permute-start.4 = (bf16[384,512]{1,0:T(8,128)(2,1)S(1)}, bf16[384,512]{1,0:T(8,128)(2,1)S(1)}, u32[]{:S(2)}, u32[]{:S(2)}) collective-permute-start(bf16[384,512]{1,0:T(8,128)(2,1)S(1)} %get-tuple-element.84), channel_id=1, source_target_pairs={{0,2},{1,3},{2,4},{3,5},{4,6},{5,7},{6,0},{7,1},{8,10},{9,11},{10,... | collective-permute-start | bytes 1179656 | tf_op jit(solution)/shard_map/ppermute | solution.py:38
  15.5 14.0 %collective-permute-start.5 = (bf16[384,512]{1,0:T(8,128)(2,1)S(1)}, bf16[384,512]{1,0:T(8,128)(2,1)S(1)}, u32[]{:S(2)}, u32[]{:S(2)}) collective-permute-start(bf16[384,512]{1,0:T(8,128)(2,1)S(1)} %get-tuple-element.85), channel_id=1, source_target_pairs={{0,6},{1,7},{2,0},{3,1},{4,2},{5,3},{6,4},{7,5},{8,14},{9,15},{10,... | collective-permute-start | bytes 1179656 | tf_op jit(solution)/shard_map/ppermute | solution.py:38
  17.2 8.8 %collective-permute-start.6 = (bf16[128,512]{1,0:T(8,128)(2,1)S(1)}, bf16[128,512]{1,0:T(8,128)(2,1)S(1)}, u32[]{:S(2)}, u32[]{:S(2)}) collective-permute-start(bf16[128,512]{1,0:T(8,128)(2,1)S(1)} %get-tuple-element.86), channel_id=1, source_target_pairs={{0,14},{1,15},{2,8},{3,9},{4,10},{5,11},{6,12},{7,13},{8,6},{9,7},... | collective-permute-start | bytes 393224 | tf_op jit(solution)/shard_map/ppermute | solution.py:38
  18.9 9.1 %collective-permute-start.7 = (bf16[128,512]{1,0:T(8,128)(2,1)S(1)}, bf16[128,512]{1,0:T(8,128)(2,1)S(1)}, u32[]{:S(2)}, u32[]{:S(2)}) collective-permute-start(bf16[128,512]{1,0:T(8,128)(2,1)S(1)} %get-tuple-element.87), channel_id=1, source_target_pairs={{0,10},{1,11},{2,12},{3,13},{4,14},{5,15},{6,8},{7,9},{8,2},{9,3},... | collective-permute-start | bytes 393224 | tf_op jit(solution)/shard_map/ppermute | solution.py:38
  29.6 2.7 %collective-permute-start.8 = (bf16[1024,512]{1,0:T(8,128)(2,1)S(1)}, bf16[1024,512]{1,0:T(8,128)(2,1)S(1)}, u32[]{:S(2)}, u32[]{:S(2)}) collective-permute-start(bf16[1024,512]{1,0:T(8,128)(2,1)S(1)} %shard_map.99.far_ref), channel_id=1, source_target_pairs={{0,1},{1,0},{2,3},{3,2},{4,5},{5,4},{6,7},{7,6},{8,9},{9,8},{10,11... | collective-permute-start | bytes 3145736 | tf_op jit(solution)/shard_map/ppermute | solution.py:38
  32.3 21.2 %collective-permute-start.9 = (bf16[256,4096]{1,0:T(8,128)(2,1)}, bf16[256,4096]{1,0:T(8,128)(2,1)S(1)}, u32[]{:S(2)}, u32[]{:S(2)}) collective-permute-start(bf16[256,4096]{1,0:T(8,128)(2,1)} %shard_map.95), channel_id=1, source_target_pairs={{0,1},{1,0},{2,3},{3,2},{4,5},{5,4},{6,7},{7,6},{8,9},{9,8},{10,11... | collective-permute-start | bytes 6291464 | tf_op jit(solution)/shard_map/ppermute | solution.py:38
  33.8 2.9 %collective-permute-start.10 = (bf16[256,256]{1,0:T(8,128)(2,1)S(1)}, bf16[256,256]{1,0:T(8,128)(2,1)S(1)}, u32[]{:S(2)}, u32[]{:S(2)}) collective-permute-start(bf16[256,256]{1,0:T(8,128)(2,1)S(1)} %get-tuple-element.95.own_ref), channel_id=1, source_target_pairs={{0,1},{1,0},{2,3},{3,2},{4,5},{5,4},{6,7},{7,6},{8,9},{9,8},{10,11... | collective-permute-start | bytes 393224 | tf_op jit(solution)/shard_map/ppermute | solution.py:38
  34.3 15.3 %collective-permute-start.11 = (bf16[256,128]{1,0:T(8,128)(2,1)S(1)}, bf16[256,128]{1,0:T(8,128)(2,1)S(1)}, u32[]{:S(2)}, u32[]{:S(2)}) collective-permute-start(bf16[256,128]{1,0:T(8,128)(2,1)S(1)} %get-tuple-element.98), channel_id=1, source_target_pairs={{0,0},{1,2},{2,4},{3,6},{4,8},{5,10},{6,12},{7,14},{8,1},{9,3},{10... | collective-permute-start | bytes 196616 | tf_op jit(solution)/shard_map/ppermute | solution.py:710
  50.8 2.7 %collective-permute-start.12 = (bf16[256,512]{1,0:T(8,128)(2,1)S(1)}, bf16[256,512]{1,0:T(8,128)(2,1)S(1)}, u32[]{:S(2)}, u32[]{:S(2)}) collective-permute-start(bf16[256,512]{1,0:T(8,128)(2,1)S(1)} %get-tuple-element.99.own_ref), channel_id=1, source_target_pairs={{0,1},{1,0},{2,3},{3,2},{4,5},{5,4},{6,7},{7,6},{8,9},{9,8},{10,11... | collective-permute-start | bytes 786440 | tf_op jit(solution)/shard_map/ppermute | solution.py:38
  50.9 2.6 %collective-permute-start.13 = (f32[256,4]{1,0:T(8,128)S(1)}, f32[256,4]{1,0:T(8,128)S(1)}, u32[]{:S(2)}, u32[]{:S(2)}) collective-permute-start(f32[256,4]{1,0:T(8,128)S(1)} %get-tuple-element.100.own_level), channel_id=1, source_target_pairs={{0,1},{1,0},{2,3},{3,2},{4,5},{5,4},{6,7},{7,6},{8,9},{9,8},{10,11... | collective-permute-start | bytes 12296 | tf_op jit(solution)/shard_map/ppermute | solution.py:38
  56.1 16.4 %collective-permute-start.16 = (bf16[384,512]{1,0:T(8,128)(2,1)S(1)}, bf16[384,512]{1,0:T(8,128)(2,1)S(1)}, u32[]{:S(2)}, u32[]{:S(2)}) collective-permute-start(bf16[384,512]{1,0:T(8,128)(2,1)S(1)} %get-tuple-element.110), channel_id=1, source_target_pairs={{0,2},{1,3},{2,4},{3,5},{4,6},{5,7},{6,0},{7,1},{8,10},{9,11},{10,... | collective-permute-start | bytes 1179656 | tf_op jit(solution)/shard_map/ppermute | solution.py:38
  58.7 13.9 %collective-permute-start.17 = (bf16[384,512]{1,0:T(8,128)(2,1)S(1)}, bf16[384,512]{1,0:T(8,128)(2,1)S(1)}, u32[]{:S(2)}, u32[]{:S(2)}) collective-permute-start(bf16[384,512]{1,0:T(8,128)(2,1)S(1)} %get-tuple-element.111), channel_id=1, source_target_pairs={{0,6},{1,7},{2,0},{3,1},{4,2},{5,3},{6,4},{7,5},{8,14},{9,15},{10,... | collective-permute-start | bytes 1179656 | tf_op jit(solution)/shard_map/ppermute | solution.py:38
  60.1 7.0 %collective-permute-start.15 = (bf16[4,4,8,256]{3,2,1,0:T(8,128)(2,1)S(1)}, bf16[4,4,8,256]{3,2,1,0:T(8,128)(2,1)S(1)}, u32[]{:S(2)}, u32[]{:S(2)}) collective-permute-start(bf16[4,4,8,256]{3,2,1,0:T(8,128)(2,1)S(1)} %bitcast.64), channel_id=1, source_target_pairs={{0,64},{1,65},{2,66},{3,67},{4,68},{5,69},{6,70},{7,71},{8,72},{9,... | collective-permute-start | bytes 196616 | tf_op jit(solution)/shard_map/ppermute | solution.py:777
  61.4 10.1 %collective-permute-start.18 = (bf16[128,512]{1,0:T(8,128)(2,1)S(1)}, bf16[128,512]{1,0:T(8,128)(2,1)S(1)}, u32[]{:S(2)}, u32[]{:S(2)}) collective-permute-start(bf16[128,512]{1,0:T(8,128)(2,1)S(1)} %get-tuple-element.112), channel_id=1, source_target_pairs={{0,10},{1,11},{2,12},{3,13},{4,14},{5,15},{6,8},{7,9},{8,2},{9,3},... | collective-permute-start | bytes 393224 | tf_op jit(solution)/shard_map/ppermute | solution.py:38
  64.8 7.7 %collective-permute-start.19 = (bf16[128,512]{1,0:T(8,128)(2,1)S(1)}, bf16[128,512]{1,0:T(8,128)(2,1)S(1)}, u32[]{:S(2)}, u32[]{:S(2)}) collective-permute-start(bf16[128,512]{1,0:T(8,128)(2,1)S(1)} %get-tuple-element.113), channel_id=1, source_target_pairs={{0,14},{1,15},{2,8},{3,9},{4,10},{5,11},{6,12},{7,13},{8,6},{9,7},... | collective-permute-start | bytes 393224 | tf_op jit(solution)/shard_map/ppermute | solution.py:38
  67.1 11.7 %collective-permute-start.23 = (bf16[2,4,8,256]{3,2,1,0:T(8,128)(2,1)S(1)}, bf16[2,4,8,256]{3,2,1,0:T(8,128)(2,1)S(1)}, u32[]{:S(2)}, u32[]{:S(2)}) collective-permute-start(bf16[2,4,8,256]{3,2,1,0:T(8,128)(2,1)S(1)} %slice.42), channel_id=1, source_target_pairs={{0,32},{64,96},{1,33},{65,97},{2,34},{66,98},{3,35},{67,99},{4,36}... | collective-permute-start | bytes 98312 | tf_op jit(solution)/shard_map/ppermute | solution.py:796
  72.8 9.4 %collective-permute-start.20 = (bf16[256,512]{1,0:T(8,128)(2,1)S(1)}, bf16[256,512]{1,0:T(8,128)(2,1)S(1)}, u32[]{:S(2)}, u32[]{:S(2)}) collective-permute-start(bf16[256,512]{1,0:T(8,128)(2,1)S(1)} %get-tuple-element.114), channel_id=1, source_target_pairs={{0,2},{1,3},{2,4},{3,5},{4,6},{5,7},{6,0},{7,1},{8,10},{9,11},{10,... | collective-permute-start | bytes 786440 | tf_op jit(solution)/shard_map/ppermute | solution.py:38
  73.2 8.9 %collective-permute-start.21 = (bf16[256,512]{1,0:T(8,128)(2,1)S(1)}, bf16[256,512]{1,0:T(8,128)(2,1)S(1)}, u32[]{:S(2)}, u32[]{:S(2)}) collective-permute-start(bf16[256,512]{1,0:T(8,128)(2,1)S(1)} %get-tuple-element.115), channel_id=1, source_target_pairs={{0,6},{1,7},{2,0},{3,1},{4,2},{5,3},{6,4},{7,5},{8,14},{9,15},{10,... | collective-permute-start | bytes 786440 | tf_op jit(solution)/shard_map/ppermute | solution.py:38
  76.1 7.9 %collective-permute-start.22 = (bf16[256,512]{1,0:T(8,128)(2,1)S(1)}, bf16[256,512]{1,0:T(8,128)(2,1)S(1)}, u32[]{:S(2)}, u32[]{:S(2)}) collective-permute-start(bf16[256,512]{1,0:T(8,128)(2,1)S(1)} %get-tuple-element.116), channel_id=1, source_target_pairs={{0,8},{1,9},{2,10},{3,11},{4,12},{5,13},{6,14},{7,15},{8,0},{9,1},... | collective-permute-start | bytes 786440 | tf_op jit(solution)/shard_map/ppermute | solution.py:38
  78.8 2.7 %collective-permute-start.24 = (bf16[1,4,8,256]{3,2,1,0:T(8,128)(2,1)S(1)}, bf16[1,4,8,256]{3,2,1,0:T(8,128)(2,1)S(1)}, u32[]{:S(2)}, u32[]{:S(2)}) collective-permute-start(bf16[1,4,8,256]{3,2,1,0:T(8,128)(2,1)S(1)} %slice.44), channel_id=1, source_target_pairs={{0,16},{32,48},{64,80},{96,112},{1,17},{33,49},{65,81},{97,113},{2... | collective-permute-start | bytes 49160 | tf_op jit(solution)/shard_map/ppermute | solution.py:798
  (7 other events, 42.0 us)

commit v9 on v8

--- a/solution.py
+++ b/solution.py
@@ -333,24 +333,17 @@
     return total.astype(jnp.bfloat16)
 
 
+def partner_kernel(partner_ref, from_last, from_next, partner):
+    partner[...] = total_of(partner_ref[...], from_last[:TOK], from_next[:TOK])
+
+
 def second_message_kernel(
-    arrived_ref,
-    next_ref,
-    last_ref,
-    partner_ref,
-    from_last,
-    from_next,
-    up,
-    down,
-    plus,
-    minus,
-    partner,
+    arrived_ref, sent_ref, next_ref, last_ref, from_last, from_next, up, down, plus, minus
 ):
     plus[:HALF] = total_of(next_ref[:HALF], from_last[TOK:], up[...])
     plus[HALF:] = next_ref[HALF:]
     minus[:HALF] = last_ref[:HALF]
     minus[HALF:] = total_of(last_ref[HALF:], from_next[TOK:], down[...])
-    partner[...] = total_of(partner_ref[...], from_last[:TOK], from_next[:TOK])
 
 
 def total_kernel(here_ref, from_last, from_next, from_partner, out_ref):
@@ -776,18 +769,18 @@
     blocks = blocks.reshape(group_count, slot_count, BS // 2, 2 * HD)
     arrived = lax.ppermute(blocks[4:], "group", [(0, 4)])
 
-    plus, minus, partner = called(
+    (partner,) = called(partner_kernel, (shard,), None, partner_part, from_last, from_next)
+    plus, minus = called(
         second_message_kernel,
-        (shard, shard, shard),
+        (shard, shard),
         None,
         next_part,
         last_part,
-        partner_part,
         from_last,
         from_next,
         up,
         down,
-        streamed=(arrived,),
+        streamed=(arrived, partner),
     )
     from_last, from_next = moved(plus, 0, 1, 0), moved(minus, 0, 3, 0)
     from_partner = moved(partner, 1, 0, 0)

time: 85.1 us -> 85.1 us (level)
    pallas_call x12 -> x13, Pallas kernels: 13.1 us -> 13.1 us  [called(): pl.pallas_call(kernel, in_specs=specs, out_specs=tuple((whole for _ in sh...]
  transfers between devices with their start and end apart: 25 -> 25, of which waited for: 13 -> 12; matrix products, arithmetic and copies ran while one was open for 6% -> 6% of each run, Pallas kernels for 28% -> 28%
where the time goes in v9:
time: 85.1 us; the launch traced here: 84.9 us
  starting transfers between devices  36.3 us (43%)
  Pallas kernels  28.2 us (33%)
  waiting for transfers between devices  13.3 us (16%)
  other arithmetic  4.22 us (5%)
  local copies, waits for them, and re-layouts  1.85 us (2%)
  between operations  1.01 us (1%)
    ppermute x21, starting transfers between devices, moved(): return lax.ppermute(shard, 'tp', pairs)  31.7 us
    pallas_call x13, Pallas kernels, called(): pl.pallas_call(kernel, in_specs=specs, out_specs=tuple((whole for _ in sh...  13.1 us
    pallas_call x1, Pallas kernels, prefill_part(): pl.pallas_call(prefill_kernel, in_specs=[small, small, whole, whole, ther...  12.9 us
    ppermute x21, waiting for transfers between devices, moved(): return lax.ppermute(shard, 'tp', pairs)  11.9 us
    pallas_call x1, Pallas kernels, cut_columns(): pl.pallas_call(cut_kernel, in_specs=[pl.BlockSpec(memory_space=pltpu.SMEM...  2.22 us
  transfers between devices with their start and end apart: 25, of which 12 were waited for; matrix products, arithmetic and copies ran while one was open for 6% of the time, Pallas kernels for 28%

profile of v9, /device:TPU:0, one launch (start us, length us, event | category | flops | bytes accessed | tf_op | source)
XLA Modules:
  0.0 84.9 jit_solution(1382186373187145328)
XLA Ops:
  0.6 3.2 %collective-permute-start = (bf16[256,512]{1,0:T(8,128)(2,1)}, bf16[256,512]{1,0:T(8,128)(2,1)S(1)}, u32[]{:S(2)}, u32[]{:S(2)}) collective-permute-start(bf16[256,512]{1,0:T(8,128)(2,1)} %bitcast.48), channel_id=1, source_target_pairs={{0,8},{1,9},{2,10},{3,11},{4,12},{5,13},{6,14},{7,15},{8,0},{9,1},... | collective-permute-start | bytes 786440 | tf_op jit(solution)/shard_map/ppermute | solution.py:38
  3.8 1.6 %collective-permute-start.1 = (bf16[256,512]{1,0:T(8,128)(2,1)}, bf16[256,512]{1,0:T(8,128)(2,1)S(1)}, u32[]{:S(2)}, u32[]{:S(2)}) collective-permute-start(bf16[256,512]{1,0:T(8,128)(2,1)} %bitcast.49), channel_id=1, source_target_pairs={{0,2},{1,3},{2,4},{3,5},{4,6},{5,7},{6,0},{7,1},{8,10},{9,11},{10,... | collective-permute-start | bytes 786440 | tf_op jit(solution)/shard_map/ppermute | solution.py:38
  5.4 1.7 %collective-permute-start.2 = (bf16[256,512]{1,0:T(8,128)(2,1)}, bf16[256,512]{1,0:T(8,128)(2,1)S(1)}, u32[]{:S(2)}, u32[]{:S(2)}) collective-permute-start(bf16[256,512]{1,0:T(8,128)(2,1)} %bitcast.50), channel_id=1, source_target_pairs={{0,6},{1,7},{2,0},{3,1},{4,2},{5,3},{6,4},{7,5},{8,14},{9,15},{10,... | collective-permute-start | bytes 786440 | tf_op jit(solution)/shard_map/ppermute | solution.py:38
  13.9 1.6 %collective-permute-start.4 = (bf16[384,512]{1,0:T(8,128)(2,1)S(1)}, bf16[384,512]{1,0:T(8,128)(2,1)S(1)}, u32[]{:S(2)}, u32[]{:S(2)}) collective-permute-start(bf16[384,512]{1,0:T(8,128)(2,1)S(1)} %get-tuple-element.83), channel_id=1, source_target_pairs={{0,2},{1,3},{2,4},{3,5},{4,6},{5,7},{6,0},{7,1},{8,10},{9,11},{10,... | collective-permute-start | bytes 1179656 | tf_op jit(solution)/shard_map/ppermute | solution.py:38
  15.5 1.7 %collective-permute-start.5 = (bf16[384,512]{1,0:T(8,128)(2,1)S(1)}, bf16[384,512]{1,0:T(8,128)(2,1)S(1)}, u32[]{:S(2)}, u32[]{:S(2)}) collective-permute-start(bf16[384,512]{1,0:T(8,128)(2,1)S(1)} %get-tuple-element.84), channel_id=1, source_target_pairs={{0,6},{1,7},{2,0},{3,1},{4,2},{5,3},{6,4},{7,5},{8,14},{9,15},{10,... | collective-permute-start | bytes 1179656 | tf_op jit(solution)/shard_map/ppermute | solution.py:38
  17.2 1.7 %collective-permute-start.6 = (bf16[128,512]{1,0:T(8,128)(2,1)S(1)}, bf16[128,512]{1,0:T(8,128)(2,1)S(1)}, u32[]{:S(2)}, u32[]{:S(2)}) collective-permute-start(bf16[128,512]{1,0:T(8,128)(2,1)S(1)} %get-tuple-element.85), channel_id=1, source_target_pairs={{0,14},{1,15},{2,8},{3,9},{4,10},{5,11},{6,12},{7,13},{8,6},{9,7},... | collective-permute-start | bytes 393224 | tf_op jit(solution)/shard_map/ppermute | solution.py:38
  18.9 2.7 %collective-permute-start.7 = (bf16[128,512]{1,0:T(8,128)(2,1)S(1)}, bf16[128,512]{1,0:T(8,128)(2,1)S(1)}, u32[]{:S(2)}, u32[]{:S(2)}) collective-permute-start(bf16[128,512]{1,0:T(8,128)(2,1)S(1)} %get-tuple-element.86), channel_id=1, source_target_pairs={{0,10},{1,11},{2,12},{3,13},{4,14},{5,15},{6,8},{7,9},{8,2},{9,3},... | collective-permute-start | bytes 393224 | tf_op jit(solution)/shard_map/ppermute | solution.py:38
  21.6 2.2 %shard_map.95 = bf16[256,4096]{1,0:T(8,128)(2,1)} custom-call(s32[43]{0:T(128)S(1)} %concatenate.12.scalar_ref, bf16[256,8192]{1,0:T(8,128)(2,1)S(1)} %copy-done.1), custom_call_target="tpu_custom_call" | custom-call | tf_op jit(solution)/shard_map/pallas_call | solution.py:571
  23.9 1.8 %shard_map.98 = (f32[256,256]{1,0:T(8,128)S(1)}, f32[256,128]{1,0:T(8,128)S(1)}, f32[8,128]{1,0:T(8,128)S(1)}) custom-call(s32[43]{0:T(128)S(1)} %concatenate.12.scalar_ref, bf16[8192,256]{1,0:T(8,128)(2,1)S(1)} %copy-done, bf16[8192,128]{1,0:T(8,128)(2,1)S(1)} %copy-done.3, bf16[1024,512]{1,0:T(8,128)(2,1)S(1)} %get-tuple-element.81.near_ref, ...), custom_call_target="tpu_custom_call" | custom-call | flops 805306368 | bytes 2097152 | tf_op jit(solution)/shard_map/pallas_call | solution.py:480
  26.0 2.1 %collective-permute-done.7.lower_ref = bf16[128,512]{1,0:T(8,128)(2,1)S(1)} collective-permute-done((bf16[128,512]{1,0:T(8,128)(2,1)S(1)}, bf16[128,512]{1,0:T(8,128)(2,1)S(1)}, u32[]{:S(2)}, u32[]{:S(2)}) %collective-permute-start.7) | collective-permute-done | bytes 131104 | tf_op jit(solution)/shard_map/ppermute | solution.py:38
  28.1 1.4 %collective-permute-done.4.last_ref = bf16[384,512]{1,0:T(8,128)(2,1)S(1)} collective-permute-done((bf16[384,512]{1,0:T(8,128)(2,1)S(1)}, bf16[384,512]{1,0:T(8,128)(2,1)S(1)}, u32[]{:S(2)}, u32[]{:S(2)}) %collective-permute-start.4) | collective-permute-done | bytes 393248 | tf_op jit(solution)/shard_map/ppermute | solution.py:38
  34.9 1.7 %collective-permute-done.10.other_ref = bf16[256,256]{1,0:T(8,128)(2,1)S(1)} collective-permute-done((bf16[256,256]{1,0:T(8,128)(2,1)S(1)}, bf16[256,256]{1,0:T(8,128)(2,1)S(1)}, u32[]{:S(2)}, u32[]{:S(2)}) %collective-permute-start.10) | collective-permute-done | bytes 131104 | tf_op jit(solution)/shard_map/ppermute | solution.py:38
  36.7 12.9 %conditional.1 = ((bf16[256,512]{1,0:T(8,128)(2,1)S(1)}, f32[256,4]{1,0:T(8,128)S(1)})) conditional(s32[]{:T(128)} %convert_element_type.8, (bf16[256,256]{1,0:T(8,128)(2,1)S(1)}, bf16[256,256]{1,0:T(8,128)(2,1)S(1)}, s32[43]{0:T(128)S(1)}, s32[64]{0:T(128)S(1)}, bf16[64,256,128]{2,1,0:T(8,128)(2,1)}, ...), branch_computations={%region_1.2_spmd, %region_2.3_spmd} | conditional | flops 524288 | bytes 2629656 | solution.py:706
  36.7 12.9 %branch_1_fun.1 = (bf16[256,512]{1,0:T(8,128)(2,1)S(1)}, f32[256,4]{1,0:T(8,128)S(1)}) custom-call(s32[43]{0:T(128)S(1)} %get-tuple-element.32.scalar_ref, s32[64]{0:T(128)S(1)} %get-tuple-element.33.length_ref, bf16[256,256]{1,0:T(8,128)(2,1)S(1)} %get-tuple-element.34.own_ref, bf16[256,256]{1,0:T(8,128)(2,1)S(1)} %get-tuple-element.35.other_ref, ...), custom_call_target="tpu_custom_call" | custom-call | tf_op jit(solution)/shard_map/cond/branch_1_fun/pallas_call | solution.py:503
  51.7 1.8 %shard_map.102 = (bf16[256,512]{1,0:T(8,128)(2,1)S(1)}, f32[256,4]{1,0:T(8,128)S(1)}) custom-call(s32[43]{0:T(128)S(1)} %concatenate.12.scalar_ref, bf16[256,256]{1,0:T(8,128)(2,1)S(1)} %get-tuple-element.94.own_ref, bf16[256,256]{1,0:T(8,128)(2,1)S(1)} %collective-permute-done.10.other_ref, bf16[256,128]{1,0:T(8,128)(2,1)S(1)} %collective-permute-done.11.held_ref, ...), custom_call_target="tpu_custom_call" | custom-call | flops 6000000000 | bytes 2097152 | tf_op jit(solution)/shard_map/pallas_call | solution.py:480
  53.5 2.6 %shard_map.103 = (bf16[384,512]{1,0:T(8,128)(2,1)S(1)}, bf16[384,512]{1,0:T(8,128)(2,1)S(1)}, bf16[128,512]{1,0:T(8,128)(2,1)S(1)}, bf16[128,512]{1,0:T(8,128)(2,1)S(1)}, bf16[256,512]{1,0:T(8,128)(2,1)S(1)}) custom-call(s32[43]{0:T(128)S(1)} %concatenate.12.scalar_ref, bf16[256,4096]{1,0:T(8,128)(2,1)S(1)} %collective-permute-done.9.swapped_ref, ...), custom_call_target="tpu_custom_call" | custom-call | flops 536870912 | bytes 2097152 | tf_op jit(solution)/shard_map/pallas_call | solution.py:480
  56.1 2.5 %collective-permute-start.16 = (bf16[384,512]{1,0:T(8,128)(2,1)S(1)}, bf16[384,512]{1,0:T(8,128)(2,1)S(1)}, u32[]{:S(2)}, u32[]{:S(2)}) collective-permute-start(bf16[384,512]{1,0:T(8,128)(2,1)S(1)} %get-tuple-element.107), channel_id=1, source_target_pairs={{0,2},{1,3},{2,4},{3,5},{4,6},{5,7},{6,0},{7,1},{8,10},{9,11},{10,... | collective-permute-start | bytes 1179656 | tf_op jit(solution)/shard_map/ppermute | solution.py:38
  61.4 3.5 %collective-permute-start.18 = (bf16[128,512]{1,0:T(8,128)(2,1)S(1)}, bf16[128,512]{1,0:T(8,128)(2,1)S(1)}, u32[]{:S(2)}, u32[]{:S(2)}) collective-permute-start(bf16[128,512]{1,0:T(8,128)(2,1)S(1)} %get-tuple-element.111), channel_id=1, source_target_pairs={{0,10},{1,11},{2,12},{3,13},{4,14},{5,15},{6,8},{7,9},{8,2},{9,3},... | collective-permute-start | bytes 393224 | tf_op jit(solution)/shard_map/ppermute | solution.py:38
  64.8 2.3 %collective-permute-start.19 = (bf16[128,512]{1,0:T(8,128)(2,1)S(1)}, bf16[128,512]{1,0:T(8,128)(2,1)S(1)}, u32[]{:S(2)}, u32[]{:S(2)}) collective-permute-start(bf16[128,512]{1,0:T(8,128)(2,1)S(1)} %get-tuple-element.112), channel_id=1, source_target_pairs={{0,14},{1,15},{2,8},{3,9},{4,10},{5,11},{6,12},{7,13},{8,6},{9,7},... | collective-permute-start | bytes 393224 | tf_op jit(solution)/shard_map/ppermute | solution.py:38
  68.4 1.9 %shard_map.104 = (bf16[256,512]{1,0:T(8,128)(2,1)S(1)}, bf16[256,512]{1,0:T(8,128)(2,1)S(1)}, bf16[256,512]{1,0:T(8,128)(2,1)S(1)}, bf16[256,512]{1,0:T(8,128)(2,1)S(1)}) custom-call(s32[43]{0:T(128)S(1)} %concatenate.12.scalar_ref, bf16[256,4096]{1,0:T(8,128)(2,1)S(1)} %collective-permute-done.9.swapped_ref, bf16[256,8192]{1,0:T(8,128)(2,1)S(1)} %copy-done.2, ...), custom_call_target="tpu_custom_call" | custom-call | flops 536870912 | bytes 2097152 | tf_op jit(solution)/shard_map/pallas_call | solution.py:480
  72.7 2.8 %collective-permute-start.22 = (bf16[256,512]{1,0:T(8,128)(2,1)S(1)}, bf16[256,512]{1,0:T(8,128)(2,1)S(1)}, u32[]{:S(2)}, u32[]{:S(2)}) collective-permute-start(bf16[256,512]{1,0:T(8,128)(2,1)S(1)} %shard_map.106.sent_ref), channel_id=1, source_target_pairs={{0,8},{1,9},{2,10},{3,11},{4,12},{5,13},{6,14},{7,15},{8,0},{9,1},... | collective-permute-start | bytes 786440 | tf_op jit(solution)/shard_map/ppermute | solution.py:38
  76.0 2.9 %collective-permute-start.21 = (bf16[256,512]{1,0:T(8,128)(2,1)S(1)}, bf16[256,512]{1,0:T(8,128)(2,1)S(1)}, u32[]{:S(2)}, u32[]{:S(2)}) collective-permute-start(bf16[256,512]{1,0:T(8,128)(2,1)S(1)} %get-tuple-element.114), channel_id=1, source_target_pairs={{0,6},{1,7},{2,0},{3,1},{4,2},{5,3},{6,4},{7,5},{8,14},{9,15},{10,... | collective-permute-start | bytes 786440 | tf_op jit(solution)/shard_map/ppermute | solution.py:38
  80.2 1.4 %collective-permute-done.24 = bf16[1,4,8,256]{3,2,1,0:T(8,128)(2,1)S(1)} collective-permute-done((bf16[1,4,8,256]{3,2,1,0:T(8,128)(2,1)S(1)}, bf16[1,4,8,256]{3,2,1,0:T(8,128)(2,1)S(1)}, u32[]{:S(2)}, u32[]{:S(2)}) %collective-permute-start.24) | collective-permute-done | bytes 16416 | tf_op jit(solution)/shard_map/ppermute | solution.py:791
  82.2 1.8 %collective-permute-done.20.from_last = bf16[256,512]{1,0:T(8,128)(2,1)S(1)} collective-permute-done((bf16[256,512]{1,0:T(8,128)(2,1)S(1)}, bf16[256,512]{1,0:T(8,128)(2,1)S(1)}, u32[]{:S(2)}, u32[]{:S(2)}) %collective-permute-start.20) | collective-permute-done | bytes 262176 | tf_op jit(solution)/shard_map/ppermute | solution.py:38
  (73 shorter events, 24.2 us)
Async XLA Ops:
  0.6 11.2 %collective-permute-start = (bf16[256,512]{1,0:T(8,128)(2,1)}, bf16[256,512]{1,0:T(8,128)(2,1)S(1)}, u32[]{:S(2)}, u32[]{:S(2)}) collective-permute-start(bf16[256,512]{1,0:T(8,128)(2,1)} %bitcast.48), channel_id=1, source_target_pairs={{0,8},{1,9},{2,10},{3,11},{4,12},{5,13},{6,14},{7,15},{8,0},{9,1},... | collective-permute-start | bytes 786440 | tf_op jit(solution)/shard_map/ppermute | solution.py:38
  3.8 9.3 %collective-permute-start.1 = (bf16[256,512]{1,0:T(8,128)(2,1)}, bf16[256,512]{1,0:T(8,128)(2,1)S(1)}, u32[]{:S(2)}, u32[]{:S(2)}) collective-permute-start(bf16[256,512]{1,0:T(8,128)(2,1)} %bitcast.49), channel_id=1, source_target_pairs={{0,2},{1,3},{2,4},{3,5},{4,6},{5,7},{6,0},{7,1},{8,10},{9,11},{10,... | collective-permute-start | bytes 786440 | tf_op jit(solution)/shard_map/ppermute | solution.py:38
  5.4 7.7 %collective-permute-start.2 = (bf16[256,512]{1,0:T(8,128)(2,1)}, bf16[256,512]{1,0:T(8,128)(2,1)S(1)}, u32[]{:S(2)}, u32[]{:S(2)}) collective-permute-start(bf16[256,512]{1,0:T(8,128)(2,1)} %bitcast.50), channel_id=1, source_target_pairs={{0,6},{1,7},{2,0},{3,1},{4,2},{5,3},{6,4},{7,5},{8,14},{9,15},{10,... | collective-permute-start | bytes 786440 | tf_op jit(solution)/shard_map/ppermute | solution.py:38
  13.8 10.1 %collective-permute-start.3 = (bf16[1024,512]{1,0:T(8,128)(2,1)S(1)}, bf16[1024,512]{1,0:T(8,128)(2,1)S(1)}, u32[]{:S(2)}, u32[]{:S(2)}) collective-permute-start(bf16[1024,512]{1,0:T(8,128)(2,1)S(1)} %get-tuple-element.81.near_ref), channel_id=1, source_target_pairs={{0,1},{1,0},{2,3},{3,2},{4,5},{5,4},{6,7},{7,6},{8,9},{9,8},{10,11... | collective-permute-start | bytes 3145736 | tf_op jit(solution)/shard_map/ppermute | solution.py:38
  13.9 15.6 %collective-permute-start.4 = (bf16[384,512]{1,0:T(8,128)(2,1)S(1)}, bf16[384,512]{1,0:T(8,128)(2,1)S(1)}, u32[]{:S(2)}, u32[]{:S(2)}) collective-permute-start(bf16[384,512]{1,0:T(8,128)(2,1)S(1)} %get-tuple-element.83), channel_id=1, source_target_pairs={{0,2},{1,3},{2,4},{3,5},{4,6},{5,7},{6,0},{7,1},{8,10},{9,11},{10,... | collective-permute-start | bytes 1179656 | tf_op jit(solution)/shard_map/ppermute | solution.py:38
  15.5 14.0 %collective-permute-start.5 = (bf16[384,512]{1,0:T(8,128)(2,1)S(1)}, bf16[384,512]{1,0:T(8,128)(2,1)S(1)}, u32[]{:S(2)}, u32[]{:S(2)}) collective-permute-start(bf16[384,512]{1,0:T(8,128)(2,1)S(1)} %get-tuple-element.84), channel_id=1, source_target_pairs={{0,6},{1,7},{2,0},{3,1},{4,2},{5,3},{6,4},{7,5},{8,14},{9,15},{10,... | collective-permute-start | bytes 1179656 | tf_op jit(solution)/shard_map/ppermute | solution.py:38
  17.2 8.8 %collective-permute-start.6 = (bf16[128,512]{1,0:T(8,128)(2,1)S(1)}, bf16[128,512]{1,0:T(8,128)(2,1)S(1)}, u32[]{:S(2)}, u32[]{:S(2)}) collective-permute-start(bf16[128,512]{1,0:T(8,128)(2,1)S(1)} %get-tuple-element.85), channel_id=1, source_target_pairs={{0,14},{1,15},{2,8},{3,9},{4,10},{5,11},{6,12},{7,13},{8,6},{9,7},... | collective-permute-start | bytes 393224 | tf_op jit(solution)/shard_map/ppermute | solution.py:38
  18.9 9.1 %collective-permute-start.7 = (bf16[128,512]{1,0:T(8,128)(2,1)S(1)}, bf16[128,512]{1,0:T(8,128)(2,1)S(1)}, u32[]{:S(2)}, u32[]{:S(2)}) collective-permute-start(bf16[128,512]{1,0:T(8,128)(2,1)S(1)} %get-tuple-element.86), channel_id=1, source_target_pairs={{0,10},{1,11},{2,12},{3,13},{4,14},{5,15},{6,8},{7,9},{8,2},{9,3},... | collective-permute-start | bytes 393224 | tf_op jit(solution)/shard_map/ppermute | solution.py:38
  29.6 2.7 %collective-permute-start.8 = (bf16[1024,512]{1,0:T(8,128)(2,1)S(1)}, bf16[1024,512]{1,0:T(8,128)(2,1)S(1)}, u32[]{:S(2)}, u32[]{:S(2)}) collective-permute-start(bf16[1024,512]{1,0:T(8,128)(2,1)S(1)} %shard_map.99.far_ref), channel_id=1, source_target_pairs={{0,1},{1,0},{2,3},{3,2},{4,5},{5,4},{6,7},{7,6},{8,9},{9,8},{10,11... | collective-permute-start | bytes 3145736 | tf_op jit(solution)/shard_map/ppermute | solution.py:38
  32.3 21.2 %collective-permute-start.9 = (bf16[256,4096]{1,0:T(8,128)(2,1)}, bf16[256,4096]{1,0:T(8,128)(2,1)S(1)}, u32[]{:S(2)}, u32[]{:S(2)}) collective-permute-start(bf16[256,4096]{1,0:T(8,128)(2,1)} %shard_map.95), channel_id=1, source_target_pairs={{0,1},{1,0},{2,3},{3,2},{4,5},{5,4},{6,7},{7,6},{8,9},{9,8},{10,11... | collective-permute-start | bytes 6291464 | tf_op jit(solution)/shard_map/ppermute | solution.py:38
  33.8 2.9 %collective-permute-start.10 = (bf16[256,256]{1,0:T(8,128)(2,1)S(1)}, bf16[256,256]{1,0:T(8,128)(2,1)S(1)}, u32[]{:S(2)}, u32[]{:S(2)}) collective-permute-start(bf16[256,256]{1,0:T(8,128)(2,1)S(1)} %get-tuple-element.94.own_ref), channel_id=1, source_target_pairs={{0,1},{1,0},{2,3},{3,2},{4,5},{5,4},{6,7},{7,6},{8,9},{9,8},{10,11... | collective-permute-start | bytes 393224 | tf_op jit(solution)/shard_map/ppermute | solution.py:38
  34.3 15.3 %collective-permute-start.11 = (bf16[256,128]{1,0:T(8,128)(2,1)S(1)}, bf16[256,128]{1,0:T(8,128)(2,1)S(1)}, u32[]{:S(2)}, u32[]{:S(2)}) collective-permute-start(bf16[256,128]{1,0:T(8,128)(2,1)S(1)} %get-tuple-element.97), channel_id=1, source_target_pairs={{0,0},{1,2},{2,4},{3,6},{4,8},{5,10},{6,12},{7,14},{8,1},{9,3},{10... | collective-permute-start | bytes 196616 | tf_op jit(solution)/shard_map/ppermute | solution.py:703
  50.8 2.7 %collective-permute-start.12 = (bf16[256,512]{1,0:T(8,128)(2,1)S(1)}, bf16[256,512]{1,0:T(8,128)(2,1)S(1)}, u32[]{:S(2)}, u32[]{:S(2)}) collective-permute-start(bf16[256,512]{1,0:T(8,128)(2,1)S(1)} %get-tuple-element.98.own_ref), channel_id=1, source_target_pairs={{0,1},{1,0},{2,3},{3,2},{4,5},{5,4},{6,7},{7,6},{8,9},{9,8},{10,11... | collective-permute-start | bytes 786440 | tf_op jit(solution)/shard_map/ppermute | solution.py:38
  50.9 2.6 %collective-permute-start.13 = (f32[256,4]{1,0:T(8,128)S(1)}, f32[256,4]{1,0:T(8,128)S(1)}, u32[]{:S(2)}, u32[]{:S(2)}) collective-permute-start(f32[256,4]{1,0:T(8,128)S(1)} %get-tuple-element.99.own_level), channel_id=1, source_target_pairs={{0,1},{1,0},{2,3},{3,2},{4,5},{5,4},{6,7},{7,6},{8,9},{9,8},{10,11... | collective-permute-start | bytes 12296 | tf_op jit(solution)/shard_map/ppermute | solution.py:38
  56.1 15.5 %collective-permute-start.16 = (bf16[384,512]{1,0:T(8,128)(2,1)S(1)}, bf16[384,512]{1,0:T(8,128)(2,1)S(1)}, u32[]{:S(2)}, u32[]{:S(2)}) collective-permute-start(bf16[384,512]{1,0:T(8,128)(2,1)S(1)} %get-tuple-element.107), channel_id=1, source_target_pairs={{0,2},{1,3},{2,4},{3,5},{4,6},{5,7},{6,0},{7,1},{8,10},{9,11},{10,... | collective-permute-start | bytes 1179656 | tf_op jit(solution)/shard_map/ppermute | solution.py:38
  58.7 13.9 %collective-permute-start.17 = (bf16[384,512]{1,0:T(8,128)(2,1)S(1)}, bf16[384,512]{1,0:T(8,128)(2,1)S(1)}, u32[]{:S(2)}, u32[]{:S(2)}) collective-permute-start(bf16[384,512]{1,0:T(8,128)(2,1)S(1)} %get-tuple-element.108), channel_id=1, source_target_pairs={{0,6},{1,7},{2,0},{3,1},{4,2},{5,3},{6,4},{7,5},{8,14},{9,15},{10,... | collective-permute-start | bytes 1179656 | tf_op jit(solution)/shard_map/ppermute | solution.py:38
  60.1 7.0 %collective-permute-start.15 = (bf16[4,4,8,256]{3,2,1,0:T(8,128)(2,1)S(1)}, bf16[4,4,8,256]{3,2,1,0:T(8,128)(2,1)S(1)}, u32[]{:S(2)}, u32[]{:S(2)}) collective-permute-start(bf16[4,4,8,256]{3,2,1,0:T(8,128)(2,1)S(1)} %bitcast.64), channel_id=1, source_target_pairs={{0,64},{1,65},{2,66},{3,67},{4,68},{5,69},{6,70},{7,71},{8,72},{9,... | collective-permute-start | bytes 196616 | tf_op jit(solution)/shard_map/ppermute | solution.py:770
  61.4 14.1 %collective-permute-start.18 = (bf16[128,512]{1,0:T(8,128)(2,1)S(1)}, bf16[128,512]{1,0:T(8,128)(2,1)S(1)}, u32[]{:S(2)}, u32[]{:S(2)}) collective-permute-start(bf16[128,512]{1,0:T(8,128)(2,1)S(1)} %get-tuple-element.111), channel_id=1, source_target_pairs={{0,10},{1,11},{2,12},{3,13},{4,14},{5,15},{6,8},{7,9},{8,2},{9,3},... | collective-permute-start | bytes 393224 | tf_op jit(solution)/shard_map/ppermute | solution.py:38
  64.8 10.6 %collective-permute-start.19 = (bf16[128,512]{1,0:T(8,128)(2,1)S(1)}, bf16[128,512]{1,0:T(8,128)(2,1)S(1)}, u32[]{:S(2)}, u32[]{:S(2)}) collective-permute-start(bf16[128,512]{1,0:T(8,128)(2,1)S(1)} %get-tuple-element.112), channel_id=1, source_target_pairs={{0,14},{1,15},{2,8},{3,9},{4,10},{5,11},{6,12},{7,13},{8,6},{9,7},... | collective-permute-start | bytes 393224 | tf_op jit(solution)/shard_map/ppermute | solution.py:38
  67.1 11.8 %collective-permute-start.23 = (bf16[2,4,8,256]{3,2,1,0:T(8,128)(2,1)S(1)}, bf16[2,4,8,256]{3,2,1,0:T(8,128)(2,1)S(1)}, u32[]{:S(2)}, u32[]{:S(2)}) collective-permute-start(bf16[2,4,8,256]{3,2,1,0:T(8,128)(2,1)S(1)} %slice.42), channel_id=1, source_target_pairs={{0,32},{64,96},{1,33},{65,97},{2,34},{66,98},{3,35},{67,99},{4,36}... | collective-permute-start | bytes 98312 | tf_op jit(solution)/shard_map/ppermute | solution.py:789
  72.7 11.3 %collective-permute-start.22 = (bf16[256,512]{1,0:T(8,128)(2,1)S(1)}, bf16[256,512]{1,0:T(8,128)(2,1)S(1)}, u32[]{:S(2)}, u32[]{:S(2)}) collective-permute-start(bf16[256,512]{1,0:T(8,128)(2,1)S(1)} %shard_map.106.sent_ref), channel_id=1, source_target_pairs={{0,8},{1,9},{2,10},{3,11},{4,12},{5,13},{6,14},{7,15},{8,0},{9,1},... | collective-permute-start | bytes 786440 | tf_op jit(solution)/shard_map/ppermute | solution.py:38
  75.6 8.4 %collective-permute-start.20 = (bf16[256,512]{1,0:T(8,128)(2,1)S(1)}, bf16[256,512]{1,0:T(8,128)(2,1)S(1)}, u32[]{:S(2)}, u32[]{:S(2)}) collective-permute-start(bf16[256,512]{1,0:T(8,128)(2,1)S(1)} %get-tuple-element.113), channel_id=1, source_target_pairs={{0,2},{1,3},{2,4},{3,5},{4,6},{5,7},{6,0},{7,1},{8,10},{9,11},{10,... | collective-permute-start | bytes 786440 | tf_op jit(solution)/shard_map/ppermute | solution.py:38
  76.0 8.0 %collective-permute-start.21 = (bf16[256,512]{1,0:T(8,128)(2,1)S(1)}, bf16[256,512]{1,0:T(8,128)(2,1)S(1)}, u32[]{:S(2)}, u32[]{:S(2)}) collective-permute-start(bf16[256,512]{1,0:T(8,128)(2,1)S(1)} %get-tuple-element.114), channel_id=1, source_target_pairs={{0,6},{1,7},{2,0},{3,1},{4,2},{5,3},{6,4},{7,5},{8,14},{9,15},{10,... | collective-permute-start | bytes 786440 | tf_op jit(solution)/shard_map/ppermute | solution.py:38
  78.9 2.7 %collective-permute-start.24 = (bf16[1,4,8,256]{3,2,1,0:T(8,128)(2,1)S(1)}, bf16[1,4,8,256]{3,2,1,0:T(8,128)(2,1)S(1)}, u32[]{:S(2)}, u32[]{:S(2)}) collective-permute-start(bf16[1,4,8,256]{3,2,1,0:T(8,128)(2,1)S(1)} %slice.44), channel_id=1, source_target_pairs={{0,16},{32,48},{64,80},{96,112},{1,17},{33,49},{65,81},{97,113},{2... | collective-permute-start | bytes 49160 | tf_op jit(solution)/shard_map/ppermute | solution.py:791
  (7 other events, 42.0 us)
